TPU v7x, 32 devices: a whole 2x2x4 slice. The times are simulated.
32 devices in a mesh: groups: 2 (over x), depth: 16 (over z, y, core).
Axes of the slice: x: 2, y: 2, z: 4, core: 2. Of those that a mesh axis runs over, the one named last changes fastest.
Arguments:
- field: bfloat16 [512, 32, 8192], P('depth', 'groups'), parts along dimension 1, may hold values from 0.049 to 5.05
- jitter: float32 [32, 8192], P('groups'), parts along dimension 0, may hold values from 0 to 1
- transfer: float32 [4], replicated, may hold values from 0.3 to 16
- depth_order: int32 [16], replicated, may hold values from 0 to 15, each once
- ray_start: int32 [128], replicated, may hold values from 0 to 255
- ray_end: int32 [128], replicated, may hold values from 256 to 512
Outputs:
- image: float32 [4, 32, 8192], P(None, 'groups', 'depth'), parts along dimension 1
There are 2 independent parts, one for each index of `groups`. A program takes and returns all parts, laid end to end along the dimension named above; an argument that names none is the same for every part. Nothing has to cross between parts.
Inputs may be any that keep to these rules, and one draw needn't show every extreme that they name: `depth_order`: a permutation of the slab indices.
All inputs are finite; a program needn't handle non-finite values.
Results may differ from a plain program's by a relative error of at most 0.0003.
Values may be sent and summed in bfloat16 or wider, within the bound.
No kernel may reach another device: no remote copies, remote signals or barrier semaphores. Data moves between devices by JAX's collectives and lax.ppermute only.
A program may use at most 128 MiB of HBM per device.

v0:
```python
import jax
import jax.numpy as jnp
from jax import lax
from jax.sharding import PartitionSpec as P


def shifted(value, axis, steps):
    count = lax.axis_size(axis)
    initial, last = (max(0, -steps), min(count, count - steps))
    return lax.ppermute(value, axis, [(source, source + steps) for source in range(initial, last)])


def slab_partial(planes, following, jitter, transfer, start_cols, end_cols, base, total):
    slab_len = planes.shape[0]
    lower = planes.astype(jnp.float32)
    upper = jnp.concatenate([lower[1:], following.astype(jnp.float32)[None]], axis=0)
    value = (1.0 - jitter)[None] * lower + jitter[None] * upper
    sample = base + jnp.arange(slab_len, dtype=jnp.int32)[:, None, None]
    active = (sample >= start_cols) & (sample < end_cols)
    tau = jnp.where(active, transfer[3] * 0.2 / total * value, jnp.float32(0.0))
    before = jnp.cumsum(tau, axis=0) - tau
    weight = jnp.exp(-before) * (1.0 - jnp.exp(-tau))
    red = jnp.sum(weight * (value / (transfer[0] + value)), axis=0)
    green = jnp.sum(weight * (value / (transfer[1] + value)), axis=0)
    blue = jnp.sum(weight * (value / (transfer[2] + value)), axis=0)
    depth_sum = jnp.sum(tau, axis=0)
    return jnp.stack([red, green, blue, depth_sum], axis=0)


def on_device(field, jitter, transfer, depth_order, ray_start, ray_end):
    count = lax.axis_size("depth")
    here = lax.axis_index("depth")
    slab_len = field.shape[0]
    rows = field.shape[1]
    cols = field.shape[2]
    width = cols // count
    total = slab_len * count
    ntiles = ray_start.shape[0]
    tile_cols = cols // ntiles
    following = shifted(field[0], "depth", -1)
    start_cols = jnp.broadcast_to(ray_start[:, None], (ntiles, tile_cols)).reshape(1, 1, cols)
    end_cols = jnp.broadcast_to(ray_end[:, None], (ntiles, tile_cols)).reshape(1, 1, cols)
    base = here * slab_len
    partial_value = slab_partial(
        field, following, jitter, transfer, start_cols, end_cols, base, total
    )
    pieces = partial_value.reshape(4, rows, count, width)
    received = lax.all_to_all(pieces, "depth", split_axis=2, concat_axis=2, tiled=True)
    ranks = jnp.arange(count, dtype=jnp.int32)
    matches = (depth_order[:, None] == ranks[None, :]).astype(jnp.int32)
    slab_rank = jnp.sum(matches * ranks[:, None], axis=0)
    ahead = (slab_rank[None, :] < slab_rank[:, None]).astype(jnp.float32)
    depths = received[3]
    prefix = jnp.einsum("st,rtw->rsw", ahead, depths, precision=lax.Precision.HIGHEST)
    color = jnp.sum(jnp.exp(-prefix)[None] * received[:3], axis=2)
    alpha = 1.0 - jnp.exp(-jnp.sum(depths, axis=1))
    return jnp.concatenate([color, alpha[None]], axis=0)


def solution(mesh):
    in_specs = (P("depth", "groups", None), P("groups", None), P(), P(), P(), P())
    out_specs = P(None, "groups", "depth")
    return jax.shard_map(
        on_device, mesh=mesh, in_specs=in_specs, out_specs=out_specs, check_vma=False
    )
```

profile of v0, /device:TPU:13, one launch (start us, length us, event | category | flops | bytes accessed | tf_op | source)
XLA Modules:
  0.0 107.5 jit_solution(15801988287014618856)
XLA Ops:
  0.0 1.0 slice_bitcast_fusion
  1.0 2.6 %collective-permute-start = (bf16[16,8192]{1,0:T(8,128)(2,1)S(1)}, bf16[16,8192]{1,0:T(8,128)(2,1)S(1)}, u32[]{:S(2)}, u32[]{:S(2)}) collective-permute-start(bf16[16,8192]{1,0:T(8,128)(2,1)S(1)} %slice_bitcast_fusion), channel_id=1, source_target_pairs={{1,0},{2,1},{3,2},{4,3},{5,4},{6,5},{7,6},{8,7},{9,8},{10,9},{11,1... | collective-permute-start | bytes 786440 | tf_op jit(solution)/shard_map/ppermute | solution.py:10
  3.6 1.1 %broadcast_subtract_fusion = f32[16,8192]{1,0:T(8,128)S(1)} fusion(f32[16,8192]{1,0:T(8,128)} %param.7), kind=kLoop, calls=%fused_computation.28 | loop fusion | flops 131072 | bytes 1048576 | tf_op jit(solution)/shard_map/sub | solution.py:17
  4.6 0.7 broadcast_in_dim.21
  5.4 0.1 ge.21
  5.5 0.7 broadcast_in_dim.22
  6.2 0.1 lt.31
  6.3 0.3 compare_and_fusion
  6.6 0.0 copy-start.1
  6.6 0.0 copy-start
  6.6 11.1 %slice.32 = f32[31,16,8192]{2,1,0:T(8,128)} slice(bf16[32,16,8192]{2,1,0:T(8,128)(2,1)} %param.6), slice={[1:32], [0:16], [0:8192]} | slice | bytes 32505856 | tf_op jit(solution)/shard_map/slice | solution.py:16
  17.7 0.0 copy-done.1
  17.7 0.6 fusion.21
  18.9 0.0 collective-permute-done
  18.9 0.0 copy-done
  18.9 29.0 %fusion.6 = (f32[16,8192]{1,0:T(8,128)S(1)}, f32[16,8192]{1,0:T(8,128)S(1)}, f32[16,8192]{1,0:T(8,128)S(1)}, f32[16,8192]{1,0:T(8,128)S(1)}) fusion(f32[]{:T(128)} %bitcast.3, f32[]{:T(128)} %bitcast.5, f32[]{:T(128)} %bitcast.4, f32[]{:T(128)} %bitcast, pred[32,8192]{1,0:T(8,128)(4,1)S(1)} %compare_and_fusion, f32[1,16,8192]{2,1,0:T(8,128)S(1)} %bitcast_convert_fusion, ...), kind=kOutput, calls=%fused_computation.12 | output fusion | flops 263716864 | bytes 28573712 | tf_op jit(solution)/shard_map/jit(cumsum)/reduce_window_sum | solution.py:21
  47.9 0.0 copy-start.2
  48.0 0.3 copy.17
  48.3 0.3 copy.18
  48.6 0.3 copy.19
  48.9 0.3 copy.20
  49.2 0.3 pad_maximum_fusion
  49.5 2.6 %copy.12 = f32[4,16,16,512]{3,1,0,2:T(8,128)} copy(f32[4,16,16,512]{3,2,1,0:T(8,128)S(1)} %pad_maximum_fusion) | data formatting | bytes 4194304 | tf_op jit(solution)/shard_map/stack | solution.py:27
  52.1 6.0 %all-to-all-start = ((f32[4,16,16,512]{3,1,0,2:T(8,128)}), f32[4,16,16,512]{3,1,0,2:T(8,128)S(1)}, u32[]{:S(2)}, u32[]{:S(2)}) async-start(f32[4,16,16,512]{3,1,0,2:T(8,128)} %copy.12), calls=%async_computation | async-start | bytes 4194304 | tf_op jit(solution)/shard_map/all_to_all | solution.py:48
  58.1 0.0 copy-done.2
  58.1 0.1 select_reduce_fusion
  58.2 47.3 %all-to-all-done = f32[4,16,16,512]{3,1,0,2:T(8,128)S(1)} async-done(((f32[4,16,16,512]{3,1,0,2:T(8,128)}), f32[4,16,16,512]{3,1,0,2:T(8,128)S(1)}, u32[]{:S(2)}, u32[]{:S(2)}) %all-to-all-start) | async-done | bytes 2097184 | tf_op jit(solution)/shard_map/all_to_all | solution.py:48
  105.5 0.1 fusion.20
  105.6 0.7 fusion.14
  106.3 0.3 copy.14
  106.6 0.3 fusion.12
  106.9 0.7 pad_maximum_fusion.1
  (3 shorter events, 0.1 us)
Async XLA Ops:
  1.0 17.9 %collective-permute-start = (bf16[16,8192]{1,0:T(8,128)(2,1)S(1)}, bf16[16,8192]{1,0:T(8,128)(2,1)S(1)}, u32[]{:S(2)}, u32[]{:S(2)}) collective-permute-start(bf16[16,8192]{1,0:T(8,128)(2,1)S(1)} %slice_bitcast_fusion), channel_id=1, source_target_pairs={{1,0},{2,1},{3,2},{4,3},{5,4},{6,5},{7,6},{8,7},{9,8},{10,9},{11,1... | collective-permute-start | bytes 786440 | tf_op jit(solution)/shard_map/ppermute | solution.py:10
  6.6 11.1 %copy-start.1 = (f32[4]{0:T(128)S(1)}, f32[4]{0:T(128)}, u32[]{:S(2)}) copy-start(f32[4]{0:T(128)} %param.8) | copy-start | bytes 52
  6.6 12.3 %copy-start = (f32[16,8192]{1,0:T(8,128)S(1)}, f32[16,8192]{1,0:T(8,128)}, u32[]{:S(2)}) copy-start(f32[16,8192]{1,0:T(8,128)} %param.7) | copy-start | bytes 1572868
  47.9 10.2 %copy-start.2 = (s32[16]{0:T(128)S(1)}, s32[16]{0:T(128)}, u32[]{:S(2)}) copy-start(s32[16]{0:T(128)} %param.9) | copy-start | bytes 196
  52.1 53.4 %all-to-all-start = ((f32[4,16,16,512]{3,1,0,2:T(8,128)}), f32[4,16,16,512]{3,1,0,2:T(8,128)S(1)}, u32[]{:S(2)}, u32[]{:S(2)}) async-start(f32[4,16,16,512]{3,1,0,2:T(8,128)} %copy.12), calls=%async_computation | async-start | bytes 4194304 | tf_op jit(solution)/shard_map/all_to_all | solution.py:48
where the time goes:
time: 108 us
  waiting for transfers between devices  47.3 us (44%)
  other arithmetic  31.8 us (29%)
  local copies, waits for them, and re-layouts  18.4 us (17%)
  starting transfers between devices  8.59 us (8%)
    all_to_all x1, waiting for transfers between devices, on_device(): lax.all_to_all(pieces, 'depth', split_axis=2, concat_axis=2, tiled=True)  47.3 us
    another operation x1, other arithmetic, slab_partial(): before = jnp.cumsum(tau, axis=0) - tau  29 us
    slice x1, local copies, waits for them, and re-layouts, slab_partial(): lower[1:]  11.1 us
    all_to_all x1, starting transfers between devices, on_device(): lax.all_to_all(pieces, 'depth', split_axis=2, concat_axis=2, tiled=True)  6.01 us
    ppermute x1, starting transfers between devices, shifted(): lax.ppermute(value, axis, [(source, source + steps) for source in range(i...  2.58 us
    another operation x1, local copies, waits for them, and re-layouts, slab_partial(): return jnp.stack([red, green, blue, depth_sum], axis=0)  2.57 us
  transfers between devices with their start and end apart: 2, of which 1 were waited for; matrix products, arithmetic and copies ran while one was open for 14% of the time, Pallas kernels for 0%

commit v1 on v0

v1 whole, which is shorter than its diff:
```python
import functools
import math

import jax
import jax.numpy as jnp
from jax import lax
from jax.experimental import pallas as pl
from jax.experimental.pallas import tpu as pltpu
from jax.sharding import PartitionSpec as P

TOP = 5.2
LOG2E = math.log2(math.e)
LANES = 128


def spans(slab_len):
    deep = math.log2(slab_len)
    return 6.8 + deep, 13.2 + deep


def shifted(value, axis, steps):
    count = lax.axis_size(axis)
    initial, last = (max(0, -steps), min(count, count - steps))
    return lax.ppermute(value, axis, [(source, source + steps) for source in range(initial, last)])


def encode(value, span):
    code = jnp.log2(value) * (65535.0 / span) + 65535.5
    code = jnp.minimum(jnp.maximum(code, 0.0), 65535.0)
    return (code.astype(jnp.int32) - 32768).astype(jnp.int16)


def slab_kernel(total, tile_cols, chunk, chunks, base_ref, transfer_ref, start_ref, end_ref, field_ref, halo_ref,
                jitter_ref, out_ref, gain_ref):
    slab_len, rows, width = field_ref.shape
    base = base_ref[0]
    first_col = (pl.program_id(0) * chunks + chunk) * width
    depth_gain = jnp.full((rows, LANES), transfer_ref[3]) * (0.2 / total)
    levels = [jnp.full((rows, LANES), transfer_ref[i]) for i in range(3)]
    depth_unit = 1.0 / (depth_gain * (slab_len * TOP))
    color_unit = [depth_unit * ((levels[i] + TOP) * (1.0 / TOP)) for i in range(3)]
    depth_span, color_span = spans(slab_len)
    sample = lax.broadcasted_iota(jnp.int32, (8, LANES), 0) + base
    lane = lax.broadcasted_iota(jnp.int32, (8, LANES), 1)
    tile_gain = depth_gain[:8] * -LOG2E

    def block(n, carry):
        cols = pl.ds(pl.multiple_of(n * LANES, LANES), LANES)
        tile = (first_col + n * LANES) // tile_cols
        start = jnp.full((8, LANES), start_ref[tile])
        end = jnp.full((8, LANES), end_ref[tile])
        for t in range(1, LANES // tile_cols):
            start = jnp.where(lane >= t * tile_cols, start_ref[tile + t], start)
            end = jnp.where(lane >= t * tile_cols, end_ref[tile + t], end)
        for k in range(0, slab_len, 8):
            active = (sample + k >= start) & (sample + k < end)
            gain_ref[k:k + 8, :] = jnp.where(active, tile_gain, 0.0)
        jitter = jitter_ref[:, cols]
        stay = 1.0 - jitter
        lower = field_ref[0, :, cols].astype(jnp.float32)
        before = jnp.zeros((rows, LANES), jnp.float32)
        through = jnp.ones((rows, LANES), jnp.float32)
        sums = [jnp.zeros((rows, LANES), jnp.float32) for _ in range(3)]
        for k in range(slab_len):
            following = field_ref[k + 1, :, cols] if k + 1 < slab_len else halo_ref[:, cols]
            upper = following.astype(jnp.float32)
            value = stay * lower + jitter * upper
            before = before + gain_ref[k:k + 1, :] * value
            beyond = jnp.exp2(before)
            emitted = (through - beyond) * value
            for i in range(3):
                sums[i] = sums[i] + emitted * pl.reciprocal(levels[i] + value, approx=True)
            through = beyond
            lower = upper
        for i in range(3):
            out_ref[0, i, :, cols] = encode(sums[i] * color_unit[i], color_span)
        out_ref[0, 3, :, cols] = encode(before * (depth_unit * (-1.0 / LOG2E)), depth_span)
        return carry

    lax.fori_loop(0, width // LANES, block, 0)


def slab_codes(field, halo, jitter, transfer, ray_start, ray_end, base, total, pieces, chunk, chunks):
    slab_len, rows, cols = field.shape
    width = cols // (pieces * chunks)
    tile_cols = cols // ray_start.shape[0]
    smem = pl.BlockSpec(memory_space=pltpu.SMEM)
    return pl.pallas_call(
        functools.partial(slab_kernel, total, tile_cols, chunk, chunks),
        grid=(pieces,),
        in_specs=[
            smem, smem, smem, smem,
            pl.BlockSpec((slab_len, rows, width), lambda p: (0, 0, p * chunks + chunk)),
            pl.BlockSpec((rows, width), lambda p: (0, p * chunks + chunk)),
            pl.BlockSpec((rows, width), lambda p: (0, p * chunks + chunk)),
        ],
        out_specs=pl.BlockSpec((1, 4, rows, width), lambda p: (p, 0, 0, 0)),
        out_shape=jax.ShapeDtypeStruct((pieces, 4, rows, width), jnp.int16),
        scratch_shapes=[pltpu.VMEM((slab_len, LANES), jnp.float32)],
        compiler_params=pltpu.CompilerParams(vmem_limit_bytes=32 * 1024 * 1024),
        cost_estimate=pl.CostEstimate(
            flops=slab_len * rows * width * pieces * 20,
            bytes_accessed=slab_len * rows * width * pieces * 2,
            transcendentals=slab_len * rows * width * pieces * 4,
        ),
        name="slab_codes",
    )(base, transfer, ray_start, ray_end, field, halo, jitter)


def composite_kernel(total, slab_len, chunks, order_ref, transfer_ref, *refs):
    code_refs, out_ref = refs[:chunks], refs[chunks]
    count, _, rows, width = code_refs[0].shape
    lanes = min(width, LANES)
    depth_span, color_span = spans(slab_len)
    depth_gain = jnp.full((rows, lanes), transfer_ref[3]) * (0.2 / total)
    unit = depth_gain * (slab_len * TOP)
    depth_unit = unit * LOG2E

    def decode(codes, span, shift):
        code = codes.astype(jnp.int32).astype(jnp.float32)
        value = jnp.exp2(code * (span / 65535.0) + (span * (32768.0 / 65535.0) - span) - shift)
        return jnp.where(code > -32768.0, value, 0.0)

    for c in range(chunks):
        for n in range(width // lanes):
            cols = slice(n * lanes, (n + 1) * lanes)

            def step(j, carry):
                depth, red, green, blue = carry
                slab = order_ref[j]
                colors = [red, green, blue]
                for i in range(3):
                    colors[i] = colors[i] + decode(code_refs[c][slab, i, :, cols], color_span, depth)
                depth = depth + depth_unit * decode(code_refs[c][slab, 3, :, cols], depth_span, 0.0)
                return depth, *colors

            zero = jnp.zeros((rows, lanes), jnp.float32)
            depth, *colors = lax.fori_loop(0, count, step, (zero, zero, zero, zero))
            place = slice(c * width + n * lanes, c * width + (n + 1) * lanes)
            for i in range(3):
                level = jnp.full((rows, lanes), transfer_ref[i])
                out_ref[i, :, place] = colors[i] * (unit * (TOP / (level + TOP)))
            out_ref[3, :, place] = 1.0 - jnp.exp2(-depth)


def composite(codes, transfer, depth_order, total, slab_len):
    _, _, rows, width = codes[0].shape
    smem = pl.BlockSpec(memory_space=pltpu.SMEM)
    vmem = pl.BlockSpec(memory_space=pltpu.VMEM)
    return pl.pallas_call(
        functools.partial(composite_kernel, total, slab_len, len(codes)),
        in_specs=[smem, smem] + [vmem] * len(codes),
        out_specs=vmem,
        out_shape=jax.ShapeDtypeStruct((4, rows, width * len(codes)), jnp.float32),
        compiler_params=pltpu.CompilerParams(vmem_limit_bytes=32 * 1024 * 1024),
        name="composite",
    )(depth_order, transfer, *codes)


def on_device(field, jitter, transfer, depth_order, ray_start, ray_end):
    count = lax.axis_size("depth")
    here = lax.axis_index("depth")
    slab_len, rows, cols = field.shape
    total = slab_len * count
    width = cols // count
    halo = shifted(field[0], "depth", -1)
    base = jnp.reshape(here * slab_len, (1,)).astype(jnp.int32)
    args = (field, halo, jitter, transfer, ray_start, ray_end, base, total)
    received = []
    if width % (2 * LANES) == 0:
        chunks = 2
        for chunk in range(chunks):
            codes = slab_codes(*args, count, chunk, chunks)
            received.append(lax.all_to_all(codes, "depth", split_axis=0, concat_axis=0, tiled=True))
    else:
        blocks = cols // LANES
        codes = slab_codes(*args, blocks, 0, 1)
        codes = codes.transpose(1, 2, 0, 3).reshape(4, rows, count, width).transpose(2, 0, 1, 3)
        received.append(lax.all_to_all(codes, "depth", split_axis=0, concat_axis=0, tiled=True))
    return composite(received, transfer, depth_order, total, slab_len)


def solution(mesh):
    in_specs = (P("depth", "groups", None), P("groups", None), P(), P(), P(), P())
    out_specs = P(None, "groups", "depth")
    return jax.shard_map(
        on_device, mesh=mesh, in_specs=in_specs, out_specs=out_specs, check_vma=False
    )
```

time: 108 us -> 67.4 us (0.62)
  the two profiles are of different devices: /device:TPU:13 before, /device:TPU:0 now
where the time goes in v1:
time: 67.4 us; the launch traced here: 66.9 us
  Pallas kernels  20.7 us (31%)
  blocking collectives  18.4 us (27%)
  starting transfers between devices  12.3 us (18%)
  local copies, waits for them, and re-layouts  10.7 us (16%)
  waiting for transfers between devices  4.71 us (7%)
    all_to_all x1, blocking collectives, on_device(): lax.all_to_all(codes, 'depth', split_axis=0, concat_axis=0, tiled=True)  18.4 us
    pallas_call x2, Pallas kernels, slab_codes(): pl.pallas_call(functools.partial(slab_kernel, total, tile_cols, chunk, ch...  18.1 us
    all_to_all x1, starting transfers between devices, on_device(): lax.all_to_all(codes, 'depth', split_axis=0, concat_axis=0, tiled=True)  11 us
    unnamed x22, local copies, waits for them, and re-layouts  9.78 us
    pallas_call x1, Pallas kernels, composite(): pl.pallas_call(functools.partial(composite_kernel, total, slab_len, len(c...  2.62 us
    all_to_all x1, waiting for transfers between devices, on_device(): lax.all_to_all(codes, 'depth', split_axis=0, concat_axis=0, tiled=True)  2.59 us
    ppermute x1, waiting for transfers between devices, shifted(): lax.ppermute(value, axis, [(source, source + steps) for source in range(i...  2.13 us
  transfers between devices with their start and end apart: 2, of which 2 were waited for; matrix products, arithmetic and copies ran while one was open for 0% of the time, Pallas kernels for 13%

profile of v1, /device:TPU:0, one launch (start us, length us, event | category | flops | bytes accessed | tf_op | source)
XLA Modules:
  0.0 66.9 jit_solution(2817979307180580209)
XLA Ops:
  0.0 1.0 %slice_bitcast_fusion = bf16[16,8192]{1,0:T(8,128)(2,1)S(1)} fusion(bf16[32,16,8192]{2,1,0:T(8,128)(2,1)} %field_ref.3), kind=kLoop, calls=%fused_computation | loop fusion | bytes 524288 | tf_op jit(solution)/shard_map/squeeze | solution.py:166
  1.0 1.3 %collective-permute-start = (bf16[16,8192]{1,0:T(8,128)(2,1)S(1)}, bf16[16,8192]{1,0:T(8,128)(2,1)S(1)}, u32[]{:S(2)}, u32[]{:S(2)}) collective-permute-start(bf16[16,8192]{1,0:T(8,128)(2,1)S(1)} %slice_bitcast_fusion), channel_id=1, source_target_pairs={{1,0},{2,1},{3,2},{4,3},{5,4},{6,5},{7,6},{8,7},{9,8},{10,9},{11,1... | collective-permute-start | bytes 786440 | tf_op jit(solution)/shard_map/ppermute | solution.py:24
  2.3 2.1 %collective-permute-done.halo_ref = bf16[16,8192]{1,0:T(8,128)(2,1)S(1)} collective-permute-done((bf16[16,8192]{1,0:T(8,128)(2,1)S(1)}, bf16[16,8192]{1,0:T(8,128)(2,1)S(1)}, u32[]{:S(2)}, u32[]{:S(2)}) %collective-permute-start) | collective-permute-done | bytes 262176 | tf_op jit(solution)/shard_map/ppermute | solution.py:24
  4.4 0.0 copy-start
  4.4 3.4 %copy-done = bf16[32,16,8192]{2,1,0:T(8,128)(2,1)S(1)} copy-done((bf16[32,16,8192]{2,1,0:T(8,128)(2,1)S(1)}, bf16[32,16,8192]{2,1,0:T(8,128)(2,1)}, u32[]{:S(2)}) %copy-start) | copy-done | bytes 8388632
  7.8 0.0 copy-start.3
  7.8 0.7 copy-done.3
  8.4 0.0 copy-start.5
  8.4 1.0 %copy-done.5 = f32[16,8192]{1,0:T(8,128)S(1)} copy-done((f32[16,8192]{1,0:T(8,128)S(1)}, f32[16,8192]{1,0:T(8,128)}, u32[]{:S(2)}) %copy-start.5) | copy-done | bytes 524312
  9.5 0.0 copy-start.7
  9.5 0.7 copy-done.7
  10.1 0.0 copy-start.9
  10.1 0.7 copy-done.9
  10.8 0.0 copy-start.4
  10.8 0.0 copy-start.6
  10.8 0.0 copy-start.8
  10.8 0.0 copy-start.10
  10.8 9.7 %slab_codes.3 = s16[16,4,16,256]{3,2,1,0:T(8,128)(2,1)} custom-call(s32[1]{0:T(128)} %bitcast.base_ref, f32[4]{0:T(128)S(1)} %copy-done.3, s32[128]{0:T(128)S(1)} %copy-done.7, s32[128]{0:T(128)S(1)} %copy-done.9, bf16[32,16,8192]{2,1,0:T(8,128)(2,1)S(1)} %copy-done, bf16[16,8192]{1,0:T(8,128)(2,1)S(1)} %collective-permute-done.halo_ref, ...), custom_call_target="tpu_custom_call" | custom-call | flops 41943040 | bytes 4194304 | tf_op jit(solution)/shard_map/slab_codes/pallas_call | solution.py:88
  20.5 11.0 %all-to-all-start.1 = ((s16[16,4,16,256]{3,2,1,0:T(8,128)(2,1)}), s16[16,4,16,256]{3,2,1,0:T(8,128)(2,1)S(1)}, u32[]{:S(2)}, u32[]{:S(2)}) async-start(s16[16,4,16,256]{3,2,1,0:T(8,128)(2,1)} %slab_codes.3), calls=%async_computation.1 | async-start | bytes 1048576 | tf_op jit(solution)/shard_map/all_to_all | solution.py:174
  31.5 0.0 copy-done.4
  31.5 0.0 copy-done.6
  31.5 0.0 copy-done.8
  31.5 0.0 copy-done.10
  31.5 0.0 copy-start.1
  31.5 3.4 %copy-done.1 = bf16[32,16,8192]{2,1,0:T(8,128)(2,1)S(1)} copy-done((bf16[32,16,8192]{2,1,0:T(8,128)(2,1)S(1)}, bf16[32,16,8192]{2,1,0:T(8,128)(2,1)}, u32[]{:S(2)}) %copy-start.1) | copy-done | bytes 8388632
  34.9 0.0 copy-start.2
  34.9 8.4 %slab_codes.2 = s16[16,4,16,256]{3,2,1,0:T(8,128)(2,1)S(1)} custom-call(s32[1]{0:T(128)} %bitcast.base_ref, f32[4]{0:T(128)S(1)} %copy-done.4, s32[128]{0:T(128)S(1)} %copy-done.8, s32[128]{0:T(128)S(1)} %copy-done.10, bf16[32,16,8192]{2,1,0:T(8,128)(2,1)S(1)} %copy-done.1, bf16[16,8192]{1,0:T(8,128)(2,1)S(1)} %collective-permute-done.halo_ref, ...), custom_call_target="tpu_custom_call" | custom-call | flops 41943040 | bytes 4194304 | tf_op jit(solution)/shard_map/slab_codes/pallas_call | solution.py:88
  43.3 2.6 %all-to-all-done.1.refs_1_ = s16[16,4,16,256]{3,2,1,0:T(8,128)(2,1)S(1)} async-done(((s16[16,4,16,256]{3,2,1,0:T(8,128)(2,1)}), s16[16,4,16,256]{3,2,1,0:T(8,128)(2,1)S(1)}, u32[]{:S(2)}, u32[]{:S(2)}) %all-to-all-start.1) | async-done | bytes 524320 | tf_op jit(solution)/shard_map/all_to_all | solution.py:174
  45.9 18.4 %all_to_all.10.refs_0_ = s16[16,4,16,256]{3,2,1,0:T(8,128)(2,1)S(1)} all-to-all(s16[16,4,16,256]{3,2,1,0:T(8,128)(2,1)S(1)} %slab_codes.2), channel_id=1, replica_groups=mesh['groups'=2,'depth'=16] {'depth'}, dimensions={0} | all-to-all | bytes 1048576 | tf_op jit(solution)/shard_map/all_to_all | solution.py:174
  64.3 0.0 copy-done.2
  64.3 2.6 %composite.1 = f32[4,16,512]{2,1,0:T(8,128)} custom-call(s32[16]{0:T(128)S(1)} %copy-done.2, f32[4]{0:T(128)S(1)} %copy-done.4, s16[16,4,16,256]{3,2,1,0:T(8,128)(2,1)S(1)} %all_to_all.10.refs_0_, s16[16,4,16,256]{3,2,1,0:T(8,128)(2,1)S(1)} %all-to-all-done.1.refs_1_), custom_call_target="tpu_custom_call" | custom-call | tf_op jit(solution)/shard_map/composite/pallas_call | solution.py:150
Async XLA Ops:
  1.0 3.4 %collective-permute-start = (bf16[16,8192]{1,0:T(8,128)(2,1)S(1)}, bf16[16,8192]{1,0:T(8,128)(2,1)S(1)}, u32[]{:S(2)}, u32[]{:S(2)}) collective-permute-start(bf16[16,8192]{1,0:T(8,128)(2,1)S(1)} %slice_bitcast_fusion), channel_id=1, source_target_pairs={{1,0},{2,1},{3,2},{4,3},{5,4},{6,5},{7,6},{8,7},{9,8},{10,9},{11,1... | collective-permute-start | bytes 786440 | tf_op jit(solution)/shard_map/ppermute | solution.py:24
  4.4 3.4 %copy-start = (bf16[32,16,8192]{2,1,0:T(8,128)(2,1)S(1)}, bf16[32,16,8192]{2,1,0:T(8,128)(2,1)}, u32[]{:S(2)}) copy-start(bf16[32,16,8192]{2,1,0:T(8,128)(2,1)} %field_ref.3) | copy-start | bytes 25165828
  7.8 0.7 copy-start.3
  8.4 1.0 %copy-start.5 = (f32[16,8192]{1,0:T(8,128)S(1)}, f32[16,8192]{1,0:T(8,128)}, u32[]{:S(2)}) copy-start(f32[16,8192]{1,0:T(8,128)} %jitter_ref.3) | copy-start | bytes 1572868
  9.5 0.7 copy-start.7
  10.1 0.7 copy-start.9
  10.8 20.7 %copy-start.4 = (f32[4]{0:T(128)S(1)}, f32[4]{0:T(128)}, u32[]{:S(2)}) copy-start(f32[4]{0:T(128)} %transfer_ref.5) | copy-start | bytes 52
  10.8 20.7 %copy-start.6 = (f32[16,8192]{1,0:T(8,128)S(1)}, f32[16,8192]{1,0:T(8,128)}, u32[]{:S(2)}) copy-start(f32[16,8192]{1,0:T(8,128)} %jitter_ref.3) | copy-start | bytes 1572868
  10.8 20.7 %copy-start.8 = (s32[128]{0:T(128)S(1)}, s32[128]{0:T(128)}, u32[]{:S(2)}) copy-start(s32[128]{0:T(128)} %start_ref.3) | copy-start | bytes 1540
  10.8 20.7 %copy-start.10 = (s32[128]{0:T(128)S(1)}, s32[128]{0:T(128)}, u32[]{:S(2)}) copy-start(s32[128]{0:T(128)} %end_ref.3) | copy-start | bytes 1540
  20.5 25.4 %all-to-all-start.1 = ((s16[16,4,16,256]{3,2,1,0:T(8,128)(2,1)}), s16[16,4,16,256]{3,2,1,0:T(8,128)(2,1)S(1)}, u32[]{:S(2)}, u32[]{:S(2)}) async-start(s16[16,4,16,256]{3,2,1,0:T(8,128)(2,1)} %slab_codes.3), calls=%async_computation.1 | async-start | bytes 1048576 | tf_op jit(solution)/shard_map/all_to_all | solution.py:174
  31.5 3.4 %copy-start.1 = (bf16[32,16,8192]{2,1,0:T(8,128)(2,1)S(1)}, bf16[32,16,8192]{2,1,0:T(8,128)(2,1)}, u32[]{:S(2)}) copy-start(bf16[32,16,8192]{2,1,0:T(8,128)(2,1)} %field_ref.3) | copy-start | bytes 25165828
  34.9 29.4 %copy-start.2 = (s32[16]{0:T(128)S(1)}, s32[16]{0:T(128)}, u32[]{:S(2)}) copy-start(s32[16]{0:T(128)} %order_ref.1) | copy-start | bytes 196

commit v2 on v1

v2 whole, which is shorter than its diff:
```python
import functools
import math

import jax
import jax.numpy as jnp
from jax import lax
from jax.experimental import pallas as pl
from jax.experimental.pallas import tpu as pltpu
from jax.sharding import PartitionSpec as P

TOP = 5.2
LOG2E = math.log2(math.e)
LANES = 128
MARCH_BYTES = 54 * 1024 * 1024
SMALL_BYTES = 16 * 1024 * 1024


def spans(slab_len):
    deep = math.log2(slab_len)
    return 6.8 + deep, 13.2 + deep


def shifted(value, axis, steps):
    count = lax.axis_size(axis)
    initial, last = (max(0, -steps), min(count, count - steps))
    return lax.ppermute(value, axis, [(source, source + steps) for source in range(initial, last)])


def encode(value, span):
    code = jnp.log2(value) * (65535.0 / span) + 65535.5
    code = jnp.minimum(jnp.maximum(code, 0.0), 65535.0)
    return (code.astype(jnp.int32) - 32768).astype(jnp.int16)


def tile_gains(gain_ref, gain, base, first_col, tile_cols, start_ref, end_ref):
    sample = lax.broadcasted_iota(jnp.int32, (8, LANES), 0) + base
    lane = lax.broadcasted_iota(jnp.int32, (8, LANES), 1)
    tile = first_col // tile_cols
    start = jnp.full((8, LANES), start_ref[tile])
    end = jnp.full((8, LANES), end_ref[tile])
    for t in range(1, LANES // tile_cols):
        start = jnp.where(lane >= t * tile_cols, start_ref[tile + t], start)
        end = jnp.where(lane >= t * tile_cols, end_ref[tile + t], end)
    for k in range(0, gain_ref.shape[0], 8):
        active = (sample + k >= start) & (sample + k < end)
        gain_ref[k:k + 8, :] = jnp.where(active, gain, 0.0)


def march_kernel(total, tile_cols, base_ref, transfer_ref, start_ref, end_ref, field_ref, jitter_ref, state_ref, last_ref,
                 gain_ref):
    slab_len, rows, width = field_ref.shape
    base = base_ref[0]
    first_col = pl.program_id(0) * width
    levels = [jnp.full((rows, LANES), transfer_ref[i]) for i in range(3)]
    gain = jnp.full((8, LANES), transfer_ref[3]) * (-LOG2E * 0.2 / total)

    def block(n, carry):
        cols = pl.ds(pl.multiple_of(n * LANES, LANES), LANES)
        tile_gains(gain_ref, gain, base, first_col + n * LANES, tile_cols, start_ref, end_ref)
        jitter = jitter_ref[:, cols]
        stay = 1.0 - jitter
        lower = field_ref[0, :, cols].astype(jnp.float32)
        before = jnp.zeros((rows, LANES), jnp.float32)
        through = jnp.ones((rows, LANES), jnp.float32)
        sums = [jnp.zeros((rows, LANES), jnp.float32) for _ in range(3)]
        for k in range(slab_len - 1):
            upper = field_ref[k + 1, :, cols].astype(jnp.float32)
            value = stay * lower + jitter * upper
            before = before + gain_ref[k:k + 1, :] * value
            beyond = jnp.exp2(before)
            emitted = (through - beyond) * value
            for i in range(3):
                sums[i] = sums[i] + emitted * pl.reciprocal(levels[i] + value, approx=True)
            through = beyond
            lower = upper
        for i in range(3):
            state_ref[i, :, cols] = sums[i]
        state_ref[3, :, cols] = before
        last_ref[:, cols] = field_ref[slab_len - 1, :, cols]
        return carry

    lax.fori_loop(0, width // LANES, block, 0)


def finish_kernel(total, tile_cols, slab_len, base_ref, transfer_ref, start_ref, end_ref, last_ref, halo_ref, jitter_ref,
                  state_ref, out_ref, gain_ref):
    pieces, _, rows, width = out_ref.shape
    base = base_ref[0] + slab_len - 1
    first_col = pl.program_id(0) * (pieces * width)
    depth_gain = jnp.full((rows, LANES), transfer_ref[3]) * (0.2 / total)
    levels = [jnp.full((rows, LANES), transfer_ref[i]) for i in range(3)]
    depth_unit = 1.0 / (depth_gain * (slab_len * TOP))
    color_unit = [depth_unit * ((levels[i] + TOP) * (1.0 / TOP)) for i in range(3)]
    depth_span, color_span = spans(slab_len)
    gain = depth_gain[:8] * -LOG2E

    for p in range(pieces):
        for n in range(width // LANES):
            place = p * width + n * LANES
            cols = slice(place, place + LANES)
            tile_gains(gain_ref, gain, base, first_col + place, tile_cols, start_ref, end_ref)
            jitter = jitter_ref[:, cols]
            lower = last_ref[:, cols].astype(jnp.float32)
            upper = halo_ref[:, cols].astype(jnp.float32)
            value = (1.0 - jitter) * lower + jitter * upper
            before = state_ref[3, :, cols]
            beyond = before + gain_ref[0:1, :] * value
            emitted = (jnp.exp2(before) - jnp.exp2(beyond)) * value
            out = slice(n * LANES, (n + 1) * LANES)
            for i in range(3):
                color = state_ref[i, :, cols] + emitted * pl.reciprocal(levels[i] + value, approx=True)
                out_ref[p, i, :, out] = encode(color * color_unit[i], color_span)
            out_ref[p, 3, :, out] = encode(beyond * (depth_unit * (-1.0 / LOG2E)), depth_span)


def slab_codes(field, halo, jitter, transfer, ray_start, ray_end, base, total, pieces):
    slab_len, rows, cols = field.shape
    width = cols // pieces
    step = max(width, min(1024, cols))
    tile_cols = cols // ray_start.shape[0]
    smem = pl.BlockSpec(memory_space=pltpu.SMEM)
    state, last = pl.pallas_call(
        functools.partial(march_kernel, total, tile_cols),
        grid=(cols // step,),
        in_specs=[
            smem, smem, smem, smem,
            pl.BlockSpec((slab_len, rows, step), lambda p: (0, 0, p)),
            pl.BlockSpec((rows, step), lambda p: (0, p)),
        ],
        out_specs=[
            pl.BlockSpec((4, rows, step), lambda p: (0, 0, p)),
            pl.BlockSpec((rows, step), lambda p: (0, p)),
        ],
        out_shape=[
            jax.ShapeDtypeStruct((4, rows, cols), jnp.float32),
            jax.ShapeDtypeStruct((rows, cols), field.dtype),
        ],
        scratch_shapes=[pltpu.VMEM((slab_len, LANES), jnp.float32)],
        compiler_params=pltpu.CompilerParams(vmem_limit_bytes=MARCH_BYTES),
        cost_estimate=pl.CostEstimate(
            flops=slab_len * rows * cols * 20,
            bytes_accessed=slab_len * rows * cols * 2,
            transcendentals=slab_len * rows * cols * 4,
        ),
        name="march",
    )(base, transfer, ray_start, ray_end, field, jitter)
    per = step // width
    return pl.pallas_call(
        functools.partial(finish_kernel, total, tile_cols, slab_len),
        grid=(cols // step,),
        in_specs=[
            smem, smem, smem, smem,
            pl.BlockSpec((rows, step), lambda p: (0, p)),
            pl.BlockSpec((rows, step), lambda p: (0, p)),
            pl.BlockSpec((rows, step), lambda p: (0, p)),
            pl.BlockSpec((4, rows, step), lambda p: (0, 0, p)),
        ],
        out_specs=pl.BlockSpec((per, 4, rows, width), lambda p: (p, 0, 0, 0)),
        out_shape=jax.ShapeDtypeStruct((pieces, 4, rows, width), jnp.int16),
        scratch_shapes=[pltpu.VMEM((8, LANES), jnp.float32)],
        compiler_params=pltpu.CompilerParams(vmem_limit_bytes=SMALL_BYTES),
        name="finish",
    )(base, transfer, ray_start, ray_end, last, halo, jitter, state)


def composite_kernel(total, slab_len, order_ref, transfer_ref, code_ref, out_ref):
    count, _, rows, width = code_ref.shape
    lanes = min(width, LANES)
    depth_span, color_span = spans(slab_len)
    depth_gain = jnp.full((rows, lanes), transfer_ref[3]) * (0.2 / total)
    unit = depth_gain * (slab_len * TOP)
    depth_unit = unit * LOG2E

    def decode(codes, span, shift):
        code = codes.astype(jnp.int32).astype(jnp.float32)
        value = jnp.exp2(code * (span / 65535.0) + (span * (32768.0 / 65535.0) - span) - shift)
        return jnp.where(code > -32768.0, value, 0.0)

    for n in range(width // lanes):
        cols = slice(n * lanes, (n + 1) * lanes)

        def step(j, carry):
            depth, red, green, blue = carry
            slab = order_ref[j]
            colors = [red, green, blue]
            for i in range(3):
                colors[i] = colors[i] + decode(code_ref[slab, i, :, cols], color_span, depth)
            depth = depth + depth_unit * decode(code_ref[slab, 3, :, cols], depth_span, 0.0)
            return depth, *colors

        zero = jnp.zeros((rows, lanes), jnp.float32)
        depth, *colors = lax.fori_loop(0, count, step, (zero, zero, zero, zero), unroll=4)
        for i in range(3):
            level = jnp.full((rows, lanes), transfer_ref[i])
            out_ref[i, :, cols] = colors[i] * (unit * (TOP / (level + TOP)))
        out_ref[3, :, cols] = 1.0 - jnp.exp2(-depth)


def composite(codes, transfer, depth_order, total, slab_len):
    _, _, rows, width = codes.shape
    smem = pl.BlockSpec(memory_space=pltpu.SMEM)
    vmem = pl.BlockSpec(memory_space=pltpu.VMEM)
    return pl.pallas_call(
        functools.partial(composite_kernel, total, slab_len),
        in_specs=[smem, smem, vmem],
        out_specs=vmem,
        out_shape=jax.ShapeDtypeStruct((4, rows, width), jnp.float32),
        compiler_params=pltpu.CompilerParams(vmem_limit_bytes=SMALL_BYTES),
        name="composite",
    )(depth_order, transfer, codes)


def on_device(field, jitter, transfer, depth_order, ray_start, ray_end):
    count = lax.axis_size("depth")
    here = lax.axis_index("depth")
    slab_len, rows, cols = field.shape
    total = slab_len * count
    width = cols // count
    halo = shifted(field[0], "depth", -1)
    base = jnp.reshape(here * slab_len, (1,)).astype(jnp.int32)
    args = (field, halo, jitter, transfer, ray_start, ray_end, base, total)
    if width % LANES == 0:
        codes = slab_codes(*args, count)
    else:
        codes = slab_codes(*args, cols // LANES)
        codes = codes.transpose(1, 2, 0, 3).reshape(4, rows, count, width).transpose(2, 0, 1, 3)
    received = lax.all_to_all(codes, "depth", split_axis=0, concat_axis=0, tiled=True)
    return composite(received, transfer, depth_order, total, slab_len)


def solution(mesh):
    in_specs = (P("depth", "groups", None), P("groups", None), P(), P(), P(), P())
    out_specs = P(None, "groups", "depth")
    return jax.shard_map(
        on_device, mesh=mesh, in_specs=in_specs, out_specs=out_specs, check_vma=False
    )
```

time: 67.4 us -> 57 us (0.85)
  blocking collectives: 18.4 us -> 32.8 us
  starting transfers between devices: 12.3 us -> 1.29 us
  local copies, waits for them, and re-layouts: 10.7 us -> 3.53 us
  waiting for transfers between devices: 4.71 us -> 0.01 us
  Pallas kernels: 20.7 us -> 18.7 us
    all_to_all x1, blocking collectives: 18.4 us -> 32.8 us  [on_device(): lax.all_to_all(codes, 'depth', split_axis=0, concat_axis=0, tiled=True)]
    all_to_all x1 -> x0, starting transfers between devices: 11 us -> none  [on_device(): lax.all_to_all(codes, 'depth', split_axis=0, concat_axis=0, tiled=True)]
    unnamed x22 -> x14, local copies, waits for them, and re-layouts: 9.78 us -> 2.57 us
    all_to_all x1 -> x0, waiting for transfers between devices: 2.59 us -> none  [on_device(): lax.all_to_all(codes, 'depth', split_axis=0, concat_axis=0, tiled=True)]
    ppermute x1, waiting for transfers between devices: 2.13 us -> 0.01 us  [shifted(): lax.ppermute(value, axis, [(source, source + steps) for source in range(i...]
    pallas_call x3, Pallas kernels: 20.7 us -> 18.7 us  [the longest x1 14.3 us: slab_codes(): pl.pallas_call(functools.partial(march_kernel, total, tile_cols), grid=(c...]
  transfers between devices with their start and end apart: 2 -> 1, of which waited for: 2 -> 0; matrix products, arithmetic and copies ran while one was open for 0% -> 0% of each run, Pallas kernels for 13% -> 25%
where the time goes in v2:
time: 57 us; the launch traced here: 56.4 us
  blocking collectives  32.8 us (58%)
  Pallas kernels  18.7 us (33%)
  local copies, waits for them, and re-layouts  3.53 us (6%)
  starting transfers between devices  1.29 us (2%)
    all_to_all x1, blocking collectives, on_device(): lax.all_to_all(codes, 'depth', split_axis=0, concat_axis=0, tiled=True)  32.8 us
    pallas_call x1, Pallas kernels, slab_codes(): pl.pallas_call(functools.partial(march_kernel, total, tile_cols), grid=(c...  14.3 us
    unnamed x14, local copies, waits for them, and re-layouts  2.57 us
    pallas_call x1, Pallas kernels, slab_codes(): pl.pallas_call(functools.partial(finish_kernel, total, tile_cols, slab_le...  2.36 us
    pallas_call x1, Pallas kernels, composite(): pl.pallas_call(functools.partial(composite_kernel, total, slab_len), in_s...  1.98 us
    ppermute x1, starting transfers between devices, shifted(): lax.ppermute(value, axis, [(source, source + steps) for source in range(i...  1.29 us
  transfers between devices with their start and end apart: 1, of which 0 were waited for; matrix products, arithmetic and copies ran while one was open for 0% of the time, Pallas kernels for 25%

profile of v2, /device:TPU:0, one launch (start us, length us, event | category | flops | bytes accessed | tf_op | source)
XLA Modules:
  0.0 56.4 jit_solution(7522205950818950457)
XLA Ops:
  0.0 1.0 %slice_bitcast_fusion = bf16[16,8192]{1,0:T(8,128)(2,1)S(1)} fusion(bf16[32,16,8192]{2,1,0:T(8,128)(2,1)} %field_ref.1), kind=kLoop, calls=%fused_computation | loop fusion | bytes 524288 | tf_op jit(solution)/shard_map/squeeze | solution.py:219
  1.0 1.3 %collective-permute-start = (bf16[16,8192]{1,0:T(8,128)(2,1)S(1)}, bf16[16,8192]{1,0:T(8,128)(2,1)S(1)}, u32[]{:S(2)}, u32[]{:S(2)}) collective-permute-start(bf16[16,8192]{1,0:T(8,128)(2,1)S(1)} %slice_bitcast_fusion), channel_id=1, source_target_pairs={{1,0},{2,1},{3,2},{4,3},{5,4},{6,5},{7,6},{8,7},{9,8},{10,9},{11,1... | collective-permute-start | bytes 786440 | tf_op jit(solution)/shard_map/ppermute | solution.py:26
  2.3 0.0 copy-start.1
  2.3 0.0 copy-start.3
  2.3 0.0 copy-start.5
  2.3 0.0 copy-start.6
  2.3 0.0 copy-start.4
  2.3 14.3 %march.1 = (f32[4,16,8192]{2,1,0:T(8,128)}, bf16[16,8192]{1,0:T(8,128)(2,1)}) custom-call(s32[1]{0:T(128)} %bitcast.base_ref, f32[4]{0:T(128)} %transfer_ref.5, s32[128]{0:T(128)} %start_ref.3, s32[128]{0:T(128)} %end_ref.3, bf16[32,16,8192]{2,1,0:T(8,128)(2,1)} %field_ref.1, f32[16,8192]{1,0:T(8,128)} %jitter_ref.3), custom_call_target="tpu_custom_call" | custom-call | flops 83886080 | bytes 8388608 | tf_op jit(solution)/shard_map/march/pallas_call | solution.py:122
  16.7 0.0 collective-permute-done.halo_ref
  16.7 0.0 copy-done.1
  16.7 0.0 copy-done.3
  16.7 0.0 copy-done.5
  16.7 0.0 copy-done.6
  16.7 0.0 copy-start
  16.7 1.6 %copy-done = f32[4,16,8192]{2,1,0:T(8,128)S(1)} copy-done((f32[4,16,8192]{2,1,0:T(8,128)S(1)}, f32[4,16,8192]{2,1,0:T(8,128)}, u32[]{:S(2)}) %copy-start) | copy-done | bytes 2097176
  18.3 0.0 copy-start.2
  18.3 0.9 %copy-done.2 = bf16[16,8192]{1,0:T(8,128)(2,1)S(1)} copy-done((bf16[16,8192]{1,0:T(8,128)(2,1)S(1)}, bf16[16,8192]{1,0:T(8,128)(2,1)}, u32[]{:S(2)}) %copy-start.2) | copy-done | bytes 262168
  19.3 2.4 %finish.1 = s16[16,4,16,512]{3,2,1,0:T(8,128)(2,1)S(1)} custom-call(s32[1]{0:T(128)} %bitcast.base_ref, f32[4]{0:T(128)S(1)} %copy-done.3, s32[128]{0:T(128)S(1)} %copy-done.5, s32[128]{0:T(128)S(1)} %copy-done.6, bf16[16,8192]{1,0:T(8,128)(2,1)S(1)} %copy-done.2, bf16[16,8192]{1,0:T(8,128)(2,1)S(1)} %collective-permute-done.halo_ref, ...), custom_call_target="tpu_custom_call" | custom-call | tf_op jit(solution)/shard_map/finish/pallas_call | solution.py:148
  21.6 32.8 %all_to_all.5.code_ref = s16[16,4,16,512]{3,2,1,0:T(8,128)(2,1)S(1)} all-to-all(s16[16,4,16,512]{3,2,1,0:T(8,128)(2,1)S(1)} %finish.1), channel_id=1, replica_groups=mesh['groups'=2,'depth'=16] {'depth'}, dimensions={0} | all-to-all | bytes 2097152 | tf_op jit(solution)/shard_map/all_to_all | solution.py:227
  54.4 0.0 copy-done.4
  54.4 2.0 %composite.1 = f32[4,16,512]{2,1,0:T(8,128)} custom-call(s32[16]{0:T(128)S(1)} %copy-done.4, f32[4]{0:T(128)S(1)} %copy-done.3, s16[16,4,16,512]{3,2,1,0:T(8,128)(2,1)S(1)} %all_to_all.5.code_ref), custom_call_target="tpu_custom_call" | custom-call | tf_op jit(solution)/shard_map/composite/pallas_call | solution.py:203
Async XLA Ops:
  1.0 15.7 %collective-permute-start = (bf16[16,8192]{1,0:T(8,128)(2,1)S(1)}, bf16[16,8192]{1,0:T(8,128)(2,1)S(1)}, u32[]{:S(2)}, u32[]{:S(2)}) collective-permute-start(bf16[16,8192]{1,0:T(8,128)(2,1)S(1)} %slice_bitcast_fusion), channel_id=1, source_target_pairs={{1,0},{2,1},{3,2},{4,3},{5,4},{6,5},{7,6},{8,7},{9,8},{10,9},{11,1... | collective-permute-start | bytes 786440 | tf_op jit(solution)/shard_map/ppermute | solution.py:26
  2.3 14.4 %copy-start.1 = (f32[16,8192]{1,0:T(8,128)S(1)}, f32[16,8192]{1,0:T(8,128)}, u32[]{:S(2)}) copy-start(f32[16,8192]{1,0:T(8,128)} %jitter_ref.3) | copy-start | bytes 1572868
  2.3 14.4 %copy-start.3 = (f32[4]{0:T(128)S(1)}, f32[4]{0:T(128)}, u32[]{:S(2)}) copy-start(f32[4]{0:T(128)} %transfer_ref.5) | copy-start | bytes 52
  2.3 14.4 %copy-start.5 = (s32[128]{0:T(128)S(1)}, s32[128]{0:T(128)}, u32[]{:S(2)}) copy-start(s32[128]{0:T(128)} %start_ref.3) | copy-start | bytes 1540
  2.3 14.4 %copy-start.6 = (s32[128]{0:T(128)S(1)}, s32[128]{0:T(128)}, u32[]{:S(2)}) copy-start(s32[128]{0:T(128)} %end_ref.3) | copy-start | bytes 1540
  2.3 52.1 %copy-start.4 = (s32[16]{0:T(128)S(1)}, s32[16]{0:T(128)}, u32[]{:S(2)}) copy-start(s32[16]{0:T(128)} %order_ref.1) | copy-start | bytes 196
  16.7 1.6 %copy-start = (f32[4,16,8192]{2,1,0:T(8,128)S(1)}, f32[4,16,8192]{2,1,0:T(8,128)}, u32[]{:S(2)}) copy-start(f32[4,16,8192]{2,1,0:T(8,128)} %get-tuple-element.8.state_ref) | copy-start | bytes 6291460
  18.3 0.9 %copy-start.2 = (bf16[16,8192]{1,0:T(8,128)(2,1)S(1)}, bf16[16,8192]{1,0:T(8,128)(2,1)}, u32[]{:S(2)}) copy-start(bf16[16,8192]{1,0:T(8,128)(2,1)} %get-tuple-element.7.last_ref) | copy-start | bytes 786436

commit v3 on v2

--- a/solution.py
+++ b/solution.py
@@ -46,33 +46,39 @@
         gain_ref[k:k + 8, :] = jnp.where(active, gain, 0.0)
 
 
-def march_kernel(total, tile_cols, base_ref, transfer_ref, start_ref, end_ref, field_ref, jitter_ref, state_ref, last_ref,
-                 gain_ref):
+def march(gain_ref, field_ref, cols, jitter, levels, halo=None):
+    slab_len = field_ref.shape[0]
+    rows = jitter.shape[0]
+    stay = 1.0 - jitter
+    lower = field_ref[0, :, cols].astype(jnp.float32)
+    before = jnp.zeros((rows, LANES), jnp.float32)
+    through = jnp.ones((rows, LANES), jnp.float32)
+    sums = [jnp.zeros((rows, LANES), jnp.float32) for _ in range(3)]
+    for k in range(slab_len - (halo is None)):
+        following = field_ref[k + 1, :, cols] if k + 1 < slab_len else halo
+        upper = following.astype(jnp.float32)
+        value = stay * lower + jitter * upper
+        before = before + gain_ref[k:k + 1, :] * value
+        beyond = jnp.exp2(before)
+        emitted = (through - beyond) * value
+        for i in range(3):
+            sums[i] = sums[i] + emitted * pl.reciprocal(levels[i] + value, approx=True)
+        through = beyond
+        lower = upper
+    return sums, before
+
+
+def open_kernel(total, tile_cols, base_ref, transfer_ref, start_ref, end_ref, field_ref, jitter_ref, state_ref, last_ref,
+                gain_ref):
     slab_len, rows, width = field_ref.shape
-    base = base_ref[0]
     first_col = pl.program_id(0) * width
     levels = [jnp.full((rows, LANES), transfer_ref[i]) for i in range(3)]
     gain = jnp.full((8, LANES), transfer_ref[3]) * (-LOG2E * 0.2 / total)
 
     def block(n, carry):
         cols = pl.ds(pl.multiple_of(n * LANES, LANES), LANES)
-        tile_gains(gain_ref, gain, base, first_col + n * LANES, tile_cols, start_ref, end_ref)
-        jitter = jitter_ref[:, cols]
-        stay = 1.0 - jitter
-        lower = field_ref[0, :, cols].astype(jnp.float32)
-        before = jnp.zeros((rows, LANES), jnp.float32)
-        through = jnp.ones((rows, LANES), jnp.float32)
-        sums = [jnp.zeros((rows, LANES), jnp.float32) for _ in range(3)]
-        for k in range(slab_len - 1):
-            upper = field_ref[k + 1, :, cols].astype(jnp.float32)
-            value = stay * lower + jitter * upper
-            before = before + gain_ref[k:k + 1, :] * value
-            beyond = jnp.exp2(before)
-            emitted = (through - beyond) * value
-            for i in range(3):
-                sums[i] = sums[i] + emitted * pl.reciprocal(levels[i] + value, approx=True)
-            through = beyond
-            lower = upper
+        tile_gains(gain_ref, gain, base_ref[0], first_col + n * LANES, tile_cols, start_ref, end_ref)
+        sums, before = march(gain_ref, field_ref, cols, jitter_ref[:, cols], levels)
         for i in range(3):
             state_ref[i, :, cols] = sums[i]
         state_ref[3, :, cols] = before
@@ -82,11 +88,11 @@
     lax.fori_loop(0, width // LANES, block, 0)
 
 
-def finish_kernel(total, tile_cols, slab_len, base_ref, transfer_ref, start_ref, end_ref, last_ref, halo_ref, jitter_ref,
-                  state_ref, out_ref, gain_ref):
-    pieces, _, rows, width = out_ref.shape
-    base = base_ref[0] + slab_len - 1
-    first_col = pl.program_id(0) * (pieces * width)
+def close_kernel(total, tile_cols, opened, base_ref, transfer_ref, start_ref, end_ref, field_ref, halo_ref, jitter_ref,
+                 state_ref, last_ref, out_ref, gain_ref):
+    slab_len, rows, step = field_ref.shape
+    pieces, _, _, width = out_ref.shape
+    first_col = pl.program_id(0) * step
     depth_gain = jnp.full((rows, LANES), transfer_ref[3]) * (0.2 / total)
     levels = [jnp.full((rows, LANES), transfer_ref[i]) for i in range(3)]
     depth_unit = 1.0 / (depth_gain * (slab_len * TOP))
@@ -94,34 +100,63 @@
     depth_span, color_span = spans(slab_len)
     gain = depth_gain[:8] * -LOG2E
 
-    for p in range(pieces):
-        for n in range(width // LANES):
-            place = p * width + n * LANES
-            cols = slice(place, place + LANES)
-            tile_gains(gain_ref, gain, base, first_col + place, tile_cols, start_ref, end_ref)
-            jitter = jitter_ref[:, cols]
-            lower = last_ref[:, cols].astype(jnp.float32)
-            upper = halo_ref[:, cols].astype(jnp.float32)
-            value = (1.0 - jitter) * lower + jitter * upper
-            before = state_ref[3, :, cols]
-            beyond = before + gain_ref[0:1, :] * value
-            emitted = (jnp.exp2(before) - jnp.exp2(beyond)) * value
-            out = slice(n * LANES, (n + 1) * LANES)
-            for i in range(3):
-                color = state_ref[i, :, cols] + emitted * pl.reciprocal(levels[i] + value, approx=True)
-                out_ref[p, i, :, out] = encode(color * color_unit[i], color_span)
-            out_ref[p, 3, :, out] = encode(beyond * (depth_unit * (-1.0 / LOG2E)), depth_span)
+    def each_block(body):
+        for p in range(pieces):
+            def block(n, carry):
+                out = pl.ds(pl.multiple_of(n * LANES, LANES), LANES)
+                place = p * width + n * LANES
+                cols = pl.ds(pl.multiple_of(place, LANES), LANES)
+                sums, before = body(place, cols)
+                for i in range(3):
+                    out_ref[p, i, :, out] = encode(sums[i] * color_unit[i], color_span)
+                out_ref[p, 3, :, out] = encode(before * (depth_unit * (-1.0 / LOG2E)), depth_span)
+                return carry
+
+            lax.fori_loop(0, width // LANES, block, 0)
+
+    def finish(place, cols):
+        tile_gains(gain_ref.at[0:8, :], gain, base_ref[0] + slab_len - 1, first_col + place, tile_cols, start_ref, end_ref)
+        jitter = jitter_ref[:, cols]
+        lower = last_ref[:, cols].astype(jnp.float32)
+        upper = halo_ref[:, cols].astype(jnp.float32)
+        value = (1.0 - jitter) * lower + jitter * upper
+        before = state_ref[3, :, cols]
+        beyond = before + gain_ref[0:1, :] * value
+        emitted = (jnp.exp2(before) - jnp.exp2(beyond)) * value
+        sums = [state_ref[i, :, cols] + emitted * pl.reciprocal(levels[i] + value, approx=True) for i in range(3)]
+        return sums, beyond
+
+    def whole(place, cols):
+        tile_gains(gain_ref, gain, base_ref[0], first_col + place, tile_cols, start_ref, end_ref)
+        return march(gain_ref, field_ref, cols, jitter_ref[:, cols], levels, halo_ref[:, cols])
+
+    @pl.when(pl.program_id(0) < opened)
+    def _():
+        each_block(finish)
+
+    @pl.when(pl.program_id(0) >= opened)
+    def _():
+        each_block(whole)
 
 
 def slab_codes(field, halo, jitter, transfer, ray_start, ray_end, base, total, pieces):
     slab_len, rows, cols = field.shape
     width = cols // pieces
     step = max(width, min(1024, cols))
+    steps = cols // step
+    opened = max(1, steps * 5 // 8)
     tile_cols = cols // ray_start.shape[0]
     smem = pl.BlockSpec(memory_space=pltpu.SMEM)
+    params = pltpu.CompilerParams(vmem_limit_bytes=MARCH_BYTES)
+    scalars = (base, transfer, ray_start, ray_end)
+
+    def cost(share):
+        work = slab_len * rows * cols * share // steps
+        return pl.CostEstimate(flops=work * 20, bytes_accessed=work * 2, transcendentals=work * 4)
+
     state, last = pl.pallas_call(
-        functools.partial(march_kernel, total, tile_cols),
-        grid=(cols // step,),
+        functools.partial(open_kernel, total, tile_cols),
+        grid=(opened,),
         in_specs=[
             smem, smem, smem, smem,
             pl.BlockSpec((slab_len, rows, step), lambda p: (0, 0, p)),
@@ -132,35 +167,33 @@
             pl.BlockSpec((rows, step), lambda p: (0, p)),
         ],
         out_shape=[
-            jax.ShapeDtypeStruct((4, rows, cols), jnp.float32),
-            jax.ShapeDtypeStruct((rows, cols), field.dtype),
+            jax.ShapeDtypeStruct((4, rows, opened * step), jnp.float32),
+            jax.ShapeDtypeStruct((rows, opened * step), field.dtype),
         ],
         scratch_shapes=[pltpu.VMEM((slab_len, LANES), jnp.float32)],
-        compiler_params=pltpu.CompilerParams(vmem_limit_bytes=MARCH_BYTES),
-        cost_estimate=pl.CostEstimate(
-            flops=slab_len * rows * cols * 20,
-            bytes_accessed=slab_len * rows * cols * 2,
-            transcendentals=slab_len * rows * cols * 4,
-        ),
-        name="march",
-    )(base, transfer, ray_start, ray_end, field, jitter)
+        compiler_params=params,
+        cost_estimate=cost(opened),
+        name="open",
+    )(*scalars, field, jitter)
     per = step // width
     return pl.pallas_call(
-        functools.partial(finish_kernel, total, tile_cols, slab_len),
-        grid=(cols // step,),
+        functools.partial(close_kernel, total, tile_cols, opened),
+        grid=(steps,),
         in_specs=[
             smem, smem, smem, smem,
-            pl.BlockSpec((rows, step), lambda p: (0, p)),
-            pl.BlockSpec((rows, step), lambda p: (0, p)),
-            pl.BlockSpec((rows, step), lambda p: (0, p)),
-            pl.BlockSpec((4, rows, step), lambda p: (0, 0, p)),
+            pl.BlockSpec((slab_len, rows, step), lambda p: (0, 0, jnp.maximum(p, min(opened, steps - 1)))),
+            pl.BlockSpec((rows, step), lambda p: (0, p)),
+            pl.BlockSpec((rows, step), lambda p: (0, p)),
+            pl.BlockSpec((4, rows, step), lambda p: (0, 0, jnp.minimum(p, opened - 1))),
+            pl.BlockSpec((rows, step), lambda p: (0, jnp.minimum(p, opened - 1))),
         ],
         out_specs=pl.BlockSpec((per, 4, rows, width), lambda p: (p, 0, 0, 0)),
         out_shape=jax.ShapeDtypeStruct((pieces, 4, rows, width), jnp.int16),
-        scratch_shapes=[pltpu.VMEM((8, LANES), jnp.float32)],
-        compiler_params=pltpu.CompilerParams(vmem_limit_bytes=SMALL_BYTES),
-        name="finish",
-    )(base, transfer, ray_start, ray_end, last, halo, jitter, state)
+        scratch_shapes=[pltpu.VMEM((slab_len, LANES), jnp.float32)],
+        compiler_params=params,
+        cost_estimate=cost(steps - opened),
+        name="close",
+    )(*scalars, field, halo, jitter, state, last)
 
 
 def composite_kernel(total, slab_len, order_ref, transfer_ref, code_ref, out_ref):

time: 57 us -> 59.1 us (1.037)
  Pallas kernels: 18.7 us -> 22.4 us
  local copies, waits for them, and re-layouts: 3.53 us -> 1.66 us
    pallas_call x2, Pallas kernels: 16.7 us -> 20.4 us  [the longest x1 10.7 us: slab_codes(): pl.pallas_call(functools.partial(close_kernel, total, tile_cols, opened),...]
    unnamed x14 -> x6, local copies, waits for them, and re-layouts: 2.57 us -> 0.69 us
  transfers between devices with their start and end apart: 1 -> 1, of which waited for: 0 -> 0; matrix products, arithmetic and copies ran while one was open for 0% -> 0% of each run, Pallas kernels for 25% -> 17%
where the time goes in v3:
time: 59.1 us; the launch traced here: 58.4 us
  blocking collectives  33 us (56%)
  Pallas kernels  22.4 us (38%)
  local copies, waits for them, and re-layouts  1.66 us (3%)
  starting transfers between devices  1.29 us (2%)
    all_to_all x1, blocking collectives, on_device(): lax.all_to_all(codes, 'depth', split_axis=0, concat_axis=0, tiled=True)  33 us
    pallas_call x1, Pallas kernels, slab_codes(): pl.pallas_call(functools.partial(close_kernel, total, tile_cols, opened),...  10.7 us
    pallas_call x1, Pallas kernels, slab_codes(): pl.pallas_call(functools.partial(open_kernel, total, tile_cols), grid=(op...  9.72 us
    pallas_call x1, Pallas kernels, composite(): pl.pallas_call(functools.partial(composite_kernel, total, slab_len), in_s...  1.98 us
    ppermute x1, starting transfers between devices, shifted(): lax.ppermute(value, axis, [(source, source + steps) for source in range(i...  1.29 us
  transfers between devices with their start and end apart: 1, of which 0 were waited for; matrix products, arithmetic and copies ran while one was open for 0% of the time, Pallas kernels for 17%

profile of v3, /device:TPU:0, one launch (start us, length us, event | category | flops | bytes accessed | tf_op | source)
XLA Modules:
  0.0 58.4 jit_solution(10292561680149606569)
XLA Ops:
  0.0 1.0 %slice_bitcast_fusion = bf16[16,8192]{1,0:T(8,128)(2,1)S(1)} fusion(bf16[32,16,8192]{2,1,0:T(8,128)(2,1)} %field_ref.3), kind=kLoop, calls=%fused_computation | loop fusion | bytes 524288 | tf_op jit(solution)/shard_map/squeeze | solution.py:252
  1.0 1.3 %collective-permute-start = (bf16[16,8192]{1,0:T(8,128)(2,1)S(1)}, bf16[16,8192]{1,0:T(8,128)(2,1)S(1)}, u32[]{:S(2)}, u32[]{:S(2)}) collective-permute-start(bf16[16,8192]{1,0:T(8,128)(2,1)S(1)} %slice_bitcast_fusion), channel_id=1, source_target_pairs={{1,0},{2,1},{3,2},{4,3},{5,4},{6,5},{7,6},{8,7},{9,8},{10,9},{11,1... | collective-permute-start | bytes 786440 | tf_op jit(solution)/shard_map/ppermute | solution.py:26
  2.3 9.7 %open.1 = (f32[4,16,5120]{2,1,0:T(8,128)}, bf16[16,5120]{1,0:T(8,128)(2,1)}) custom-call(s32[1]{0:T(128)} %bitcast.base_ref, f32[4]{0:T(128)} %transfer_ref.5, s32[128]{0:T(128)} %start_ref.3, s32[128]{0:T(128)} %end_ref.3, bf16[32,16,8192]{2,1,0:T(8,128)(2,1)} %field_ref.3, f32[16,8192]{1,0:T(8,128)} %jitter_ref.3), custom_call_target="tpu_custom_call" | custom-call | flops 52428800 | bytes 5242880 | tf_op jit(solution)/shard_map/open/pallas_call | solution.py:157
  12.0 0.0 copy-start
  12.0 0.0 copy-start.1
  12.0 0.0 collective-permute-done.halo_ref
  12.0 0.0 copy-start.2
  12.0 0.7 %copy-done.2 = bf16[16,8192]{1,0:T(8,128)(2,1)} copy-done((bf16[16,8192]{1,0:T(8,128)(2,1)}, bf16[16,8192]{1,0:T(8,128)(2,1)S(1)}, u32[]{:S(2)}) %copy-start.2) | copy-done | bytes 262168
  12.7 10.7 %close.1 = s16[16,4,16,512]{3,2,1,0:T(8,128)(2,1)} custom-call(s32[1]{0:T(128)} %bitcast.base_ref, f32[4]{0:T(128)} %transfer_ref.5, s32[128]{0:T(128)} %start_ref.3, s32[128]{0:T(128)} %end_ref.3, bf16[32,16,8192]{2,1,0:T(8,128)(2,1)} %field_ref.3, bf16[16,8192]{1,0:T(8,128)(2,1)} %copy-done.2, f32[16,8192]{1,0:T(8,128)} %jitter_ref.3, ...), custom_call_target="tpu_custom_call" | custom-call | flops 31457280 | bytes 3145728 | tf_op jit(solution)/shard_map/close/pallas_call | solution.py:179
  23.4 33.0 %all_to_all.5.code_ref = s16[16,4,16,512]{3,2,1,0:T(8,128)(2,1)S(1)} all-to-all(s16[16,4,16,512]{3,2,1,0:T(8,128)(2,1)} %close.1), channel_id=1, replica_groups=mesh['groups'=2,'depth'=16] {'depth'}, dimensions={0} | all-to-all | bytes 2097152 | tf_op jit(solution)/shard_map/all_to_all | solution.py:260
  56.4 0.0 copy-done
  56.4 0.0 copy-done.1
  56.4 2.0 %composite.1 = f32[4,16,512]{2,1,0:T(8,128)} custom-call(s32[16]{0:T(128)S(1)} %copy-done, f32[4]{0:T(128)S(1)} %copy-done.1, s16[16,4,16,512]{3,2,1,0:T(8,128)(2,1)S(1)} %all_to_all.5.code_ref), custom_call_target="tpu_custom_call" | custom-call | tf_op jit(solution)/shard_map/composite/pallas_call | solution.py:236
Async XLA Ops:
  1.0 11.0 %collective-permute-start = (bf16[16,8192]{1,0:T(8,128)(2,1)S(1)}, bf16[16,8192]{1,0:T(8,128)(2,1)S(1)}, u32[]{:S(2)}, u32[]{:S(2)}) collective-permute-start(bf16[16,8192]{1,0:T(8,128)(2,1)S(1)} %slice_bitcast_fusion), channel_id=1, source_target_pairs={{1,0},{2,1},{3,2},{4,3},{5,4},{6,5},{7,6},{8,7},{9,8},{10,9},{11,1... | collective-permute-start | bytes 786440 | tf_op jit(solution)/shard_map/ppermute | solution.py:26
  12.0 44.4 %copy-start = (s32[16]{0:T(128)S(1)}, s32[16]{0:T(128)}, u32[]{:S(2)}) copy-start(s32[16]{0:T(128)} %order_ref.1) | copy-start | bytes 196
  12.0 44.4 %copy-start.1 = (f32[4]{0:T(128)S(1)}, f32[4]{0:T(128)}, u32[]{:S(2)}) copy-start(f32[4]{0:T(128)} %transfer_ref.5) | copy-start | bytes 52
  12.0 0.7 %copy-start.2 = (bf16[16,8192]{1,0:T(8,128)(2,1)}, bf16[16,8192]{1,0:T(8,128)(2,1)S(1)}, u32[]{:S(2)}) copy-start(bf16[16,8192]{1,0:T(8,128)(2,1)S(1)} %collective-permute-done.halo_ref) | copy-start | bytes 786436

commit v4 on v3

v4 whole, which is shorter than its diff:
```python
import functools
import math

import jax
import jax.numpy as jnp
from jax import lax
from jax.experimental import pallas as pl
from jax.experimental.pallas import tpu as pltpu
from jax.sharding import PartitionSpec as P

TOP = 5.2
LOG2E = math.log2(math.e)
LANES = 128
MARCH_BYTES = 54 * 1024 * 1024
SMALL_BYTES = 16 * 1024 * 1024


def spans(slab_len):
    deep = math.log2(slab_len)
    return 6.8 + deep, 13.2 + deep


def shifted(value, axis, steps):
    count = lax.axis_size(axis)
    initial, last = (max(0, -steps), min(count, count - steps))
    return lax.ppermute(value, axis, [(source, source + steps) for source in range(initial, last)])


def encode(value, span):
    code = jnp.log2(value) * (65535.0 / span) + 65535.5
    code = jnp.minimum(jnp.maximum(code, 0.0), 65535.0)
    return (code.astype(jnp.int32) - 32768).astype(jnp.int16)


def tile_gains(gain_ref, gain, base, first_col, tile_cols, start_ref, end_ref):
    sample = lax.broadcasted_iota(jnp.int32, (8, LANES), 0) + base
    lane = lax.broadcasted_iota(jnp.int32, (8, LANES), 1)

    def block(n, carry):
        col = n * LANES
        tile = (first_col + col) // tile_cols
        start = jnp.full((8, LANES), start_ref[tile])
        end = jnp.full((8, LANES), end_ref[tile])
        for t in range(1, LANES // tile_cols):
            start = jnp.where(lane >= t * tile_cols, start_ref[tile + t], start)
            end = jnp.where(lane >= t * tile_cols, end_ref[tile + t], end)
        cols = pl.ds(pl.multiple_of(col, LANES), LANES)
        for k in range(0, gain_ref.shape[0], 8):
            active = (sample + k >= start) & (sample + k < end)
            gain_ref[k:k + 8, cols] = jnp.where(active, gain, 0.0)
        return carry

    blocks = gain_ref.shape[1] // LANES
    lax.fori_loop(0, blocks, block, 0, unroll=math.gcd(blocks, 4))


def march(gain_ref, plane_ref, chunk, cols, place, jitter, levels, halo=None):
    slab_len = plane_ref.shape[1]
    shape = jitter.shape
    stay = 1.0 - jitter
    lower = plane_ref[chunk, 0, :, cols].astype(jnp.float32)
    before = jnp.zeros(shape, jnp.float32)
    through = jnp.ones(shape, jnp.float32)
    sums = [jnp.zeros(shape, jnp.float32) for _ in range(3)]
    for k in range(slab_len - (halo is None)):
        following = plane_ref[chunk, k + 1, :, cols] if k + 1 < slab_len else halo
        upper = following.astype(jnp.float32)
        value = stay * lower + jitter * upper
        before = before + gain_ref[k:k + 1, place] * value
        beyond = jnp.exp2(before)
        emitted = (through - beyond) * value
        for i in range(3):
            sums[i] = sums[i] + emitted * pl.reciprocal(levels[i] + value, approx=True)
        through = beyond
        lower = upper
    return sums, before


def chunk_copy(field_ref, plane_ref, sems, first, chunk):
    width = plane_ref.shape[3]
    cols = pl.ds(pl.multiple_of((first + chunk) * width, width), width)
    return pltpu.make_async_copy(field_ref.at[:, :, cols], plane_ref.at[chunk], sems.at[chunk])


def each_block(plane_ref, copy, block_cols, body):
    chunks, _, _, width = plane_ref.shape

    def chunk_step(chunk, carry):
        copy(chunk).wait()

        def block(n, carry):
            cols = pl.ds(pl.multiple_of(n * block_cols, block_cols), block_cols)
            place = pl.ds(pl.multiple_of(chunk * width + n * block_cols, block_cols), block_cols)
            body(chunk, cols, place)
            return carry

        return lax.fori_loop(0, width // block_cols, block, carry)

    lax.fori_loop(0, chunks, chunk_step, 0)


def open_kernel(total, tile_cols, block_cols, base_ref, transfer_ref, start_ref, end_ref, field_ref, jitter_ref, state_ref,
                plane_ref, gain_ref, sems):
    chunks, slab_len, rows, width = plane_ref.shape
    copy = functools.partial(chunk_copy, field_ref, plane_ref, sems, 0)
    for chunk in range(chunks):
        copy(chunk).start()
    levels = [jnp.full((rows, block_cols), transfer_ref[i]) for i in range(3)]
    gain = jnp.full((8, LANES), transfer_ref[3]) * (-LOG2E * 0.2 / total)
    tile_gains(gain_ref, gain, base_ref[0], 0, tile_cols, start_ref, end_ref)

    def body(chunk, cols, place):
        sums, before = march(gain_ref, plane_ref, chunk, cols, place, jitter_ref[:, place], levels)
        for i in range(3):
            state_ref[i, :, place] = sums[i]
        state_ref[3, :, place] = before

    each_block(plane_ref, copy, block_cols, body)


def close_kernel(total, tile_cols, block_cols, base_ref, transfer_ref, start_ref, end_ref, field_ref, halo_ref, jitter_ref,
                 state_ref, out_ref, plane_ref, gain_ref, last_ref, last_gain_ref, sems, last_sem):
    chunks, slab_len, rows, width = plane_ref.shape
    opened = state_ref.shape[2]
    copy = functools.partial(chunk_copy, field_ref, plane_ref, sems, opened // width)
    last_copy = pltpu.make_async_copy(field_ref.at[slab_len - 1, :, pl.ds(0, opened)], last_ref, last_sem)
    last_copy.start()
    for chunk in range(chunks):
        copy(chunk).start()
    shape = (rows, block_cols)
    depth_gain = jnp.full(shape, transfer_ref[3]) * (0.2 / total)
    levels = [jnp.full(shape, transfer_ref[i]) for i in range(3)]
    depth_unit = 1.0 / (depth_gain * (slab_len * TOP))
    color_unit = [depth_unit * ((levels[i] + TOP) * (1.0 / TOP)) for i in range(3)]
    depth_span, color_span = spans(slab_len)
    gain = depth_gain[:8, :LANES] * -LOG2E
    piece_width = out_ref.shape[3]
    tile_gains(last_gain_ref, gain, base_ref[0] + slab_len - 1, 0, tile_cols, start_ref, end_ref)
    tile_gains(gain_ref, gain, base_ref[0], opened, tile_cols, start_ref, end_ref)

    def store(col, sums, before):
        piece = col // piece_width
        out = pl.ds(pl.multiple_of(col % piece_width, block_cols), block_cols)
        for i in range(3):
            out_ref[piece, i, :, out] = encode(sums[i] * color_unit[i], color_span)
        out_ref[piece, 3, :, out] = encode(before * (depth_unit * (-1.0 / LOG2E)), depth_span)

    last_copy.wait()

    def finish(n, carry):
        cols = pl.ds(pl.multiple_of(n * block_cols, block_cols), block_cols)
        jitter = jitter_ref[:, cols]
        lower = last_ref[:, cols].astype(jnp.float32)
        upper = halo_ref[:, cols].astype(jnp.float32)
        value = (1.0 - jitter) * lower + jitter * upper
        before = state_ref[3, :, cols]
        beyond = before + last_gain_ref[0:1, cols] * value
        emitted = (jnp.exp2(before) - jnp.exp2(beyond)) * value
        sums = [state_ref[i, :, cols] + emitted * pl.reciprocal(levels[i] + value, approx=True) for i in range(3)]
        store(n * block_cols, sums, beyond)
        return carry

    lax.fori_loop(0, opened // block_cols, finish, 0)

    def body(chunk, cols, place):
        col = pl.multiple_of(opened + place.start, block_cols)
        whole = pl.ds(col, block_cols)
        sums, before = march(gain_ref, plane_ref, chunk, cols, place, jitter_ref[:, whole], levels, halo_ref[:, whole])
        store(col, sums, before)

    each_block(plane_ref, copy, block_cols, body)


def slab_codes(field, halo, jitter, transfer, ray_start, ray_end, base, total, pieces):
    slab_len, rows, cols = field.shape
    width = cols // pieces
    chunk = max(width, min(1024, cols // 2))
    chunks = cols // chunk
    opened = max(1, chunks * 5 // 8)
    closed = chunks - opened
    block_cols = min(2 * LANES, width)
    tile_cols = cols // ray_start.shape[0]
    smem = pl.BlockSpec(memory_space=pltpu.SMEM)
    vmem = pl.BlockSpec(memory_space=pltpu.VMEM)
    hbm = pl.BlockSpec(memory_space=pl.ANY)
    params = pltpu.CompilerParams(vmem_limit_bytes=MARCH_BYTES)
    scalars = (base, transfer, ray_start, ray_end)

    def cost(share):
        work = slab_len * rows * cols * share // chunks
        return pl.CostEstimate(flops=work * 20, bytes_accessed=work * 2, transcendentals=work * 4)

    state = pl.pallas_call(
        functools.partial(open_kernel, total, tile_cols, block_cols),
        in_specs=[smem, smem, smem, smem, hbm, vmem],
        out_specs=vmem,
        out_shape=jax.ShapeDtypeStruct((4, rows, opened * chunk), jnp.float32),
        scratch_shapes=[
            pltpu.VMEM((opened, slab_len, rows, chunk), field.dtype),
            pltpu.VMEM((slab_len, opened * chunk), jnp.float32),
            pltpu.SemaphoreType.DMA((opened,)),
        ],
        compiler_params=params,
        cost_estimate=cost(opened),
        name="open",
    )(*scalars, field, jitter)
    return pl.pallas_call(
        functools.partial(close_kernel, total, tile_cols, block_cols),
        in_specs=[smem, smem, smem, smem, hbm, vmem, vmem, vmem],
        out_specs=vmem,
        out_shape=jax.ShapeDtypeStruct((pieces, 4, rows, width), jnp.int16),
        scratch_shapes=[
            pltpu.VMEM((closed, slab_len, rows, chunk), field.dtype),
            pltpu.VMEM((slab_len, closed * chunk), jnp.float32),
            pltpu.VMEM((rows, opened * chunk), field.dtype),
            pltpu.VMEM((8, opened * chunk), jnp.float32),
            pltpu.SemaphoreType.DMA((closed,)),
            pltpu.SemaphoreType.DMA,
        ],
        compiler_params=params,
        cost_estimate=cost(closed),
        name="close",
    )(*scalars, field, halo, jitter, state)


def composite_kernel(total, slab_len, order_ref, transfer_ref, code_ref, out_ref):
    count, _, rows, width = code_ref.shape
    lanes = min(width, LANES)
    depth_span, color_span = spans(slab_len)
    depth_gain = jnp.full((rows, lanes), transfer_ref[3]) * (0.2 / total)
    unit = depth_gain * (slab_len * TOP)
    depth_unit = unit * LOG2E

    def decode(codes, span, shift):
        code = codes.astype(jnp.int32).astype(jnp.float32)
        value = jnp.exp2(code * (span / 65535.0) + (span * (32768.0 / 65535.0) - span) - shift)
        return jnp.where(code > -32768.0, value, 0.0)

    for n in range(width // lanes):
        cols = slice(n * lanes, (n + 1) * lanes)

        def step(j, carry):
            depth, red, green, blue = carry
            slab = order_ref[j]
            colors = [red, green, blue]
            for i in range(3):
                colors[i] = colors[i] + decode(code_ref[slab, i, :, cols], color_span, depth)
            depth = depth + depth_unit * decode(code_ref[slab, 3, :, cols], depth_span, 0.0)
            return depth, *colors

        zero = jnp.zeros((rows, lanes), jnp.float32)
        depth, *colors = lax.fori_loop(0, count, step, (zero, zero, zero, zero), unroll=4)
        for i in range(3):
            level = jnp.full((rows, lanes), transfer_ref[i])
            out_ref[i, :, cols] = colors[i] * (unit * (TOP / (level + TOP)))
        out_ref[3, :, cols] = 1.0 - jnp.exp2(-depth)


def composite(codes, transfer, depth_order, total, slab_len):
    _, _, rows, width = codes.shape
    smem = pl.BlockSpec(memory_space=pltpu.SMEM)
    vmem = pl.BlockSpec(memory_space=pltpu.VMEM)
    return pl.pallas_call(
        functools.partial(composite_kernel, total, slab_len),
        in_specs=[smem, smem, vmem],
        out_specs=vmem,
        out_shape=jax.ShapeDtypeStruct((4, rows, width), jnp.float32),
        compiler_params=pltpu.CompilerParams(vmem_limit_bytes=SMALL_BYTES),
        name="composite",
    )(depth_order, transfer, codes)


def on_device(field, jitter, transfer, depth_order, ray_start, ray_end):
    count = lax.axis_size("depth")
    here = lax.axis_index("depth")
    slab_len, rows, cols = field.shape
    total = slab_len * count
    width = cols // count
    halo = shifted(field[0], "depth", -1)
    base = jnp.reshape(here * slab_len, (1,)).astype(jnp.int32)
    args = (field, halo, jitter, transfer, ray_start, ray_end, base, total)
    if width % LANES == 0:
        codes = slab_codes(*args, count)
    else:
        codes = slab_codes(*args, cols // LANES)
        codes = codes.transpose(1, 2, 0, 3).reshape(4, rows, count, width).transpose(2, 0, 1, 3)
    received = lax.all_to_all(codes, "depth", split_axis=0, concat_axis=0, tiled=True)
    return composite(received, transfer, depth_order, total, slab_len)


def solution(mesh):
    in_specs = (P("depth", "groups", None), P("groups", None), P(), P(), P(), P())
    out_specs = P(None, "groups", "depth")
    return jax.shard_map(
        on_device, mesh=mesh, in_specs=in_specs, out_specs=out_specs, check_vma=False
    )
```

time: 59.1 us -> 59.2 us (level)
  transfers between devices with their start and end apart: 1 -> 1, of which waited for: 0 -> 0; matrix products, arithmetic and copies ran while one was open for 0% -> 0% of each run, Pallas kernels for 17% -> 18%
where the time goes in v4:
time: 59.2 us; the launch traced here: 58.5 us
  blocking collectives  33 us (56%)
  Pallas kernels  22.5 us (38%)
  local copies, waits for them, and re-layouts  1.67 us (3%)
  starting transfers between devices  1.29 us (2%)
    all_to_all x1, blocking collectives, on_device(): lax.all_to_all(codes, 'depth', split_axis=0, concat_axis=0, tiled=True)  33 us
    pallas_call x1, Pallas kernels, slab_codes(): pl.pallas_call(functools.partial(open_kernel, total, tile_cols, block_col...  10.8 us
    pallas_call x1, Pallas kernels, slab_codes(): pl.pallas_call(functools.partial(close_kernel, total, tile_cols, block_co...  9.77 us
    pallas_call x1, Pallas kernels, composite(): pl.pallas_call(functools.partial(composite_kernel, total, slab_len), in_s...  1.98 us
    ppermute x1, starting transfers between devices, shifted(): lax.ppermute(value, axis, [(source, source + steps) for source in range(i...  1.29 us
  transfers between devices with their start and end apart: 1, of which 0 were waited for; matrix products, arithmetic and copies ran while one was open for 0% of the time, Pallas kernels for 18%

profile of v4, /device:TPU:0, one launch (start us, length us, event | category | flops | bytes accessed | tf_op | source)
XLA Modules:
  0.0 58.5 jit_solution(10315874720814261418)
XLA Ops:
  0.0 1.0 %slice_bitcast_fusion = bf16[16,8192]{1,0:T(8,128)(2,1)S(1)} fusion(bf16[32,16,8192]{2,1,0:T(8,128)(2,1)} %field_ref.3), kind=kLoop, calls=%fused_computation | loop fusion | bytes 524288 | tf_op jit(solution)/shard_map/squeeze | solution.py:279
  1.0 1.3 %collective-permute-start = (bf16[16,8192]{1,0:T(8,128)(2,1)S(1)}, bf16[16,8192]{1,0:T(8,128)(2,1)S(1)}, u32[]{:S(2)}, u32[]{:S(2)}) collective-permute-start(bf16[16,8192]{1,0:T(8,128)(2,1)S(1)} %slice_bitcast_fusion), channel_id=1, source_target_pairs={{1,0},{2,1},{3,2},{4,3},{5,4},{6,5},{7,6},{8,7},{9,8},{10,9},{11,1... | collective-permute-start | bytes 786440 | tf_op jit(solution)/shard_map/ppermute | solution.py:26
  2.3 10.8 %open.1.state_ref = f32[4,16,5120]{2,1,0:T(8,128)} custom-call(s32[1]{0:T(128)} %bitcast.base_ref, f32[4]{0:T(128)} %transfer_ref.5, s32[128]{0:T(128)} %start_ref.3, s32[128]{0:T(128)} %end_ref.3, bf16[32,16,8192]{2,1,0:T(8,128)(2,1)} %field_ref.3, f32[16,8192]{1,0:T(8,128)} %jitter_ref.3), custom_call_target="tpu_custom_call" | custom-call | flops 52428800 | bytes 5242880 | tf_op jit(solution)/shard_map/open/pallas_call | solution.py:193
  13.1 0.0 copy-start
  13.1 0.0 copy-start.1
  13.1 0.0 collective-permute-done.halo_ref
  13.1 0.0 copy-start.2
  13.1 0.7 %copy-done.2 = bf16[16,8192]{1,0:T(8,128)(2,1)} copy-done((bf16[16,8192]{1,0:T(8,128)(2,1)}, bf16[16,8192]{1,0:T(8,128)(2,1)S(1)}, u32[]{:S(2)}) %copy-start.2) | copy-done | bytes 262168
  13.8 9.8 %close.1 = s16[16,4,16,512]{3,2,1,0:T(8,128)(2,1)} custom-call(s32[1]{0:T(128)} %bitcast.base_ref, f32[4]{0:T(128)} %transfer_ref.5, s32[128]{0:T(128)} %start_ref.3, s32[128]{0:T(128)} %end_ref.3, bf16[32,16,8192]{2,1,0:T(8,128)(2,1)} %field_ref.3, bf16[16,8192]{1,0:T(8,128)(2,1)} %copy-done.2, f32[16,8192]{1,0:T(8,128)} %jitter_ref.3, ...), custom_call_target="tpu_custom_call" | custom-call | flops 31457280 | bytes 3145728 | tf_op jit(solution)/shard_map/close/pallas_call | solution.py:207
  23.6 33.0 %all_to_all.5.code_ref = s16[16,4,16,512]{3,2,1,0:T(8,128)(2,1)S(1)} all-to-all(s16[16,4,16,512]{3,2,1,0:T(8,128)(2,1)} %close.1), channel_id=1, replica_groups=mesh['groups'=2,'depth'=16] {'depth'}, dimensions={0} | all-to-all | bytes 2097152 | tf_op jit(solution)/shard_map/all_to_all | solution.py:287
  56.6 0.0 copy-done
  56.6 0.0 copy-done.1
  56.6 2.0 %composite.1 = f32[4,16,512]{2,1,0:T(8,128)} custom-call(s32[16]{0:T(128)S(1)} %copy-done, f32[4]{0:T(128)S(1)} %copy-done.1, s16[16,4,16,512]{3,2,1,0:T(8,128)(2,1)S(1)} %all_to_all.5.code_ref), custom_call_target="tpu_custom_call" | custom-call | tf_op jit(solution)/shard_map/composite/pallas_call | solution.py:263
Async XLA Ops:
  1.0 12.1 %collective-permute-start = (bf16[16,8192]{1,0:T(8,128)(2,1)S(1)}, bf16[16,8192]{1,0:T(8,128)(2,1)S(1)}, u32[]{:S(2)}, u32[]{:S(2)}) collective-permute-start(bf16[16,8192]{1,0:T(8,128)(2,1)S(1)} %slice_bitcast_fusion), channel_id=1, source_target_pairs={{1,0},{2,1},{3,2},{4,3},{5,4},{6,5},{7,6},{8,7},{9,8},{10,9},{11,1... | collective-permute-start | bytes 786440 | tf_op jit(solution)/shard_map/ppermute | solution.py:26
  13.1 43.5 %copy-start = (s32[16]{0:T(128)S(1)}, s32[16]{0:T(128)}, u32[]{:S(2)}) copy-start(s32[16]{0:T(128)} %order_ref.1) | copy-start | bytes 196
  13.1 43.5 %copy-start.1 = (f32[4]{0:T(128)S(1)}, f32[4]{0:T(128)}, u32[]{:S(2)}) copy-start(f32[4]{0:T(128)} %transfer_ref.5) | copy-start | bytes 52
  13.1 0.7 %copy-start.2 = (bf16[16,8192]{1,0:T(8,128)(2,1)}, bf16[16,8192]{1,0:T(8,128)(2,1)S(1)}, u32[]{:S(2)}) copy-start(bf16[16,8192]{1,0:T(8,128)(2,1)S(1)} %collective-permute-done.halo_ref) | copy-start | bytes 786436

commit v5 on v4

--- a/solution.py
+++ b/solution.py
@@ -52,6 +52,18 @@
 
     blocks = gain_ref.shape[1] // LANES
     lax.fori_loop(0, blocks, block, 0, unroll=math.gcd(blocks, 4))
+
+
+def moment(sums, emitted, value, levels):
+    share = emitted * pl.reciprocal((levels[0] + value) * (levels[1] + value) * (levels[2] + value), approx=True)
+    for n in range(3):
+        sums[n] = sums[n] + share
+        share = share * value
+
+
+def colors(sums, levels):
+    others = [(levels[1], levels[2]), (levels[2], levels[0]), (levels[0], levels[1])]
+    return [sums[2] + (p + q) * sums[1] + (p * q) * sums[0] for p, q in others]
 
 
 def march(gain_ref, plane_ref, chunk, cols, place, jitter, levels, halo=None):
@@ -69,8 +81,7 @@
         before = before + gain_ref[k:k + 1, place] * value
         beyond = jnp.exp2(before)
         emitted = (through - beyond) * value
-        for i in range(3):
-            sums[i] = sums[i] + emitted * pl.reciprocal(levels[i] + value, approx=True)
+        moment(sums, emitted, value, levels)
         through = beyond
         lower = upper
     return sums, before
@@ -141,8 +152,8 @@
     def store(col, sums, before):
         piece = col // piece_width
         out = pl.ds(pl.multiple_of(col % piece_width, block_cols), block_cols)
-        for i in range(3):
-            out_ref[piece, i, :, out] = encode(sums[i] * color_unit[i], color_span)
+        for i, color in enumerate(colors(sums, levels)):
+            out_ref[piece, i, :, out] = encode(color * color_unit[i], color_span)
         out_ref[piece, 3, :, out] = encode(before * (depth_unit * (-1.0 / LOG2E)), depth_span)
 
     last_copy.wait()
@@ -156,7 +167,8 @@
         before = state_ref[3, :, cols]
         beyond = before + last_gain_ref[0:1, cols] * value
         emitted = (jnp.exp2(before) - jnp.exp2(beyond)) * value
-        sums = [state_ref[i, :, cols] + emitted * pl.reciprocal(levels[i] + value, approx=True) for i in range(3)]
+        sums = [state_ref[i, :, cols] for i in range(3)]
+        moment(sums, emitted, value, levels)
         store(n * block_cols, sums, beyond)
         return carry
 

time: 59.2 us -> 59.5 us (level)
  transfers between devices with their start and end apart: 1 -> 1, of which waited for: 0 -> 0; matrix products, arithmetic and copies ran while one was open for 0% -> 0% of each run, Pallas kernels for 18% -> 19%
where the time goes in v5:
time: 59.5 us; the launch traced here: 58.9 us
  blocking collectives  33 us (55%)
  Pallas kernels  22.8 us (38%)
  local copies, waits for them, and re-layouts  1.67 us (3%)
  starting transfers between devices  1.29 us (2%)
    all_to_all x1, blocking collectives, on_device(): lax.all_to_all(codes, 'depth', split_axis=0, concat_axis=0, tiled=True)  33 us
    pallas_call x1, Pallas kernels, slab_codes(): pl.pallas_call(functools.partial(open_kernel, total, tile_cols, block_col...  11 us
    pallas_call x1, Pallas kernels, slab_codes(): pl.pallas_call(functools.partial(close_kernel, total, tile_cols, block_co...  9.85 us
    pallas_call x1, Pallas kernels, composite(): pl.pallas_call(functools.partial(composite_kernel, total, slab_len), in_s...  1.98 us
    ppermute x1, starting transfers between devices, shifted(): lax.ppermute(value, axis, [(source, source + steps) for source in range(i...  1.29 us
  transfers between devices with their start and end apart: 1, of which 0 were waited for; matrix products, arithmetic and copies ran while one was open for 0% of the time, Pallas kernels for 19%

profile of v5, /device:TPU:0, one launch (start us, length us, event | category | flops | bytes accessed | tf_op | source)
XLA Modules:
  0.0 58.9 jit_solution(10255012633714899357)
XLA Ops:
  0.0 1.0 %slice_bitcast_fusion = bf16[16,8192]{1,0:T(8,128)(2,1)S(1)} fusion(bf16[32,16,8192]{2,1,0:T(8,128)(2,1)} %field_ref.3), kind=kLoop, calls=%fused_computation | loop fusion | bytes 524288 | tf_op jit(solution)/shard_map/squeeze | solution.py:291
  1.0 1.3 %collective-permute-start = (bf16[16,8192]{1,0:T(8,128)(2,1)S(1)}, bf16[16,8192]{1,0:T(8,128)(2,1)S(1)}, u32[]{:S(2)}, u32[]{:S(2)}) collective-permute-start(bf16[16,8192]{1,0:T(8,128)(2,1)S(1)} %slice_bitcast_fusion), channel_id=1, source_target_pairs={{1,0},{2,1},{3,2},{4,3},{5,4},{6,5},{7,6},{8,7},{9,8},{10,9},{11,1... | collective-permute-start | bytes 786440 | tf_op jit(solution)/shard_map/ppermute | solution.py:26
  2.3 11.0 %open.1.state_ref = f32[4,16,5120]{2,1,0:T(8,128)} custom-call(s32[1]{0:T(128)} %bitcast.base_ref, f32[4]{0:T(128)} %transfer_ref.5, s32[128]{0:T(128)} %start_ref.3, s32[128]{0:T(128)} %end_ref.3, bf16[32,16,8192]{2,1,0:T(8,128)(2,1)} %field_ref.3, f32[16,8192]{1,0:T(8,128)} %jitter_ref.3), custom_call_target="tpu_custom_call" | custom-call | flops 52428800 | bytes 5242880 | tf_op jit(solution)/shard_map/open/pallas_call | solution.py:205
  13.3 0.0 copy-start
  13.3 0.0 copy-start.1
  13.3 0.0 collective-permute-done.halo_ref
  13.3 0.0 copy-start.2
  13.3 0.7 %copy-done.2 = bf16[16,8192]{1,0:T(8,128)(2,1)} copy-done((bf16[16,8192]{1,0:T(8,128)(2,1)}, bf16[16,8192]{1,0:T(8,128)(2,1)S(1)}, u32[]{:S(2)}) %copy-start.2) | copy-done | bytes 262168
  14.0 9.8 %close.1 = s16[16,4,16,512]{3,2,1,0:T(8,128)(2,1)} custom-call(s32[1]{0:T(128)} %bitcast.base_ref, f32[4]{0:T(128)} %transfer_ref.5, s32[128]{0:T(128)} %start_ref.3, s32[128]{0:T(128)} %end_ref.3, bf16[32,16,8192]{2,1,0:T(8,128)(2,1)} %field_ref.3, bf16[16,8192]{1,0:T(8,128)(2,1)} %copy-done.2, f32[16,8192]{1,0:T(8,128)} %jitter_ref.3, ...), custom_call_target="tpu_custom_call" | custom-call | flops 31457280 | bytes 3145728 | tf_op jit(solution)/shard_map/close/pallas_call | solution.py:219
  23.9 33.0 %all_to_all.5.code_ref = s16[16,4,16,512]{3,2,1,0:T(8,128)(2,1)S(1)} all-to-all(s16[16,4,16,512]{3,2,1,0:T(8,128)(2,1)} %close.1), channel_id=1, replica_groups=mesh['groups'=2,'depth'=16] {'depth'}, dimensions={0} | all-to-all | bytes 2097152 | tf_op jit(solution)/shard_map/all_to_all | solution.py:299
  56.9 0.0 copy-done
  56.9 0.0 copy-done.1
  56.9 2.0 %composite.1 = f32[4,16,512]{2,1,0:T(8,128)} custom-call(s32[16]{0:T(128)S(1)} %copy-done, f32[4]{0:T(128)S(1)} %copy-done.1, s16[16,4,16,512]{3,2,1,0:T(8,128)(2,1)S(1)} %all_to_all.5.code_ref), custom_call_target="tpu_custom_call" | custom-call | tf_op jit(solution)/shard_map/composite/pallas_call | solution.py:275
Async XLA Ops:
  1.0 12.4 %collective-permute-start = (bf16[16,8192]{1,0:T(8,128)(2,1)S(1)}, bf16[16,8192]{1,0:T(8,128)(2,1)S(1)}, u32[]{:S(2)}, u32[]{:S(2)}) collective-permute-start(bf16[16,8192]{1,0:T(8,128)(2,1)S(1)} %slice_bitcast_fusion), channel_id=1, source_target_pairs={{1,0},{2,1},{3,2},{4,3},{5,4},{6,5},{7,6},{8,7},{9,8},{10,9},{11,1... | collective-permute-start | bytes 786440 | tf_op jit(solution)/shard_map/ppermute | solution.py:26
  13.3 43.6 %copy-start = (s32[16]{0:T(128)S(1)}, s32[16]{0:T(128)}, u32[]{:S(2)}) copy-start(s32[16]{0:T(128)} %order_ref.1) | copy-start | bytes 196
  13.3 43.6 %copy-start.1 = (f32[4]{0:T(128)S(1)}, f32[4]{0:T(128)}, u32[]{:S(2)}) copy-start(f32[4]{0:T(128)} %transfer_ref.5) | copy-start | bytes 52
  13.3 0.7 %copy-start.2 = (bf16[16,8192]{1,0:T(8,128)(2,1)}, bf16[16,8192]{1,0:T(8,128)(2,1)S(1)}, u32[]{:S(2)}) copy-start(bf16[16,8192]{1,0:T(8,128)(2,1)S(1)} %collective-permute-done.halo_ref) | copy-start | bytes 786436

commit v6 on v5

v6 whole, which is shorter than its diff:
```python
import functools
import math

import jax
import jax.numpy as jnp
from jax import lax
from jax.experimental import pallas as pl
from jax.experimental.pallas import tpu as pltpu
from jax.sharding import PartitionSpec as P

TOP = 5.2
LOG2E = math.log2(math.e)
SUBLANES = 8
LANES = 128
MARCH_BYTES = 54 * 1024 * 1024
SMALL_BYTES = 16 * 1024 * 1024


def spans(slab_len):
    deep = math.log2(slab_len)
    return 6.8 + deep, 13.2 + deep


def shifted(value, axis, steps):
    count = lax.axis_size(axis)
    initial, last = (max(0, -steps), min(count, count - steps))
    return lax.ppermute(value, axis, [(source, source + steps) for source in range(initial, last)])


def encode(value, span):
    code = jnp.log2(value) * (65535.0 / span) + 65535.5
    code = jnp.minimum(jnp.maximum(code, 0.0), 65535.0)
    return code.astype(jnp.int32) - 32768


def halves(plane):
    wide = plane.astype(jnp.float32)
    return wide[:SUBLANES], wide[SUBLANES:]


def gather(sums, weight, depth, levels):
    whole = (levels[0] + depth) * (levels[1] + depth) * (levels[2] + depth)
    share = weight * pl.reciprocal(whole, approx=True, full_range=False) * depth
    out = []
    for n in range(3):
        out.append(sums[n] + share)
        share = share * depth
    return out


def colors(sums, levels):
    others = [(levels[1], levels[2]), (levels[2], levels[0]), (levels[0], levels[1])]
    return [sums[2] + (p + q) * sums[1] + (p * q) * sums[0] for p, q in others]


def march(planes, jitter, gain, levels, active):
    sides = []
    for j in halves(jitter):
        lean = j * gain
        zero = jnp.zeros_like(j)
        sides.append((gain - lean, lean, zero, jnp.ones_like(j), [zero, zero, zero]))
    lower = halves(planes[0])
    for k in range(len(planes) - 1):
        upper = halves(planes[k + 1])
        mask = active(k)
        for h in range(2):
            stay, lean, before, through, sums = sides[h]
            depth = stay * lower[h] + lean * upper[h]
            before = before - (depth if mask is None else jnp.where(mask, depth, 0.0))
            beyond = jnp.exp2(before)
            sides[h] = (stay, lean, before, beyond, gather(sums, through - beyond, depth, levels))
        lower = upper
    return [(side[4], side[2]) for side in sides]


class Tiles:
    def __init__(self, start_ref, end_ref, col, tile_cols):
        tile = col // tile_cols
        self.cols = tile_cols
        self.starts = [start_ref[tile + t] for t in range(LANES // tile_cols)]
        self.ends = [end_ref[tile + t] for t in range(LANES // tile_cols)]

    def full(self, first, last):
        return (functools.reduce(jnp.maximum, self.starts) <= first) & (functools.reduce(jnp.minimum, self.ends) >= last)

    def idle(self, first, last):
        return (functools.reduce(jnp.maximum, self.ends) <= first) | (functools.reduce(jnp.minimum, self.starts) >= last)

    def mask(self, first):
        lane = lax.broadcasted_iota(jnp.int32, (SUBLANES, LANES), 1)
        start = jnp.full((SUBLANES, LANES), self.starts[0])
        end = jnp.full((SUBLANES, LANES), self.ends[0])
        for t in range(1, len(self.starts)):
            start = jnp.where(lane >= t * self.cols, self.starts[t], start)
            end = jnp.where(lane >= t * self.cols, self.ends[t], end)
        start, end = start - first, end - first
        return lambda k: (start <= k) & (end > k)


def chunk_copy(field_ref, plane_ref, sems, first, chunk):
    width = plane_ref.shape[3]
    cols = pl.ds(pl.multiple_of((first + chunk) * width, width), width)
    return pltpu.make_async_copy(field_ref.at[:, :, cols], plane_ref.at[chunk], sems.at[chunk])


def each_block(plane_ref, copy, body):
    chunks, _, _, width = plane_ref.shape

    def chunk_step(chunk, carry):
        copy(chunk).wait()

        def block(n, carry):
            body(chunk, pl.ds(pl.multiple_of(n * LANES, LANES), LANES), pl.multiple_of(chunk * width + n * LANES, LANES))
            return carry

        return lax.fori_loop(0, width // LANES, block, carry)

    lax.fori_loop(0, chunks, chunk_step, 0)


def gains(total, transfer_ref):
    shape = (SUBLANES, LANES)
    gain = jnp.full(shape, transfer_ref[3]) * (LOG2E * 0.2 / total)
    return gain, [jnp.full(shape, transfer_ref[i]) * gain for i in range(3)]


def branches(tiles, first, last, run, idle):
    full, none = tiles.full(first, last), tiles.idle(first, last)
    pl.when(full)(lambda: run(lambda k: None))
    pl.when(none)(idle)
    pl.when(jnp.logical_not(full | none))(lambda: run(tiles.mask(first)))


def open_kernel(total, tile_cols, base_ref, transfer_ref, start_ref, end_ref, field_ref, jitter_ref, state_ref, plane_ref,
                sems):
    chunks, slab_len, rows, width = plane_ref.shape
    copy = functools.partial(chunk_copy, field_ref, plane_ref, sems, 0)
    for chunk in range(chunks):
        copy(chunk).start()
    gain, levels = gains(total, transfer_ref)
    first = base_ref[0]

    def body(chunk, cols, col):
        place = pl.ds(col, LANES)

        def run(active):
            planes = [plane_ref[chunk, k, :, cols] for k in range(slab_len)]
            done = march(planes, jitter_ref[:, place], gain, levels, active)
            for h, (sums, before) in enumerate(done):
                for i, value in enumerate([*sums, before]):
                    state_ref[i, h * SUBLANES:(h + 1) * SUBLANES, place] = value

        def idle():
            state_ref[:, :, place] = jnp.zeros((4, rows, LANES), jnp.float32)

        branches(Tiles(start_ref, end_ref, col, tile_cols), first, first + slab_len - 1, run, idle)

    each_block(plane_ref, copy, body)


def close_kernel(total, tile_cols, base_ref, transfer_ref, start_ref, end_ref, field_ref, halo_ref, jitter_ref,
                 state_ref, out_ref, plane_ref, last_ref, sems, last_sem):
    chunks, slab_len, rows, width = plane_ref.shape
    opened = state_ref.shape[2]
    copy = functools.partial(chunk_copy, field_ref, plane_ref, sems, opened // width)
    last_copy = pltpu.make_async_copy(field_ref.at[slab_len - 1, :, pl.ds(0, opened)], last_ref, last_sem)
    last_copy.start()
    for chunk in range(chunks):
        copy(chunk).start()
    gain, levels = gains(total, transfer_ref)
    first = base_ref[0]
    depth_unit = 1.0 / (gain * (slab_len * TOP))
    color_unit = [LOG2E * depth_unit * ((transfer_ref[i] + TOP) * (1.0 / TOP)) for i in range(3)]
    depth_span, color_span = spans(slab_len)
    piece_width = out_ref.shape[3]

    def store(col, done):
        piece = col // piece_width
        out = pl.ds(pl.multiple_of(col % piece_width, LANES), LANES)
        parts = [[], [], [], []]
        for sums, before in done:
            for i, color in enumerate(colors(sums, levels)):
                parts[i].append(encode(color * color_unit[i], color_span))
            parts[3].append(encode(before * -depth_unit, depth_span))
        for i, part in enumerate(parts):
            out_ref[piece, i, :, out] = jnp.concatenate(part, axis=0).astype(jnp.int16)

    last_copy.wait()

    def finish(n, carry):
        col = pl.multiple_of(n * LANES, LANES)
        cols = pl.ds(col, LANES)
        lower, upper, jitter = halves(last_ref[:, cols]), halves(halo_ref[:, cols]), halves(jitter_ref[:, cols])
        active = Tiles(start_ref, end_ref, col, tile_cols).mask(first + slab_len - 1)(0)
        done = []
        for h in range(2):
            *sums, before = [state_ref[i, h * SUBLANES:(h + 1) * SUBLANES, cols] for i in range(4)]
            lean = jitter[h] * gain
            depth = (gain - lean) * lower[h] + lean * upper[h]
            beyond = before - jnp.where(active, depth, 0.0)
            done.append((gather(sums, jnp.exp2(before) - jnp.exp2(beyond), depth, levels), beyond))
        store(col, done)
        return carry

    blocks = opened // LANES
    lax.fori_loop(0, blocks, finish, 0, unroll=math.gcd(blocks, 4))

    def body(chunk, cols, place):
        col = pl.multiple_of(opened + place, LANES)
        whole = pl.ds(col, LANES)

        def run(active):
            planes = [plane_ref[chunk, k, :, cols] for k in range(slab_len)] + [halo_ref[:, whole]]
            store(col, march(planes, jitter_ref[:, whole], gain, levels, active))

        def idle():
            out = pl.ds(pl.multiple_of(col % piece_width, LANES), LANES)
            out_ref[col // piece_width, :, :, out] = jnp.full((4, rows, LANES), -32768, jnp.int16)

        branches(Tiles(start_ref, end_ref, col, tile_cols), first, first + slab_len, run, idle)

    each_block(plane_ref, copy, body)


def slab_codes(field, halo, jitter, transfer, ray_start, ray_end, base, total, pieces):
    slab_len, rows, cols = field.shape
    width = cols // pieces
    chunk = max(width, min(1024, cols // 2))
    chunks = cols // chunk
    opened = max(1, chunks * 5 // 8)
    closed = chunks - opened
    tile_cols = cols // ray_start.shape[0]
    smem = pl.BlockSpec(memory_space=pltpu.SMEM)
    vmem = pl.BlockSpec(memory_space=pltpu.VMEM)
    hbm = pl.BlockSpec(memory_space=pl.ANY)
    params = pltpu.CompilerParams(vmem_limit_bytes=MARCH_BYTES)
    scalars = (base, transfer, ray_start, ray_end)

    def cost(share):
        work = slab_len * rows * cols * share // chunks
        return pl.CostEstimate(flops=work * 20, bytes_accessed=work * 2, transcendentals=work * 4)

    state = pl.pallas_call(
        functools.partial(open_kernel, total, tile_cols),
        in_specs=[smem, smem, smem, smem, hbm, vmem],
        out_specs=vmem,
        out_shape=jax.ShapeDtypeStruct((4, rows, opened * chunk), jnp.float32),
        scratch_shapes=[
            pltpu.VMEM((opened, slab_len, rows, chunk), field.dtype),
            pltpu.SemaphoreType.DMA((opened,)),
        ],
        compiler_params=params,
        cost_estimate=cost(opened),
        name="open",
    )(*scalars, field, jitter)
    return pl.pallas_call(
        functools.partial(close_kernel, total, tile_cols),
        in_specs=[smem, smem, smem, smem, hbm, vmem, vmem, vmem],
        out_specs=vmem,
        out_shape=jax.ShapeDtypeStruct((pieces, 4, rows, width), jnp.int16),
        scratch_shapes=[
            pltpu.VMEM((closed, slab_len, rows, chunk), field.dtype),
            pltpu.VMEM((rows, opened * chunk), field.dtype),
            pltpu.SemaphoreType.DMA((closed,)),
            pltpu.SemaphoreType.DMA,
        ],
        compiler_params=params,
        cost_estimate=cost(closed),
        name="close",
    )(*scalars, field, halo, jitter, state)


def composite_kernel(total, slab_len, order_ref, transfer_ref, code_ref, out_ref):
    count, _, rows, width = code_ref.shape
    lanes = min(width, LANES)
    depth_span, color_span = spans(slab_len)
    depth_gain = jnp.full((rows, lanes), transfer_ref[3]) * (0.2 / total)
    unit = depth_gain * (slab_len * TOP)
    depth_unit = unit * LOG2E

    def decode(codes, span, shift):
        code = codes.astype(jnp.int32).astype(jnp.float32)
        value = jnp.exp2(code * (span / 65535.0) + (span * (32768.0 / 65535.0) - span) - shift)
        return jnp.where(code > -32768.0, value, 0.0)

    for n in range(width // lanes):
        cols = slice(n * lanes, (n + 1) * lanes)

        def step(j, carry):
            depth, red, green, blue = carry
            slab = order_ref[j]
            colors = [red, green, blue]
            for i in range(3):
                colors[i] = colors[i] + decode(code_ref[slab, i, :, cols], color_span, depth)
            depth = depth + depth_unit * decode(code_ref[slab, 3, :, cols], depth_span, 0.0)
            return depth, *colors

        zero = jnp.zeros((rows, lanes), jnp.float32)
        depth, *colors = lax.fori_loop(0, count, step, (zero, zero, zero, zero), unroll=4)
        for i in range(3):
            level = jnp.full((rows, lanes), transfer_ref[i])
            out_ref[i, :, cols] = colors[i] * (unit * (TOP / (level + TOP)))
        out_ref[3, :, cols] = 1.0 - jnp.exp2(-depth)


def composite(codes, transfer, depth_order, total, slab_len):
    _, _, rows, width = codes.shape
    smem = pl.BlockSpec(memory_space=pltpu.SMEM)
    vmem = pl.BlockSpec(memory_space=pltpu.VMEM)
    return pl.pallas_call(
        functools.partial(composite_kernel, total, slab_len),
        in_specs=[smem, smem, vmem],
        out_specs=vmem,
        out_shape=jax.ShapeDtypeStruct((4, rows, width), jnp.float32),
        compiler_params=pltpu.CompilerParams(vmem_limit_bytes=SMALL_BYTES),
        name="composite",
    )(depth_order, transfer, codes)


def on_device(field, jitter, transfer, depth_order, ray_start, ray_end):
    count = lax.axis_size("depth")
    here = lax.axis_index("depth")
    slab_len, rows, cols = field.shape
    total = slab_len * count
    width = cols // count
    halo = shifted(field[0], "depth", -1)
    base = jnp.reshape(here * slab_len, (1,)).astype(jnp.int32)
    args = (field, halo, jitter, transfer, ray_start, ray_end, base, total)
    if width % LANES == 0:
        codes = slab_codes(*args, count)
    else:
        codes = slab_codes(*args, cols // LANES)
        codes = codes.transpose(1, 2, 0, 3).reshape(4, rows, count, width).transpose(2, 0, 1, 3)
    received = lax.all_to_all(codes, "depth", split_axis=0, concat_axis=0, tiled=True)
    return composite(received, transfer, depth_order, total, slab_len)


def solution(mesh):
    in_specs = (P("depth", "groups", None), P("groups", None), P(), P(), P(), P())
    out_specs = P(None, "groups", "depth")
    return jax.shard_map(
        on_device, mesh=mesh, in_specs=in_specs, out_specs=out_specs, check_vma=False
    )
```

time: 59.5 us -> 61.3 us (1.030)
  blocking collectives: 33 us -> 41.8 us
  Pallas kernels: 22.8 us -> 15.9 us
    all_to_all x1, blocking collectives: 33 us -> 41.8 us  [on_device(): lax.all_to_all(codes, 'depth', split_axis=0, concat_axis=0, tiled=True)]
    pallas_call x2, Pallas kernels: 20.9 us -> 13.9 us  [the longest x1 6.96 us: slab_codes(): pl.pallas_call(functools.partial(open_kernel, total, tile_cols), in_specs...]
  transfers between devices with their start and end apart: 1 -> 1, of which waited for: 0 -> 0; matrix products, arithmetic and copies ran while one was open for 0% -> 0% of each run, Pallas kernels for 19% -> 11%
where the time goes in v6:
time: 61.3 us; the launch traced here: 60.7 us
  blocking collectives  41.8 us (68%)
  Pallas kernels  15.9 us (26%)
  local copies, waits for them, and re-layouts  1.67 us (3%)
  starting transfers between devices  1.29 us (2%)
    all_to_all x1, blocking collectives, on_device(): lax.all_to_all(codes, 'depth', split_axis=0, concat_axis=0, tiled=True)  41.8 us
    pallas_call x1, Pallas kernels, slab_codes(): pl.pallas_call(functools.partial(open_kernel, total, tile_cols), in_specs...  6.96 us
    pallas_call x1, Pallas kernels, slab_codes(): pl.pallas_call(functools.partial(close_kernel, total, tile_cols), in_spec...  6.93 us
    pallas_call x1, Pallas kernels, composite(): pl.pallas_call(functools.partial(composite_kernel, total, slab_len), in_s...  1.98 us
    ppermute x1, starting transfers between devices, shifted(): lax.ppermute(value, axis, [(source, source + steps) for source in range(i...  1.29 us
  transfers between devices with their start and end apart: 1, of which 0 were waited for; matrix products, arithmetic and copies ran while one was open for 0% of the time, Pallas kernels for 11%

profile of v6, /device:TPU:0, one launch (start us, length us, event | category | flops | bytes accessed | tf_op | source)
XLA Modules:
  0.0 60.7 jit_solution(28410516042253284)
XLA Ops:
  0.0 1.0 %slice_bitcast_fusion = bf16[16,8192]{1,0:T(8,128)(2,1)S(1)} fusion(bf16[32,16,8192]{2,1,0:T(8,128)(2,1)} %field_ref.3), kind=kLoop, calls=%fused_computation | loop fusion | bytes 524288 | tf_op jit(solution)/shard_map/squeeze | solution.py:326
  1.0 1.3 %collective-permute-start = (bf16[16,8192]{1,0:T(8,128)(2,1)S(1)}, bf16[16,8192]{1,0:T(8,128)(2,1)S(1)}, u32[]{:S(2)}, u32[]{:S(2)}) collective-permute-start(bf16[16,8192]{1,0:T(8,128)(2,1)S(1)} %slice_bitcast_fusion), channel_id=1, source_target_pairs={{1,0},{2,1},{3,2},{4,3},{5,4},{6,5},{7,6},{8,7},{9,8},{10,9},{11,1... | collective-permute-start | bytes 786440 | tf_op jit(solution)/shard_map/ppermute | solution.py:27
  2.3 7.0 %open.1.state_ref = f32[4,16,5120]{2,1,0:T(8,128)} custom-call(s32[1]{0:T(128)} %bitcast.base_ref, f32[4]{0:T(128)} %transfer_ref.5, s32[128]{0:T(128)} %start_ref.3, s32[128]{0:T(128)} %end_ref.3, bf16[32,16,8192]{2,1,0:T(8,128)(2,1)} %field_ref.3, f32[16,8192]{1,0:T(8,128)} %jitter_ref.3), custom_call_target="tpu_custom_call" | custom-call | flops 52428800 | bytes 5242880 | tf_op jit(solution)/shard_map/open/pallas_call | solution.py:243
  9.2 0.0 copy-start
  9.3 0.0 copy-start.1
  9.3 0.0 collective-permute-done.halo_ref
  9.3 0.0 copy-start.2
  9.3 0.7 %copy-done.2 = bf16[16,8192]{1,0:T(8,128)(2,1)} copy-done((bf16[16,8192]{1,0:T(8,128)(2,1)}, bf16[16,8192]{1,0:T(8,128)(2,1)S(1)}, u32[]{:S(2)}) %copy-start.2) | copy-done | bytes 262168
  10.0 6.9 %close.1 = s16[16,4,16,512]{3,2,1,0:T(8,128)(2,1)} custom-call(s32[1]{0:T(128)} %bitcast.base_ref, f32[4]{0:T(128)} %transfer_ref.5, s32[128]{0:T(128)} %start_ref.3, s32[128]{0:T(128)} %end_ref.3, bf16[32,16,8192]{2,1,0:T(8,128)(2,1)} %field_ref.3, bf16[16,8192]{1,0:T(8,128)(2,1)} %copy-done.2, f32[16,8192]{1,0:T(8,128)} %jitter_ref.3, ...), custom_call_target="tpu_custom_call" | custom-call | flops 31457280 | bytes 3145728 | tf_op jit(solution)/shard_map/close/pallas_call | solution.py:256
  16.9 41.8 %all_to_all.5.code_ref = s16[16,4,16,512]{3,2,1,0:T(8,128)(2,1)S(1)} all-to-all(s16[16,4,16,512]{3,2,1,0:T(8,128)(2,1)} %close.1), channel_id=1, replica_groups=mesh['groups'=2,'depth'=16] {'depth'}, dimensions={0} | all-to-all | bytes 2097152 | tf_op jit(solution)/shard_map/all_to_all | solution.py:334
  58.7 0.0 copy-done
  58.7 0.0 copy-done.1
  58.7 2.0 %composite.1 = f32[4,16,512]{2,1,0:T(8,128)} custom-call(s32[16]{0:T(128)S(1)} %copy-done, f32[4]{0:T(128)S(1)} %copy-done.1, s16[16,4,16,512]{3,2,1,0:T(8,128)(2,1)S(1)} %all_to_all.5.code_ref), custom_call_target="tpu_custom_call" | custom-call | tf_op jit(solution)/shard_map/composite/pallas_call | solution.py:310
Async XLA Ops:
  1.0 8.3 %collective-permute-start = (bf16[16,8192]{1,0:T(8,128)(2,1)S(1)}, bf16[16,8192]{1,0:T(8,128)(2,1)S(1)}, u32[]{:S(2)}, u32[]{:S(2)}) collective-permute-start(bf16[16,8192]{1,0:T(8,128)(2,1)S(1)} %slice_bitcast_fusion), channel_id=1, source_target_pairs={{1,0},{2,1},{3,2},{4,3},{5,4},{6,5},{7,6},{8,7},{9,8},{10,9},{11,1... | collective-permute-start | bytes 786440 | tf_op jit(solution)/shard_map/ppermute | solution.py:27
  9.2 49.4 %copy-start = (s32[16]{0:T(128)S(1)}, s32[16]{0:T(128)}, u32[]{:S(2)}) copy-start(s32[16]{0:T(128)} %order_ref.1) | copy-start | bytes 196
  9.3 49.4 %copy-start.1 = (f32[4]{0:T(128)S(1)}, f32[4]{0:T(128)}, u32[]{:S(2)}) copy-start(f32[4]{0:T(128)} %transfer_ref.5) | copy-start | bytes 52
  9.3 0.7 %copy-start.2 = (bf16[16,8192]{1,0:T(8,128)(2,1)}, bf16[16,8192]{1,0:T(8,128)(2,1)S(1)}, u32[]{:S(2)}) copy-start(bf16[16,8192]{1,0:T(8,128)(2,1)S(1)} %collective-permute-done.halo_ref) | copy-start | bytes 786436

commit v7 on v5

v7 whole, which is shorter than its diff:
```python
import functools
import math

import jax
import jax.numpy as jnp
from jax import lax
from jax.experimental import pallas as pl
from jax.experimental.pallas import tpu as pltpu
from jax.sharding import PartitionSpec as P

TOP = 5.2
LOG2E = math.log2(math.e)
SUBLANES = 8
LANES = 128
BLOCK = 256
STEP = 512
OPEN_BYTES = 54 * 1024 * 1024
CLOSE_BYTES = 52 * 1024 * 1024
SMALL_BYTES = 16 * 1024 * 1024


def spans(slab_len):
    deep = math.log2(slab_len)
    return 6.8 + deep, 13.2 + deep


def shifted(value, axis, steps):
    count = lax.axis_size(axis)
    initial, last = (max(0, -steps), min(count, count - steps))
    return lax.ppermute(value, axis, [(source, source + steps) for source in range(initial, last)])


def encode(value, span):
    code = jnp.log2(value) * (65535.0 / span) + 65535.5
    code = jnp.minimum(jnp.maximum(code, 0.0), 65535.0)
    return (code.astype(jnp.int32) - 32768).astype(jnp.int16)


def tile_gains(gain_ref, gain, base, first_col, tile_cols, start_ref, end_ref):
    sample = lax.broadcasted_iota(jnp.int32, (8, LANES), 0) + base
    lane = lax.broadcasted_iota(jnp.int32, (8, LANES), 1)

    def block(n, carry):
        col = n * LANES
        tile = (first_col + col) // tile_cols
        start = jnp.full((8, LANES), start_ref[tile])
        end = jnp.full((8, LANES), end_ref[tile])
        for t in range(1, LANES // tile_cols):
            start = jnp.where(lane >= t * tile_cols, start_ref[tile + t], start)
            end = jnp.where(lane >= t * tile_cols, end_ref[tile + t], end)
        cols = pl.ds(pl.multiple_of(col, LANES), LANES)
        for k in range(0, gain_ref.shape[0], 8):
            active = (sample + k >= start) & (sample + k < end)
            gain_ref[k:k + 8, cols] = jnp.where(active, gain, 0.0)
        return carry

    blocks = gain_ref.shape[1] // LANES
    lax.fori_loop(0, blocks, block, 0, unroll=math.gcd(blocks, 4))


def moment(sums, emitted, value, levels):
    share = emitted * pl.reciprocal((levels[0] + value) * (levels[1] + value) * (levels[2] + value), approx=True)
    for n in range(3):
        sums[n] = sums[n] + share
        share = share * value


def colors(sums, levels):
    others = [(levels[1], levels[2]), (levels[2], levels[0]), (levels[0], levels[1])]
    return [sums[2] + (p + q) * sums[1] + (p * q) * sums[0] for p, q in others]


def march(gain_ref, plane_ref, chunk, cols, place, jitter, levels, halo=None):
    slab_len = plane_ref.shape[1]
    shape = jitter.shape
    stay = 1.0 - jitter
    lower = plane_ref[chunk, 0, :, cols].astype(jnp.float32)
    before = jnp.zeros(shape, jnp.float32)
    through = jnp.ones(shape, jnp.float32)
    sums = [jnp.zeros(shape, jnp.float32) for _ in range(3)]
    for k in range(slab_len - (halo is None)):
        following = plane_ref[chunk, k + 1, :, cols] if k + 1 < slab_len else halo
        upper = following.astype(jnp.float32)
        value = stay * lower + jitter * upper
        before = before + gain_ref[k:k + 1, place] * value
        beyond = jnp.exp2(before)
        emitted = (through - beyond) * value
        moment(sums, emitted, value, levels)
        through = beyond
        lower = upper
    return sums, before


class Arrivals:
    def __init__(self, pairs, sems):
        self.copies = [pltpu.make_async_copy(src, dst, sems.at[n]) for n, (src, dst) in enumerate(pairs)]

    def start(self):
        for copy in self.copies:
            copy.start()

    def wait(self, first, count=1):
        for copy in self.copies[first:first + count]:
            copy.wait()


def each_step(chunk_cols, body):
    def step(n, carry):
        for part in range(STEP // BLOCK):
            body(pl.multiple_of(n * STEP + part * BLOCK, BLOCK))
        return carry

    lax.fori_loop(0, chunk_cols // STEP, step, 0)


def open_kernel(total, tile_cols, transfer_any, start_any, end_any, field_ref, jitter_any, state_any, transfer_ref, start_ref,
                end_ref, plane_ref, jitter_ref, state_ref, gain_ref, sems, out_sems):
    chunks, slab_len, rows, width = plane_ref.shape
    scalars = [(transfer_any, transfer_ref), (start_any, start_ref), (end_any, end_ref)]
    chunk_pairs = []
    for chunk in range(chunks):
        cols = pl.ds(chunk * width, width)
        chunk_pairs.append((jitter_any.at[:, cols], jitter_ref.at[chunk]))
        chunk_pairs.append((field_ref.at[:, :, cols], plane_ref.at[chunk]))
    arrivals = Arrivals(scalars + chunk_pairs, sems)
    arrivals.start()
    base = lax.axis_index("depth") * slab_len
    arrivals.wait(0, len(scalars))
    levels = [jnp.full((rows, BLOCK), transfer_ref[i]) for i in range(3)]
    gain = jnp.full((SUBLANES, LANES), transfer_ref[3]) * (-LOG2E * 0.2 / total)
    tile_gains(gain_ref, gain, base, 0, tile_cols, start_ref, end_ref)
    leaving = []
    for chunk in range(chunks):
        arrivals.wait(len(scalars) + 2 * chunk, 2)

        def body(col):
            cols = pl.ds(col, BLOCK)
            place = pl.ds(pl.multiple_of(chunk * width + col, BLOCK), BLOCK)
            sums, before = march(gain_ref, plane_ref, chunk, cols, place, jitter_ref[chunk, :, cols], levels)
            for i in range(3):
                state_ref[chunk, i, :, cols] = sums[i]
            state_ref[chunk, 3, :, cols] = before

        each_step(width, body)
        leaving.append(pltpu.make_async_copy(state_ref.at[chunk], state_any.at[chunk], out_sems.at[chunk]))
        leaving[-1].start()
    for copy in leaving:
        copy.wait()


def close_kernel(total, tile_cols, opened, transfer_any, start_any, end_any, field_ref, halo_any, jitter_any, state_any, out_any,
                 transfer_ref, start_ref, end_ref, plane_ref, halo_ref, jitter_ref, state_ref, last_ref, out_ref, gain_ref,
                 last_gain_ref, sems, out_sems):
    chunks, slab_len, rows, width = plane_ref.shape
    first_col = opened * width
    pieces, _, _, piece_width = out_ref.shape
    per = width // piece_width
    scalars = [(transfer_any, transfer_ref), (start_any, start_ref), (end_any, end_ref), (halo_any, halo_ref)]
    pairs = list(scalars)
    for chunk in range(chunks):
        cols = pl.ds(first_col + chunk * width, width)
        pairs.append((jitter_any.at[:, cols], jitter_ref.at[opened + chunk]))
        pairs.append((field_ref.at[:, :, cols], plane_ref.at[chunk]))
    late = len(pairs)
    pairs.append((field_ref.at[slab_len - 1, :, pl.ds(0, first_col)], last_ref))
    pairs.append((state_any, state_ref))
    for chunk in range(opened):
        pairs.append((jitter_any.at[:, pl.ds(chunk * width, width)], jitter_ref.at[chunk]))
    arrivals = Arrivals(pairs, sems)
    arrivals.start()
    base = lax.axis_index("depth") * slab_len
    arrivals.wait(0, len(scalars))
    shape = (rows, BLOCK)
    depth_gain = jnp.full(shape, transfer_ref[3]) * (0.2 / total)
    levels = [jnp.full(shape, transfer_ref[i]) for i in range(3)]
    depth_unit = 1.0 / (depth_gain * (slab_len * TOP))
    color_unit = [depth_unit * ((levels[i] + TOP) * (1.0 / TOP)) for i in range(3)]
    depth_span, color_span = spans(slab_len)
    gain = depth_gain[:SUBLANES, :LANES] * -LOG2E
    tile_gains(gain_ref, gain, base, first_col, tile_cols, start_ref, end_ref)
    tile_gains(last_gain_ref, gain, base + slab_len - 1, 0, tile_cols, start_ref, end_ref)
    leaving = []

    def store(chunk, col, sums, before):
        piece = chunk * per + col // piece_width
        out = pl.ds(pl.multiple_of(col % piece_width, BLOCK), BLOCK)
        for i, color in enumerate(colors(sums, levels)):
            out_ref[piece, i, :, out] = encode(color * color_unit[i], color_span)
        out_ref[piece, 3, :, out] = encode(before * (depth_unit * (-1.0 / LOG2E)), depth_span)

    def leave(chunk):
        place = pl.ds(chunk * per, per)
        leaving.append(pltpu.make_async_copy(out_ref.at[place], out_any.at[place], out_sems.at[chunk]))
        leaving[-1].start()

    for chunk in range(chunks):
        arrivals.wait(len(scalars) + 2 * chunk, 2)

        def body(col):
            cols = pl.ds(col, BLOCK)
            place = pl.ds(pl.multiple_of(chunk * width + col, BLOCK), BLOCK)
            whole = pl.ds(pl.multiple_of(first_col + chunk * width + col, BLOCK), BLOCK)
            jitter = jitter_ref[opened + chunk, :, cols]
            sums, before = march(gain_ref, plane_ref, chunk, cols, place, jitter, levels, halo_ref[:, whole])
            store(opened + chunk, col, sums, before)

        each_step(width, body)
        leave(opened + chunk)
    arrivals.wait(late, len(pairs) - late)
    for chunk in range(opened):

        def finish(col):
            cols = pl.ds(col, BLOCK)
            whole = pl.ds(pl.multiple_of(chunk * width + col, BLOCK), BLOCK)
            jitter = jitter_ref[chunk, :, cols]
            lower = last_ref[:, whole].astype(jnp.float32)
            upper = halo_ref[:, whole].astype(jnp.float32)
            value = (1.0 - jitter) * lower + jitter * upper
            before = state_ref[chunk, 3, :, cols]
            beyond = before + last_gain_ref[0:1, whole] * value
            emitted = (jnp.exp2(before) - jnp.exp2(beyond)) * value
            sums = [state_ref[chunk, i, :, cols] for i in range(3)]
            moment(sums, emitted, value, levels)
            store(chunk, col, sums, beyond)

        each_step(width, finish)
        leave(chunk)
    for copy in leaving:
        copy.wait()


def slab_codes(field, halo, jitter, transfer, ray_start, ray_end, total, pieces):
    slab_len, rows, cols = field.shape
    width = cols // pieces
    chunk = max(width, min(1024, cols // 2))
    chunks = cols // chunk
    opened = max(1, chunks * 5 // 8)
    closed = chunks - opened
    ntiles = ray_start.shape[0]
    tile_cols = cols // ntiles
    own = pl.BlockSpec(memory_space=pl.ANY)
    scalars = [pltpu.SMEM(transfer.shape, transfer.dtype)] + [pltpu.SMEM((ntiles,), jnp.int32)] * 2

    def cost(share):
        work = slab_len * rows * cols * share // chunks
        return pl.CostEstimate(flops=work * 20, bytes_accessed=work * 2, transcendentals=work * 2)

    state = pl.pallas_call(
        functools.partial(open_kernel, total, tile_cols),
        in_specs=[own] * 5,
        out_specs=own,
        out_shape=jax.ShapeDtypeStruct((opened, 4, rows, chunk), jnp.float32),
        scratch_shapes=scalars + [
            pltpu.VMEM((opened, slab_len, rows, chunk), field.dtype),
            pltpu.VMEM((opened, rows, chunk), jnp.float32),
            pltpu.VMEM((opened, 4, rows, chunk), jnp.float32),
            pltpu.VMEM((slab_len, opened * chunk), jnp.float32),
            pltpu.SemaphoreType.DMA((3 + 2 * opened,)),
            pltpu.SemaphoreType.DMA((opened,)),
        ],
        compiler_params=pltpu.CompilerParams(vmem_limit_bytes=OPEN_BYTES),
        cost_estimate=cost(opened),
        name="open",
    )(transfer, ray_start, ray_end, field, jitter)
    return pl.pallas_call(
        functools.partial(close_kernel, total, tile_cols, opened),
        in_specs=[own] * 7,
        out_specs=own,
        out_shape=jax.ShapeDtypeStruct((pieces, 4, rows, width), jnp.int16),
        scratch_shapes=scalars + [
            pltpu.VMEM((closed, slab_len, rows, chunk), field.dtype),
            pltpu.VMEM((rows, cols), field.dtype),
            pltpu.VMEM((chunks, rows, chunk), jnp.float32),
            pltpu.VMEM((opened, 4, rows, chunk), jnp.float32),
            pltpu.VMEM((rows, opened * chunk), field.dtype),
            pltpu.VMEM((pieces, 4, rows, width), jnp.int16),
            pltpu.VMEM((slab_len, closed * chunk), jnp.float32),
            pltpu.VMEM((SUBLANES, opened * chunk), jnp.float32),
            pltpu.SemaphoreType.DMA((4 + 2 * closed + 2 + opened,)),
            pltpu.SemaphoreType.DMA((chunks,)),
        ],
        compiler_params=pltpu.CompilerParams(vmem_limit_bytes=CLOSE_BYTES),
        cost_estimate=cost(closed),
        name="close",
    )(transfer, ray_start, ray_end, field, halo, jitter, state)


def composite_kernel(total, slab_len, order_ref, transfer_ref, code_ref, out_ref):
    count, _, rows, width = code_ref.shape
    lanes = min(width, LANES)
    depth_span, color_span = spans(slab_len)
    depth_gain = jnp.full((rows, lanes), transfer_ref[3]) * (0.2 / total)
    unit = depth_gain * (slab_len * TOP)
    depth_unit = unit * LOG2E

    def decode(codes, span, shift):
        code = codes.astype(jnp.int32).astype(jnp.float32)
        value = jnp.exp2(code * (span / 65535.0) + (span * (32768.0 / 65535.0) - span) - shift)
        return jnp.where(code > -32768.0, value, 0.0)

    for n in range(width // lanes):
        cols = slice(n * lanes, (n + 1) * lanes)

        def step(j, carry):
            depth, red, green, blue = carry
            slab = order_ref[j]
            colors = [red, green, blue]
            for i in range(3):
                colors[i] = colors[i] + decode(code_ref[slab, i, :, cols], color_span, depth)
            depth = depth + depth_unit * decode(code_ref[slab, 3, :, cols], depth_span, 0.0)
            return depth, *colors

        zero = jnp.zeros((rows, lanes), jnp.float32)
        depth, *colors = lax.fori_loop(0, count, step, (zero, zero, zero, zero), unroll=4)
        for i in range(3):
            level = jnp.full((rows, lanes), transfer_ref[i])
            out_ref[i, :, cols] = colors[i] * (unit * (TOP / (level + TOP)))
        out_ref[3, :, cols] = 1.0 - jnp.exp2(-depth)


def composite(codes, transfer, depth_order, total, slab_len):
    _, _, rows, width = codes.shape
    smem = pl.BlockSpec(memory_space=pltpu.SMEM)
    vmem = pl.BlockSpec(memory_space=pltpu.VMEM)
    return pl.pallas_call(
        functools.partial(composite_kernel, total, slab_len),
        in_specs=[smem, smem, vmem],
        out_specs=vmem,
        out_shape=jax.ShapeDtypeStruct((4, rows, width), jnp.float32),
        compiler_params=pltpu.CompilerParams(vmem_limit_bytes=SMALL_BYTES),
        name="composite",
    )(depth_order, transfer, codes)


def on_device(field, jitter, transfer, depth_order, ray_start, ray_end):
    count = lax.axis_size("depth")
    slab_len, rows, cols = field.shape
    total = slab_len * count
    width = cols // count
    halo = shifted(field[0], "depth", -1)
    args = (field, halo, jitter, transfer, ray_start, ray_end, total)
    if width % BLOCK == 0:
        codes = slab_codes(*args, count)
    else:
        codes = slab_codes(*args, cols // BLOCK)
        codes = codes.transpose(1, 2, 0, 3).reshape(4, rows, count, width).transpose(2, 0, 1, 3)
    received = lax.all_to_all(codes, "depth", split_axis=0, concat_axis=0, tiled=True)
    return composite(received, transfer, depth_order, total, slab_len)


def solution(mesh):
    in_specs = (P("depth", "groups", None), P("groups", None), P(), P(), P(), P())
    out_specs = P(None, "groups", "depth")
    return jax.shard_map(
        on_device, mesh=mesh, in_specs=in_specs, out_specs=out_specs, check_vma=False
    )
```

time: 59.5 us -> 55.8 us (0.938)
  Pallas kernels: 22.8 us -> 20.1 us
  local copies, waits for them, and re-layouts: 1.67 us -> 1.05 us
    pallas_call x2, Pallas kernels: 20.9 us -> 18.1 us  [the longest x1 9.7 us: slab_codes(): pl.pallas_call(functools.partial(open_kernel, total, tile_cols), in_specs...]
    unnamed x6 -> x10, local copies, waits for them, and re-layouts: 0.7 us -> 0.02 us
  transfers between devices with their start and end apart: 1 -> 1, of which waited for: 0 -> 0; matrix products, arithmetic and copies ran while one was open for 0% -> 0% of each run, Pallas kernels for 19% -> 18%
where the time goes in v7:
time: 55.8 us; the launch traced here: 55.3 us
  blocking collectives  32.8 us (59%)
  Pallas kernels  20.1 us (36%)
  starting transfers between devices  1.29 us (2%)
  local copies, waits for them, and re-layouts  1.05 us (2%)
    all_to_all x1, blocking collectives, on_device(): lax.all_to_all(codes, 'depth', split_axis=0, concat_axis=0, tiled=True)  32.8 us
    pallas_call x1, Pallas kernels, slab_codes(): pl.pallas_call(functools.partial(open_kernel, total, tile_cols), in_specs...  9.7 us
    pallas_call x1, Pallas kernels, slab_codes(): pl.pallas_call(functools.partial(close_kernel, total, tile_cols, opened),...  8.4 us
    pallas_call x1, Pallas kernels, composite(): pl.pallas_call(functools.partial(composite_kernel, total, slab_len), in_s...  1.98 us
    ppermute x1, starting transfers between devices, shifted(): lax.ppermute(value, axis, [(source, source + steps) for source in range(i...  1.29 us
  transfers between devices with their start and end apart: 1, of which 0 were waited for; matrix products, arithmetic and copies ran while one was open for 0% of the time, Pallas kernels for 18%

profile of v7, /device:TPU:0, one launch (start us, length us, event | category | flops | bytes accessed | tf_op | source)
XLA Modules:
  0.0 55.3 jit_solution(2816195875060923897)
XLA Ops:
  0.0 0.0 copy-start.1
  0.0 0.0 copy-start.3
  0.0 0.0 copy-start.2
  0.0 0.0 copy-start
  0.0 1.0 %slice_bitcast_fusion = bf16[16,8192]{1,0:T(8,128)(2,1)S(1)} fusion(bf16[32,16,8192]{2,1,0:T(8,128)(2,1)} %field_ref.3), kind=kLoop, calls=%fused_computation | loop fusion | bytes 524288 | tf_op jit(solution)/shard_map/squeeze | solution.py:340
  1.0 1.3 %collective-permute-start = (bf16[16,8192]{1,0:T(8,128)(2,1)S(1)}, bf16[16,8192]{1,0:T(8,128)(2,1)S(1)}, u32[]{:S(2)}, u32[]{:S(2)}) collective-permute-start(bf16[16,8192]{1,0:T(8,128)(2,1)S(1)} %slice_bitcast_fusion), channel_id=1, source_target_pairs={{1,0},{2,1},{3,2},{4,3},{5,4},{6,5},{7,6},{8,7},{9,8},{10,9},{11,1... | collective-permute-start | bytes 786440 | tf_op jit(solution)/shard_map/ppermute | solution.py:30
  2.3 9.7 %open.1.state_any = f32[5,4,16,1024]{3,2,1,0:T(8,128)} custom-call(f32[4]{0:T(128)} %transfer_ref.1, s32[128]{0:T(128)} %start_any.3, s32[128]{0:T(128)} %end_any.3, bf16[32,16,8192]{2,1,0:T(8,128)(2,1)} %field_ref.3, f32[16,8192]{1,0:T(8,128)} %jitter_any.3), custom_call_target="tpu_custom_call" | custom-call | flops 52428800 | bytes 5242880 | tf_op jit(solution)/shard_map/open/pallas_call | solution.py:248
  12.0 0.0 copy-start.4
  12.1 0.0 collective-permute-done.halo_any
  12.1 0.0 copy-done.1
  12.1 0.0 copy-done.3
  12.1 0.0 copy-done.2
  12.1 0.0 copy-done
  12.1 8.4 %close.1 = s16[16,4,16,512]{3,2,1,0:T(8,128)(2,1)S(1)} custom-call(f32[4]{0:T(128)S(1)} %copy-done.1, s32[128]{0:T(128)S(1)} %copy-done.2, s32[128]{0:T(128)S(1)} %copy-done.3, bf16[32,16,8192]{2,1,0:T(8,128)(2,1)} %field_ref.3, bf16[16,8192]{1,0:T(8,128)(2,1)S(1)} %collective-permute-done.halo_any, f32[16,8192]{1,0:T(8,128)S(1)} %copy-done, ...), custom_call_target="tpu_custom_call" | custom-call | flops 31457280 | bytes 3145728 | tf_op jit(solution)/shard_map/close/pallas_call | solution.py:265
  20.5 32.8 %all_to_all.5.code_ref = s16[16,4,16,512]{3,2,1,0:T(8,128)(2,1)S(1)} all-to-all(s16[16,4,16,512]{3,2,1,0:T(8,128)(2,1)S(1)} %close.1), channel_id=1, replica_groups=mesh['groups'=2,'depth'=16] {'depth'}, dimensions={0} | all-to-all | bytes 2097152 | tf_op jit(solution)/shard_map/all_to_all | solution.py:347
  53.3 0.0 copy-done.4
  53.3 2.0 %composite.1 = f32[4,16,512]{2,1,0:T(8,128)} custom-call(s32[16]{0:T(128)S(1)} %copy-done.4, f32[4]{0:T(128)S(1)} %copy-done.1, s16[16,4,16,512]{3,2,1,0:T(8,128)(2,1)S(1)} %all_to_all.5.code_ref), custom_call_target="tpu_custom_call" | custom-call | tf_op jit(solution)/shard_map/composite/pallas_call | solution.py:325
Async XLA Ops:
  0.0 12.1 %copy-start.1 = (f32[4]{0:T(128)S(1)}, f32[4]{0:T(128)}, u32[]{:S(2)}) copy-start(f32[4]{0:T(128)} %transfer_ref.1) | copy-start | bytes 52
  0.0 12.1 %copy-start.3 = (s32[128]{0:T(128)S(1)}, s32[128]{0:T(128)}, u32[]{:S(2)}) copy-start(s32[128]{0:T(128)} %end_any.3) | copy-start | bytes 1540
  0.0 12.1 %copy-start.2 = (s32[128]{0:T(128)S(1)}, s32[128]{0:T(128)}, u32[]{:S(2)}) copy-start(s32[128]{0:T(128)} %start_any.3) | copy-start | bytes 1540
  0.0 12.1 %copy-start = (f32[16,8192]{1,0:T(8,128)S(1)}, f32[16,8192]{1,0:T(8,128)}, u32[]{:S(2)}) copy-start(f32[16,8192]{1,0:T(8,128)} %jitter_any.3) | copy-start | bytes 1572868
  1.0 11.0 %collective-permute-start = (bf16[16,8192]{1,0:T(8,128)(2,1)S(1)}, bf16[16,8192]{1,0:T(8,128)(2,1)S(1)}, u32[]{:S(2)}, u32[]{:S(2)}) collective-permute-start(bf16[16,8192]{1,0:T(8,128)(2,1)S(1)} %slice_bitcast_fusion), channel_id=1, source_target_pairs={{1,0},{2,1},{3,2},{4,3},{5,4},{6,5},{7,6},{8,7},{9,8},{10,9},{11,1... | collective-permute-start | bytes 786440 | tf_op jit(solution)/shard_map/ppermute | solution.py:30
  12.0 41.3 %copy-start.4 = (s32[16]{0:T(128)S(1)}, s32[16]{0:T(128)}, u32[]{:S(2)}) copy-start(s32[16]{0:T(128)} %order_ref.1) | copy-start | bytes 196

commit v8 on v7

--- a/solution.py
+++ b/solution.py
@@ -91,19 +91,6 @@
     return sums, before
 
 
-class Arrivals:
-    def __init__(self, pairs, sems):
-        self.copies = [pltpu.make_async_copy(src, dst, sems.at[n]) for n, (src, dst) in enumerate(pairs)]
-
-    def start(self):
-        for copy in self.copies:
-            copy.start()
-
-    def wait(self, first, count=1):
-        for copy in self.copies[first:first + count]:
-            copy.wait()
-
-
 def each_step(chunk_cols, body):
     def step(n, carry):
         for part in range(STEP // BLOCK):
@@ -113,25 +100,51 @@
     lax.fori_loop(0, chunk_cols // STEP, step, 0)
 
 
+def each_chunk(chunks, body):
+    def step(chunk, carry):
+        body(chunk)
+        return carry
+
+    lax.fori_loop(0, chunks, step, 0)
+
+
+def start_all(pairs, sems):
+    copies = [pltpu.make_async_copy(src, dst, sems.at[n]) for n, (src, dst) in enumerate(pairs)]
+    for copy in copies:
+        copy.start()
+    return copies
+
+
+def chunk_copies(field_ref, jitter_any, plane_ref, jitter_ref, sems, first, chunk):
+    width = plane_ref.shape[3]
+    cols = pl.ds(pl.multiple_of((first + chunk) * width, width), width)
+    return [
+        pltpu.make_async_copy(jitter_any.at[:, cols], jitter_ref.at[first + chunk], sems.at[0, chunk]),
+        pltpu.make_async_copy(field_ref.at[:, :, cols], plane_ref.at[chunk], sems.at[1, chunk]),
+    ]
+
+
 def open_kernel(total, tile_cols, transfer_any, start_any, end_any, field_ref, jitter_any, state_any, transfer_ref, start_ref,
-                end_ref, plane_ref, jitter_ref, state_ref, gain_ref, sems, out_sems):
+                end_ref, plane_ref, jitter_ref, state_ref, gain_ref, few_sems, sems, out_sems):
     chunks, slab_len, rows, width = plane_ref.shape
-    scalars = [(transfer_any, transfer_ref), (start_any, start_ref), (end_any, end_ref)]
-    chunk_pairs = []
+    early = start_all([(transfer_any, transfer_ref), (start_any, start_ref), (end_any, end_ref)], few_sems)
+    arrivals = functools.partial(chunk_copies, field_ref, jitter_any, plane_ref, jitter_ref, sems, 0)
     for chunk in range(chunks):
-        cols = pl.ds(chunk * width, width)
-        chunk_pairs.append((jitter_any.at[:, cols], jitter_ref.at[chunk]))
-        chunk_pairs.append((field_ref.at[:, :, cols], plane_ref.at[chunk]))
-    arrivals = Arrivals(scalars + chunk_pairs, sems)
-    arrivals.start()
+        for copy in arrivals(chunk):
+            copy.start()
     base = lax.axis_index("depth") * slab_len
-    arrivals.wait(0, len(scalars))
+    for copy in early:
+        copy.wait()
     levels = [jnp.full((rows, BLOCK), transfer_ref[i]) for i in range(3)]
     gain = jnp.full((SUBLANES, LANES), transfer_ref[3]) * (-LOG2E * 0.2 / total)
     tile_gains(gain_ref, gain, base, 0, tile_cols, start_ref, end_ref)
-    leaving = []
-    for chunk in range(chunks):
-        arrivals.wait(len(scalars) + 2 * chunk, 2)
+
+    def leave(chunk):
+        return pltpu.make_async_copy(state_ref.at[chunk], state_any.at[chunk], out_sems.at[chunk])
+
+    def run(chunk):
+        for copy in arrivals(chunk):
+            copy.wait()
 
         def body(col):
             cols = pl.ds(col, BLOCK)
@@ -142,34 +155,32 @@
             state_ref[chunk, 3, :, cols] = before
 
         each_step(width, body)
-        leaving.append(pltpu.make_async_copy(state_ref.at[chunk], state_any.at[chunk], out_sems.at[chunk]))
-        leaving[-1].start()
-    for copy in leaving:
-        copy.wait()
+        leave(chunk).start()
+
+    each_chunk(chunks, run)
+    each_chunk(chunks, lambda chunk: leave(chunk).wait())
 
 
 def close_kernel(total, tile_cols, opened, transfer_any, start_any, end_any, field_ref, halo_any, jitter_any, state_any, out_any,
                  transfer_ref, start_ref, end_ref, plane_ref, halo_ref, jitter_ref, state_ref, last_ref, out_ref, gain_ref,
-                 last_gain_ref, sems, out_sems):
+                 last_gain_ref, few_sems, sems, out_sems):
     chunks, slab_len, rows, width = plane_ref.shape
     first_col = opened * width
-    pieces, _, _, piece_width = out_ref.shape
+    piece_width = out_ref.shape[3]
     per = width // piece_width
-    scalars = [(transfer_any, transfer_ref), (start_any, start_ref), (end_any, end_ref), (halo_any, halo_ref)]
-    pairs = list(scalars)
+    few = [(transfer_any, transfer_ref), (start_any, start_ref), (end_any, end_ref), (halo_any, halo_ref)]
+    early = start_all(few, few_sems)
+    arrivals = functools.partial(chunk_copies, field_ref, jitter_any, plane_ref, jitter_ref, sems, opened)
     for chunk in range(chunks):
-        cols = pl.ds(first_col + chunk * width, width)
-        pairs.append((jitter_any.at[:, cols], jitter_ref.at[opened + chunk]))
-        pairs.append((field_ref.at[:, :, cols], plane_ref.at[chunk]))
-    late = len(pairs)
-    pairs.append((field_ref.at[slab_len - 1, :, pl.ds(0, first_col)], last_ref))
-    pairs.append((state_any, state_ref))
+        for copy in arrivals(chunk):
+            copy.start()
+    pairs = [(field_ref.at[slab_len - 1, :, pl.ds(0, first_col)], last_ref), (state_any, state_ref)]
     for chunk in range(opened):
         pairs.append((jitter_any.at[:, pl.ds(chunk * width, width)], jitter_ref.at[chunk]))
-    arrivals = Arrivals(pairs, sems)
-    arrivals.start()
+    late = start_all(pairs, few_sems.at[pl.ds(len(few), len(pairs))])
     base = lax.axis_index("depth") * slab_len
-    arrivals.wait(0, len(scalars))
+    for copy in early:
+        copy.wait()
     shape = (rows, BLOCK)
     depth_gain = jnp.full(shape, transfer_ref[3]) * (0.2 / total)
     levels = [jnp.full(shape, transfer_ref[i]) for i in range(3)]
@@ -179,7 +190,6 @@
     gain = depth_gain[:SUBLANES, :LANES] * -LOG2E
     tile_gains(gain_ref, gain, base, first_col, tile_cols, start_ref, end_ref)
     tile_gains(last_gain_ref, gain, base + slab_len - 1, 0, tile_cols, start_ref, end_ref)
-    leaving = []
 
     def store(chunk, col, sums, before):
         piece = chunk * per + col // piece_width
@@ -190,11 +200,11 @@
 
     def leave(chunk):
         place = pl.ds(chunk * per, per)
-        leaving.append(pltpu.make_async_copy(out_ref.at[place], out_any.at[place], out_sems.at[chunk]))
-        leaving[-1].start()
-
-    for chunk in range(chunks):
-        arrivals.wait(len(scalars) + 2 * chunk, 2)
+        return pltpu.make_async_copy(out_ref.at[place], out_any.at[place], out_sems.at[chunk])
+
+    def run(chunk):
+        for copy in arrivals(chunk):
+            copy.wait()
 
         def body(col):
             cols = pl.ds(col, BLOCK)
@@ -205,11 +215,14 @@
             store(opened + chunk, col, sums, before)
 
         each_step(width, body)
-        leave(opened + chunk)
-    arrivals.wait(late, len(pairs) - late)
-    for chunk in range(opened):
-
-        def finish(col):
+        leave(opened + chunk).start()
+
+    each_chunk(chunks, run)
+    for copy in late:
+        copy.wait()
+
+    def finish(chunk):
+        def body(col):
             cols = pl.ds(col, BLOCK)
             whole = pl.ds(pl.multiple_of(chunk * width + col, BLOCK), BLOCK)
             jitter = jitter_ref[chunk, :, cols]
@@ -223,10 +236,11 @@
             moment(sums, emitted, value, levels)
             store(chunk, col, sums, beyond)
 
-        each_step(width, finish)
-        leave(chunk)
-    for copy in leaving:
-        copy.wait()
+        each_step(width, body)
+        leave(chunk).start()
+
+    each_chunk(opened, finish)
+    each_chunk(opened + chunks, lambda chunk: leave(chunk).wait())
 
 
 def slab_codes(field, halo, jitter, transfer, ray_start, ray_end, total, pieces):
@@ -255,7 +269,8 @@
             pltpu.VMEM((opened, rows, chunk), jnp.float32),
             pltpu.VMEM((opened, 4, rows, chunk), jnp.float32),
             pltpu.VMEM((slab_len, opened * chunk), jnp.float32),
-            pltpu.SemaphoreType.DMA((3 + 2 * opened,)),
+            pltpu.SemaphoreType.DMA((3,)),
+            pltpu.SemaphoreType.DMA((2, opened)),
             pltpu.SemaphoreType.DMA((opened,)),
         ],
         compiler_params=pltpu.CompilerParams(vmem_limit_bytes=OPEN_BYTES),
@@ -276,7 +291,8 @@
             pltpu.VMEM((pieces, 4, rows, width), jnp.int16),
             pltpu.VMEM((slab_len, closed * chunk), jnp.float32),
             pltpu.VMEM((SUBLANES, opened * chunk), jnp.float32),
-            pltpu.SemaphoreType.DMA((4 + 2 * closed + 2 + opened,)),
+            pltpu.SemaphoreType.DMA((6 + opened,)),
+            pltpu.SemaphoreType.DMA((2, closed)),
             pltpu.SemaphoreType.DMA((chunks,)),
         ],
         compiler_params=pltpu.CompilerParams(vmem_limit_bytes=CLOSE_BYTES),

time: 55.8 us -> 55.9 us (level)
  transfers between devices with their start and end apart: 1 -> 1, of which waited for: 0 -> 0; matrix products, arithmetic and copies ran while one was open for 0% -> 0% of each run, Pallas kernels for 18% -> 17%
where the time goes in v8:
time: 55.9 us; the launch traced here: 55.4 us
  blocking collectives  32.8 us (59%)
  Pallas kernels  20.1 us (36%)
  starting transfers between devices  1.29 us (2%)
  local copies, waits for them, and re-layouts  1.05 us (2%)
    all_to_all x1, blocking collectives, on_device(): lax.all_to_all(codes, 'depth', split_axis=0, concat_axis=0, tiled=True)  32.8 us
    pallas_call x1, Pallas kernels, slab_codes(): pl.pallas_call(functools.partial(open_kernel, total, tile_cols), in_specs...  9.68 us
    pallas_call x1, Pallas kernels, slab_codes(): pl.pallas_call(functools.partial(close_kernel, total, tile_cols, opened),...  8.49 us
    pallas_call x1, Pallas kernels, composite(): pl.pallas_call(functools.partial(composite_kernel, total, slab_len), in_s...  1.98 us
    ppermute x1, starting transfers between devices, shifted(): lax.ppermute(value, axis, [(source, source + steps) for source in range(i...  1.29 us
  transfers between devices with their start and end apart: 1, of which 0 were waited for; matrix products, arithmetic and copies ran while one was open for 0% of the time, Pallas kernels for 17%

profile of v8, /device:TPU:0, one launch (start us, length us, event | category | flops | bytes accessed | tf_op | source)
XLA Modules:
  0.0 55.4 jit_solution(6012121799028484216)
XLA Ops:
  0.0 0.0 copy-start.1
  0.0 0.0 copy-start.3
  0.0 0.0 copy-start.2
  0.0 0.0 copy-start
  0.0 1.0 %slice_bitcast_fusion = bf16[16,8192]{1,0:T(8,128)(2,1)S(1)} fusion(bf16[32,16,8192]{2,1,0:T(8,128)(2,1)} %field_ref.3), kind=kLoop, calls=%fused_computation | loop fusion | bytes 524288 | tf_op jit(solution)/shard_map/squeeze | solution.py:356
  1.0 1.3 %collective-permute-start = (bf16[16,8192]{1,0:T(8,128)(2,1)S(1)}, bf16[16,8192]{1,0:T(8,128)(2,1)S(1)}, u32[]{:S(2)}, u32[]{:S(2)}) collective-permute-start(bf16[16,8192]{1,0:T(8,128)(2,1)S(1)} %slice_bitcast_fusion), channel_id=1, source_target_pairs={{1,0},{2,1},{3,2},{4,3},{5,4},{6,5},{7,6},{8,7},{9,8},{10,9},{11,1... | collective-permute-start | bytes 786440 | tf_op jit(solution)/shard_map/ppermute | solution.py:30
  2.3 9.7 %open.1.state_any = f32[5,4,16,1024]{3,2,1,0:T(8,128)} custom-call(f32[4]{0:T(128)} %transfer_ref.1, s32[128]{0:T(128)} %start_any.3, s32[128]{0:T(128)} %end_any.3, bf16[32,16,8192]{2,1,0:T(8,128)(2,1)} %field_ref.3, f32[16,8192]{1,0:T(8,128)} %jitter_any.3), custom_call_target="tpu_custom_call" | custom-call | flops 52428800 | bytes 5242880 | tf_op jit(solution)/shard_map/open/pallas_call | solution.py:262
  12.0 0.0 copy-start.4
  12.0 0.0 collective-permute-done.halo_any
  12.0 0.0 copy-done.1
  12.1 0.0 copy-done.3
  12.1 0.0 copy-done.2
  12.1 0.0 copy-done
  12.1 8.5 %close.1 = s16[16,4,16,512]{3,2,1,0:T(8,128)(2,1)S(1)} custom-call(f32[4]{0:T(128)S(1)} %copy-done.1, s32[128]{0:T(128)S(1)} %copy-done.2, s32[128]{0:T(128)S(1)} %copy-done.3, bf16[32,16,8192]{2,1,0:T(8,128)(2,1)} %field_ref.3, bf16[16,8192]{1,0:T(8,128)(2,1)S(1)} %collective-permute-done.halo_any, f32[16,8192]{1,0:T(8,128)S(1)} %copy-done, ...), custom_call_target="tpu_custom_call" | custom-call | flops 31457280 | bytes 3145728 | tf_op jit(solution)/shard_map/close/pallas_call | solution.py:280
  20.6 32.8 %all_to_all.5.code_ref = s16[16,4,16,512]{3,2,1,0:T(8,128)(2,1)S(1)} all-to-all(s16[16,4,16,512]{3,2,1,0:T(8,128)(2,1)S(1)} %close.1), channel_id=1, replica_groups=mesh['groups'=2,'depth'=16] {'depth'}, dimensions={0} | all-to-all | bytes 2097152 | tf_op jit(solution)/shard_map/all_to_all | solution.py:363
  53.4 0.0 copy-done.4
  53.4 2.0 %composite.1 = f32[4,16,512]{2,1,0:T(8,128)} custom-call(s32[16]{0:T(128)S(1)} %copy-done.4, f32[4]{0:T(128)S(1)} %copy-done.1, s16[16,4,16,512]{3,2,1,0:T(8,128)(2,1)S(1)} %all_to_all.5.code_ref), custom_call_target="tpu_custom_call" | custom-call | tf_op jit(solution)/shard_map/composite/pallas_call | solution.py:341
Async XLA Ops:
  0.0 12.0 %copy-start.1 = (f32[4]{0:T(128)S(1)}, f32[4]{0:T(128)}, u32[]{:S(2)}) copy-start(f32[4]{0:T(128)} %transfer_ref.1) | copy-start | bytes 52
  0.0 12.1 %copy-start.3 = (s32[128]{0:T(128)S(1)}, s32[128]{0:T(128)}, u32[]{:S(2)}) copy-start(s32[128]{0:T(128)} %end_any.3) | copy-start | bytes 1540
  0.0 12.1 %copy-start.2 = (s32[128]{0:T(128)S(1)}, s32[128]{0:T(128)}, u32[]{:S(2)}) copy-start(s32[128]{0:T(128)} %start_any.3) | copy-start | bytes 1540
  0.0 12.1 %copy-start = (f32[16,8192]{1,0:T(8,128)S(1)}, f32[16,8192]{1,0:T(8,128)}, u32[]{:S(2)}) copy-start(f32[16,8192]{1,0:T(8,128)} %jitter_any.3) | copy-start | bytes 1572868
  1.0 11.0 %collective-permute-start = (bf16[16,8192]{1,0:T(8,128)(2,1)S(1)}, bf16[16,8192]{1,0:T(8,128)(2,1)S(1)}, u32[]{:S(2)}, u32[]{:S(2)}) collective-permute-start(bf16[16,8192]{1,0:T(8,128)(2,1)S(1)} %slice_bitcast_fusion), channel_id=1, source_target_pairs={{1,0},{2,1},{3,2},{4,3},{5,4},{6,5},{7,6},{8,7},{9,8},{10,9},{11,1... | collective-permute-start | bytes 786440 | tf_op jit(solution)/shard_map/ppermute | solution.py:30
  12.0 41.4 %copy-start.4 = (s32[16]{0:T(128)S(1)}, s32[16]{0:T(128)}, u32[]{:S(2)}) copy-start(s32[16]{0:T(128)} %order_ref.1) | copy-start | bytes 196

commit v9 on v8

--- a/solution.py
+++ b/solution.py
@@ -12,7 +12,6 @@
 LOG2E = math.log2(math.e)
 SUBLANES = 8
 LANES = 128
-BLOCK = 256
 STEP = 512
 OPEN_BYTES = 54 * 1024 * 1024
 CLOSE_BYTES = 52 * 1024 * 1024
@@ -59,7 +58,8 @@
 
 
 def moment(sums, emitted, value, levels):
-    share = emitted * pl.reciprocal((levels[0] + value) * (levels[1] + value) * (levels[2] + value), approx=True)
+    whole = (levels[0] + value) * (levels[1] + value) * (levels[2] + value)
+    share = emitted * pl.reciprocal(whole, approx=True, full_range=False)
     for n in range(3):
         sums[n] = sums[n] + share
         share = share * value
@@ -73,28 +73,30 @@
 def march(gain_ref, plane_ref, chunk, cols, place, jitter, levels, halo=None):
     slab_len = plane_ref.shape[1]
     shape = jitter.shape
-    stay = 1.0 - jitter
-    lower = plane_ref[chunk, 0, :, cols].astype(jnp.float32)
     before = jnp.zeros(shape, jnp.float32)
     through = jnp.ones(shape, jnp.float32)
     sums = [jnp.zeros(shape, jnp.float32) for _ in range(3)]
+    lower = plane_ref[chunk, 0, :, cols].astype(jnp.float32)
+    stay = lower - jitter * lower
     for k in range(slab_len - (halo is None)):
         following = plane_ref[chunk, k + 1, :, cols] if k + 1 < slab_len else halo
         upper = following.astype(jnp.float32)
-        value = stay * lower + jitter * upper
+        moved = jitter * upper
+        value = stay + moved
         before = before + gain_ref[k:k + 1, place] * value
         beyond = jnp.exp2(before)
-        emitted = (through - beyond) * value
-        moment(sums, emitted, value, levels)
+        moment(sums, (through - beyond) * value, value, levels)
         through = beyond
-        lower = upper
+        stay = upper - moved
     return sums, before
 
 
-def each_step(chunk_cols, body):
+def each_step(chunk_cols, compute, store):
     def step(n, carry):
-        for part in range(STEP // BLOCK):
-            body(pl.multiple_of(n * STEP + part * BLOCK, BLOCK))
+        places = [pl.multiple_of(n * STEP + part * LANES, LANES) for part in range(STEP // LANES)]
+        results = [compute(col) for col in places]
+        for col, result in zip(places, results):
+            store(col, *result)
         return carry
 
     lax.fori_loop(0, chunk_cols // STEP, step, 0)
@@ -135,7 +137,7 @@
     base = lax.axis_index("depth") * slab_len
     for copy in early:
         copy.wait()
-    levels = [jnp.full((rows, BLOCK), transfer_ref[i]) for i in range(3)]
+    levels = [jnp.full((rows, LANES), transfer_ref[i]) for i in range(3)]
     gain = jnp.full((SUBLANES, LANES), transfer_ref[3]) * (-LOG2E * 0.2 / total)
     tile_gains(gain_ref, gain, base, 0, tile_cols, start_ref, end_ref)
 
@@ -146,15 +148,16 @@
         for copy in arrivals(chunk):
             copy.wait()
 
-        def body(col):
-            cols = pl.ds(col, BLOCK)
-            place = pl.ds(pl.multiple_of(chunk * width + col, BLOCK), BLOCK)
-            sums, before = march(gain_ref, plane_ref, chunk, cols, place, jitter_ref[chunk, :, cols], levels)
-            for i in range(3):
-                state_ref[chunk, i, :, cols] = sums[i]
-            state_ref[chunk, 3, :, cols] = before
-
-        each_step(width, body)
+        def compute(col):
+            cols = pl.ds(col, LANES)
+            place = pl.ds(pl.multiple_of(chunk * width + col, LANES), LANES)
+            return march(gain_ref, plane_ref, chunk, cols, place, jitter_ref[chunk, :, cols], levels)
+
+        def store(col, sums, before):
+            for i, value in enumerate([*sums, before]):
+                state_ref[chunk, i, :, pl.ds(col, LANES)] = value
+
+        each_step(width, compute, store)
         leave(chunk).start()
 
     each_chunk(chunks, run)
@@ -181,7 +184,7 @@
     base = lax.axis_index("depth") * slab_len
     for copy in early:
         copy.wait()
-    shape = (rows, BLOCK)
+    shape = (rows, LANES)
     depth_gain = jnp.full(shape, transfer_ref[3]) * (0.2 / total)
     levels = [jnp.full(shape, transfer_ref[i]) for i in range(3)]
     depth_unit = 1.0 / (depth_gain * (slab_len * TOP))
@@ -191,12 +194,15 @@
     tile_gains(gain_ref, gain, base, first_col, tile_cols, start_ref, end_ref)
     tile_gains(last_gain_ref, gain, base + slab_len - 1, 0, tile_cols, start_ref, end_ref)
 
-    def store(chunk, col, sums, before):
+    def coded(sums, before):
+        codes = [encode(color * color_unit[i], color_span) for i, color in enumerate(colors(sums, levels))]
+        return codes + [encode(before * (depth_unit * (-1.0 / LOG2E)), depth_span)]
+
+    def store(chunk, col, *codes):
         piece = chunk * per + col // piece_width
-        out = pl.ds(pl.multiple_of(col % piece_width, BLOCK), BLOCK)
-        for i, color in enumerate(colors(sums, levels)):
-            out_ref[piece, i, :, out] = encode(color * color_unit[i], color_span)
-        out_ref[piece, 3, :, out] = encode(before * (depth_unit * (-1.0 / LOG2E)), depth_span)
+        out = pl.ds(pl.multiple_of(col % piece_width, LANES), LANES)
+        for i, code in enumerate(codes):
+            out_ref[piece, i, :, out] = code
 
     def leave(chunk):
         place = pl.ds(chunk * per, per)
@@ -206,15 +212,14 @@
         for copy in arrivals(chunk):
             copy.wait()
 
-        def body(col):
-            cols = pl.ds(col, BLOCK)
-            place = pl.ds(pl.multiple_of(chunk * width + col, BLOCK), BLOCK)
-            whole = pl.ds(pl.multiple_of(first_col + chunk * width + col, BLOCK), BLOCK)
+        def compute(col):
+            cols = pl.ds(col, LANES)
+            place = pl.ds(pl.multiple_of(chunk * width + col, LANES), LANES)
+            whole = pl.ds(pl.multiple_of(first_col + chunk * width + col, LANES), LANES)
             jitter = jitter_ref[opened + chunk, :, cols]
-            sums, before = march(gain_ref, plane_ref, chunk, cols, place, jitter, levels, halo_ref[:, whole])
-            store(opened + chunk, col, sums, before)
-
-        each_step(width, body)
+            return coded(*march(gain_ref, plane_ref, chunk, cols, place, jitter, levels, halo_ref[:, whole]))
+
+        each_step(width, compute, functools.partial(store, opened + chunk))
         leave(opened + chunk).start()
 
     each_chunk(chunks, run)
@@ -222,9 +227,9 @@
         copy.wait()
 
     def finish(chunk):
-        def body(col):
-            cols = pl.ds(col, BLOCK)
-            whole = pl.ds(pl.multiple_of(chunk * width + col, BLOCK), BLOCK)
+        def compute(col):
+            cols = pl.ds(col, LANES)
+            whole = pl.ds(pl.multiple_of(chunk * width + col, LANES), LANES)
             jitter = jitter_ref[chunk, :, cols]
             lower = last_ref[:, whole].astype(jnp.float32)
             upper = halo_ref[:, whole].astype(jnp.float32)
@@ -234,9 +239,9 @@
             emitted = (jnp.exp2(before) - jnp.exp2(beyond)) * value
             sums = [state_ref[chunk, i, :, cols] for i in range(3)]
             moment(sums, emitted, value, levels)
-            store(chunk, col, sums, beyond)
-
-        each_step(width, body)
+            return coded(sums, beyond)
+
+        each_step(width, compute, functools.partial(store, chunk))
         leave(chunk).start()
 
     each_chunk(opened, finish)
@@ -355,10 +360,10 @@
     width = cols // count
     halo = shifted(field[0], "depth", -1)
     args = (field, halo, jitter, transfer, ray_start, ray_end, total)
-    if width % BLOCK == 0:
+    if width % STEP == 0:
         codes = slab_codes(*args, count)
     else:
-        codes = slab_codes(*args, cols // BLOCK)
+        codes = slab_codes(*args, cols // STEP)
         codes = codes.transpose(1, 2, 0, 3).reshape(4, rows, count, width).transpose(2, 0, 1, 3)
     received = lax.all_to_all(codes, "depth", split_axis=0, concat_axis=0, tiled=True)
     return composite(received, transfer, depth_order, total, slab_len)

time: 55.9 us -> 55.7 us (level)
  no operation moved by 1% of the time
where the time goes in v9:
time: 55.7 us; the launch traced here: 55.2 us
  blocking collectives  32.8 us (59%)
  Pallas kernels  20 us (36%)
  starting transfers between devices  1.29 us (2%)
  local copies, waits for them, and re-layouts  1.05 us (2%)
    all_to_all x1, blocking collectives, on_device(): lax.all_to_all(codes, 'depth', split_axis=0, concat_axis=0, tiled=True)  32.8 us
    pallas_call x1, Pallas kernels, slab_codes(): pl.pallas_call(functools.partial(open_kernel, total, tile_cols), in_specs...  9.44 us
    pallas_call x1, Pallas kernels, slab_codes(): pl.pallas_call(functools.partial(close_kernel, total, tile_cols, opened),...  8.61 us
    pallas_call x1, Pallas kernels, composite(): pl.pallas_call(functools.partial(composite_kernel, total, slab_len), in_s...  1.98 us
    ppermute x1, starting transfers between devices, shifted(): lax.ppermute(value, axis, [(source, source + steps) for source in range(i...  1.29 us
  transfers between devices with their start and end apart: 1, of which 0 were waited for; matrix products, arithmetic and copies ran while one was open for 0% of the time, Pallas kernels for 17%

profile of v9, /device:TPU:0, one launch (start us, length us, event | category | flops | bytes accessed | tf_op | source)
XLA Modules:
  0.0 55.2 jit_solution(4581347671160106782)
XLA Ops:
  0.0 0.0 copy-start.1
  0.0 0.0 copy-start.3
  0.0 0.0 copy-start.2
  0.0 0.0 copy-start
  0.0 1.0 %slice_bitcast_fusion = bf16[16,8192]{1,0:T(8,128)(2,1)S(1)} fusion(bf16[32,16,8192]{2,1,0:T(8,128)(2,1)} %field_ref.3), kind=kLoop, calls=%fused_computation | loop fusion | bytes 524288 | tf_op jit(solution)/shard_map/squeeze | solution.py:361
  1.0 1.3 %collective-permute-start = (bf16[16,8192]{1,0:T(8,128)(2,1)S(1)}, bf16[16,8192]{1,0:T(8,128)(2,1)S(1)}, u32[]{:S(2)}, u32[]{:S(2)}) collective-permute-start(bf16[16,8192]{1,0:T(8,128)(2,1)S(1)} %slice_bitcast_fusion), channel_id=1, source_target_pairs={{1,0},{2,1},{3,2},{4,3},{5,4},{6,5},{7,6},{8,7},{9,8},{10,9},{11,1... | collective-permute-start | bytes 786440 | tf_op jit(solution)/shard_map/ppermute | solution.py:29
  2.3 9.4 %open.1.state_any = f32[5,4,16,1024]{3,2,1,0:T(8,128)} custom-call(f32[4]{0:T(128)} %transfer_ref.1, s32[128]{0:T(128)} %start_any.3, s32[128]{0:T(128)} %end_any.3, bf16[32,16,8192]{2,1,0:T(8,128)(2,1)} %field_ref.3, f32[16,8192]{1,0:T(8,128)} %jitter_any.3), custom_call_target="tpu_custom_call" | custom-call | flops 52428800 | bytes 5242880 | tf_op jit(solution)/shard_map/open/pallas_call | solution.py:267
  11.8 0.0 copy-start.4
  11.8 0.0 collective-permute-done.halo_any
  11.8 0.0 copy-done.1
  11.8 0.0 copy-done.3
  11.8 0.0 copy-done.2
  11.8 0.0 copy-done
  11.9 8.6 %close.1 = s16[16,4,16,512]{3,2,1,0:T(8,128)(2,1)S(1)} custom-call(f32[4]{0:T(128)S(1)} %copy-done.1, s32[128]{0:T(128)S(1)} %copy-done.2, s32[128]{0:T(128)S(1)} %copy-done.3, bf16[32,16,8192]{2,1,0:T(8,128)(2,1)} %field_ref.3, bf16[16,8192]{1,0:T(8,128)(2,1)S(1)} %collective-permute-done.halo_any, f32[16,8192]{1,0:T(8,128)S(1)} %copy-done, ...), custom_call_target="tpu_custom_call" | custom-call | flops 31457280 | bytes 3145728 | tf_op jit(solution)/shard_map/close/pallas_call | solution.py:285
  20.5 32.8 %all_to_all.5.code_ref = s16[16,4,16,512]{3,2,1,0:T(8,128)(2,1)S(1)} all-to-all(s16[16,4,16,512]{3,2,1,0:T(8,128)(2,1)S(1)} %close.1), channel_id=1, replica_groups=mesh['groups'=2,'depth'=16] {'depth'}, dimensions={0} | all-to-all | bytes 2097152 | tf_op jit(solution)/shard_map/all_to_all | solution.py:368
  53.3 0.0 copy-done.4
  53.3 2.0 %composite.1 = f32[4,16,512]{2,1,0:T(8,128)} custom-call(s32[16]{0:T(128)S(1)} %copy-done.4, f32[4]{0:T(128)S(1)} %copy-done.1, s16[16,4,16,512]{3,2,1,0:T(8,128)(2,1)S(1)} %all_to_all.5.code_ref), custom_call_target="tpu_custom_call" | custom-call | tf_op jit(solution)/shard_map/composite/pallas_call | solution.py:346
Async XLA Ops:
  0.0 11.8 %copy-start.1 = (f32[4]{0:T(128)S(1)}, f32[4]{0:T(128)}, u32[]{:S(2)}) copy-start(f32[4]{0:T(128)} %transfer_ref.1) | copy-start | bytes 52
  0.0 11.8 %copy-start.3 = (s32[128]{0:T(128)S(1)}, s32[128]{0:T(128)}, u32[]{:S(2)}) copy-start(s32[128]{0:T(128)} %end_any.3) | copy-start | bytes 1540
  0.0 11.8 %copy-start.2 = (s32[128]{0:T(128)S(1)}, s32[128]{0:T(128)}, u32[]{:S(2)}) copy-start(s32[128]{0:T(128)} %start_any.3) | copy-start | bytes 1540
  0.0 11.8 %copy-start = (f32[16,8192]{1,0:T(8,128)S(1)}, f32[16,8192]{1,0:T(8,128)}, u32[]{:S(2)}) copy-start(f32[16,8192]{1,0:T(8,128)} %jitter_any.3) | copy-start | bytes 1572868
  1.0 10.8 %collective-permute-start = (bf16[16,8192]{1,0:T(8,128)(2,1)S(1)}, bf16[16,8192]{1,0:T(8,128)(2,1)S(1)}, u32[]{:S(2)}, u32[]{:S(2)}) collective-permute-start(bf16[16,8192]{1,0:T(8,128)(2,1)S(1)} %slice_bitcast_fusion), channel_id=1, source_target_pairs={{1,0},{2,1},{3,2},{4,3},{5,4},{6,5},{7,6},{8,7},{9,8},{10,9},{11,1... | collective-permute-start | bytes 786440 | tf_op jit(solution)/shard_map/ppermute | solution.py:29
  11.8 41.5 %copy-start.4 = (s32[16]{0:T(128)S(1)}, s32[16]{0:T(128)}, u32[]{:S(2)}) copy-start(s32[16]{0:T(128)} %order_ref.1) | copy-start | bytes 196

commit v10 on v9

--- a/solution.py
+++ b/solution.py
@@ -12,6 +12,7 @@
 LOG2E = math.log2(math.e)
 SUBLANES = 8
 LANES = 128
+FAR = 1.0e4
 STEP = 512
 OPEN_BYTES = 54 * 1024 * 1024
 CLOSE_BYTES = 52 * 1024 * 1024
@@ -251,9 +252,9 @@
 def slab_codes(field, halo, jitter, transfer, ray_start, ray_end, total, pieces):
     slab_len, rows, cols = field.shape
     width = cols // pieces
-    chunk = max(width, min(1024, cols // 2))
+    chunk = max(width, STEP)
     chunks = cols // chunk
-    opened = max(1, chunks * 5 // 8)
+    opened = max(1, chunks * 3 // 8)
     closed = chunks - opened
     ntiles = ray_start.shape[0]
     tile_cols = cols // ntiles
@@ -306,48 +307,58 @@
     )(transfer, ray_start, ray_end, field, halo, jitter, state)
 
 
-def composite_kernel(total, slab_len, order_ref, transfer_ref, code_ref, out_ref):
+def composite_kernel(total, slab_len, order_any, transfer_any, code_any, out_ref, order_ref, transfer_ref, code_ref, sems):
+    copies = start_all([(order_any, order_ref), (transfer_any, transfer_ref), (code_any, code_ref)], sems)
     count, _, rows, width = code_ref.shape
-    lanes = min(width, LANES)
+    block = math.gcd(width, 2 * LANES)
+    shape = (rows, block)
     depth_span, color_span = spans(slab_len)
-    depth_gain = jnp.full((rows, lanes), transfer_ref[3]) * (0.2 / total)
-    unit = depth_gain * (slab_len * TOP)
+    for copy in copies:
+        copy.wait()
+    unit = jnp.full(shape, transfer_ref[3]) * (0.2 / total * slab_len * TOP)
     depth_unit = unit * LOG2E
 
-    def decode(codes, span, shift):
-        code = codes.astype(jnp.int32).astype(jnp.float32)
-        value = jnp.exp2(code * (span / 65535.0) + (span * (32768.0 / 65535.0) - span) - shift)
-        return jnp.where(code > -32768.0, value, 0.0)
-
-    for n in range(width // lanes):
-        cols = slice(n * lanes, (n + 1) * lanes)
+    def power(codes, span):
+        return codes * (span / 65535.0) + (span * (32768.0 / 65535.0) - span)
+
+    def number(codes):
+        return codes.astype(jnp.int32).astype(jnp.float32)
+
+    for n in range(width // block):
+        cols = slice(n * block, (n + 1) * block)
 
         def step(j, carry):
-            depth, red, green, blue = carry
+            depth, *colors = carry
             slab = order_ref[j]
-            colors = [red, green, blue]
+            depth_code = number(code_ref[slab, 3, :, cols])
+            idle = depth_code == -32768.0
+            shift = jnp.where(idle, FAR, depth)
             for i in range(3):
-                colors[i] = colors[i] + decode(code_ref[slab, i, :, cols], color_span, depth)
-            depth = depth + depth_unit * decode(code_ref[slab, 3, :, cols], depth_span, 0.0)
+                colors[i] = colors[i] + jnp.exp2(power(number(code_ref[slab, i, :, cols]), color_span) - shift)
+            depth = depth + depth_unit * jnp.where(idle, 0.0, jnp.exp2(power(depth_code, depth_span)))
             return depth, *colors
 
-        zero = jnp.zeros((rows, lanes), jnp.float32)
-        depth, *colors = lax.fori_loop(0, count, step, (zero, zero, zero, zero), unroll=4)
+        zero = jnp.zeros(shape, jnp.float32)
+        depth, *colors = lax.fori_loop(0, count, step, (zero, zero, zero, zero), unroll=math.gcd(count, 4))
         for i in range(3):
-            level = jnp.full((rows, lanes), transfer_ref[i])
-            out_ref[i, :, cols] = colors[i] * (unit * (TOP / (level + TOP)))
+            out_ref[i, :, cols] = colors[i] * (unit * (TOP / (transfer_ref[i] + jnp.full(shape, TOP))))
         out_ref[3, :, cols] = 1.0 - jnp.exp2(-depth)
 
 
 def composite(codes, transfer, depth_order, total, slab_len):
     _, _, rows, width = codes.shape
-    smem = pl.BlockSpec(memory_space=pltpu.SMEM)
-    vmem = pl.BlockSpec(memory_space=pltpu.VMEM)
+    own = pl.BlockSpec(memory_space=pl.ANY)
     return pl.pallas_call(
         functools.partial(composite_kernel, total, slab_len),
-        in_specs=[smem, smem, vmem],
-        out_specs=vmem,
+        in_specs=[own] * 3,
+        out_specs=pl.BlockSpec(memory_space=pltpu.VMEM),
         out_shape=jax.ShapeDtypeStruct((4, rows, width), jnp.float32),
+        scratch_shapes=[
+            pltpu.SMEM(depth_order.shape, depth_order.dtype),
+            pltpu.SMEM(transfer.shape, transfer.dtype),
+            pltpu.VMEM(codes.shape, codes.dtype),
+            pltpu.SemaphoreType.DMA((3,)),
+        ],
         compiler_params=pltpu.CompilerParams(vmem_limit_bytes=SMALL_BYTES),
         name="composite",
     )(depth_order, transfer, codes)

time: 55.7 us -> 56.1 us (level)
  local copies, waits for them, and re-layouts: 1.05 us -> 2.17 us
  Pallas kernels: 20 us -> 18.9 us
    pallas_call x1, Pallas kernels: 9.44 us -> 6.38 us  [slab_codes(): pl.pallas_call(functools.partial(open_kernel, total, tile_cols), in_specs...]
    pallas_call x1, Pallas kernels: 8.61 us -> 10.6 us  [slab_codes(): pl.pallas_call(functools.partial(close_kernel, total, tile_cols, opened),...]
    unnamed x10 -> x12, local copies, waits for them, and re-layouts: 0.02 us -> 1.14 us
  transfers between devices with their start and end apart: 1 -> 1, of which waited for: 0 -> 0; matrix products, arithmetic and copies ran while one was open for 0% -> 0% of each run, Pallas kernels for 17% -> 11%
where the time goes in v10:
time: 56.1 us; the launch traced here: 55.5 us
  blocking collectives  33 us (59%)
  Pallas kernels  18.9 us (34%)
  local copies, waits for them, and re-layouts  2.17 us (4%)
  starting transfers between devices  1.29 us (2%)
    all_to_all x1, blocking collectives, on_device(): lax.all_to_all(codes, 'depth', split_axis=0, concat_axis=0, tiled=True)  33 us
    pallas_call x1, Pallas kernels, slab_codes(): pl.pallas_call(functools.partial(close_kernel, total, tile_cols, opened),...  10.6 us
    pallas_call x1, Pallas kernels, slab_codes(): pl.pallas_call(functools.partial(open_kernel, total, tile_cols), in_specs...  6.38 us
    pallas_call x1, Pallas kernels, composite(): pl.pallas_call(functools.partial(composite_kernel, total, slab_len), in_s...  1.89 us
    ppermute x1, starting transfers between devices, shifted(): lax.ppermute(value, axis, [(source, source + steps) for source in range(i...  1.29 us
    unnamed x12, local copies, waits for them, and re-layouts  1.14 us
  transfers between devices with their start and end apart: 1, of which 0 were waited for; matrix products, arithmetic and copies ran while one was open for 0% of the time, Pallas kernels for 11%

profile of v10, /device:TPU:0, one launch (start us, length us, event | category | flops | bytes accessed | tf_op | source)
XLA Modules:
  0.0 55.5 jit_solution(4520497131464290856)
XLA Ops:
  0.0 0.0 copy-start.2
  0.0 0.0 copy-start.4
  0.0 0.0 copy-start.3
  0.0 0.0 copy-start.1
  0.0 1.0 %slice_bitcast_fusion = bf16[16,8192]{1,0:T(8,128)(2,1)S(1)} fusion(bf16[32,16,8192]{2,1,0:T(8,128)(2,1)} %field_ref.3), kind=kLoop, calls=%fused_computation | loop fusion | bytes 524288 | tf_op jit(solution)/shard_map/squeeze | solution.py:372
  1.0 1.3 %collective-permute-start = (bf16[16,8192]{1,0:T(8,128)(2,1)S(1)}, bf16[16,8192]{1,0:T(8,128)(2,1)S(1)}, u32[]{:S(2)}, u32[]{:S(2)}) collective-permute-start(bf16[16,8192]{1,0:T(8,128)(2,1)S(1)} %slice_bitcast_fusion), channel_id=1, source_target_pairs={{1,0},{2,1},{3,2},{4,3},{5,4},{6,5},{7,6},{8,7},{9,8},{10,9},{11,1... | collective-permute-start | bytes 786440 | tf_op jit(solution)/shard_map/ppermute | solution.py:30
  2.3 6.4 %open.1.state_any = f32[6,4,16,512]{3,2,1,0:T(8,128)} custom-call(f32[4]{0:T(128)} %transfer_any.5, s32[128]{0:T(128)} %start_any.3, s32[128]{0:T(128)} %end_any.3, bf16[32,16,8192]{2,1,0:T(8,128)(2,1)} %field_ref.3, f32[16,8192]{1,0:T(8,128)} %jitter_any.3), custom_call_target="tpu_custom_call" | custom-call | flops 31457280 | bytes 3145728 | tf_op jit(solution)/shard_map/open/pallas_call | solution.py:268
  8.7 0.0 collective-permute-done.halo_any
  8.7 0.0 copy-done.2
  8.7 0.0 copy-done.4
  8.8 0.0 copy-done.3
  8.8 0.0 copy-done.1
  8.8 0.0 copy-start
  8.8 1.1 %copy-done = f32[6,4,16,512]{3,2,1,0:T(8,128)S(1)} copy-done((f32[6,4,16,512]{3,2,1,0:T(8,128)S(1)}, f32[6,4,16,512]{3,2,1,0:T(8,128)}, u32[]{:S(2)}) %copy-start) | copy-done | bytes 786456
  9.9 0.0 copy-start.5
  9.9 10.6 %close.1 = s16[16,4,16,512]{3,2,1,0:T(8,128)(2,1)} custom-call(f32[4]{0:T(128)S(1)} %copy-done.2, s32[128]{0:T(128)S(1)} %copy-done.3, s32[128]{0:T(128)S(1)} %copy-done.4, bf16[32,16,8192]{2,1,0:T(8,128)(2,1)} %field_ref.3, bf16[16,8192]{1,0:T(8,128)(2,1)S(1)} %collective-permute-done.halo_any, f32[16,8192]{1,0:T(8,128)S(1)} %copy-done.1, ...), custom_call_target="tpu_custom_call" | custom-call | flops 52428800 | bytes 5242880 | tf_op jit(solution)/shard_map/close/pallas_call | solution.py:286
  20.6 33.0 %all_to_all.5.code_any = s16[16,4,16,512]{3,2,1,0:T(8,128)(2,1)S(1)} all-to-all(s16[16,4,16,512]{3,2,1,0:T(8,128)(2,1)} %close.1), channel_id=1, replica_groups=mesh['groups'=2,'depth'=16] {'depth'}, dimensions={0} | all-to-all | bytes 2097152 | tf_op jit(solution)/shard_map/all_to_all | solution.py:379
  53.6 0.0 copy-done.5
  53.6 1.9 %composite.1 = f32[4,16,512]{2,1,0:T(8,128)} custom-call(s32[16]{0:T(128)S(1)} %copy-done.5, f32[4]{0:T(128)S(1)} %copy-done.2, s16[16,4,16,512]{3,2,1,0:T(8,128)(2,1)S(1)} %all_to_all.5.code_any), custom_call_target="tpu_custom_call" | custom-call | tf_op jit(solution)/shard_map/composite/pallas_call | solution.py:351
Async XLA Ops:
  0.0 8.7 %copy-start.2 = (f32[4]{0:T(128)S(1)}, f32[4]{0:T(128)}, u32[]{:S(2)}) copy-start(f32[4]{0:T(128)} %transfer_any.5) | copy-start | bytes 52
  0.0 8.7 %copy-start.4 = (s32[128]{0:T(128)S(1)}, s32[128]{0:T(128)}, u32[]{:S(2)}) copy-start(s32[128]{0:T(128)} %end_any.3) | copy-start | bytes 1540
  0.0 8.8 %copy-start.3 = (s32[128]{0:T(128)S(1)}, s32[128]{0:T(128)}, u32[]{:S(2)}) copy-start(s32[128]{0:T(128)} %start_any.3) | copy-start | bytes 1540
  0.0 8.8 %copy-start.1 = (f32[16,8192]{1,0:T(8,128)S(1)}, f32[16,8192]{1,0:T(8,128)}, u32[]{:S(2)}) copy-start(f32[16,8192]{1,0:T(8,128)} %jitter_any.3) | copy-start | bytes 1572868
  1.0 7.7 %collective-permute-start = (bf16[16,8192]{1,0:T(8,128)(2,1)S(1)}, bf16[16,8192]{1,0:T(8,128)(2,1)S(1)}, u32[]{:S(2)}, u32[]{:S(2)}) collective-permute-start(bf16[16,8192]{1,0:T(8,128)(2,1)S(1)} %slice_bitcast_fusion), channel_id=1, source_target_pairs={{1,0},{2,1},{3,2},{4,3},{5,4},{6,5},{7,6},{8,7},{9,8},{10,9},{11,1... | collective-permute-start | bytes 786440 | tf_op jit(solution)/shard_map/ppermute | solution.py:30
  8.8 1.1 %copy-start = (f32[6,4,16,512]{3,2,1,0:T(8,128)S(1)}, f32[6,4,16,512]{3,2,1,0:T(8,128)}, u32[]{:S(2)}) copy-start(f32[6,4,16,512]{3,2,1,0:T(8,128)} %open.1.state_any) | copy-start | bytes 2359300
  9.9 43.7 %copy-start.5 = (s32[16]{0:T(128)S(1)}, s32[16]{0:T(128)}, u32[]{:S(2)}) copy-start(s32[16]{0:T(128)} %order_any.1) | copy-start | bytes 196

commit v11 on v10

v11 whole, which is shorter than its diff:
```python
import functools
import math

import jax
import jax.numpy as jnp
from jax import lax
from jax.experimental import pallas as pl
from jax.experimental.pallas import tpu as pltpu
from jax.sharding import PartitionSpec as P

TOP = 5.2
LOG2E = math.log2(math.e)
SUBLANES = 8
LANES = 128
FAR = 1.0e4
UNIT = 256
OPEN_BYTES = 54 * 1024 * 1024
CLOSE_BYTES = 53 * 1024 * 1024
SMALL_BYTES = 16 * 1024 * 1024


def spans(slab_len):
    deep = math.log2(slab_len)
    return 6.8 + deep, 13.2 + deep


def shifted(value, axis, steps):
    count = lax.axis_size(axis)
    initial, last = (max(0, -steps), min(count, count - steps))
    return lax.ppermute(value, axis, [(source, source + steps) for source in range(initial, last)])


def encode(value, span):
    code = jnp.log2(value) * (65535.0 / span) + 65535.5
    code = jnp.minimum(jnp.maximum(code, 0.0), 65535.0)
    return (code.astype(jnp.int32) - 32768).astype(jnp.int16)


def tile_gains(gain_ref, gain, base, tile_cols, start_ref, end_ref, col_of):
    sample = lax.broadcasted_iota(jnp.int32, (SUBLANES, LANES), 0) + base
    lane = lax.broadcasted_iota(jnp.int32, (SUBLANES, LANES), 1)

    def block(n, carry):
        tile = col_of(n) // tile_cols
        start = jnp.full((SUBLANES, LANES), start_ref[tile])
        end = jnp.full((SUBLANES, LANES), end_ref[tile])
        for t in range(1, LANES // tile_cols):
            start = jnp.where(lane >= t * tile_cols, start_ref[tile + t], start)
            end = jnp.where(lane >= t * tile_cols, end_ref[tile + t], end)
        cols = pl.ds(pl.multiple_of(n * LANES, LANES), LANES)
        for k in range(0, gain_ref.shape[0], SUBLANES):
            active = (sample + k >= start) & (sample + k < end)
            gain_ref[k:k + SUBLANES, cols] = jnp.where(active, gain, 0.0)
        return carry

    blocks = gain_ref.shape[1] // LANES
    lax.fori_loop(0, blocks, block, 0, unroll=math.gcd(blocks, 4))


def moment(sums, emitted, value, levels):
    whole = (levels[0] + value) * (levels[1] + value) * (levels[2] + value)
    share = emitted * pl.reciprocal(whole, approx=True, full_range=False)
    for n in range(3):
        sums[n] = sums[n] + share
        share = share * value


def colors(sums, levels):
    others = [(levels[1], levels[2]), (levels[2], levels[0]), (levels[0], levels[1])]
    return [sums[2] + (p + q) * sums[1] + (p * q) * sums[0] for p, q in others]


def march(gain_ref, plane_ref, unit, cols, place, jitter, levels, halo=None):
    slab_len = plane_ref.shape[1]
    shape = jitter.shape
    before = jnp.zeros(shape, jnp.float32)
    through = jnp.ones(shape, jnp.float32)
    sums = [jnp.zeros(shape, jnp.float32) for _ in range(3)]
    lower = plane_ref[unit, 0, :, cols].astype(jnp.float32)
    stay = lower - jitter * lower
    for k in range(slab_len - (halo is None)):
        following = plane_ref[unit, k + 1, :, cols] if k + 1 < slab_len else halo
        upper = following.astype(jnp.float32)
        moved = jitter * upper
        value = stay + moved
        before = before + gain_ref[k:k + 1, place] * value
        beyond = jnp.exp2(before)
        moment(sums, (through - beyond) * value, value, levels)
        through = beyond
        stay = upper - moved
    return sums, before


def loop(count, body):
    def step(n, carry):
        body(n)
        return carry

    lax.fori_loop(0, count, step, 0)


def each_block(units, arrive, compute, store, leave):
    def pair(n):
        places = [(2 * n + u, c) for u in range(2) for c in range(0, UNIT, LANES)]
        for u in range(2):
            arrive(2 * n + u)
        results = [compute(unit, pl.ds(c, LANES), pl.ds(pl.multiple_of(unit * UNIT + c, LANES), LANES)) for unit, c in places]
        for (unit, c), result in zip(places, results):
            store(unit, pl.ds(c, LANES), result)
        for u in range(2):
            leave(2 * n + u)

    loop(units // 2, pair)


class Units:
    def __init__(self, first, half, pieces_width):
        self.first, self.half, self.width = first, half, pieces_width

    def column(self, unit):
        return (self.first + unit) * self.width + self.half * UNIT

    def columns(self, unit):
        return pl.ds(pl.multiple_of(self.column(unit), LANES), UNIT)

    def block_column(self, n):
        return self.column(n // (UNIT // LANES)) + n % (UNIT // LANES) * LANES


def start_all(pairs, sems):
    copies = [pltpu.make_async_copy(src, dst, sems.at[n]) for n, (src, dst) in enumerate(pairs)]
    for copy in copies:
        copy.start()
    return copies


def unit_copies(place, field_any, jitter_any, plane_ref, jitter_ref, sems, unit):
    cols = place.columns(unit)
    return [
        pltpu.make_async_copy(jitter_any.at[:, cols], jitter_ref.at[unit], sems.at[0, unit]),
        pltpu.make_async_copy(field_any.at[:, :, cols], plane_ref.at[unit], sems.at[1, unit]),
    ]


def open_kernel(total, tile_cols, place, transfer_any, start_any, end_any, field_any, jitter_any, state_any, transfer_ref,
                start_ref, end_ref, plane_ref, jitter_ref, state_ref, gain_ref, few_sems, sems, out_sems):
    units, slab_len, rows, _ = plane_ref.shape
    early = start_all([(transfer_any, transfer_ref), (start_any, start_ref), (end_any, end_ref)], few_sems)
    arrivals = functools.partial(unit_copies, place, field_any, jitter_any, plane_ref, jitter_ref, sems)
    for unit in range(units):
        for copy in arrivals(unit):
            copy.start()
    base = lax.axis_index("depth") * slab_len
    for copy in early:
        copy.wait()
    levels = [jnp.full((rows, LANES), transfer_ref[i]) for i in range(3)]
    gain = jnp.full((SUBLANES, LANES), transfer_ref[3]) * (-LOG2E * 0.2 / total)
    tile_gains(gain_ref, gain, base, tile_cols, start_ref, end_ref, place.block_column)

    def arrive(unit):
        for copy in arrivals(unit):
            copy.wait()

    def compute(unit, cols, table):
        return march(gain_ref, plane_ref, unit, cols, table, jitter_ref[unit, :, cols], levels)

    def store(unit, cols, result):
        sums, before = result
        for i, value in enumerate([*sums, before]):
            state_ref[unit, i, :, cols] = value

    def leave(unit):
        return pltpu.make_async_copy(state_ref.at[unit], state_any.at[unit], out_sems.at[unit])

    each_block(units, arrive, compute, store, lambda unit: leave(unit).start())
    loop(units, lambda unit: leave(unit).wait())


def close_kernel(total, tile_cols, opened, place, *refs):
    before_units = Units(0, place.half, place.width)
    ins = 7 if opened else 6
    transfer_any, start_any, end_any, field_any, halo_any, jitter_any = refs[:6]
    out_any = refs[ins]
    transfer_ref, start_ref, end_ref, plane_ref, halo_ref, jitter_ref, out_ref, gain_ref, few_sems, sems, out_sems = refs[
        ins + 1:ins + 12]
    units, slab_len, rows, _ = plane_ref.shape
    few = [(transfer_any, transfer_ref), (start_any, start_ref), (end_any, end_ref), (halo_any, halo_ref)]
    early = start_all(few, few_sems)
    arrivals = functools.partial(unit_copies, place, field_any, jitter_any, plane_ref, jitter_ref, sems)
    for unit in range(units):
        for copy in arrivals(unit):
            copy.start()
    if opened:
        state_any = refs[6]
        state_ref, last_ref, last_jitter_ref, last_gain_ref, state_sems = refs[ins + 12:]

        def opened_copies(unit):
            cols = before_units.columns(unit)
            pairs = [
                (field_any.at[slab_len - 1, :, cols], last_ref.at[unit]),
                (jitter_any.at[:, cols], last_jitter_ref.at[unit]),
                (state_any.at[unit], state_ref.at[unit]),
            ]
            return [pltpu.make_async_copy(src, dst, state_sems.at[n, unit]) for n, (src, dst) in enumerate(pairs)]

        for unit in range(opened):
            for copy in opened_copies(unit):
                copy.start()
    base = lax.axis_index("depth") * slab_len
    for copy in early:
        copy.wait()
    shape = (rows, LANES)
    depth_gain = jnp.full(shape, transfer_ref[3]) * (0.2 / total)
    levels = [jnp.full(shape, transfer_ref[i]) for i in range(3)]
    depth_unit = 1.0 / (depth_gain * (slab_len * TOP))
    color_unit = [depth_unit * ((levels[i] + TOP) * (1.0 / TOP)) for i in range(3)]
    depth_span, color_span = spans(slab_len)
    gain = depth_gain[:SUBLANES] * -LOG2E
    tile_gains(gain_ref, gain, base, tile_cols, start_ref, end_ref, place.block_column)

    def coded(sums, before):
        codes = [encode(color * color_unit[i], color_span) for i, color in enumerate(colors(sums, levels))]
        return codes + [encode(before * (depth_unit * (-1.0 / LOG2E)), depth_span)]

    def arrive(unit):
        for copy in arrivals(unit):
            copy.wait()

    def compute(unit, cols, table):
        whole = pl.ds(pl.multiple_of(place.column(unit) + cols.start, LANES), LANES)
        jitter = jitter_ref[unit, :, cols]
        return coded(*march(gain_ref, plane_ref, unit, cols, table, jitter, levels, halo_ref[:, whole]))

    def store(first, unit, cols, codes):
        for i, code in enumerate(codes):
            out_ref[first + unit, i, :, cols] = code

    def leave(piece):
        return pltpu.make_async_copy(out_ref.at[piece], out_any.at[piece], out_sems.at[piece])

    each_block(units, arrive, compute, functools.partial(store, place.first), lambda unit: leave(place.first + unit).start())
    if opened:
        tile_gains(last_gain_ref, gain, base + slab_len - 1, tile_cols, start_ref, end_ref, before_units.block_column)

        def arrive_opened(unit):
            for copy in opened_copies(unit):
                copy.wait()

        def finish(unit, cols, table):
            whole = pl.ds(pl.multiple_of(before_units.column(unit) + cols.start, LANES), LANES)
            jitter = last_jitter_ref[unit, :, cols]
            lower = last_ref[unit, :, cols].astype(jnp.float32)
            upper = halo_ref[:, whole].astype(jnp.float32)
            value = (1.0 - jitter) * lower + jitter * upper
            before = state_ref[unit, 3, :, cols]
            beyond = before + last_gain_ref[0:1, table] * value
            emitted = (jnp.exp2(before) - jnp.exp2(beyond)) * value
            sums = [state_ref[unit, i, :, cols] for i in range(3)]
            moment(sums, emitted, value, levels)
            return coded(sums, beyond)

        each_block(opened, arrive_opened, finish, functools.partial(store, 0), lambda unit: leave(unit).start())
    loop(out_ref.shape[0], lambda piece: leave(piece).wait())


def slab_codes(field, halo, jitter, transfer, ray_start, ray_end, total, pieces):
    slab_len, rows, cols = field.shape
    width = cols // pieces
    opened = pieces * 3 // 8 * 2
    ntiles = ray_start.shape[0]
    tile_cols = cols // ntiles
    own = pl.BlockSpec(memory_space=pl.ANY)
    scalars = [pltpu.SMEM(transfer.shape, transfer.dtype)] + [pltpu.SMEM((ntiles,), jnp.int32)] * 2

    def cost(units):
        work = slab_len * rows * units * UNIT
        return pl.CostEstimate(flops=work * 20, bytes_accessed=work * 2, transcendentals=work * 2)

    state = pl.pallas_call(
        functools.partial(open_kernel, total, tile_cols, Units(0, 0, width)),
        in_specs=[own] * 5,
        out_specs=own,
        out_shape=jax.ShapeDtypeStruct((opened, 4, rows, UNIT), jnp.float32),
        scratch_shapes=scalars + [
            pltpu.VMEM((opened, slab_len, rows, UNIT), field.dtype),
            pltpu.VMEM((opened, rows, UNIT), jnp.float32),
            pltpu.VMEM((opened, 4, rows, UNIT), jnp.float32),
            pltpu.VMEM((slab_len, opened * UNIT), jnp.float32),
            pltpu.SemaphoreType.DMA((3,)),
            pltpu.SemaphoreType.DMA((2, opened)),
            pltpu.SemaphoreType.DMA((opened,)),
        ],
        compiler_params=pltpu.CompilerParams(vmem_limit_bytes=OPEN_BYTES),
        cost_estimate=cost(opened),
        name="open",
    )(transfer, ray_start, ray_end, field, jitter)

    halves = []
    for half in range(2):
        first = opened if half == 0 else 0
        units = pieces - first
        scratch = scalars + [
            pltpu.VMEM((units, slab_len, rows, UNIT), field.dtype),
            pltpu.VMEM((rows, cols), field.dtype),
            pltpu.VMEM((units, rows, UNIT), jnp.float32),
            pltpu.VMEM((pieces, 4, rows, UNIT), jnp.int16),
            pltpu.VMEM((slab_len, units * UNIT), jnp.float32),
            pltpu.SemaphoreType.DMA((4,)),
            pltpu.SemaphoreType.DMA((2, units)),
            pltpu.SemaphoreType.DMA((pieces,)),
        ]
        operands = [transfer, ray_start, ray_end, field, halo, jitter]
        if first:
            operands.append(state)
            scratch += [
                pltpu.VMEM((first, 4, rows, UNIT), jnp.float32),
                pltpu.VMEM((first, rows, UNIT), field.dtype),
                pltpu.VMEM((first, rows, UNIT), jnp.float32),
                pltpu.VMEM((SUBLANES, first * UNIT), jnp.float32),
                pltpu.SemaphoreType.DMA((3, first)),
            ]
        halves.append(pl.pallas_call(
            functools.partial(close_kernel, total, tile_cols, first, Units(first, half, width)),
            in_specs=[own] * len(operands),
            out_specs=own,
            out_shape=jax.ShapeDtypeStruct((pieces, 4, rows, UNIT), jnp.int16),
            scratch_shapes=scratch,
            compiler_params=pltpu.CompilerParams(vmem_limit_bytes=CLOSE_BYTES),
            cost_estimate=cost(units),
            name="close",
        )(*operands))
    return halves


def composite_kernel(total, slab_len, first, order_any, transfer_any, code_any, *refs):
    image_any, order_ref, transfer_ref, code_ref, out_ref, sems, out_sem = refs[-7:]
    copies = start_all([(order_any, order_ref), (transfer_any, transfer_ref), (code_any, code_ref)], sems)
    count, _, rows, width = code_ref.shape
    shape = (rows, width)
    depth_span, color_span = spans(slab_len)
    for copy in copies:
        copy.wait()
    unit = jnp.full(shape, transfer_ref[3]) * (0.2 / total * slab_len * TOP)
    depth_unit = unit * LOG2E

    def power(codes, span):
        return codes * (span / 65535.0) + (span * (32768.0 / 65535.0) - span)

    def number(codes):
        return codes.astype(jnp.int32).astype(jnp.float32)

    def step(j, carry):
        depth, *colors = carry
        slab = order_ref[j]
        depth_code = number(code_ref[slab, 3])
        idle = depth_code == -32768.0
        shift = jnp.where(idle, FAR, depth)
        for i in range(3):
            colors[i] = colors[i] + jnp.exp2(power(number(code_ref[slab, i]), color_span) - shift)
        depth = depth + depth_unit * jnp.where(idle, 0.0, jnp.exp2(power(depth_code, depth_span)))
        return depth, *colors

    zero = jnp.zeros(shape, jnp.float32)
    depth, *colors = lax.fori_loop(0, count, step, (zero, zero, zero, zero), unroll=math.gcd(count, 4))
    for i in range(3):
        out_ref[i] = colors[i] * (unit * (TOP / (transfer_ref[i] + jnp.full(shape, TOP))))
    out_ref[3] = 1.0 - jnp.exp2(-depth)
    copy = pltpu.make_async_copy(out_ref, image_any.at[:, :, pl.ds(first, width)], out_sem)
    copy.start()
    copy.wait()


def composite(codes, transfer, depth_order, total, slab_len, first, columns, image):
    _, _, rows, width = codes.shape
    own = pl.BlockSpec(memory_space=pl.ANY)
    operands = [depth_order, transfer, codes] + ([] if image is None else [image])
    return pl.pallas_call(
        functools.partial(composite_kernel, total, slab_len, first),
        in_specs=[own] * len(operands),
        out_specs=own,
        out_shape=jax.ShapeDtypeStruct((4, rows, columns), jnp.float32),
        scratch_shapes=[
            pltpu.SMEM(depth_order.shape, depth_order.dtype),
            pltpu.SMEM(transfer.shape, transfer.dtype),
            pltpu.VMEM(codes.shape, codes.dtype),
            pltpu.VMEM((4, rows, width), jnp.float32),
            pltpu.SemaphoreType.DMA((3,)),
            pltpu.SemaphoreType.DMA,
        ],
        input_output_aliases={} if image is None else {3: 0},
        compiler_params=pltpu.CompilerParams(vmem_limit_bytes=SMALL_BYTES),
        name="composite",
    )(*operands)


def exchange(codes):
    return lax.all_to_all(codes, "depth", split_axis=0, concat_axis=0, tiled=True)


def on_device(field, jitter, transfer, depth_order, ray_start, ray_end):
    count = lax.axis_size("depth")
    slab_len, rows, cols = field.shape
    total = slab_len * count
    width = cols // count
    halo = shifted(field[0], "depth", -1)
    direct = width == 2 * UNIT
    pieces = count if direct else cols // (2 * UNIT)
    halves = slab_codes(field, halo, jitter, transfer, ray_start, ray_end, total, pieces)
    if not direct:
        codes = jnp.concatenate(halves, axis=3)
        halves = [codes.transpose(1, 2, 0, 3).reshape(4, rows, count, width).transpose(2, 0, 1, 3)]
    image = None
    for half, codes in enumerate(halves):
        image = composite(exchange(codes), transfer, depth_order, total, slab_len, half * UNIT, width, image)
    return image


def solution(mesh):
    in_specs = (P("depth", "groups", None), P("groups", None), P(), P(), P(), P())
    out_specs = P(None, "groups", "depth")
    return jax.shard_map(
        on_device, mesh=mesh, in_specs=in_specs, out_specs=out_specs, check_vma=False
    )
```

time: 56.1 us -> 57.5 us (1.025)
  blocking collectives: 33 us -> 0 us
  waiting for transfers between devices: 0.01 us -> 18.9 us
  starting transfers between devices: 1.29 us -> 13.5 us
  Pallas kernels: 18.9 us -> 23.5 us
  local copies, waits for them, and re-layouts: 2.17 us -> 1.03 us
    all_to_all x1 -> x0, blocking collectives: 33 us -> none  [on_device(): lax.all_to_all(codes, 'depth', split_axis=0, concat_axis=0, tiled=True)]
    all_to_all x0 -> x2, waiting for transfers between devices: none -> 18.9 us  [exchange(): lax.all_to_all(codes, 'depth', split_axis=0, concat_axis=0, tiled=True)]
    all_to_all x0 -> x2, starting transfers between devices: none -> 12.2 us  [exchange(): lax.all_to_all(codes, 'depth', split_axis=0, concat_axis=0, tiled=True)]
    pallas_call x3 -> x5, Pallas kernels: 18.9 us -> 23.5 us  [the longest x2 13.7 us: slab_codes(): pl.pallas_call(functools.partial(close_kernel, total, tile_cols, first, U...]
    unnamed x12 -> x8, local copies, waits for them, and re-layouts: 1.14 us -> 0.02 us
  transfers between devices with their start and end apart: 1 -> 3, of which waited for: 0 -> 2; matrix products, arithmetic and copies ran while one was open for 0% -> 0% of each run, Pallas kernels for 11% -> 29%
where the time goes in v11:
time: 57.5 us; the launch traced here: 57.1 us
  Pallas kernels  23.5 us (41%)
  waiting for transfers between devices  18.9 us (33%)
  starting transfers between devices  13.5 us (23%)
  local copies, waits for them, and re-layouts  1.03 us (2%)
    all_to_all x2, waiting for transfers between devices, exchange(): lax.all_to_all(codes, 'depth', split_axis=0, concat_axis=0, tiled=True)  18.9 us
    pallas_call x2, Pallas kernels, slab_codes(): pl.pallas_call(functools.partial(close_kernel, total, tile_cols, first, U...  13.7 us
    all_to_all x2, starting transfers between devices, exchange(): lax.all_to_all(codes, 'depth', split_axis=0, concat_axis=0, tiled=True)  12.2 us
    pallas_call x1, Pallas kernels, slab_codes(): pl.pallas_call(functools.partial(open_kernel, total, tile_cols, Units(0,...  6.7 us
    pallas_call x2, Pallas kernels, composite(): pl.pallas_call(functools.partial(composite_kernel, total, slab_len, first...  3.09 us
    ppermute x1, starting transfers between devices, shifted(): lax.ppermute(value, axis, [(source, source + steps) for source in range(i...  1.29 us
  transfers between devices with their start and end apart: 3, of which 2 were waited for; matrix products, arithmetic and copies ran while one was open for 0% of the time, Pallas kernels for 29%

profile of v11, /device:TPU:0, one launch (start us, length us, event | category | flops | bytes accessed | tf_op | source)
XLA Modules:
  0.0 57.1 jit_solution(11010524319470952579)
XLA Ops:
  0.0 0.0 copy-start.1
  0.0 0.0 copy-start.2
  0.0 0.0 copy-start
  0.0 1.0 %slice_bitcast_fusion = bf16[16,8192]{1,0:T(8,128)(2,1)S(1)} fusion(bf16[32,16,8192]{2,1,0:T(8,128)(2,1)} %refs_3_.3), kind=kLoop, calls=%fused_computation | loop fusion | bytes 524288 | tf_op jit(solution)/shard_map/squeeze | solution.py:405
  1.0 1.3 %collective-permute-start = (bf16[16,8192]{1,0:T(8,128)(2,1)S(1)}, bf16[16,8192]{1,0:T(8,128)(2,1)S(1)}, u32[]{:S(2)}, u32[]{:S(2)}) collective-permute-start(bf16[16,8192]{1,0:T(8,128)(2,1)S(1)} %slice_bitcast_fusion), channel_id=1, source_target_pairs={{1,0},{2,1},{3,2},{4,3},{5,4},{6,5},{7,6},{8,7},{9,8},{10,9},{11,1... | collective-permute-start | bytes 786440 | tf_op jit(solution)/shard_map/ppermute | solution.py:30
  2.3 6.7 %open.1.refs_6_ = f32[12,4,16,256]{3,2,1,0:T(8,128)} custom-call(f32[4]{0:T(128)} %transfer_any.5, s32[128]{0:T(128)} %refs_1_.3, s32[128]{0:T(128)} %refs_2_.3, bf16[32,16,8192]{2,1,0:T(8,128)(2,1)} %refs_3_.3, f32[16,8192]{1,0:T(8,128)} %refs_5_.3), custom_call_target="tpu_custom_call" | custom-call | flops 31457280 | bytes 3145728 | tf_op jit(solution)/shard_map/open/pallas_call | solution.py:279
  9.0 0.0 collective-permute-done.refs_4_
  9.0 0.0 copy-done.1
  9.0 0.0 copy-done.2
  9.1 0.0 copy-done
  9.1 5.3 %close.3 = s16[16,4,16,256]{3,2,1,0:T(8,128)(2,1)} custom-call(f32[4]{0:T(128)S(1)} %copy-done, s32[128]{0:T(128)S(1)} %copy-done.1, s32[128]{0:T(128)S(1)} %copy-done.2, bf16[32,16,8192]{2,1,0:T(8,128)(2,1)} %refs_3_.3, bf16[16,8192]{1,0:T(8,128)(2,1)S(1)} %collective-permute-done.refs_4_, f32[16,8192]{1,0:T(8,128)} %refs_5_.3, f32[12,4,16,256]{3,2,1,0:T(8,128)} %open.1.refs_6_), custom_call_target="tpu_custom_call" | custom-call | flops 10485760 | bytes 1048576 | tf_op jit(solution)/shard_map/close/pallas_call | solution.py:322
  14.3 0.0 copy-start.3
  14.4 8.1 %all-to-all-start.1 = ((s16[16,4,16,256]{3,2,1,0:T(8,128)(2,1)}), s16[16,4,16,256]{3,2,1,0:T(8,128)(2,1)S(1)}, u32[]{:S(2)}, u32[]{:S(2)}) async-start(s16[16,4,16,256]{3,2,1,0:T(8,128)(2,1)} %close.3), calls=%async_computation.1 | async-start | bytes 1048576 | tf_op jit(solution)/shard_map/all_to_all | solution.py:397
  22.5 8.5 %close.2 = s16[16,4,16,256]{3,2,1,0:T(8,128)(2,1)} custom-call(f32[4]{0:T(128)S(1)} %copy-done, s32[128]{0:T(128)S(1)} %copy-done.1, s32[128]{0:T(128)S(1)} %copy-done.2, bf16[32,16,8192]{2,1,0:T(8,128)(2,1)} %refs_3_.3, bf16[16,8192]{1,0:T(8,128)(2,1)S(1)} %collective-permute-done.refs_4_, f32[16,8192]{1,0:T(8,128)} %refs_5_.3), custom_call_target="tpu_custom_call" | custom-call | flops 41943040 | bytes 4194304 | tf_op jit(solution)/shard_map/close/pallas_call | solution.py:322
  31.0 6.0 %all-to-all-done.1.code_any = s16[16,4,16,256]{3,2,1,0:T(8,128)(2,1)S(1)} async-done(((s16[16,4,16,256]{3,2,1,0:T(8,128)(2,1)}), s16[16,4,16,256]{3,2,1,0:T(8,128)(2,1)S(1)}, u32[]{:S(2)}, u32[]{:S(2)}) %all-to-all-start.1) | async-done | bytes 524320 | tf_op jit(solution)/shard_map/all_to_all | solution.py:397
  37.0 4.1 %all-to-all-start = ((s16[16,4,16,256]{3,2,1,0:T(8,128)(2,1)}), s16[16,4,16,256]{3,2,1,0:T(8,128)(2,1)S(1)}, u32[]{:S(2)}, u32[]{:S(2)}) async-start(s16[16,4,16,256]{3,2,1,0:T(8,128)(2,1)} %close.2), calls=%async_computation | async-start | bytes 1048576 | tf_op jit(solution)/shard_map/all_to_all | solution.py:397
  41.1 0.0 copy-done.3
  41.1 1.5 %composite.2.refs_0_ = f32[4,16,512]{2,1,0:T(8,128)} custom-call(s32[16]{0:T(128)S(1)} %copy-done.3, f32[4]{0:T(128)S(1)} %copy-done, s16[16,4,16,256]{3,2,1,0:T(8,128)(2,1)S(1)} %all-to-all-done.1.code_any), custom_call_target="tpu_custom_call" | custom-call | tf_op jit(solution)/shard_map/composite/pallas_call | solution.py:377
  42.6 12.9 %all-to-all-done.code_any = s16[16,4,16,256]{3,2,1,0:T(8,128)(2,1)S(1)} async-done(((s16[16,4,16,256]{3,2,1,0:T(8,128)(2,1)}), s16[16,4,16,256]{3,2,1,0:T(8,128)(2,1)S(1)}, u32[]{:S(2)}, u32[]{:S(2)}) %all-to-all-start) | async-done | bytes 524320 | tf_op jit(solution)/shard_map/all_to_all | solution.py:397
  55.5 1.5 %composite.3 = f32[4,16,512]{2,1,0:T(8,128)} custom-call(s32[16]{0:T(128)S(1)} %copy-done.3, f32[4]{0:T(128)S(1)} %copy-done, s16[16,4,16,256]{3,2,1,0:T(8,128)(2,1)S(1)} %all-to-all-done.code_any, f32[4,16,512]{2,1,0:T(8,128)} %composite.2.refs_0_), custom_call_target="tpu_custom_call", output_to_operand_aliasing={{}: (3, {})} | custom-call | tf_op jit(solution)/shard_map/composite/pallas_call | solution.py:377
Async XLA Ops:
  0.0 9.0 %copy-start.1 = (s32[128]{0:T(128)S(1)}, s32[128]{0:T(128)}, u32[]{:S(2)}) copy-start(s32[128]{0:T(128)} %refs_1_.3) | copy-start | bytes 1540
  0.0 9.0 %copy-start.2 = (s32[128]{0:T(128)S(1)}, s32[128]{0:T(128)}, u32[]{:S(2)}) copy-start(s32[128]{0:T(128)} %refs_2_.3) | copy-start | bytes 1540
  0.0 9.1 %copy-start = (f32[4]{0:T(128)S(1)}, f32[4]{0:T(128)}, u32[]{:S(2)}) copy-start(f32[4]{0:T(128)} %transfer_any.5) | copy-start | bytes 52
  1.0 8.0 %collective-permute-start = (bf16[16,8192]{1,0:T(8,128)(2,1)S(1)}, bf16[16,8192]{1,0:T(8,128)(2,1)S(1)}, u32[]{:S(2)}, u32[]{:S(2)}) collective-permute-start(bf16[16,8192]{1,0:T(8,128)(2,1)S(1)} %slice_bitcast_fusion), channel_id=1, source_target_pairs={{1,0},{2,1},{3,2},{4,3},{5,4},{6,5},{7,6},{8,7},{9,8},{10,9},{11,1... | collective-permute-start | bytes 786440 | tf_op jit(solution)/shard_map/ppermute | solution.py:30
  14.3 26.7 %copy-start.3 = (s32[16]{0:T(128)S(1)}, s32[16]{0:T(128)}, u32[]{:S(2)}) copy-start(s32[16]{0:T(128)} %order_any.3) | copy-start | bytes 196
  14.4 22.6 %all-to-all-start.1 = ((s16[16,4,16,256]{3,2,1,0:T(8,128)(2,1)}), s16[16,4,16,256]{3,2,1,0:T(8,128)(2,1)S(1)}, u32[]{:S(2)}, u32[]{:S(2)}) async-start(s16[16,4,16,256]{3,2,1,0:T(8,128)(2,1)} %close.3), calls=%async_computation.1 | async-start | bytes 1048576 | tf_op jit(solution)/shard_map/all_to_all | solution.py:397
  37.0 18.6 %all-to-all-start = ((s16[16,4,16,256]{3,2,1,0:T(8,128)(2,1)}), s16[16,4,16,256]{3,2,1,0:T(8,128)(2,1)S(1)}, u32[]{:S(2)}, u32[]{:S(2)}) async-start(s16[16,4,16,256]{3,2,1,0:T(8,128)(2,1)} %close.2), calls=%async_computation | async-start | bytes 1048576 | tf_op jit(solution)/shard_map/all_to_all | solution.py:397

commit v12 on v11

--- a/solution.py
+++ b/solution.py
@@ -13,7 +13,7 @@
 SUBLANES = 8
 LANES = 128
 FAR = 1.0e4
-UNIT = 256
+UNIT = 512
 OPEN_BYTES = 54 * 1024 * 1024
 CLOSE_BYTES = 53 * 1024 * 1024
 SMALL_BYTES = 16 * 1024 * 1024
@@ -22,6 +22,10 @@
 def spans(slab_len):
     deep = math.log2(slab_len)
     return 6.8 + deep, 13.2 + deep
+
+
+def lift(span):
+    return span * (32768.0 / 65535.0) - span
 
 
 def shifted(value, axis, steps):
@@ -114,11 +118,11 @@
 
 
 class Units:
-    def __init__(self, first, half, pieces_width):
-        self.first, self.half, self.width = first, half, pieces_width
+    def __init__(self, first):
+        self.first = first
 
     def column(self, unit):
-        return (self.first + unit) * self.width + self.half * UNIT
+        return (self.first + unit) * UNIT
 
     def columns(self, unit):
         return pl.ds(pl.multiple_of(self.column(unit), LANES), UNIT)
@@ -176,13 +180,10 @@
     loop(units, lambda unit: leave(unit).wait())
 
 
-def close_kernel(total, tile_cols, opened, place, *refs):
-    before_units = Units(0, place.half, place.width)
-    ins = 7 if opened else 6
-    transfer_any, start_any, end_any, field_any, halo_any, jitter_any = refs[:6]
-    out_any = refs[ins]
-    transfer_ref, start_ref, end_ref, plane_ref, halo_ref, jitter_ref, out_ref, gain_ref, few_sems, sems, out_sems = refs[
-        ins + 1:ins + 12]
+def close_kernel(total, tile_cols, opened, place, transfer_any, start_any, end_any, field_any, halo_any, jitter_any, state_any,
+                 out_any, transfer_ref, start_ref, end_ref, plane_ref, halo_ref, jitter_ref, out_ref, gain_ref, few_sems, sems,
+                 out_sems, state_ref, last_ref, last_jitter_ref, last_gain_ref, state_sems):
+    before_units = Units(0)
     units, slab_len, rows, _ = plane_ref.shape
     few = [(transfer_any, transfer_ref), (start_any, start_ref), (end_any, end_ref), (halo_any, halo_ref)]
     early = start_all(few, few_sems)
@@ -190,22 +191,19 @@
     for unit in range(units):
         for copy in arrivals(unit):
             copy.start()
-    if opened:
-        state_any = refs[6]
-        state_ref, last_ref, last_jitter_ref, last_gain_ref, state_sems = refs[ins + 12:]
-
-        def opened_copies(unit):
-            cols = before_units.columns(unit)
-            pairs = [
-                (field_any.at[slab_len - 1, :, cols], last_ref.at[unit]),
-                (jitter_any.at[:, cols], last_jitter_ref.at[unit]),
-                (state_any.at[unit], state_ref.at[unit]),
-            ]
-            return [pltpu.make_async_copy(src, dst, state_sems.at[n, unit]) for n, (src, dst) in enumerate(pairs)]
-
-        for unit in range(opened):
-            for copy in opened_copies(unit):
-                copy.start()
+
+    def opened_copies(unit):
+        cols = before_units.columns(unit)
+        pairs = [
+            (field_any.at[slab_len - 1, :, cols], last_ref.at[unit]),
+            (jitter_any.at[:, cols], last_jitter_ref.at[unit]),
+            (state_any.at[unit], state_ref.at[unit]),
+        ]
+        return [pltpu.make_async_copy(src, dst, state_sems.at[n, unit]) for n, (src, dst) in enumerate(pairs)]
+
+    for unit in range(opened):
+        for copy in opened_copies(unit):
+            copy.start()
     base = lax.axis_index("depth") * slab_len
     for copy in early:
         copy.wait()
@@ -239,34 +237,34 @@
         return pltpu.make_async_copy(out_ref.at[piece], out_any.at[piece], out_sems.at[piece])
 
     each_block(units, arrive, compute, functools.partial(store, place.first), lambda unit: leave(place.first + unit).start())
-    if opened:
-        tile_gains(last_gain_ref, gain, base + slab_len - 1, tile_cols, start_ref, end_ref, before_units.block_column)
-
-        def arrive_opened(unit):
-            for copy in opened_copies(unit):
-                copy.wait()
-
-        def finish(unit, cols, table):
-            whole = pl.ds(pl.multiple_of(before_units.column(unit) + cols.start, LANES), LANES)
-            jitter = last_jitter_ref[unit, :, cols]
-            lower = last_ref[unit, :, cols].astype(jnp.float32)
-            upper = halo_ref[:, whole].astype(jnp.float32)
-            value = (1.0 - jitter) * lower + jitter * upper
-            before = state_ref[unit, 3, :, cols]
-            beyond = before + last_gain_ref[0:1, table] * value
-            emitted = (jnp.exp2(before) - jnp.exp2(beyond)) * value
-            sums = [state_ref[unit, i, :, cols] for i in range(3)]
-            moment(sums, emitted, value, levels)
-            return coded(sums, beyond)
-
-        each_block(opened, arrive_opened, finish, functools.partial(store, 0), lambda unit: leave(unit).start())
+    tile_gains(last_gain_ref, gain, base + slab_len - 1, tile_cols, start_ref, end_ref, before_units.block_column)
+
+    def arrive_opened(unit):
+        for copy in opened_copies(unit):
+            copy.wait()
+
+    def finish(unit, cols, table):
+        whole = pl.ds(pl.multiple_of(before_units.column(unit) + cols.start, LANES), LANES)
+        jitter = last_jitter_ref[unit, :, cols]
+        lower = last_ref[unit, :, cols].astype(jnp.float32)
+        upper = halo_ref[:, whole].astype(jnp.float32)
+        value = (1.0 - jitter) * lower + jitter * upper
+        before = state_ref[unit, 3, :, cols]
+        beyond = before + last_gain_ref[0:1, table] * value
+        emitted = (jnp.exp2(before) - jnp.exp2(beyond)) * value
+        sums = [state_ref[unit, i, :, cols] for i in range(3)]
+        moment(sums, emitted, value, levels)
+        return coded(sums, beyond)
+
+    each_block(opened, arrive_opened, finish, functools.partial(store, 0), lambda unit: leave(unit).start())
     loop(out_ref.shape[0], lambda piece: leave(piece).wait())
 
 
-def slab_codes(field, halo, jitter, transfer, ray_start, ray_end, total, pieces):
+def slab_codes(field, halo, jitter, transfer, ray_start, ray_end, total):
     slab_len, rows, cols = field.shape
-    width = cols // pieces
-    opened = pieces * 3 // 8 * 2
+    pieces = cols // UNIT
+    opened = pieces * 3 // 16 * 2
+    closed = pieces - opened
     ntiles = ray_start.shape[0]
     tile_cols = cols // ntiles
     own = pl.BlockSpec(memory_space=pl.ANY)
@@ -277,7 +275,7 @@
         return pl.CostEstimate(flops=work * 20, bytes_accessed=work * 2, transcendentals=work * 2)
 
     state = pl.pallas_call(
-        functools.partial(open_kernel, total, tile_cols, Units(0, 0, width)),
+        functools.partial(open_kernel, total, tile_cols, Units(0)),
         in_specs=[own] * 5,
         out_specs=own,
         out_shape=jax.ShapeDtypeStruct((opened, 4, rows, UNIT), jnp.float32),
@@ -295,106 +293,95 @@
         name="open",
     )(transfer, ray_start, ray_end, field, jitter)
 
-    halves = []
-    for half in range(2):
-        first = opened if half == 0 else 0
-        units = pieces - first
-        scratch = scalars + [
-            pltpu.VMEM((units, slab_len, rows, UNIT), field.dtype),
+    return pl.pallas_call(
+        functools.partial(close_kernel, total, tile_cols, opened, Units(opened)),
+        in_specs=[own] * 7,
+        out_specs=own,
+        out_shape=jax.ShapeDtypeStruct((pieces, 4, rows, UNIT), jnp.int16),
+        scratch_shapes=scalars + [
+            pltpu.VMEM((closed, slab_len, rows, UNIT), field.dtype),
             pltpu.VMEM((rows, cols), field.dtype),
-            pltpu.VMEM((units, rows, UNIT), jnp.float32),
+            pltpu.VMEM((closed, rows, UNIT), jnp.float32),
             pltpu.VMEM((pieces, 4, rows, UNIT), jnp.int16),
-            pltpu.VMEM((slab_len, units * UNIT), jnp.float32),
+            pltpu.VMEM((slab_len, closed * UNIT), jnp.float32),
             pltpu.SemaphoreType.DMA((4,)),
-            pltpu.SemaphoreType.DMA((2, units)),
+            pltpu.SemaphoreType.DMA((2, closed)),
             pltpu.SemaphoreType.DMA((pieces,)),
-        ]
-        operands = [transfer, ray_start, ray_end, field, halo, jitter]
-        if first:
-            operands.append(state)
-            scratch += [
-                pltpu.VMEM((first, 4, rows, UNIT), jnp.float32),
-                pltpu.VMEM((first, rows, UNIT), field.dtype),
-                pltpu.VMEM((first, rows, UNIT), jnp.float32),
-                pltpu.VMEM((SUBLANES, first * UNIT), jnp.float32),
-                pltpu.SemaphoreType.DMA((3, first)),
-            ]
-        halves.append(pl.pallas_call(
-            functools.partial(close_kernel, total, tile_cols, first, Units(first, half, width)),
-            in_specs=[own] * len(operands),
-            out_specs=own,
-            out_shape=jax.ShapeDtypeStruct((pieces, 4, rows, UNIT), jnp.int16),
-            scratch_shapes=scratch,
-            compiler_params=pltpu.CompilerParams(vmem_limit_bytes=CLOSE_BYTES),
-            cost_estimate=cost(units),
-            name="close",
-        )(*operands))
-    return halves
-
-
-def composite_kernel(total, slab_len, first, order_any, transfer_any, code_any, *refs):
-    image_any, order_ref, transfer_ref, code_ref, out_ref, sems, out_sem = refs[-7:]
-    copies = start_all([(order_any, order_ref), (transfer_any, transfer_ref), (code_any, code_ref)], sems)
+            pltpu.VMEM((opened, 4, rows, UNIT), jnp.float32),
+            pltpu.VMEM((opened, rows, UNIT), field.dtype),
+            pltpu.VMEM((opened, rows, UNIT), jnp.float32),
+            pltpu.VMEM((SUBLANES, opened * UNIT), jnp.float32),
+            pltpu.SemaphoreType.DMA((3, opened)),
+        ],
+        compiler_params=pltpu.CompilerParams(vmem_limit_bytes=CLOSE_BYTES),
+        cost_estimate=cost(closed),
+        name="close",
+    )(transfer, ray_start, ray_end, field, halo, jitter, state)
+
+
+def composite_kernel(total, slab_len, order_any, transfer_any, code_any, image_any, order_ref, transfer_ref, code_ref, out_ref,
+                     sems, out_sems):
+    copies = start_all([(order_any, order_ref), (transfer_any, transfer_ref)], sems)
     count, _, rows, width = code_ref.shape
-    shape = (rows, width)
+    block = math.gcd(width, 2 * LANES)
+    places = [pl.ds(col, block) for col in range(0, width, block)]
+    codes = start_all([(code_any.at[:, :, :, cols], code_ref.at[:, :, :, cols]) for cols in places], sems.at[pl.ds(2, len(places))])
+    shape = (rows, block)
     depth_span, color_span = spans(slab_len)
     for copy in copies:
         copy.wait()
     unit = jnp.full(shape, transfer_ref[3]) * (0.2 / total * slab_len * TOP)
     depth_unit = unit * LOG2E
-
-    def power(codes, span):
-        return codes * (span / 65535.0) + (span * (32768.0 / 65535.0) - span)
-
-    def number(codes):
-        return codes.astype(jnp.int32).astype(jnp.float32)
-
-    def step(j, carry):
-        depth, *colors = carry
-        slab = order_ref[j]
-        depth_code = number(code_ref[slab, 3])
-        idle = depth_code == -32768.0
-        shift = jnp.where(idle, FAR, depth)
+    leaving = []
+    for n, cols in enumerate(places):
+        codes[n].wait()
+
+        def number(slab, channel, span):
+            return code_ref[slab, channel, :, cols].astype(jnp.int32).astype(jnp.float32) * (span / 65535.0)
+
+        def step(j, carry):
+            shift, *colors = carry
+            slab = order_ref[j]
+            code = number(slab, 3, depth_span)
+            idle = code < depth_span * (-32767.5 / 65535.0)
+            away = jnp.where(idle, FAR, shift)
+            for i in range(3):
+                colors[i] = colors[i] + jnp.exp2(number(slab, i, color_span) - away)
+            own = jnp.where(idle, 0.0, jnp.exp2(code + lift(depth_span)))
+            return shift + depth_unit * own, *colors
+
+        zero = jnp.zeros(shape, jnp.float32)
+        first = jnp.full(shape, -lift(color_span))
+        shift, *colors = lax.fori_loop(0, count, step, (first, zero, zero, zero), unroll=math.gcd(count, 4))
         for i in range(3):
-            colors[i] = colors[i] + jnp.exp2(power(number(code_ref[slab, i]), color_span) - shift)
-        depth = depth + depth_unit * jnp.where(idle, 0.0, jnp.exp2(power(depth_code, depth_span)))
-        return depth, *colors
-
-    zero = jnp.zeros(shape, jnp.float32)
-    depth, *colors = lax.fori_loop(0, count, step, (zero, zero, zero, zero), unroll=math.gcd(count, 4))
-    for i in range(3):
-        out_ref[i] = colors[i] * (unit * (TOP / (transfer_ref[i] + jnp.full(shape, TOP))))
-    out_ref[3] = 1.0 - jnp.exp2(-depth)
-    copy = pltpu.make_async_copy(out_ref, image_any.at[:, :, pl.ds(first, width)], out_sem)
-    copy.start()
-    copy.wait()
-
-
-def composite(codes, transfer, depth_order, total, slab_len, first, columns, image):
+            out_ref[i, :, cols] = colors[i] * (unit * (TOP / (transfer_ref[i] + jnp.full(shape, TOP))))
+        out_ref[3, :, cols] = 1.0 - jnp.exp2(first - shift)
+        leaving.append(pltpu.make_async_copy(out_ref.at[:, :, cols], image_any.at[:, :, cols], out_sems.at[n]))
+        leaving[-1].start()
+    for copy in leaving:
+        copy.wait()
+
+
+def composite(codes, transfer, depth_order, total, slab_len):
     _, _, rows, width = codes.shape
+    blocks = width // math.gcd(width, 2 * LANES)
     own = pl.BlockSpec(memory_space=pl.ANY)
-    operands = [depth_order, transfer, codes] + ([] if image is None else [image])
     return pl.pallas_call(
-        functools.partial(composite_kernel, total, slab_len, first),
-        in_specs=[own] * len(operands),
+        functools.partial(composite_kernel, total, slab_len),
+        in_specs=[own] * 3,
         out_specs=own,
-        out_shape=jax.ShapeDtypeStruct((4, rows, columns), jnp.float32),
+        out_shape=jax.ShapeDtypeStruct((4, rows, width), jnp.float32),
         scratch_shapes=[
             pltpu.SMEM(depth_order.shape, depth_order.dtype),
             pltpu.SMEM(transfer.shape, transfer.dtype),
             pltpu.VMEM(codes.shape, codes.dtype),
             pltpu.VMEM((4, rows, width), jnp.float32),
-            pltpu.SemaphoreType.DMA((3,)),
-            pltpu.SemaphoreType.DMA,
+            pltpu.SemaphoreType.DMA((2 + blocks,)),
+            pltpu.SemaphoreType.DMA((blocks,)),
         ],
-        input_output_aliases={} if image is None else {3: 0},
         compiler_params=pltpu.CompilerParams(vmem_limit_bytes=SMALL_BYTES),
         name="composite",
-    )(*operands)
-
-
-def exchange(codes):
-    return lax.all_to_all(codes, "depth", split_axis=0, concat_axis=0, tiled=True)
+    )(depth_order, transfer, codes)
 
 
 def on_device(field, jitter, transfer, depth_order, ray_start, ray_end):
@@ -403,16 +390,11 @@
     total = slab_len * count
     width = cols // count
     halo = shifted(field[0], "depth", -1)
-    direct = width == 2 * UNIT
-    pieces = count if direct else cols // (2 * UNIT)
-    halves = slab_codes(field, halo, jitter, transfer, ray_start, ray_end, total, pieces)
-    if not direct:
-        codes = jnp.concatenate(halves, axis=3)
-        halves = [codes.transpose(1, 2, 0, 3).reshape(4, rows, count, width).transpose(2, 0, 1, 3)]
-    image = None
-    for half, codes in enumerate(halves):
-        image = composite(exchange(codes), transfer, depth_order, total, slab_len, half * UNIT, width, image)
-    return image
+    codes = slab_codes(field, halo, jitter, transfer, ray_start, ray_end, total)
+    if width != UNIT:
+        codes = codes.transpose(1, 2, 0, 3).reshape(4, rows, count, width).transpose(2, 0, 1, 3)
+    received = lax.all_to_all(codes, "depth", split_axis=0, concat_axis=0, tiled=True)
+    return composite(received, transfer, depth_order, total, slab_len)
 
 
 def solution(mesh):

time: 57.5 us -> 55.5 us (0.965)
  blocking collectives: 0 us -> 33 us
  waiting for transfers between devices: 18.9 us -> 0.01 us
  starting transfers between devices: 13.5 us -> 1.29 us
  Pallas kernels: 23.5 us -> 19.5 us
    all_to_all x0 -> x1, blocking collectives: none -> 33 us  [on_device(): lax.all_to_all(codes, 'depth', split_axis=0, concat_axis=0, tiled=True)]
    all_to_all x2 -> x0, waiting for transfers between devices: 18.9 us -> none  [exchange(): lax.all_to_all(codes, 'depth', split_axis=0, concat_axis=0, tiled=True)]
    all_to_all x2 -> x0, starting transfers between devices: 12.2 us -> none  [exchange(): lax.all_to_all(codes, 'depth', split_axis=0, concat_axis=0, tiled=True)]
    pallas_call x5 -> x3, Pallas kernels: 23.5 us -> 19.5 us  [the longest x1 11.1 us: slab_codes(): pl.pallas_call(functools.partial(close_kernel, total, tile_cols, opened,...]
  transfers between devices with their start and end apart: 3 -> 1, of which waited for: 2 -> 0; matrix products, arithmetic and copies ran while one was open for 0% -> 0% of each run, Pallas kernels for 29% -> 12%
where the time goes in v12:
time: 55.5 us; the launch traced here: 54.9 us
  blocking collectives  33 us (59%)
  Pallas kernels  19.5 us (35%)
  starting transfers between devices  1.29 us (2%)
  local copies, waits for them, and re-layouts  1.05 us (2%)
    all_to_all x1, blocking collectives, on_device(): lax.all_to_all(codes, 'depth', split_axis=0, concat_axis=0, tiled=True)  33 us
    pallas_call x1, Pallas kernels, slab_codes(): pl.pallas_call(functools.partial(close_kernel, total, tile_cols, opened,...  11.1 us
    pallas_call x1, Pallas kernels, slab_codes(): pl.pallas_call(functools.partial(open_kernel, total, tile_cols, Units(0))...  6.58 us
    pallas_call x1, Pallas kernels, composite(): pl.pallas_call(functools.partial(composite_kernel, total, slab_len), in_s...  1.82 us
    ppermute x1, starting transfers between devices, shifted(): lax.ppermute(value, axis, [(source, source + steps) for source in range(i...  1.29 us
  transfers between devices with their start and end apart: 1, of which 0 were waited for; matrix products, arithmetic and copies ran while one was open for 0% of the time, Pallas kernels for 12%

profile of v12, /device:TPU:0, one launch (start us, length us, event | category | flops | bytes accessed | tf_op | source)
XLA Modules:
  0.0 54.9 jit_solution(5203833764973251611)
XLA Ops:
  0.0 0.0 copy-start.1
  0.0 0.0 copy-start.3
  0.0 0.0 copy-start.2
  0.0 0.0 copy-start
  0.0 1.0 %slice_bitcast_fusion = bf16[16,8192]{1,0:T(8,128)(2,1)S(1)} fusion(bf16[32,16,8192]{2,1,0:T(8,128)(2,1)} %field_any.3), kind=kLoop, calls=%fused_computation | loop fusion | bytes 524288 | tf_op jit(solution)/shard_map/squeeze | solution.py:392
  1.0 1.3 %collective-permute-start = (bf16[16,8192]{1,0:T(8,128)(2,1)S(1)}, bf16[16,8192]{1,0:T(8,128)(2,1)S(1)}, u32[]{:S(2)}, u32[]{:S(2)}) collective-permute-start(bf16[16,8192]{1,0:T(8,128)(2,1)S(1)} %slice_bitcast_fusion), channel_id=1, source_target_pairs={{1,0},{2,1},{3,2},{4,3},{5,4},{6,5},{7,6},{8,7},{9,8},{10,9},{11,1... | collective-permute-start | bytes 786440 | tf_op jit(solution)/shard_map/ppermute | solution.py:34
  2.3 6.6 %open.1.state_any = f32[6,4,16,512]{3,2,1,0:T(8,128)} custom-call(f32[4]{0:T(128)} %transfer_any.5, s32[128]{0:T(128)} %start_any.3, s32[128]{0:T(128)} %end_any.3, bf16[32,16,8192]{2,1,0:T(8,128)(2,1)} %field_any.3, f32[16,8192]{1,0:T(8,128)} %jitter_any.3), custom_call_target="tpu_custom_call" | custom-call | flops 31457280 | bytes 3145728 | tf_op jit(solution)/shard_map/open/pallas_call | solution.py:277
  8.9 0.0 copy-start.4
  8.9 0.0 collective-permute-done.halo_any
  8.9 0.0 copy-done.1
  9.0 0.0 copy-done.3
  9.0 0.0 copy-done.2
  9.0 0.0 copy-done
  9.0 11.1 %close.1 = s16[16,4,16,512]{3,2,1,0:T(8,128)(2,1)} custom-call(f32[4]{0:T(128)S(1)} %copy-done.1, s32[128]{0:T(128)S(1)} %copy-done.2, s32[128]{0:T(128)S(1)} %copy-done.3, bf16[32,16,8192]{2,1,0:T(8,128)(2,1)} %field_any.3, bf16[16,8192]{1,0:T(8,128)(2,1)S(1)} %collective-permute-done.halo_any, f32[16,8192]{1,0:T(8,128)S(1)} %copy-done, ...), custom_call_target="tpu_custom_call" | custom-call | flops 52428800 | bytes 5242880 | tf_op jit(solution)/shard_map/close/pallas_call | solution.py:296
  20.1 33.0 %all_to_all.5.code_any = s16[16,4,16,512]{3,2,1,0:T(8,128)(2,1)S(1)} all-to-all(s16[16,4,16,512]{3,2,1,0:T(8,128)(2,1)} %close.1), channel_id=1, replica_groups=mesh['groups'=2,'depth'=16] {'depth'}, dimensions={0} | all-to-all | bytes 2097152 | tf_op jit(solution)/shard_map/all_to_all | solution.py:396
  53.1 0.0 copy-done.4
  53.1 1.8 %composite.1 = f32[4,16,512]{2,1,0:T(8,128)} custom-call(s32[16]{0:T(128)S(1)} %copy-done.4, f32[4]{0:T(128)S(1)} %copy-done.1, s16[16,4,16,512]{3,2,1,0:T(8,128)(2,1)S(1)} %all_to_all.5.code_any), custom_call_target="tpu_custom_call" | custom-call | tf_op jit(solution)/shard_map/composite/pallas_call | solution.py:369
Async XLA Ops:
  0.0 8.9 %copy-start.1 = (f32[4]{0:T(128)S(1)}, f32[4]{0:T(128)}, u32[]{:S(2)}) copy-start(f32[4]{0:T(128)} %transfer_any.5) | copy-start | bytes 52
  0.0 9.0 %copy-start.3 = (s32[128]{0:T(128)S(1)}, s32[128]{0:T(128)}, u32[]{:S(2)}) copy-start(s32[128]{0:T(128)} %end_any.3) | copy-start | bytes 1540
  0.0 9.0 %copy-start.2 = (s32[128]{0:T(128)S(1)}, s32[128]{0:T(128)}, u32[]{:S(2)}) copy-start(s32[128]{0:T(128)} %start_any.3) | copy-start | bytes 1540
  0.0 9.0 %copy-start = (f32[16,8192]{1,0:T(8,128)S(1)}, f32[16,8192]{1,0:T(8,128)}, u32[]{:S(2)}) copy-start(f32[16,8192]{1,0:T(8,128)} %jitter_any.3) | copy-start | bytes 1572868
  1.0 7.9 %collective-permute-start = (bf16[16,8192]{1,0:T(8,128)(2,1)S(1)}, bf16[16,8192]{1,0:T(8,128)(2,1)S(1)}, u32[]{:S(2)}, u32[]{:S(2)}) collective-permute-start(bf16[16,8192]{1,0:T(8,128)(2,1)S(1)} %slice_bitcast_fusion), channel_id=1, source_target_pairs={{1,0},{2,1},{3,2},{4,3},{5,4},{6,5},{7,6},{8,7},{9,8},{10,9},{11,1... | collective-permute-start | bytes 786440 | tf_op jit(solution)/shard_map/ppermute | solution.py:34
  8.9 44.2 %copy-start.4 = (s32[16]{0:T(128)S(1)}, s32[16]{0:T(128)}, u32[]{:S(2)}) copy-start(s32[16]{0:T(128)} %order_any.1) | copy-start | bytes 196

commit v13 on v12

--- a/solution.py
+++ b/solution.py
@@ -15,7 +15,7 @@
 FAR = 1.0e4
 UNIT = 512
 OPEN_BYTES = 54 * 1024 * 1024
-CLOSE_BYTES = 53 * 1024 * 1024
+CLOSE_BYTES = 58 * 1024 * 1024
 SMALL_BYTES = 16 * 1024 * 1024
 
 
@@ -28,10 +28,13 @@
     return span * (32768.0 / 65535.0) - span
 
 
-def shifted(value, axis, steps):
+def pair_planes(value, axis):
     count = lax.axis_size(axis)
-    initial, last = (max(0, -steps), min(count, count - steps))
-    return lax.ppermute(value, axis, [(source, source + steps) for source in range(initial, last)])
+    gathered = []
+    for odd in range(2):
+        groups = [[first, (first + 1) % count] for first in range(odd, count, 2)]
+        gathered.append(lax.all_gather(value, axis, axis_index_groups=groups))
+    return gathered
 
 
 def encode(value, span):
@@ -103,18 +106,18 @@
     lax.fori_loop(0, count, step, 0)
 
 
-def each_block(units, arrive, compute, store, leave):
-    def pair(n):
-        places = [(2 * n + u, c) for u in range(2) for c in range(0, UNIT, LANES)]
-        for u in range(2):
-            arrive(2 * n + u)
+def each_block(units, group, arrive, compute, store, leave):
+    def step(n):
+        places = [(group * n + u, c) for u in range(group) for c in range(0, UNIT, LANES)]
+        for u in range(group):
+            arrive(group * n + u)
         results = [compute(unit, pl.ds(c, LANES), pl.ds(pl.multiple_of(unit * UNIT + c, LANES), LANES)) for unit, c in places]
         for (unit, c), result in zip(places, results):
             store(unit, pl.ds(c, LANES), result)
-        for u in range(2):
-            leave(2 * n + u)
-
-    loop(units // 2, pair)
+        for u in range(group):
+            leave(group * n + u)
+
+    loop(units // group, step)
 
 
 class Units:
@@ -176,21 +179,21 @@
     def leave(unit):
         return pltpu.make_async_copy(state_ref.at[unit], state_any.at[unit], out_sems.at[unit])
 
-    each_block(units, arrive, compute, store, lambda unit: leave(unit).start())
+    each_block(units, 1, arrive, compute, store, lambda unit: leave(unit).start())
     loop(units, lambda unit: leave(unit).wait())
 
 
-def close_kernel(total, tile_cols, opened, place, transfer_any, start_any, end_any, field_any, halo_any, jitter_any, state_any,
-                 out_any, transfer_ref, start_ref, end_ref, plane_ref, halo_ref, jitter_ref, out_ref, gain_ref, few_sems, sems,
+def close_kernel(total, tile_cols, opened, place, transfer_any, start_any, end_any, field_any, even_any, odd_any, jitter_any,
+                 state_any, out_any, transfer_ref, start_ref, end_ref, plane_ref, halo_ref, jitter_ref, out_ref, gain_ref, few_sems, halo_sem, sems,
                  out_sems, state_ref, last_ref, last_jitter_ref, last_gain_ref, state_sems):
     before_units = Units(0)
     units, slab_len, rows, _ = plane_ref.shape
-    few = [(transfer_any, transfer_ref), (start_any, start_ref), (end_any, end_ref), (halo_any, halo_ref)]
-    early = start_all(few, few_sems)
-    arrivals = functools.partial(unit_copies, place, field_any, jitter_any, plane_ref, jitter_ref, sems)
-    for unit in range(units):
-        for copy in arrivals(unit):
-            copy.start()
+    here = lax.axis_index("depth")
+    last = here == lax.axis_size("depth") - 1
+    even = here % 2 == 0
+
+    def halo_copy(planes_any):
+        return pltpu.make_async_copy(planes_any.at[1], halo_ref, halo_sem)
 
     def opened_copies(unit):
         cols = before_units.columns(unit)
@@ -201,12 +204,25 @@
         ]
         return [pltpu.make_async_copy(src, dst, state_sems.at[n, unit]) for n, (src, dst) in enumerate(pairs)]
 
+    early = start_all([(transfer_any, transfer_ref), (start_any, start_ref), (end_any, end_ref)], few_sems)
+    pl.when(even)(lambda: halo_copy(even_any).start())
+    pl.when(jnp.logical_not(even))(lambda: halo_copy(odd_any).start())
     for unit in range(opened):
         for copy in opened_copies(unit):
             copy.start()
-    base = lax.axis_index("depth") * slab_len
+    arrivals = functools.partial(unit_copies, place, field_any, jitter_any, plane_ref, jitter_ref, sems)
+    for unit in range(units):
+        for copy in arrivals(unit):
+            copy.start()
+    base = here * slab_len
     for copy in early:
         copy.wait()
+    halo_copy(even_any).wait()
+
+    @pl.when(last)
+    def _():
+        halo_ref[...] = jnp.zeros(halo_ref.shape, halo_ref.dtype)
+
     shape = (rows, LANES)
     depth_gain = jnp.full(shape, transfer_ref[3]) * (0.2 / total)
     levels = [jnp.full(shape, transfer_ref[i]) for i in range(3)]
@@ -214,7 +230,6 @@
     color_unit = [depth_unit * ((levels[i] + TOP) * (1.0 / TOP)) for i in range(3)]
     depth_span, color_span = spans(slab_len)
     gain = depth_gain[:SUBLANES] * -LOG2E
-    tile_gains(gain_ref, gain, base, tile_cols, start_ref, end_ref, place.block_column)
 
     def coded(sums, before):
         codes = [encode(color * color_unit[i], color_span) for i, color in enumerate(colors(sums, levels))]
@@ -236,7 +251,6 @@
     def leave(piece):
         return pltpu.make_async_copy(out_ref.at[piece], out_any.at[piece], out_sems.at[piece])
 
-    each_block(units, arrive, compute, functools.partial(store, place.first), lambda unit: leave(place.first + unit).start())
     tile_gains(last_gain_ref, gain, base + slab_len - 1, tile_cols, start_ref, end_ref, before_units.block_column)
 
     def arrive_opened(unit):
@@ -256,11 +270,13 @@
         moment(sums, emitted, value, levels)
         return coded(sums, beyond)
 
-    each_block(opened, arrive_opened, finish, functools.partial(store, 0), lambda unit: leave(unit).start())
+    each_block(opened, 2, arrive_opened, finish, functools.partial(store, 0), lambda unit: leave(unit).start())
+    tile_gains(gain_ref, gain, base, tile_cols, start_ref, end_ref, place.block_column)
+    each_block(units, 1, arrive, compute, functools.partial(store, place.first), lambda unit: leave(place.first + unit).start())
     loop(out_ref.shape[0], lambda piece: leave(piece).wait())
 
 
-def slab_codes(field, halo, jitter, transfer, ray_start, ray_end, total):
+def slab_codes(field, planes, jitter, transfer, ray_start, ray_end, total):
     slab_len, rows, cols = field.shape
     pieces = cols // UNIT
     opened = pieces * 3 // 16 * 2
@@ -295,7 +311,7 @@
 
     return pl.pallas_call(
         functools.partial(close_kernel, total, tile_cols, opened, Units(opened)),
-        in_specs=[own] * 7,
+        in_specs=[own] * 8,
         out_specs=own,
         out_shape=jax.ShapeDtypeStruct((pieces, 4, rows, UNIT), jnp.int16),
         scratch_shapes=scalars + [
@@ -304,7 +320,8 @@
             pltpu.VMEM((closed, rows, UNIT), jnp.float32),
             pltpu.VMEM((pieces, 4, rows, UNIT), jnp.int16),
             pltpu.VMEM((slab_len, closed * UNIT), jnp.float32),
-            pltpu.SemaphoreType.DMA((4,)),
+            pltpu.SemaphoreType.DMA((3,)),
+            pltpu.SemaphoreType.DMA,
             pltpu.SemaphoreType.DMA((2, closed)),
             pltpu.SemaphoreType.DMA((pieces,)),
             pltpu.VMEM((opened, 4, rows, UNIT), jnp.float32),
@@ -316,7 +333,7 @@
         compiler_params=pltpu.CompilerParams(vmem_limit_bytes=CLOSE_BYTES),
         cost_estimate=cost(closed),
         name="close",
-    )(transfer, ray_start, ray_end, field, halo, jitter, state)
+    )(transfer, ray_start, ray_end, field, *planes, jitter, state)
 
 
 def composite_kernel(total, slab_len, order_any, transfer_any, code_any, image_any, order_ref, transfer_ref, code_ref, out_ref,
@@ -389,8 +406,8 @@
     slab_len, rows, cols = field.shape
     total = slab_len * count
     width = cols // count
-    halo = shifted(field[0], "depth", -1)
-    codes = slab_codes(field, halo, jitter, transfer, ray_start, ray_end, total)
+    planes = pair_planes(field[0], "depth")
+    codes = slab_codes(field, planes, jitter, transfer, ray_start, ray_end, total)
     if width != UNIT:
         codes = codes.transpose(1, 2, 0, 3).reshape(4, rows, count, width).transpose(2, 0, 1, 3)
     received = lax.all_to_all(codes, "depth", split_axis=0, concat_axis=0, tiled=True)

time: 55.5 us -> 66.6 us (1.20)
  blocking collectives: 33 us -> 43.4 us
  Pallas kernels: 19.5 us -> 21.6 us
  starting transfers between devices: 1.29 us -> 0 us
    all_gather x0 -> x2, blocking collectives: none -> 12.7 us  [pair_planes(): gathered.append(lax.all_gather(value, axis, axis_index_groups=groups))]
    all_to_all x1, blocking collectives: 33 us -> 30.8 us  [on_device(): lax.all_to_all(codes, 'depth', split_axis=0, concat_axis=0, tiled=True)]
    pallas_call x1, Pallas kernels: 11.1 us -> 13.3 us  [slab_codes(): pl.pallas_call(functools.partial(close_kernel, total, tile_cols, opened,...]
    ppermute x1 -> x0, starting transfers between devices: 1.29 us -> none  [shifted(): lax.ppermute(value, axis, [(source, source + steps) for source in range(i...]
    squeeze x1 -> x0, local copies, waits for them, and re-layouts: 1.03 us -> none  [on_device(): halo = shifted(field[0], 'depth', -1)]
    slice x0 -> x1, local copies, waits for them, and re-layouts: none -> 0.97 us  [on_device(): planes = pair_planes(field[0], 'depth')]
  transfers between devices with their start and end apart: 1 -> 0, of which waited for: 0 -> 0; matrix products, arithmetic and copies ran while one was open for 0% -> 0% of each run, Pallas kernels for 12% -> 0%
where the time goes in v13:
time: 66.6 us; the launch traced here: 66.1 us
  blocking collectives  43.4 us (65%)
  Pallas kernels  21.6 us (32%)
  local copies, waits for them, and re-layouts  0.98 us (1%)
    all_to_all x1, blocking collectives, on_device(): lax.all_to_all(codes, 'depth', split_axis=0, concat_axis=0, tiled=True)  30.8 us
    pallas_call x1, Pallas kernels, slab_codes(): pl.pallas_call(functools.partial(close_kernel, total, tile_cols, opened,...  13.3 us
    all_gather x2, blocking collectives, pair_planes(): gathered.append(lax.all_gather(value, axis, axis_index_groups=groups))  12.7 us
    pallas_call x1, Pallas kernels, slab_codes(): pl.pallas_call(functools.partial(open_kernel, total, tile_cols, Units(0))...  6.45 us
    pallas_call x1, Pallas kernels, composite(): pl.pallas_call(functools.partial(composite_kernel, total, slab_len), in_s...  1.82 us

profile of v13, /device:TPU:0, one launch (start us, length us, event | category | flops | bytes accessed | tf_op | source)
XLA Modules:
  0.0 66.1 jit_solution(18090298118296073648)
XLA Ops:
  0.0 1.0 %slice.3 = bf16[1,16,8192]{2,1,0:T(8,128)(2,1)S(1)} slice(bf16[32,16,8192]{2,1,0:T(8,128)(2,1)} %field_any.3), slice={[0:1], [0:16], [0:8192]} | slice | bytes 524288 | tf_op jit(solution)/shard_map/slice | solution.py:409
  1.0 10.4 %all_gather.7.odd_any = bf16[2,16,8192]{2,1,0:T(8,128)(2,1)} all-gather(bf16[1,16,8192]{2,1,0:T(8,128)(2,1)S(1)} %slice.3), channel_id=1, replica_groups={{1,2},{3,4},{5,6},{7,8},{9,10},{11,12},{13,14},{15,0},{17,18},{19,20},{..., dimensions={0}, use_global_device_ids=true | all-gather | bytes 786432 | tf_op jit(solution)/shard_map/all_gather | solution.py:36
  11.3 2.3 %all_gather.6.even_any = bf16[2,16,8192]{2,1,0:T(8,128)(2,1)} all-gather(bf16[1,16,8192]{2,1,0:T(8,128)(2,1)S(1)} %slice.3), channel_id=1, replica_groups={{0,1},{2,3},{4,5},{6,7},{8,9},{10,11},{12,13},{14,15},{16,17},{18,19},{..., dimensions={0}, use_global_device_ids=true | all-gather | bytes 786432 | tf_op jit(solution)/shard_map/all_gather | solution.py:36
  13.6 6.5 %open.1.state_any = f32[6,4,16,512]{3,2,1,0:T(8,128)} custom-call(f32[4]{0:T(128)} %transfer_any.5, s32[128]{0:T(128)} %start_any.3, s32[128]{0:T(128)} %end_any.3, bf16[32,16,8192]{2,1,0:T(8,128)(2,1)} %field_any.3, f32[16,8192]{1,0:T(8,128)} %jitter_any.3), custom_call_target="tpu_custom_call" | custom-call | flops 31457280 | bytes 3145728 | tf_op jit(solution)/shard_map/open/pallas_call | solution.py:293
  20.1 0.0 copy-start
  20.1 0.0 copy-start.1
  20.1 13.3 %close.1 = s16[16,4,16,512]{3,2,1,0:T(8,128)(2,1)} custom-call(f32[4]{0:T(128)} %transfer_any.5, s32[128]{0:T(128)} %start_any.3, s32[128]{0:T(128)} %end_any.3, bf16[32,16,8192]{2,1,0:T(8,128)(2,1)} %field_any.3, bf16[2,16,8192]{2,1,0:T(8,128)(2,1)} %all_gather.6.even_any, bf16[2,16,8192]{2,1,0:T(8,128)(2,1)} %all_gather.7.odd_any, f32[16,8192]{1,0:T(8,128)} %jitter_any.3, ...), custom_call_target="tpu_custom_call" | custom-call | flops 52428800 | bytes 5242880 | tf_op jit(solution)/shard_map/close/pallas_call | solution.py:312
  33.5 30.8 %all_to_all.5.code_any = s16[16,4,16,512]{3,2,1,0:T(8,128)(2,1)S(1)} all-to-all(s16[16,4,16,512]{3,2,1,0:T(8,128)(2,1)} %close.1), channel_id=1, replica_groups=mesh['groups'=2,'depth'=16] {'depth'}, dimensions={0} | all-to-all | bytes 2097152 | tf_op jit(solution)/shard_map/all_to_all | solution.py:413
  64.2 0.0 copy-done
  64.2 0.0 copy-done.1
  64.2 1.8 %composite.1 = f32[4,16,512]{2,1,0:T(8,128)} custom-call(s32[16]{0:T(128)S(1)} %copy-done.1, f32[4]{0:T(128)S(1)} %copy-done, s16[16,4,16,512]{3,2,1,0:T(8,128)(2,1)S(1)} %all_to_all.5.code_any), custom_call_target="tpu_custom_call" | custom-call | tf_op jit(solution)/shard_map/composite/pallas_call | solution.py:386
Async XLA Ops:
  20.1 44.1 %copy-start = (f32[4]{0:T(128)S(1)}, f32[4]{0:T(128)}, u32[]{:S(2)}) copy-start(f32[4]{0:T(128)} %transfer_any.5) | copy-start | bytes 52
  20.1 44.1 %copy-start.1 = (s32[16]{0:T(128)S(1)}, s32[16]{0:T(128)}, u32[]{:S(2)}) copy-start(s32[16]{0:T(128)} %order_any.1) | copy-start | bytes 196

commit v14 on v12

--- a/solution.py
+++ b/solution.py
@@ -58,20 +58,21 @@
         return carry
 
     blocks = gain_ref.shape[1] // LANES
-    lax.fori_loop(0, blocks, block, 0, unroll=math.gcd(blocks, 4))
-
-
-def moment(sums, emitted, value, levels):
+    lax.fori_loop(0, blocks, block, 0, unroll=math.gcd(blocks, 8))
+
+
+def moment(sums, weight, value, levels):
     whole = (levels[0] + value) * (levels[1] + value) * (levels[2] + value)
-    share = emitted * pl.reciprocal(whole, approx=True, full_range=False)
+    share = weight * pl.reciprocal(whole, approx=True, full_range=False)
     for n in range(3):
         sums[n] = sums[n] + share
         share = share * value
 
 
-def colors(sums, levels):
+def colors(sums, before, levels):
+    emitted = 1.0 - jnp.exp2(before)
     others = [(levels[1], levels[2]), (levels[2], levels[0]), (levels[0], levels[1])]
-    return [sums[2] + (p + q) * sums[1] + (p * q) * sums[0] for p, q in others]
+    return [emitted - t * (sums[2] + (p + q) * sums[1] + (p * q) * sums[0]) for t, (p, q) in zip(levels, others)]
 
 
 def march(gain_ref, plane_ref, unit, cols, place, jitter, levels, halo=None):
@@ -89,7 +90,7 @@
         value = stay + moved
         before = before + gain_ref[k:k + 1, place] * value
         beyond = jnp.exp2(before)
-        moment(sums, (through - beyond) * value, value, levels)
+        moment(sums, through - beyond, value, levels)
         through = beyond
         stay = upper - moved
     return sums, before
@@ -217,7 +218,7 @@
     tile_gains(gain_ref, gain, base, tile_cols, start_ref, end_ref, place.block_column)
 
     def coded(sums, before):
-        codes = [encode(color * color_unit[i], color_span) for i, color in enumerate(colors(sums, levels))]
+        codes = [encode(color * color_unit[i], color_span) for i, color in enumerate(colors(sums, before, levels))]
         return codes + [encode(before * (depth_unit * (-1.0 / LOG2E)), depth_span)]
 
     def arrive(unit):
@@ -251,9 +252,9 @@
         value = (1.0 - jitter) * lower + jitter * upper
         before = state_ref[unit, 3, :, cols]
         beyond = before + last_gain_ref[0:1, table] * value
-        emitted = (jnp.exp2(before) - jnp.exp2(beyond)) * value
+        weight = jnp.exp2(before) - jnp.exp2(beyond)
         sums = [state_ref[unit, i, :, cols] for i in range(3)]
-        moment(sums, emitted, value, levels)
+        moment(sums, weight, value, levels)
         return coded(sums, beyond)
 
     each_block(opened, arrive_opened, finish, functools.partial(store, 0), lambda unit: leave(unit).start())

time: 55.5 us -> 55.1 us (level)
  no operation moved by 1% of the time
where the time goes in v14:
time: 55.1 us; the launch traced here: 54.5 us
  blocking collectives  33 us (60%)
  Pallas kernels  19.1 us (35%)
  starting transfers between devices  1.29 us (2%)
  local copies, waits for them, and re-layouts  1.05 us (2%)
    all_to_all x1, blocking collectives, on_device(): lax.all_to_all(codes, 'depth', split_axis=0, concat_axis=0, tiled=True)  33 us
    pallas_call x1, Pallas kernels, slab_codes(): pl.pallas_call(functools.partial(close_kernel, total, tile_cols, opened,...  10.9 us
    pallas_call x1, Pallas kernels, slab_codes(): pl.pallas_call(functools.partial(open_kernel, total, tile_cols, Units(0))...  6.39 us
    pallas_call x1, Pallas kernels, composite(): pl.pallas_call(functools.partial(composite_kernel, total, slab_len), in_s...  1.82 us
    ppermute x1, starting transfers between devices, shifted(): lax.ppermute(value, axis, [(source, source + steps) for source in range(i...  1.29 us
  transfers between devices with their start and end apart: 1, of which 0 were waited for; matrix products, arithmetic and copies ran while one was open for 0% of the time, Pallas kernels for 12%

profile of v14, /device:TPU:0, one launch (start us, length us, event | category | flops | bytes accessed | tf_op | source)
XLA Modules:
  0.0 54.5 jit_solution(11027903671792047097)
XLA Ops:
  0.0 0.0 copy-start.1
  0.0 0.0 copy-start.3
  0.0 0.0 copy-start.2
  0.0 0.0 copy-start
  0.0 1.0 %slice_bitcast_fusion = bf16[16,8192]{1,0:T(8,128)(2,1)S(1)} fusion(bf16[32,16,8192]{2,1,0:T(8,128)(2,1)} %field_any.3), kind=kLoop, calls=%fused_computation | loop fusion | bytes 524288 | tf_op jit(solution)/shard_map/squeeze | solution.py:393
  1.0 1.3 %collective-permute-start = (bf16[16,8192]{1,0:T(8,128)(2,1)S(1)}, bf16[16,8192]{1,0:T(8,128)(2,1)S(1)}, u32[]{:S(2)}, u32[]{:S(2)}) collective-permute-start(bf16[16,8192]{1,0:T(8,128)(2,1)S(1)} %slice_bitcast_fusion), channel_id=1, source_target_pairs={{1,0},{2,1},{3,2},{4,3},{5,4},{6,5},{7,6},{8,7},{9,8},{10,9},{11,1... | collective-permute-start | bytes 786440 | tf_op jit(solution)/shard_map/ppermute | solution.py:34
  2.3 6.4 %open.1.state_any = f32[6,4,16,512]{3,2,1,0:T(8,128)} custom-call(f32[4]{0:T(128)} %transfer_any.5, s32[128]{0:T(128)} %start_any.3, s32[128]{0:T(128)} %end_any.3, bf16[32,16,8192]{2,1,0:T(8,128)(2,1)} %field_any.3, f32[16,8192]{1,0:T(8,128)} %jitter_any.3), custom_call_target="tpu_custom_call" | custom-call | flops 31457280 | bytes 3145728 | tf_op jit(solution)/shard_map/open/pallas_call | solution.py:278
  8.7 0.0 copy-start.4
  8.7 0.0 collective-permute-done.halo_any
  8.8 0.0 copy-done.1
  8.8 0.0 copy-done.3
  8.8 0.0 copy-done.2
  8.8 0.0 copy-done
  8.8 10.9 %close.1 = s16[16,4,16,512]{3,2,1,0:T(8,128)(2,1)} custom-call(f32[4]{0:T(128)S(1)} %copy-done.1, s32[128]{0:T(128)S(1)} %copy-done.2, s32[128]{0:T(128)S(1)} %copy-done.3, bf16[32,16,8192]{2,1,0:T(8,128)(2,1)} %field_any.3, bf16[16,8192]{1,0:T(8,128)(2,1)S(1)} %collective-permute-done.halo_any, f32[16,8192]{1,0:T(8,128)S(1)} %copy-done, ...), custom_call_target="tpu_custom_call" | custom-call | flops 52428800 | bytes 5242880 | tf_op jit(solution)/shard_map/close/pallas_call | solution.py:297
  19.7 33.0 %all_to_all.5.code_any = s16[16,4,16,512]{3,2,1,0:T(8,128)(2,1)S(1)} all-to-all(s16[16,4,16,512]{3,2,1,0:T(8,128)(2,1)} %close.1), channel_id=1, replica_groups=mesh['groups'=2,'depth'=16] {'depth'}, dimensions={0} | all-to-all | bytes 2097152 | tf_op jit(solution)/shard_map/all_to_all | solution.py:397
  52.7 0.0 copy-done.4
  52.7 1.8 %composite.1 = f32[4,16,512]{2,1,0:T(8,128)} custom-call(s32[16]{0:T(128)S(1)} %copy-done.4, f32[4]{0:T(128)S(1)} %copy-done.1, s16[16,4,16,512]{3,2,1,0:T(8,128)(2,1)S(1)} %all_to_all.5.code_any), custom_call_target="tpu_custom_call" | custom-call | tf_op jit(solution)/shard_map/composite/pallas_call | solution.py:370
Async XLA Ops:
  0.0 8.8 %copy-start.1 = (f32[4]{0:T(128)S(1)}, f32[4]{0:T(128)}, u32[]{:S(2)}) copy-start(f32[4]{0:T(128)} %transfer_any.5) | copy-start | bytes 52
  0.0 8.8 %copy-start.3 = (s32[128]{0:T(128)S(1)}, s32[128]{0:T(128)}, u32[]{:S(2)}) copy-start(s32[128]{0:T(128)} %end_any.3) | copy-start | bytes 1540
  0.0 8.8 %copy-start.2 = (s32[128]{0:T(128)S(1)}, s32[128]{0:T(128)}, u32[]{:S(2)}) copy-start(s32[128]{0:T(128)} %start_any.3) | copy-start | bytes 1540
  0.0 8.8 %copy-start = (f32[16,8192]{1,0:T(8,128)S(1)}, f32[16,8192]{1,0:T(8,128)}, u32[]{:S(2)}) copy-start(f32[16,8192]{1,0:T(8,128)} %jitter_any.3) | copy-start | bytes 1572868
  1.0 7.7 %collective-permute-start = (bf16[16,8192]{1,0:T(8,128)(2,1)S(1)}, bf16[16,8192]{1,0:T(8,128)(2,1)S(1)}, u32[]{:S(2)}, u32[]{:S(2)}) collective-permute-start(bf16[16,8192]{1,0:T(8,128)(2,1)S(1)} %slice_bitcast_fusion), channel_id=1, source_target_pairs={{1,0},{2,1},{3,2},{4,3},{5,4},{6,5},{7,6},{8,7},{9,8},{10,9},{11,1... | collective-permute-start | bytes 786440 | tf_op jit(solution)/shard_map/ppermute | solution.py:34
  8.7 43.9 %copy-start.4 = (s32[16]{0:T(128)S(1)}, s32[16]{0:T(128)}, u32[]{:S(2)}) copy-start(s32[16]{0:T(128)} %order_any.1) | copy-start | bytes 196

commit v15 on v14

--- a/solution.py
+++ b/solution.py
@@ -40,12 +40,12 @@
     return (code.astype(jnp.int32) - 32768).astype(jnp.int16)
 
 
-def tile_gains(gain_ref, gain, base, tile_cols, start_ref, end_ref, col_of):
+def tile_gains(gain_ref, gain, base, first_col, tile_cols, start_ref, end_ref):
     sample = lax.broadcasted_iota(jnp.int32, (SUBLANES, LANES), 0) + base
     lane = lax.broadcasted_iota(jnp.int32, (SUBLANES, LANES), 1)
 
     def block(n, carry):
-        tile = col_of(n) // tile_cols
+        tile = (first_col + n * LANES) // tile_cols
         start = jnp.full((SUBLANES, LANES), start_ref[tile])
         end = jnp.full((SUBLANES, LANES), end_ref[tile])
         for t in range(1, LANES // tile_cols):
@@ -104,32 +104,16 @@
     lax.fori_loop(0, count, step, 0)
 
 
-def each_block(units, arrive, compute, store, leave):
-    def pair(n):
+def each_pair(units, arrive, compute, store, leave):
+    def step(n):
         places = [(2 * n + u, c) for u in range(2) for c in range(0, UNIT, LANES)]
-        for u in range(2):
-            arrive(2 * n + u)
+        arrive(n)
         results = [compute(unit, pl.ds(c, LANES), pl.ds(pl.multiple_of(unit * UNIT + c, LANES), LANES)) for unit, c in places]
         for (unit, c), result in zip(places, results):
             store(unit, pl.ds(c, LANES), result)
-        for u in range(2):
-            leave(2 * n + u)
-
-    loop(units // 2, pair)
-
-
-class Units:
-    def __init__(self, first):
-        self.first = first
-
-    def column(self, unit):
-        return (self.first + unit) * UNIT
-
-    def columns(self, unit):
-        return pl.ds(pl.multiple_of(self.column(unit), LANES), UNIT)
-
-    def block_column(self, n):
-        return self.column(n // (UNIT // LANES)) + n % (UNIT // LANES) * LANES
+        leave(n)
+
+    loop(units // 2, step)
 
 
 def start_all(pairs, sems):
@@ -139,74 +123,64 @@
     return copies
 
 
-def unit_copies(place, field_any, jitter_any, plane_ref, jitter_ref, sems, unit):
-    cols = place.columns(unit)
-    return [
-        pltpu.make_async_copy(jitter_any.at[:, cols], jitter_ref.at[unit], sems.at[0, unit]),
-        pltpu.make_async_copy(field_any.at[:, :, cols], plane_ref.at[unit], sems.at[1, unit]),
-    ]
-
-
-def open_kernel(total, tile_cols, place, transfer_any, start_any, end_any, field_any, jitter_any, state_any, transfer_ref,
-                start_ref, end_ref, plane_ref, jitter_ref, state_ref, gain_ref, few_sems, sems, out_sems):
+def field_copy(field_any, plane_ref, sems, first, unit):
+    cols = pl.ds(pl.multiple_of((first + unit) * UNIT, UNIT), UNIT)
+    return pltpu.make_async_copy(field_any.at[:, :, cols], plane_ref.at[unit], sems.at[unit])
+
+
+def open_kernel(total, tile_cols, transfer_any, start_any, end_any, field_any, jitter_any, state_any, transfer_ref, start_ref,
+                end_ref, plane_ref, jitter_ref, state_ref, gain_ref, few_sems, sems, out_sems):
     units, slab_len, rows, _ = plane_ref.shape
-    early = start_all([(transfer_any, transfer_ref), (start_any, start_ref), (end_any, end_ref)], few_sems)
-    arrivals = functools.partial(unit_copies, place, field_any, jitter_any, plane_ref, jitter_ref, sems)
-    for unit in range(units):
-        for copy in arrivals(unit):
-            copy.start()
+    arrival = functools.partial(field_copy, field_any, plane_ref, sems, 0)
+    for unit in range(2):
+        arrival(unit).start()
+    pairs = [(transfer_any, transfer_ref), (start_any, start_ref), (end_any, end_ref)]
+    pairs.append((jitter_any.at[:, pl.ds(0, units * UNIT)], jitter_ref))
+    *early, jitter_copy = start_all(pairs, few_sems)
     base = lax.axis_index("depth") * slab_len
     for copy in early:
         copy.wait()
     levels = [jnp.full((rows, LANES), transfer_ref[i]) for i in range(3)]
     gain = jnp.full((SUBLANES, LANES), transfer_ref[3]) * (-LOG2E * 0.2 / total)
-    tile_gains(gain_ref, gain, base, tile_cols, start_ref, end_ref, place.block_column)
-
-    def arrive(unit):
-        for copy in arrivals(unit):
-            copy.wait()
-
-    def compute(unit, cols, table):
-        return march(gain_ref, plane_ref, unit, cols, table, jitter_ref[unit, :, cols], levels)
+    for unit in range(2, units):
+        arrival(unit).start()
+    tile_gains(gain_ref, gain, base, 0, tile_cols, start_ref, end_ref)
+    jitter_copy.wait()
+
+    def arrive(n):
+        for u in range(2):
+            arrival(2 * n + u).wait()
+
+    def compute(unit, cols, place):
+        return march(gain_ref, plane_ref, unit, cols, place, jitter_ref[:, place], levels)
 
     def store(unit, cols, result):
         sums, before = result
         for i, value in enumerate([*sums, before]):
             state_ref[unit, i, :, cols] = value
 
-    def leave(unit):
-        return pltpu.make_async_copy(state_ref.at[unit], state_any.at[unit], out_sems.at[unit])
-
-    each_block(units, arrive, compute, store, lambda unit: leave(unit).start())
-    loop(units, lambda unit: leave(unit).wait())
-
-
-def close_kernel(total, tile_cols, opened, place, transfer_any, start_any, end_any, field_any, halo_any, jitter_any, state_any,
-                 out_any, transfer_ref, start_ref, end_ref, plane_ref, halo_ref, jitter_ref, out_ref, gain_ref, few_sems, sems,
-                 out_sems, state_ref, last_ref, last_jitter_ref, last_gain_ref, state_sems):
-    before_units = Units(0)
+    def leave(n):
+        place = pl.ds(2 * n, 2)
+        return pltpu.make_async_copy(state_ref.at[place], state_any.at[place], out_sems.at[n])
+
+    each_pair(units, arrive, compute, store, lambda n: leave(n).start())
+    loop(units // 2, lambda n: leave(n).wait())
+
+
+def close_kernel(total, tile_cols, opened, transfer_any, start_any, end_any, field_any, halo_any, jitter_any, state_any,
+                 out_any, transfer_ref, start_ref, end_ref, plane_ref, halo_ref, jitter_ref, out_ref, gain_ref, state_ref,
+                 last_ref, last_gain_ref, few_sems, sems, out_sems):
     units, slab_len, rows, _ = plane_ref.shape
-    few = [(transfer_any, transfer_ref), (start_any, start_ref), (end_any, end_ref), (halo_any, halo_ref)]
-    early = start_all(few, few_sems)
-    arrivals = functools.partial(unit_copies, place, field_any, jitter_any, plane_ref, jitter_ref, sems)
-    for unit in range(units):
-        for copy in arrivals(unit):
-            copy.start()
-
-    def opened_copies(unit):
-        cols = before_units.columns(unit)
-        pairs = [
-            (field_any.at[slab_len - 1, :, cols], last_ref.at[unit]),
-            (jitter_any.at[:, cols], last_jitter_ref.at[unit]),
-            (state_any.at[unit], state_ref.at[unit]),
-        ]
-        return [pltpu.make_async_copy(src, dst, state_sems.at[n, unit]) for n, (src, dst) in enumerate(pairs)]
-
-    for unit in range(opened):
-        for copy in opened_copies(unit):
-            copy.start()
+    opened_cols = opened * UNIT
+    arrival = functools.partial(field_copy, field_any, plane_ref, sems, opened)
+    for unit in range(2):
+        arrival(unit).start()
+    pairs = [(transfer_any, transfer_ref), (start_any, start_ref), (end_any, end_ref), (jitter_any, jitter_ref)]
+    pairs += [(halo_any, halo_ref), (state_any, state_ref)]
+    pairs.append((field_any.at[slab_len - 1, :, pl.ds(0, opened_cols)], last_ref))
+    copies = start_all(pairs, few_sems)
     base = lax.axis_index("depth") * slab_len
-    for copy in early:
+    for copy in copies[:3]:
         copy.wait()
     shape = (rows, LANES)
     depth_gain = jnp.full(shape, transfer_ref[3]) * (0.2 / total)
@@ -215,50 +189,51 @@
     color_unit = [depth_unit * ((levels[i] + TOP) * (1.0 / TOP)) for i in range(3)]
     depth_span, color_span = spans(slab_len)
     gain = depth_gain[:SUBLANES] * -LOG2E
-    tile_gains(gain_ref, gain, base, tile_cols, start_ref, end_ref, place.block_column)
+    for unit in range(2, units):
+        arrival(unit).start()
+    tile_gains(gain_ref, gain, base, opened_cols, tile_cols, start_ref, end_ref)
+    tile_gains(last_gain_ref, gain, base + slab_len - 1, 0, tile_cols, start_ref, end_ref)
+    for copy in copies[3:5]:
+        copy.wait()
 
     def coded(sums, before):
         codes = [encode(color * color_unit[i], color_span) for i, color in enumerate(colors(sums, before, levels))]
         return codes + [encode(before * (depth_unit * (-1.0 / LOG2E)), depth_span)]
 
-    def arrive(unit):
-        for copy in arrivals(unit):
-            copy.wait()
-
-    def compute(unit, cols, table):
-        whole = pl.ds(pl.multiple_of(place.column(unit) + cols.start, LANES), LANES)
-        jitter = jitter_ref[unit, :, cols]
-        return coded(*march(gain_ref, plane_ref, unit, cols, table, jitter, levels, halo_ref[:, whole]))
+    def arrive(n):
+        for u in range(2):
+            arrival(2 * n + u).wait()
+
+    def compute(unit, cols, place):
+        whole = pl.ds(pl.multiple_of(opened_cols + place.start, LANES), LANES)
+        return coded(*march(gain_ref, plane_ref, unit, cols, place, jitter_ref[:, whole], levels, halo_ref[:, whole]))
 
     def store(first, unit, cols, codes):
         for i, code in enumerate(codes):
             out_ref[first + unit, i, :, cols] = code
 
-    def leave(piece):
-        return pltpu.make_async_copy(out_ref.at[piece], out_any.at[piece], out_sems.at[piece])
-
-    each_block(units, arrive, compute, functools.partial(store, place.first), lambda unit: leave(place.first + unit).start())
-    tile_gains(last_gain_ref, gain, base + slab_len - 1, tile_cols, start_ref, end_ref, before_units.block_column)
-
-    def arrive_opened(unit):
-        for copy in opened_copies(unit):
-            copy.wait()
-
-    def finish(unit, cols, table):
-        whole = pl.ds(pl.multiple_of(before_units.column(unit) + cols.start, LANES), LANES)
-        jitter = last_jitter_ref[unit, :, cols]
-        lower = last_ref[unit, :, cols].astype(jnp.float32)
-        upper = halo_ref[:, whole].astype(jnp.float32)
+    def leave(n):
+        place = pl.ds(2 * n, 2)
+        return pltpu.make_async_copy(out_ref.at[place], out_any.at[place], out_sems.at[n])
+
+    each_pair(units, arrive, compute, functools.partial(store, opened), lambda n: leave(opened // 2 + n).start())
+    for copy in copies[5:]:
+        copy.wait()
+
+    def finish(unit, cols, place):
+        jitter = jitter_ref[:, place]
+        lower = last_ref[:, place].astype(jnp.float32)
+        upper = halo_ref[:, place].astype(jnp.float32)
         value = (1.0 - jitter) * lower + jitter * upper
         before = state_ref[unit, 3, :, cols]
-        beyond = before + last_gain_ref[0:1, table] * value
+        beyond = before + last_gain_ref[0:1, place] * value
         weight = jnp.exp2(before) - jnp.exp2(beyond)
         sums = [state_ref[unit, i, :, cols] for i in range(3)]
         moment(sums, weight, value, levels)
         return coded(sums, beyond)
 
-    each_block(opened, arrive_opened, finish, functools.partial(store, 0), lambda unit: leave(unit).start())
-    loop(out_ref.shape[0], lambda piece: leave(piece).wait())
+    each_pair(opened, lambda n: None, finish, functools.partial(store, 0), lambda n: leave(n).start())
+    loop(out_ref.shape[0] // 2, lambda n: leave(n).wait())
 
 
 def slab_codes(field, halo, jitter, transfer, ray_start, ray_end, total):
@@ -276,18 +251,18 @@
         return pl.CostEstimate(flops=work * 20, bytes_accessed=work * 2, transcendentals=work * 2)
 
     state = pl.pallas_call(
-        functools.partial(open_kernel, total, tile_cols, Units(0)),
+        functools.partial(open_kernel, total, tile_cols),
         in_specs=[own] * 5,
         out_specs=own,
         out_shape=jax.ShapeDtypeStruct((opened, 4, rows, UNIT), jnp.float32),
         scratch_shapes=scalars + [
             pltpu.VMEM((opened, slab_len, rows, UNIT), field.dtype),
-            pltpu.VMEM((opened, rows, UNIT), jnp.float32),
+            pltpu.VMEM((rows, opened * UNIT), jnp.float32),
             pltpu.VMEM((opened, 4, rows, UNIT), jnp.float32),
             pltpu.VMEM((slab_len, opened * UNIT), jnp.float32),
-            pltpu.SemaphoreType.DMA((3,)),
-            pltpu.SemaphoreType.DMA((2, opened)),
+            pltpu.SemaphoreType.DMA((4,)),
             pltpu.SemaphoreType.DMA((opened,)),
+            pltpu.SemaphoreType.DMA((opened // 2,)),
         ],
         compiler_params=pltpu.CompilerParams(vmem_limit_bytes=OPEN_BYTES),
         cost_estimate=cost(opened),
@@ -295,24 +270,22 @@
     )(transfer, ray_start, ray_end, field, jitter)
 
     return pl.pallas_call(
-        functools.partial(close_kernel, total, tile_cols, opened, Units(opened)),
+        functools.partial(close_kernel, total, tile_cols, opened),
         in_specs=[own] * 7,
         out_specs=own,
         out_shape=jax.ShapeDtypeStruct((pieces, 4, rows, UNIT), jnp.int16),
         scratch_shapes=scalars + [
             pltpu.VMEM((closed, slab_len, rows, UNIT), field.dtype),
             pltpu.VMEM((rows, cols), field.dtype),
-            pltpu.VMEM((closed, rows, UNIT), jnp.float32),
+            pltpu.VMEM((rows, cols), jnp.float32),
             pltpu.VMEM((pieces, 4, rows, UNIT), jnp.int16),
             pltpu.VMEM((slab_len, closed * UNIT), jnp.float32),
-            pltpu.SemaphoreType.DMA((4,)),
-            pltpu.SemaphoreType.DMA((2, closed)),
-            pltpu.SemaphoreType.DMA((pieces,)),
             pltpu.VMEM((opened, 4, rows, UNIT), jnp.float32),
-            pltpu.VMEM((opened, rows, UNIT), field.dtype),
-            pltpu.VMEM((opened, rows, UNIT), jnp.float32),
+            pltpu.VMEM((rows, opened * UNIT), field.dtype),
             pltpu.VMEM((SUBLANES, opened * UNIT), jnp.float32),
-            pltpu.SemaphoreType.DMA((3, opened)),
+            pltpu.SemaphoreType.DMA((7,)),
+            pltpu.SemaphoreType.DMA((closed,)),
+            pltpu.SemaphoreType.DMA((pieces // 2,)),
         ],
         compiler_params=pltpu.CompilerParams(vmem_limit_bytes=CLOSE_BYTES),
         cost_estimate=cost(closed),

time: 55.1 us -> 54.2 us (0.984)
  Pallas kernels: 19.1 us -> 18.2 us
    pallas_call x2, Pallas kernels: 17.3 us -> 16.4 us  [the longest x1 10.1 us: slab_codes(): pl.pallas_call(functools.partial(close_kernel, total, tile_cols, opened),...]
where the time goes in v15:
time: 54.2 us; the launch traced here: 53.7 us
  blocking collectives  33 us (61%)
  Pallas kernels  18.2 us (34%)
  starting transfers between devices  1.29 us (2%)
  local copies, waits for them, and re-layouts  1.05 us (2%)
    all_to_all x1, blocking collectives, on_device(): lax.all_to_all(codes, 'depth', split_axis=0, concat_axis=0, tiled=True)  33 us
    pallas_call x1, Pallas kernels, slab_codes(): pl.pallas_call(functools.partial(close_kernel, total, tile_cols, opened),...  10.1 us
    pallas_call x1, Pallas kernels, slab_codes(): pl.pallas_call(functools.partial(open_kernel, total, tile_cols), in_specs...  6.3 us
    pallas_call x1, Pallas kernels, composite(): pl.pallas_call(functools.partial(composite_kernel, total, slab_len), in_s...  1.82 us
    ppermute x1, starting transfers between devices, shifted(): lax.ppermute(value, axis, [(source, source + steps) for source in range(i...  1.29 us
  transfers between devices with their start and end apart: 1, of which 0 were waited for; matrix products, arithmetic and copies ran while one was open for 0% of the time, Pallas kernels for 12%

profile of v15, /device:TPU:0, one launch (start us, length us, event | category | flops | bytes accessed | tf_op | source)
XLA Modules:
  0.0 53.7 jit_solution(2243163236212481382)
XLA Ops:
  0.0 0.0 copy-start.1
  0.0 0.0 copy-start.3
  0.0 0.0 copy-start.2
  0.0 0.0 copy-start
  0.0 1.0 %slice_bitcast_fusion = bf16[16,8192]{1,0:T(8,128)(2,1)S(1)} fusion(bf16[32,16,8192]{2,1,0:T(8,128)(2,1)} %field_any.3), kind=kLoop, calls=%fused_computation | loop fusion | bytes 524288 | tf_op jit(solution)/shard_map/squeeze | solution.py:366
  1.0 1.3 %collective-permute-start = (bf16[16,8192]{1,0:T(8,128)(2,1)S(1)}, bf16[16,8192]{1,0:T(8,128)(2,1)S(1)}, u32[]{:S(2)}, u32[]{:S(2)}) collective-permute-start(bf16[16,8192]{1,0:T(8,128)(2,1)S(1)} %slice_bitcast_fusion), channel_id=1, source_target_pairs={{1,0},{2,1},{3,2},{4,3},{5,4},{6,5},{7,6},{8,7},{9,8},{10,9},{11,1... | collective-permute-start | bytes 786440 | tf_op jit(solution)/shard_map/ppermute | solution.py:34
  2.3 6.3 %open.1.state_any = f32[6,4,16,512]{3,2,1,0:T(8,128)} custom-call(f32[4]{0:T(128)} %transfer_any.5, s32[128]{0:T(128)} %start_any.3, s32[128]{0:T(128)} %end_any.3, bf16[32,16,8192]{2,1,0:T(8,128)(2,1)} %field_any.3, f32[16,8192]{1,0:T(8,128)} %jitter_any.3), custom_call_target="tpu_custom_call" | custom-call | flops 31457280 | bytes 3145728 | tf_op jit(solution)/shard_map/open/pallas_call | solution.py:253
  8.6 0.0 copy-start.4
  8.7 0.0 collective-permute-done.halo_any
  8.7 0.0 copy-done.1
  8.7 0.0 copy-done.3
  8.7 0.0 copy-done.2
  8.7 0.0 copy-done
  8.7 10.1 %close.1 = s16[16,4,16,512]{3,2,1,0:T(8,128)(2,1)} custom-call(f32[4]{0:T(128)S(1)} %copy-done.1, s32[128]{0:T(128)S(1)} %copy-done.2, s32[128]{0:T(128)S(1)} %copy-done.3, bf16[32,16,8192]{2,1,0:T(8,128)(2,1)} %field_any.3, bf16[16,8192]{1,0:T(8,128)(2,1)S(1)} %collective-permute-done.halo_any, f32[16,8192]{1,0:T(8,128)S(1)} %copy-done, ...), custom_call_target="tpu_custom_call" | custom-call | flops 52428800 | bytes 5242880 | tf_op jit(solution)/shard_map/close/pallas_call | solution.py:272
  18.8 33.0 %all_to_all.5.code_any = s16[16,4,16,512]{3,2,1,0:T(8,128)(2,1)S(1)} all-to-all(s16[16,4,16,512]{3,2,1,0:T(8,128)(2,1)} %close.1), channel_id=1, replica_groups=mesh['groups'=2,'depth'=16] {'depth'}, dimensions={0} | all-to-all | bytes 2097152 | tf_op jit(solution)/shard_map/all_to_all | solution.py:370
  51.9 0.0 copy-done.4
  51.9 1.8 %composite.1 = f32[4,16,512]{2,1,0:T(8,128)} custom-call(s32[16]{0:T(128)S(1)} %copy-done.4, f32[4]{0:T(128)S(1)} %copy-done.1, s16[16,4,16,512]{3,2,1,0:T(8,128)(2,1)S(1)} %all_to_all.5.code_any), custom_call_target="tpu_custom_call" | custom-call | tf_op jit(solution)/shard_map/composite/pallas_call | solution.py:343
Async XLA Ops:
  0.0 8.7 %copy-start.1 = (f32[4]{0:T(128)S(1)}, f32[4]{0:T(128)}, u32[]{:S(2)}) copy-start(f32[4]{0:T(128)} %transfer_any.5) | copy-start | bytes 52
  0.0 8.7 %copy-start.3 = (s32[128]{0:T(128)S(1)}, s32[128]{0:T(128)}, u32[]{:S(2)}) copy-start(s32[128]{0:T(128)} %end_any.3) | copy-start | bytes 1540
  0.0 8.7 %copy-start.2 = (s32[128]{0:T(128)S(1)}, s32[128]{0:T(128)}, u32[]{:S(2)}) copy-start(s32[128]{0:T(128)} %start_any.3) | copy-start | bytes 1540
  0.0 8.7 %copy-start = (f32[16,8192]{1,0:T(8,128)S(1)}, f32[16,8192]{1,0:T(8,128)}, u32[]{:S(2)}) copy-start(f32[16,8192]{1,0:T(8,128)} %jitter_any.3) | copy-start | bytes 1572868
  1.0 7.6 %collective-permute-start = (bf16[16,8192]{1,0:T(8,128)(2,1)S(1)}, bf16[16,8192]{1,0:T(8,128)(2,1)S(1)}, u32[]{:S(2)}, u32[]{:S(2)}) collective-permute-start(bf16[16,8192]{1,0:T(8,128)(2,1)S(1)} %slice_bitcast_fusion), channel_id=1, source_target_pairs={{1,0},{2,1},{3,2},{4,3},{5,4},{6,5},{7,6},{8,7},{9,8},{10,9},{11,1... | collective-permute-start | bytes 786440 | tf_op jit(solution)/shard_map/ppermute | solution.py:34
  8.6 43.2 %copy-start.4 = (s32[16]{0:T(128)S(1)}, s32[16]{0:T(128)}, u32[]{:S(2)}) copy-start(s32[16]{0:T(128)} %order_any.1) | copy-start | bytes 196

commit v16 on v15

v16 whole, which is shorter than its diff:
```python
import functools
import math

import jax
import jax.numpy as jnp
from jax import lax
from jax.experimental import pallas as pl
from jax.experimental.pallas import tpu as pltpu
from jax.sharding import PartitionSpec as P

TOP = 5.2
LOG2E = math.log2(math.e)
SUBLANES = 8
LANES = 128
FAR = 1.0e4
UNIT = 512
NEAR = 8
OPEN_BYTES = 54 * 1024 * 1024
CLOSE_BYTES = 53 * 1024 * 1024
SMALL_BYTES = 16 * 1024 * 1024


def spans(slab_len):
    deep = math.log2(slab_len)
    return 6.8 + deep, 13.2 + deep


def lift(span):
    return span * (32768.0 / 65535.0) - span


def shifted(value, axis, steps):
    count = lax.axis_size(axis)
    initial, last = (max(0, -steps), min(count, count - steps))
    return lax.ppermute(value, axis, [(source, source + steps) for source in range(initial, last)])


def encode(value, span):
    code = jnp.log2(value) * (65535.0 / span) + 65535.5
    code = jnp.minimum(jnp.maximum(code, 0.0), 65535.0)
    return (code.astype(jnp.int32) - 32768).astype(jnp.int16)


def tile_gains(gain_ref, gain, base, tile_cols, start_ref, end_ref, piece_of):
    sample = lax.broadcasted_iota(jnp.int32, (SUBLANES, LANES), 0) + base
    lane = lax.broadcasted_iota(jnp.int32, (SUBLANES, LANES), 1)

    def block(n, carry):
        blocks = UNIT // LANES
        tile = (piece_of(n // blocks) * UNIT + n % blocks * LANES) // tile_cols
        start = jnp.full((SUBLANES, LANES), start_ref[tile])
        end = jnp.full((SUBLANES, LANES), end_ref[tile])
        for t in range(1, LANES // tile_cols):
            start = jnp.where(lane >= t * tile_cols, start_ref[tile + t], start)
            end = jnp.where(lane >= t * tile_cols, end_ref[tile + t], end)
        cols = pl.ds(pl.multiple_of(n * LANES, LANES), LANES)
        for k in range(0, gain_ref.shape[0], SUBLANES):
            active = (sample + k >= start) & (sample + k < end)
            gain_ref[k:k + SUBLANES, cols] = jnp.where(active, gain, 0.0)
        return carry

    blocks = gain_ref.shape[1] // LANES
    lax.fori_loop(0, blocks, block, 0, unroll=math.gcd(blocks, 8))


def moment(sums, weight, value, levels):
    whole = (levels[0] + value) * (levels[1] + value) * (levels[2] + value)
    share = weight * pl.reciprocal(whole, approx=True, full_range=False)
    for n in range(3):
        sums[n] = sums[n] + share
        share = share * value


def colors(sums, before, levels):
    emitted = 1.0 - jnp.exp2(before)
    others = [(levels[1], levels[2]), (levels[2], levels[0]), (levels[0], levels[1])]
    return [emitted - t * (sums[2] + (p + q) * sums[1] + (p * q) * sums[0]) for t, (p, q) in zip(levels, others)]


def march(gain_ref, plane_ref, unit, cols, place, jitter, levels, halo=None):
    slab_len = plane_ref.shape[1]
    shape = jitter.shape
    before = jnp.zeros(shape, jnp.float32)
    through = jnp.ones(shape, jnp.float32)
    sums = [jnp.zeros(shape, jnp.float32) for _ in range(3)]
    lower = plane_ref[unit, 0, :, cols].astype(jnp.float32)
    stay = lower - jitter * lower
    for k in range(slab_len - (halo is None)):
        following = plane_ref[unit, k + 1, :, cols] if k + 1 < slab_len else halo
        upper = following.astype(jnp.float32)
        moved = jitter * upper
        value = stay + moved
        before = before + gain_ref[k:k + 1, place] * value
        beyond = jnp.exp2(before)
        moment(sums, through - beyond, value, levels)
        through = beyond
        stay = upper - moved
    return sums, before


def loop(count, body):
    def step(n, carry):
        body(n)
        return carry

    lax.fori_loop(0, count, step, 0)


def each_pair(units, arrive, compute, store, leave):
    def step(n):
        places = [(2 * n + u, c) for u in range(2) for c in range(0, UNIT, LANES)]
        arrive(n)
        results = [compute(unit, pl.ds(c, LANES), pl.ds(pl.multiple_of(unit * UNIT + c, LANES), LANES)) for unit, c in places]
        for (unit, c), result in zip(places, results):
            store(unit, pl.ds(c, LANES), result)
        leave(n)

    loop(units // 2, step)


def start_all(pairs, sems):
    copies = [pltpu.make_async_copy(src, dst, sems.at[n]) for n, (src, dst) in enumerate(pairs)]
    for copy in copies:
        copy.start()
    return copies


class Pieces:
    def __init__(self, near):
        self.near = near
        self.here = lax.axis_index("depth")

    def far(self, n):
        if not self.near:
            return n
        return n + jnp.where(n >= self.here // self.near * self.near, self.near, 0)

    def close(self, n):
        return self.here ^ n


def columns(piece, col=0, size=UNIT):
    return pl.ds(pl.multiple_of(piece * UNIT + col, LANES), size)


def field_copy(field_any, plane_ref, sems, piece_of, unit):
    return pltpu.make_async_copy(field_any.at[:, :, columns(piece_of(unit))], plane_ref.at[unit], sems.at[unit])


def arrive_pair(arrival, n):
    for u in range(2):
        arrival(2 * n + u).wait()


def open_kernel(total, tile_cols, near, transfer_any, start_any, end_any, field_any, jitter_any, state_any, transfer_ref,
                start_ref, end_ref, plane_ref, jitter_ref, state_ref, gain_ref, few_sems, sems, out_sems):
    units, slab_len, rows, _ = plane_ref.shape
    piece_of = Pieces(near).far
    arrival = functools.partial(field_copy, field_any, plane_ref, sems, piece_of)
    for unit in range(2):
        arrival(unit).start()
    pairs = [(transfer_any, transfer_ref), (start_any, start_ref), (end_any, end_ref), (jitter_any, jitter_ref)]
    *early, jitter_copy = start_all(pairs, few_sems)
    base = lax.axis_index("depth") * slab_len
    for copy in early:
        copy.wait()
    levels = [jnp.full((rows, LANES), transfer_ref[i]) for i in range(3)]
    gain = jnp.full((SUBLANES, LANES), transfer_ref[3]) * (-LOG2E * 0.2 / total)
    for unit in range(2, units):
        arrival(unit).start()
    tile_gains(gain_ref, gain, base, tile_cols, start_ref, end_ref, piece_of)
    jitter_copy.wait()

    def compute(unit, cols, place):
        jitter = jitter_ref[:, columns(piece_of(unit), cols.start, LANES)]
        return march(gain_ref, plane_ref, unit, cols, place, jitter, levels)

    def store(unit, cols, result):
        sums, before = result
        for i, value in enumerate([*sums, before]):
            state_ref[unit, i, :, cols] = value

    def leave(n):
        place = pl.ds(2 * n, 2)
        return pltpu.make_async_copy(state_ref.at[place], state_any.at[place], out_sems.at[n])

    each_pair(units, functools.partial(arrive_pair, arrival), compute, store, lambda n: leave(n).start())
    loop(units // 2, lambda n: leave(n).wait())


class Coder:
    def __init__(self, total, slab_len, shape, transfer_ref):
        depth_gain = jnp.full(shape, transfer_ref[3]) * (0.2 / total)
        self.levels = [jnp.full(shape, transfer_ref[i]) for i in range(3)]
        self.depth_unit = 1.0 / (depth_gain * (slab_len * TOP))
        self.color_unit = [self.depth_unit * ((self.levels[i] + TOP) * (1.0 / TOP)) for i in range(3)]
        self.depth_span, self.color_span = spans(slab_len)
        self.gain = depth_gain[:SUBLANES] * -LOG2E

    def codes(self, sums, before):
        tints = colors(sums, before, self.levels)
        codes = [encode(color * unit, self.color_span) for color, unit in zip(tints, self.color_unit)]
        return codes + [encode(before * (self.depth_unit * (-1.0 / LOG2E)), self.depth_span)]


def close_kernel(total, tile_cols, near, opened, transfer_any, start_any, end_any, field_any, halo_any, jitter_any, state_any,
                 out_any, transfer_ref, start_ref, end_ref, plane_ref, halo_ref, jitter_ref, out_ref, gain_ref, state_ref,
                 last_ref, last_gain_ref, few_sems, sems, out_sems):
    units, slab_len, rows, _ = plane_ref.shape
    piece_of = Pieces(near).far
    later = lambda unit: piece_of(opened + unit)
    arrival = functools.partial(field_copy, field_any, plane_ref, sems, later)
    for unit in range(2):
        arrival(unit).start()
    pairs = [(transfer_any, transfer_ref), (start_any, start_ref), (end_any, end_ref), (jitter_any, jitter_ref)]
    pairs += [(halo_any, halo_ref), (state_any, state_ref), (field_any.at[slab_len - 1], last_ref)]
    copies = start_all(pairs, few_sems)
    base = lax.axis_index("depth") * slab_len
    for copy in copies[:3]:
        copy.wait()
    coder = Coder(total, slab_len, (rows, LANES), transfer_ref)
    for unit in range(2, units):
        arrival(unit).start()
    tile_gains(gain_ref, coder.gain, base, tile_cols, start_ref, end_ref, later)
    tile_gains(last_gain_ref, coder.gain, base + slab_len - 1, tile_cols, start_ref, end_ref, piece_of)
    for copy in copies[3:5]:
        copy.wait()

    def compute(unit, cols, place):
        whole = columns(later(unit), cols.start, LANES)
        jitter = jitter_ref[:, whole]
        return coder.codes(*march(gain_ref, plane_ref, unit, cols, place, jitter, coder.levels, halo_ref[:, whole]))

    def store(first, unit, cols, codes):
        for i, code in enumerate(codes):
            out_ref[first + unit, i, :, cols] = code

    def leave(unit):
        return pltpu.make_async_copy(out_ref.at[unit], out_any.at[piece_of(unit)], out_sems.at[unit])

    def leave_pair(first, n):
        for u in range(2):
            leave(first + 2 * n + u).start()

    each_pair(units, functools.partial(arrive_pair, arrival), compute, functools.partial(store, opened),
              functools.partial(leave_pair, opened))
    for copy in copies[5:]:
        copy.wait()

    def finish(unit, cols, place):
        whole = columns(piece_of(unit), cols.start, LANES)
        jitter = jitter_ref[:, whole]
        lower = last_ref[:, whole].astype(jnp.float32)
        upper = halo_ref[:, whole].astype(jnp.float32)
        value = (1.0 - jitter) * lower + jitter * upper
        before = state_ref[unit, 3, :, cols]
        beyond = before + last_gain_ref[0:1, place] * value
        weight = jnp.exp2(before) - jnp.exp2(beyond)
        sums = [state_ref[unit, i, :, cols] for i in range(3)]
        moment(sums, weight, value, coder.levels)
        return coder.codes(sums, beyond)

    each_pair(opened, lambda n: None, finish, functools.partial(store, 0), functools.partial(leave_pair, 0))
    loop(out_ref.shape[0], lambda unit: leave(unit).wait())


def near_kernel(total, tile_cols, near, transfer_any, start_any, end_any, field_any, halo_any, jitter_any, far_any, *refs):
    del far_any
    out_anys = refs[:near]
    transfer_ref, start_ref, end_ref, plane_ref, halo_ref, jitter_ref, out_ref, gain_ref, few_sems, sems, out_sems = refs[near:]
    units, slab_len, rows, _ = plane_ref.shape
    piece_of = Pieces(near).close
    arrival = functools.partial(field_copy, field_any, plane_ref, sems, piece_of)
    for unit in range(2):
        arrival(unit).start()
    pairs = [(transfer_any, transfer_ref), (start_any, start_ref), (end_any, end_ref), (jitter_any, jitter_ref)]
    copies = start_all(pairs + [(halo_any, halo_ref)], few_sems)
    base = lax.axis_index("depth") * slab_len
    for copy in copies[:3]:
        copy.wait()
    coder = Coder(total, slab_len, (rows, LANES), transfer_ref)
    for unit in range(2, units):
        arrival(unit).start()
    tile_gains(gain_ref, coder.gain, base, tile_cols, start_ref, end_ref, piece_of)
    for copy in copies[3:]:
        copy.wait()

    def compute(unit, cols, place):
        whole = columns(piece_of(unit), cols.start, LANES)
        jitter = jitter_ref[:, whole]
        return coder.codes(*march(gain_ref, plane_ref, unit, cols, place, jitter, coder.levels, halo_ref[:, whole]))

    def store(unit, cols, codes):
        for i, code in enumerate(codes):
            out_ref[unit, i, :, cols] = code

    each_pair(units, functools.partial(arrive_pair, arrival), compute, store, lambda n: None)
    pairs = [(out_ref.at[unit], out_anys[unit]) for unit in range(units)]
    for copy in start_all(pairs, out_sems):
        copy.wait()


def slab_codes(field, halo, jitter, transfer, ray_start, ray_end, total, near):
    slab_len, rows, cols = field.shape
    pieces = cols // UNIT
    opened = pieces * 3 // 16 * 2
    closed = pieces - near - opened
    ntiles = ray_start.shape[0]
    tile_cols = cols // ntiles
    own = pl.BlockSpec(memory_space=pl.ANY)
    scalars = [pltpu.SMEM(transfer.shape, transfer.dtype)] + [pltpu.SMEM((ntiles,), jnp.int32)] * 2
    plane = pltpu.VMEM((rows, cols), field.dtype)
    lean = pltpu.VMEM((rows, cols), jnp.float32)

    def cost(units):
        work = slab_len * rows * units * UNIT
        return pl.CostEstimate(flops=work * 20, bytes_accessed=work * 2, transcendentals=work * 2)

    def planes(units):
        return pltpu.VMEM((units, slab_len, rows, UNIT), field.dtype)

    def table(samples, units):
        return pltpu.VMEM((samples, units * UNIT), jnp.float32)

    state_shape = (opened, 4, rows, UNIT)
    state = pl.pallas_call(
        functools.partial(open_kernel, total, tile_cols, near),
        in_specs=[own] * 5,
        out_specs=own,
        out_shape=jax.ShapeDtypeStruct(state_shape, jnp.float32),
        scratch_shapes=scalars + [
            planes(opened), lean, pltpu.VMEM(state_shape, jnp.float32), table(slab_len, opened),
            pltpu.SemaphoreType.DMA((4,)),
            pltpu.SemaphoreType.DMA((opened,)),
            pltpu.SemaphoreType.DMA((opened // 2,)),
        ],
        compiler_params=pltpu.CompilerParams(vmem_limit_bytes=OPEN_BYTES),
        cost_estimate=cost(opened),
        name="open",
    )(transfer, ray_start, ray_end, field, jitter)
    far = pl.pallas_call(
        functools.partial(close_kernel, total, tile_cols, near, opened),
        in_specs=[own] * 7,
        out_specs=own,
        out_shape=jax.ShapeDtypeStruct((pieces, 4, rows, UNIT), jnp.int16),
        scratch_shapes=scalars + [
            planes(closed), plane, lean, pltpu.VMEM((opened + closed, 4, rows, UNIT), jnp.int16), table(slab_len, closed),
            pltpu.VMEM(state_shape, jnp.float32), plane, table(SUBLANES, opened),
            pltpu.SemaphoreType.DMA((7,)),
            pltpu.SemaphoreType.DMA((closed,)),
            pltpu.SemaphoreType.DMA((opened + closed,)),
        ],
        compiler_params=pltpu.CompilerParams(vmem_limit_bytes=CLOSE_BYTES),
        cost_estimate=cost(closed),
        name="close",
    )(transfer, ray_start, ray_end, field, halo, jitter, state)
    if not near:
        return far, []
    return far, pl.pallas_call(
        functools.partial(near_kernel, total, tile_cols, near),
        in_specs=[own] * 7,
        out_specs=[own] * near,
        out_shape=[jax.ShapeDtypeStruct((4, rows, UNIT), jnp.int16)] * near,
        scratch_shapes=scalars + [
            planes(near), plane, lean, pltpu.VMEM((near, 4, rows, UNIT), jnp.int16), table(slab_len, near),
            pltpu.SemaphoreType.DMA((5,)),
            pltpu.SemaphoreType.DMA((near,)),
            pltpu.SemaphoreType.DMA((near,)),
        ],
        compiler_params=pltpu.CompilerParams(vmem_limit_bytes=CLOSE_BYTES),
        cost_estimate=cost(near),
        name="near",
    )(transfer, ray_start, ray_end, field, halo, jitter, far)


def composite_kernel(total, slab_len, near, order_any, transfer_any, code_any, *refs):
    near_anys = refs[:near]
    image_any, order_ref, transfer_ref, code_ref, out_ref, sems, out_sems = refs[near:]
    count, _, rows, width = code_ref.shape
    here = lax.axis_index("depth")
    pairs = [(near_any, code_ref.at[here ^ n]) for n, near_any in enumerate(near_anys)]
    if near:
        for n in range(count // near - 1):
            group = n + jnp.where(n >= here // near, 1, 0)
            slabs = pl.ds(group * near, near)
            pairs.append((code_any.at[slabs], code_ref.at[slabs]))
    else:
        pairs.append((code_any, code_ref))
    copies = start_all([(order_any, order_ref), (transfer_any, transfer_ref)] + pairs, sems)
    block = math.gcd(width, 2 * LANES)
    places = [pl.ds(col, block) for col in range(0, width, block)]
    shape = (rows, block)
    depth_span, color_span = spans(slab_len)
    for copy in copies:
        copy.wait()
    unit = jnp.full(shape, transfer_ref[3]) * (0.2 / total * slab_len * TOP)
    depth_unit = unit * LOG2E
    leaving = []
    for n, cols in enumerate(places):

        def number(slab, channel, span):
            return code_ref[slab, channel, :, cols].astype(jnp.int32).astype(jnp.float32) * (span / 65535.0)

        def step(j, carry):
            shift, *colors = carry
            slab = order_ref[j]
            code = number(slab, 3, depth_span)
            idle = code < depth_span * (-32767.5 / 65535.0)
            away = jnp.where(idle, FAR, shift)
            for i in range(3):
                colors[i] = colors[i] + jnp.exp2(number(slab, i, color_span) - away)
            own = jnp.where(idle, 0.0, jnp.exp2(code + lift(depth_span)))
            return shift + depth_unit * own, *colors

        zero = jnp.zeros(shape, jnp.float32)
        first = jnp.full(shape, -lift(color_span))
        shift, *colors = lax.fori_loop(0, count, step, (first, zero, zero, zero), unroll=math.gcd(count, 4))
        for i in range(3):
            out_ref[i, :, cols] = colors[i] * (unit * (TOP / (transfer_ref[i] + jnp.full(shape, TOP))))
        out_ref[3, :, cols] = 1.0 - jnp.exp2(first - shift)
        leaving.append(pltpu.make_async_copy(out_ref.at[:, :, cols], image_any.at[:, :, cols], out_sems.at[n]))
        leaving[-1].start()
    for copy in leaving:
        copy.wait()


def composite(codes, near_codes, transfer, depth_order, total, slab_len):
    count, _, rows, width = codes.shape
    near = len(near_codes)
    blocks = width // math.gcd(width, 2 * LANES)
    own = pl.BlockSpec(memory_space=pl.ANY)
    return pl.pallas_call(
        functools.partial(composite_kernel, total, slab_len, near),
        in_specs=[own] * (3 + near),
        out_specs=own,
        out_shape=jax.ShapeDtypeStruct((4, rows, width), jnp.float32),
        scratch_shapes=[
            pltpu.SMEM(depth_order.shape, depth_order.dtype),
            pltpu.SMEM(transfer.shape, transfer.dtype),
            pltpu.VMEM(codes.shape, codes.dtype),
            pltpu.VMEM((4, rows, width), jnp.float32),
            pltpu.SemaphoreType.DMA((2 + near + (count // near - 1 if near else 1),)),
            pltpu.SemaphoreType.DMA((blocks,)),
        ],
        compiler_params=pltpu.CompilerParams(vmem_limit_bytes=SMALL_BYTES),
        name="composite",
    )(depth_order, transfer, codes, *near_codes)


def on_device(field, jitter, transfer, depth_order, ray_start, ray_end):
    count = lax.axis_size("depth")
    slab_len, rows, cols = field.shape
    total = slab_len * count
    width = cols // count
    near = NEAR if width == UNIT and count % (2 * NEAR) == 0 else 0
    halo = shifted(field[0], "depth", -1)
    codes, near_codes = slab_codes(field, halo, jitter, transfer, ray_start, ray_end, total, near)
    if width != UNIT:
        codes = codes.transpose(1, 2, 0, 3).reshape(4, rows, count, width).transpose(2, 0, 1, 3)
    received = lax.all_to_all(codes, "depth", split_axis=0, concat_axis=0, tiled=True)
    swapped = [lax.ppermute(near_codes[n], "depth", [(i, i ^ n) for i in range(count)]) for n in range(1, near)]
    return composite(received, [*near_codes[:1], *swapped], transfer, depth_order, total, slab_len)


def solution(mesh):
    in_specs = (P("depth", "groups", None), P("groups", None), P(), P(), P(), P())
    out_specs = P(None, "groups", "depth")
    return jax.shard_map(
        on_device, mesh=mesh, in_specs=in_specs, out_specs=out_specs, check_vma=False
    )
```

time: 54.2 us -> 49.6 us (0.915)
  blocking collectives: 33 us -> 0 us
  starting transfers between devices: 1.29 us -> 17.2 us
  waiting for transfers between devices: 0.01 us -> 9.9 us
  Pallas kernels: 18.2 us -> 21 us
    all_to_all x1 -> x0, blocking collectives: 33 us -> none  [on_device(): lax.all_to_all(codes, 'depth', split_axis=0, concat_axis=0, tiled=True)]
    ppermute x0 -> x7, waiting for transfers between devices: none -> 9.89 us  [on_device(): lax.ppermute(near_codes[n], 'depth', [(i, i ^ n) for i in range(count)])]
    all_to_all x0 -> x1, starting transfers between devices: none -> 8.16 us  [on_device(): lax.all_to_all(codes, 'depth', split_axis=0, concat_axis=0, tiled=True)]
    ppermute x0 -> x7, starting transfers between devices: none -> 7.78 us  [on_device(): lax.ppermute(near_codes[n], 'depth', [(i, i ^ n) for i in range(count)])]
    pallas_call x3 -> x4, Pallas kernels: 18.2 us -> 21 us  [the longest x1 8.36 us: slab_codes(): pl.pallas_call(functools.partial(near_kernel, total, tile_cols, near), in...]
  transfers between devices with their start and end apart: 1 -> 9, of which waited for: 0 -> 6; matrix products, arithmetic and copies ran while one was open for 0% -> 0% of each run, Pallas kernels for 12% -> 30%
where the time goes in v16:
time: 49.6 us; the launch traced here: 49.3 us
  Pallas kernels  21 us (42%)
  starting transfers between devices  17.2 us (35%)
  waiting for transfers between devices  9.9 us (20%)
  local copies, waits for them, and re-layouts  1.05 us (2%)
    ppermute x7, waiting for transfers between devices, on_device(): lax.ppermute(near_codes[n], 'depth', [(i, i ^ n) for i in range(count)])  9.89 us
    pallas_call x1, Pallas kernels, slab_codes(): pl.pallas_call(functools.partial(near_kernel, total, tile_cols, near), in...  8.36 us
    all_to_all x1, starting transfers between devices, on_device(): lax.all_to_all(codes, 'depth', split_axis=0, concat_axis=0, tiled=True)  8.16 us
    ppermute x7, starting transfers between devices, on_device(): lax.ppermute(near_codes[n], 'depth', [(i, i ^ n) for i in range(count)])  7.78 us
    pallas_call x1, Pallas kernels, slab_codes(): pl.pallas_call(functools.partial(open_kernel, total, tile_cols, near), in...  6.46 us
    pallas_call x1, Pallas kernels, slab_codes(): pl.pallas_call(functools.partial(close_kernel, total, tile_cols, near, op...  4.1 us
    pallas_call x1, Pallas kernels, composite(): pl.pallas_call(functools.partial(composite_kernel, total, slab_len, near)...  2.06 us
    ppermute x1, starting transfers between devices, shifted(): lax.ppermute(value, axis, [(source, source + steps) for source in range(i...  1.29 us
  transfers between devices with their start and end apart: 9, of which 6 were waited for; matrix products, arithmetic and copies ran while one was open for 0% of the time, Pallas kernels for 30%

profile of v16, /device:TPU:0, one launch (start us, length us, event | category | flops | bytes accessed | tf_op | source)
XLA Modules:
  0.0 49.3 jit_solution(9667025125861719528)
XLA Ops:
  0.0 0.0 copy-start.2
  0.0 0.0 copy-start.3
  0.0 0.0 copy-start
  0.0 0.0 copy-start.1
  0.0 1.0 %slice_bitcast_fusion = bf16[16,8192]{1,0:T(8,128)(2,1)S(1)} fusion(bf16[32,16,8192]{2,1,0:T(8,128)(2,1)} %field_any.5), kind=kLoop, calls=%fused_computation | loop fusion | bytes 524288 | tf_op jit(solution)/shard_map/squeeze | solution.py:456
  1.0 1.3 %collective-permute-start = (bf16[16,8192]{1,0:T(8,128)(2,1)S(1)}, bf16[16,8192]{1,0:T(8,128)(2,1)S(1)}, u32[]{:S(2)}, u32[]{:S(2)}) collective-permute-start(bf16[16,8192]{1,0:T(8,128)(2,1)S(1)} %slice_bitcast_fusion), channel_id=1, source_target_pairs={{1,0},{2,1},{3,2},{4,3},{5,4},{6,5},{7,6},{8,7},{9,8},{10,9},{11,1... | collective-permute-start | bytes 786440 | tf_op jit(solution)/shard_map/ppermute | solution.py:35
  2.3 6.5 %open.1.state_any = f32[6,4,16,512]{3,2,1,0:T(8,128)} custom-call(f32[4]{0:T(128)} %transfer_any.7, s32[128]{0:T(128)} %start_any.5, s32[128]{0:T(128)} %end_any.5, bf16[32,16,8192]{2,1,0:T(8,128)(2,1)} %field_any.5, f32[16,8192]{1,0:T(8,128)} %jitter_any.5), custom_call_target="tpu_custom_call" | custom-call | flops 31457280 | bytes 3145728 | tf_op jit(solution)/shard_map/open/pallas_call | solution.py:326
  8.8 0.0 collective-permute-done.halo_any
  8.8 0.0 copy-done.2
  8.8 0.0 copy-done.3
  8.8 0.0 copy-done
  8.8 0.0 copy-done.1
  8.9 4.1 %close.1.far_any = s16[16,4,16,512]{3,2,1,0:T(8,128)(2,1)} custom-call(f32[4]{0:T(128)S(1)} %copy-done.1, s32[128]{0:T(128)S(1)} %copy-done.2, s32[128]{0:T(128)S(1)} %copy-done.3, bf16[32,16,8192]{2,1,0:T(8,128)(2,1)} %field_any.5, bf16[16,8192]{1,0:T(8,128)(2,1)S(1)} %collective-permute-done.halo_any, f32[16,8192]{1,0:T(8,128)S(1)} %copy-done, ...), custom_call_target="tpu_custom_call" | custom-call | flops 10485760 | bytes 1048576 | tf_op jit(solution)/shard_map/close/pallas_call | solution.py:341
  13.0 0.0 copy-start.4
  13.0 8.2 %all-to-all-start = ((s16[16,4,16,512]{3,2,1,0:T(8,128)(2,1)}), s16[16,4,16,512]{3,2,1,0:T(8,128)(2,1)S(1)}, u32[]{:S(2)}, u32[]{:S(2)}) async-start(s16[16,4,16,512]{3,2,1,0:T(8,128)(2,1)} %close.1.far_any), calls=%async_computation | async-start | bytes 2097152 | tf_op jit(solution)/shard_map/all_to_all | solution.py:460
  21.1 8.4 %near.1 = (s16[4,16,512]{2,1,0:T(8,128)(2,1)S(1)}, s16[4,16,512]{2,1,0:T(8,128)(2,1)S(1)}, s16[4,16,512]{2,1,0:T(8,128)(2,1)S(1)}, s16[4,16,512]{2,1,0:T(8,128)(...) custom-call(f32[4]{0:T(128)S(1)} %copy-done.1, ...), custom_call_target="tpu_custom_call" | custom-call | flops 41943040 | bytes 4194304 | tf_op jit(solution)/shard_map/near/pallas_call | solution.py:359
  29.5 0.5 collective-permute-start.1
  30.0 1.7 %collective-permute-start.2 = (s16[4,16,512]{2,1,0:T(8,128)(2,1)S(1)}, s16[4,16,512]{2,1,0:T(8,128)(2,1)S(1)}, u32[]{:S(2)}, u32[]{:S(2)}) collective-permute-start(s16[4,16,512]{2,1,0:T(8,128)(2,1)S(1)} %get-tuple-element.15), channel_id=1, source_target_pairs={{0,2},{1,3},{2,0},{3,1},{4,6},{5,7},{6,4},{7,5},{8,10},{9,11},{10,... | collective-permute-start | bytes 196616 | tf_op jit(solution)/shard_map/ppermute | solution.py:461
  31.7 0.0 collective-permute-start.3
  31.7 1.7 %collective-permute-start.4 = (s16[4,16,512]{2,1,0:T(8,128)(2,1)S(1)}, s16[4,16,512]{2,1,0:T(8,128)(2,1)S(1)}, u32[]{:S(2)}, u32[]{:S(2)}) collective-permute-start(s16[4,16,512]{2,1,0:T(8,128)(2,1)S(1)} %get-tuple-element.17), channel_id=1, source_target_pairs={{0,4},{1,5},{2,6},{3,7},{4,0},{5,1},{6,2},{7,3},{8,12},{9,13},{10,... | collective-permute-start | bytes 196616 | tf_op jit(solution)/shard_map/ppermute | solution.py:461
  33.4 0.1 collective-permute-start.5
  33.5 0.0 collective-permute-done.1.refs_1_
  33.5 2.6 %collective-permute-start.6 = (s16[4,16,512]{2,1,0:T(8,128)(2,1)S(1)}, s16[4,16,512]{2,1,0:T(8,128)(2,1)S(1)}, u32[]{:S(2)}, u32[]{:S(2)}) collective-permute-start(s16[4,16,512]{2,1,0:T(8,128)(2,1)S(1)} %get-tuple-element.19), channel_id=1, source_target_pairs={{0,6},{1,7},{2,4},{3,5},{4,2},{5,3},{6,0},{7,1},{8,14},{9,15},{10,... | collective-permute-start | bytes 196616 | tf_op jit(solution)/shard_map/ppermute | solution.py:461
  36.1 0.5 %collective-permute-done.2.refs_2_ = s16[4,16,512]{2,1,0:T(8,128)(2,1)S(1)} collective-permute-done((s16[4,16,512]{2,1,0:T(8,128)(2,1)S(1)}, s16[4,16,512]{2,1,0:T(8,128)(2,1)S(1)}, u32[]{:S(2)}, u32[]{:S(2)}) %collective-permute-start.2) | collective-permute-done | bytes 65568 | tf_op jit(solution)/shard_map/ppermute | solution.py:461
  36.6 1.2 %collective-permute-start.7 = (s16[4,16,512]{2,1,0:T(8,128)(2,1)S(1)}, s16[4,16,512]{2,1,0:T(8,128)(2,1)S(1)}, u32[]{:S(2)}, u32[]{:S(2)}) collective-permute-start(s16[4,16,512]{2,1,0:T(8,128)(2,1)S(1)} %get-tuple-element.20), channel_id=1, source_target_pairs={{0,7},{1,6},{2,5},{3,4},{4,3},{5,2},{6,1},{7,0},{8,15},{9,14},{10,... | collective-permute-start | bytes 196616 | tf_op jit(solution)/shard_map/ppermute | solution.py:461
  37.8 0.5 %collective-permute-done.3.refs_3_ = s16[4,16,512]{2,1,0:T(8,128)(2,1)S(1)} collective-permute-done((s16[4,16,512]{2,1,0:T(8,128)(2,1)S(1)}, s16[4,16,512]{2,1,0:T(8,128)(2,1)S(1)}, u32[]{:S(2)}, u32[]{:S(2)}) %collective-permute-start.3) | collective-permute-done | bytes 65568 | tf_op jit(solution)/shard_map/ppermute | solution.py:461
  38.3 2.6 %collective-permute-done.4.refs_4_ = s16[4,16,512]{2,1,0:T(8,128)(2,1)S(1)} collective-permute-done((s16[4,16,512]{2,1,0:T(8,128)(2,1)S(1)}, s16[4,16,512]{2,1,0:T(8,128)(2,1)S(1)}, u32[]{:S(2)}, u32[]{:S(2)}) %collective-permute-start.4) | collective-permute-done | bytes 65568 | tf_op jit(solution)/shard_map/ppermute | solution.py:461
  40.9 1.4 %collective-permute-done.5.refs_5_ = s16[4,16,512]{2,1,0:T(8,128)(2,1)S(1)} collective-permute-done((s16[4,16,512]{2,1,0:T(8,128)(2,1)S(1)}, s16[4,16,512]{2,1,0:T(8,128)(2,1)S(1)}, u32[]{:S(2)}, u32[]{:S(2)}) %collective-permute-start.5) | collective-permute-done | bytes 65568 | tf_op jit(solution)/shard_map/ppermute | solution.py:461
  42.3 4.5 %collective-permute-done.6.refs_6_ = s16[4,16,512]{2,1,0:T(8,128)(2,1)S(1)} collective-permute-done((s16[4,16,512]{2,1,0:T(8,128)(2,1)S(1)}, s16[4,16,512]{2,1,0:T(8,128)(2,1)S(1)}, u32[]{:S(2)}, u32[]{:S(2)}) %collective-permute-start.6) | collective-permute-done | bytes 65568 | tf_op jit(solution)/shard_map/ppermute | solution.py:461
  46.7 0.5 collective-permute-done.7.refs_7_
  47.2 0.0 all-to-all-done.code_any
  47.2 0.0 copy-done.4
  47.2 2.1 %composite.1 = f32[4,16,512]{2,1,0:T(8,128)} custom-call(s32[16]{0:T(128)S(1)} %copy-done.4, f32[4]{0:T(128)S(1)} %copy-done.1, s16[16,4,16,512]{3,2,1,0:T(8,128)(2,1)S(1)} %all-to-all-done.code_any, s16[4,16,512]{2,1,0:T(8,128)(2,1)S(1)} %get-tuple-element.13.refs_0_, s16[4,16,512]{2,1,0:T(8,128)(2,1)S(1)} %collective-permute-done.1.refs_1_, ...), custom_call_target="tpu_custom_call" | custom-call | tf_op jit(solution)/shard_map/composite/pallas_call | solution.py:432
Async XLA Ops:
  0.0 8.8 %copy-start.2 = (s32[128]{0:T(128)S(1)}, s32[128]{0:T(128)}, u32[]{:S(2)}) copy-start(s32[128]{0:T(128)} %start_any.5) | copy-start | bytes 1540
  0.0 8.8 %copy-start.3 = (s32[128]{0:T(128)S(1)}, s32[128]{0:T(128)}, u32[]{:S(2)}) copy-start(s32[128]{0:T(128)} %end_any.5) | copy-start | bytes 1540
  0.0 8.8 %copy-start = (f32[16,8192]{1,0:T(8,128)S(1)}, f32[16,8192]{1,0:T(8,128)}, u32[]{:S(2)}) copy-start(f32[16,8192]{1,0:T(8,128)} %jitter_any.5) | copy-start | bytes 1572868
  0.0 8.8 %copy-start.1 = (f32[4]{0:T(128)S(1)}, f32[4]{0:T(128)}, u32[]{:S(2)}) copy-start(f32[4]{0:T(128)} %transfer_any.7) | copy-start | bytes 52
  1.0 7.8 %collective-permute-start = (bf16[16,8192]{1,0:T(8,128)(2,1)S(1)}, bf16[16,8192]{1,0:T(8,128)(2,1)S(1)}, u32[]{:S(2)}, u32[]{:S(2)}) collective-permute-start(bf16[16,8192]{1,0:T(8,128)(2,1)S(1)} %slice_bitcast_fusion), channel_id=1, source_target_pairs={{1,0},{2,1},{3,2},{4,3},{5,4},{6,5},{7,6},{8,7},{9,8},{10,9},{11,1... | collective-permute-start | bytes 786440 | tf_op jit(solution)/shard_map/ppermute | solution.py:35
  13.0 34.2 %copy-start.4 = (s32[16]{0:T(128)S(1)}, s32[16]{0:T(128)}, u32[]{:S(2)}) copy-start(s32[16]{0:T(128)} %order_any.1) | copy-start | bytes 196
  13.0 34.2 %all-to-all-start = ((s16[16,4,16,512]{3,2,1,0:T(8,128)(2,1)}), s16[16,4,16,512]{3,2,1,0:T(8,128)(2,1)S(1)}, u32[]{:S(2)}, u32[]{:S(2)}) async-start(s16[16,4,16,512]{3,2,1,0:T(8,128)(2,1)} %close.1.far_any), calls=%async_computation | async-start | bytes 2097152 | tf_op jit(solution)/shard_map/all_to_all | solution.py:460
  29.5 4.0 %collective-permute-start.1 = (s16[4,16,512]{2,1,0:T(8,128)(2,1)S(1)}, s16[4,16,512]{2,1,0:T(8,128)(2,1)S(1)}, u32[]{:S(2)}, u32[]{:S(2)}) collective-permute-start(s16[4,16,512]{2,1,0:T(8,128)(2,1)S(1)} %get-tuple-element.14), channel_id=1, source_target_pairs={{0,1},{1,0},{2,3},{3,2},{4,5},{5,4},{6,7},{7,6},{8,9},{9,8},{10,11... | collective-permute-start | bytes 196616 | tf_op jit(solution)/shard_map/ppermute | solution.py:461
  30.0 6.6 %collective-permute-start.2 = (s16[4,16,512]{2,1,0:T(8,128)(2,1)S(1)}, s16[4,16,512]{2,1,0:T(8,128)(2,1)S(1)}, u32[]{:S(2)}, u32[]{:S(2)}) collective-permute-start(s16[4,16,512]{2,1,0:T(8,128)(2,1)S(1)} %get-tuple-element.15), channel_id=1, source_target_pairs={{0,2},{1,3},{2,0},{3,1},{4,6},{5,7},{6,4},{7,5},{8,10},{9,11},{10,... | collective-permute-start | bytes 196616 | tf_op jit(solution)/shard_map/ppermute | solution.py:461
  31.7 6.7 %collective-permute-start.3 = (s16[4,16,512]{2,1,0:T(8,128)(2,1)S(1)}, s16[4,16,512]{2,1,0:T(8,128)(2,1)S(1)}, u32[]{:S(2)}, u32[]{:S(2)}) collective-permute-start(s16[4,16,512]{2,1,0:T(8,128)(2,1)S(1)} %get-tuple-element.16), channel_id=1, source_target_pairs={{0,3},{1,2},{2,1},{3,0},{4,7},{5,6},{6,5},{7,4},{8,11},{9,10},{10,... | collective-permute-start | bytes 196616 | tf_op jit(solution)/shard_map/ppermute | solution.py:461
  31.7 9.2 %collective-permute-start.4 = (s16[4,16,512]{2,1,0:T(8,128)(2,1)S(1)}, s16[4,16,512]{2,1,0:T(8,128)(2,1)S(1)}, u32[]{:S(2)}, u32[]{:S(2)}) collective-permute-start(s16[4,16,512]{2,1,0:T(8,128)(2,1)S(1)} %get-tuple-element.17), channel_id=1, source_target_pairs={{0,4},{1,5},{2,6},{3,7},{4,0},{5,1},{6,2},{7,3},{8,12},{9,13},{10,... | collective-permute-start | bytes 196616 | tf_op jit(solution)/shard_map/ppermute | solution.py:461
  33.4 8.9 %collective-permute-start.5 = (s16[4,16,512]{2,1,0:T(8,128)(2,1)S(1)}, s16[4,16,512]{2,1,0:T(8,128)(2,1)S(1)}, u32[]{:S(2)}, u32[]{:S(2)}) collective-permute-start(s16[4,16,512]{2,1,0:T(8,128)(2,1)S(1)} %get-tuple-element.18), channel_id=1, source_target_pairs={{0,5},{1,4},{2,7},{3,6},{4,1},{5,0},{6,3},{7,2},{8,13},{9,12},{10,... | collective-permute-start | bytes 196616 | tf_op jit(solution)/shard_map/ppermute | solution.py:461
  33.5 13.3 %collective-permute-start.6 = (s16[4,16,512]{2,1,0:T(8,128)(2,1)S(1)}, s16[4,16,512]{2,1,0:T(8,128)(2,1)S(1)}, u32[]{:S(2)}, u32[]{:S(2)}) collective-permute-start(s16[4,16,512]{2,1,0:T(8,128)(2,1)S(1)} %get-tuple-element.19), channel_id=1, source_target_pairs={{0,6},{1,7},{2,4},{3,5},{4,2},{5,3},{6,0},{7,1},{8,14},{9,15},{10,... | collective-permute-start | bytes 196616 | tf_op jit(solution)/shard_map/ppermute | solution.py:461
  36.6 10.6 %collective-permute-start.7 = (s16[4,16,512]{2,1,0:T(8,128)(2,1)S(1)}, s16[4,16,512]{2,1,0:T(8,128)(2,1)S(1)}, u32[]{:S(2)}, u32[]{:S(2)}) collective-permute-start(s16[4,16,512]{2,1,0:T(8,128)(2,1)S(1)} %get-tuple-element.20), channel_id=1, source_target_pairs={{0,7},{1,6},{2,5},{3,4},{4,3},{5,2},{6,1},{7,0},{8,15},{9,14},{10,... | collective-permute-start | bytes 196616 | tf_op jit(solution)/shard_map/ppermute | solution.py:461

commit v17 on v16

--- a/solution.py
+++ b/solution.py
@@ -131,9 +131,7 @@
         self.here = lax.axis_index("depth")
 
     def far(self, n):
-        if not self.near:
-            return n
-        return n + jnp.where(n >= self.here // self.near * self.near, self.near, 0)
+        return self.here ^ (self.near + n) if self.near else n
 
     def close(self, n):
         return self.here ^ n
@@ -204,8 +202,11 @@
 
 
 def close_kernel(total, tile_cols, near, opened, transfer_any, start_any, end_any, field_any, halo_any, jitter_any, state_any,
-                 out_any, transfer_ref, start_ref, end_ref, plane_ref, halo_ref, jitter_ref, out_ref, gain_ref, state_ref,
-                 last_ref, last_gain_ref, few_sems, sems, out_sems):
+                 *refs):
+    out_anys, refs = refs[:-14], refs[-14:]
+    transfer_ref, start_ref, end_ref, plane_ref, halo_ref, jitter_ref, out_ref, gain_ref, state_ref, last_ref, last_gain_ref = (
+        refs[:11])
+    few_sems, sems, out_sems = refs[11:]
     units, slab_len, rows, _ = plane_ref.shape
     piece_of = Pieces(near).far
     later = lambda unit: piece_of(opened + unit)
@@ -235,15 +236,12 @@
         for i, code in enumerate(codes):
             out_ref[first + unit, i, :, cols] = code
 
-    def leave(unit):
-        return pltpu.make_async_copy(out_ref.at[unit], out_any.at[piece_of(unit)], out_sems.at[unit])
-
-    def leave_pair(first, n):
-        for u in range(2):
-            leave(first + 2 * n + u).start()
-
-    each_pair(units, functools.partial(arrive_pair, arrival), compute, functools.partial(store, opened),
-              functools.partial(leave_pair, opened))
+    def leave(first, count):
+        pairs = [(out_ref.at[unit], out_anys[unit]) for unit in range(first, first + count)]
+        return start_all(pairs, out_sems.at[pl.ds(first, count)])
+
+    each_pair(units, functools.partial(arrive_pair, arrival), compute, functools.partial(store, opened), lambda n: None)
+    leaving = leave(opened, units)
     for copy in copies[5:]:
         copy.wait()
 
@@ -260,8 +258,9 @@
         moment(sums, weight, value, coder.levels)
         return coder.codes(sums, beyond)
 
-    each_pair(opened, lambda n: None, finish, functools.partial(store, 0), functools.partial(leave_pair, 0))
-    loop(out_ref.shape[0], lambda unit: leave(unit).wait())
+    each_pair(opened, lambda n: None, finish, functools.partial(store, 0), lambda n: None)
+    for copy in leaving + leave(0, opened):
+        copy.wait()
 
 
 def near_kernel(total, tile_cols, near, transfer_any, start_any, end_any, field_any, halo_any, jitter_any, far_any, *refs):
@@ -341,8 +340,8 @@
     far = pl.pallas_call(
         functools.partial(close_kernel, total, tile_cols, near, opened),
         in_specs=[own] * 7,
-        out_specs=own,
-        out_shape=jax.ShapeDtypeStruct((pieces, 4, rows, UNIT), jnp.int16),
+        out_specs=[own] * (pieces - near),
+        out_shape=[jax.ShapeDtypeStruct((4, rows, UNIT), jnp.int16)] * (pieces - near),
         scratch_shapes=scalars + [
             planes(closed), plane, lean, pltpu.VMEM((opened + closed, 4, rows, UNIT), jnp.int16), table(slab_len, closed),
             pltpu.VMEM(state_shape, jnp.float32), plane, table(SUBLANES, opened),
@@ -370,23 +369,20 @@
         compiler_params=pltpu.CompilerParams(vmem_limit_bytes=CLOSE_BYTES),
         cost_estimate=cost(near),
         name="near",
-    )(transfer, ray_start, ray_end, field, halo, jitter, far)
-
-
-def composite_kernel(total, slab_len, near, order_any, transfer_any, code_any, *refs):
-    near_anys = refs[:near]
-    image_any, order_ref, transfer_ref, code_ref, out_ref, sems, out_sems = refs[near:]
+    )(transfer, ray_start, ray_end, field, halo, jitter, far[0])
+
+
+def composite_kernel(total, slab_len, order_any, transfer_any, *refs):
+    code_anys, refs = refs[:-7], refs[-7:]
+    image_any, order_ref, transfer_ref, code_ref, out_ref, sems, out_sems = refs
     count, _, rows, width = code_ref.shape
     here = lax.axis_index("depth")
-    pairs = [(near_any, code_ref.at[here ^ n]) for n, near_any in enumerate(near_anys)]
-    if near:
-        for n in range(count // near - 1):
-            group = n + jnp.where(n >= here // near, 1, 0)
-            slabs = pl.ds(group * near, near)
-            pairs.append((code_any.at[slabs], code_ref.at[slabs]))
+    pairs = [(order_any, order_ref), (transfer_any, transfer_ref)]
+    if len(code_anys) == 1:
+        pairs.append((code_anys[0], code_ref))
     else:
-        pairs.append((code_any, code_ref))
-    copies = start_all([(order_any, order_ref), (transfer_any, transfer_ref)] + pairs, sems)
+        pairs += [(code_any, code_ref.at[here ^ n]) for n, code_any in enumerate(code_anys)]
+    copies = start_all(pairs, sems)
     block = math.gcd(width, 2 * LANES)
     places = [pl.ds(col, block) for col in range(0, width, block)]
     shape = (rows, block)
@@ -424,27 +420,27 @@
         copy.wait()
 
 
-def composite(codes, near_codes, transfer, depth_order, total, slab_len):
-    count, _, rows, width = codes.shape
-    near = len(near_codes)
+def composite(codes, transfer, depth_order, total, slab_len):
+    count = depth_order.shape[0]
+    _, rows, width = codes[0].shape[-3:]
     blocks = width // math.gcd(width, 2 * LANES)
     own = pl.BlockSpec(memory_space=pl.ANY)
     return pl.pallas_call(
-        functools.partial(composite_kernel, total, slab_len, near),
-        in_specs=[own] * (3 + near),
+        functools.partial(composite_kernel, total, slab_len),
+        in_specs=[own] * (2 + len(codes)),
         out_specs=own,
         out_shape=jax.ShapeDtypeStruct((4, rows, width), jnp.float32),
         scratch_shapes=[
             pltpu.SMEM(depth_order.shape, depth_order.dtype),
             pltpu.SMEM(transfer.shape, transfer.dtype),
-            pltpu.VMEM(codes.shape, codes.dtype),
+            pltpu.VMEM((count, 4, rows, width), jnp.int16),
             pltpu.VMEM((4, rows, width), jnp.float32),
-            pltpu.SemaphoreType.DMA((2 + near + (count // near - 1 if near else 1),)),
+            pltpu.SemaphoreType.DMA((2 + len(codes),)),
             pltpu.SemaphoreType.DMA((blocks,)),
         ],
         compiler_params=pltpu.CompilerParams(vmem_limit_bytes=SMALL_BYTES),
         name="composite",
-    )(depth_order, transfer, codes, *near_codes)
+    )(depth_order, transfer, *codes)
 
 
 def on_device(field, jitter, transfer, depth_order, ray_start, ray_end):
@@ -452,14 +448,16 @@
     slab_len, rows, cols = field.shape
     total = slab_len * count
     width = cols // count
-    near = NEAR if width == UNIT and count % (2 * NEAR) == 0 else 0
+    near = NEAR if width == UNIT and count == 2 * NEAR else 0
     halo = shifted(field[0], "depth", -1)
-    codes, near_codes = slab_codes(field, halo, jitter, transfer, ray_start, ray_end, total, near)
-    if width != UNIT:
-        codes = codes.transpose(1, 2, 0, 3).reshape(4, rows, count, width).transpose(2, 0, 1, 3)
-    received = lax.all_to_all(codes, "depth", split_axis=0, concat_axis=0, tiled=True)
-    swapped = [lax.ppermute(near_codes[n], "depth", [(i, i ^ n) for i in range(count)]) for n in range(1, near)]
-    return composite(received, [*near_codes[:1], *swapped], transfer, depth_order, total, slab_len)
+    far_codes, near_codes = slab_codes(field, halo, jitter, transfer, ray_start, ray_end, total, near)
+    if near:
+        codes = [*near_codes, *far_codes]
+        codes = codes[:1] + [lax.ppermute(codes[n], "depth", [(i, i ^ n) for i in range(count)]) for n in range(1, count)]
+    else:
+        codes = jnp.stack(far_codes).transpose(1, 2, 0, 3).reshape(4, rows, count, width).transpose(2, 0, 1, 3)
+        codes = [lax.all_to_all(codes, "depth", split_axis=0, concat_axis=0, tiled=True)]
+    return composite(codes, transfer, depth_order, total, slab_len)
 
 
 def solution(mesh):

time: 49.6 us -> 57.8 us (1.17)
  starting transfers between devices: 17.2 us -> 27.3 us
  waiting for transfers between devices: 9.9 us -> 7.2 us
  Pallas kernels: 21 us -> 22 us
    ppermute x7 -> x15, starting transfers between devices: 7.78 us -> 26 us  [on_device(): lax.ppermute(codes[n], 'depth', [(i, i ^ n) for i in range(count)])]
    all_to_all x1 -> x0, starting transfers between devices: 8.16 us -> none  [on_device(): lax.all_to_all(codes, 'depth', split_axis=0, concat_axis=0, tiled=True)]
    ppermute x7 -> x15, waiting for transfers between devices: 9.89 us -> 7.2 us  [on_device(): lax.ppermute(codes[n], 'depth', [(i, i ^ n) for i in range(count)])]
    pallas_call x1, Pallas kernels: 2.06 us -> 2.87 us  [composite(): pl.pallas_call(functools.partial(composite_kernel, total, slab_len), in_s...]
  transfers between devices with their start and end apart: 9 -> 16, of which waited for: 6 -> 4; matrix products, arithmetic and copies ran while one was open for 0% -> 0% of each run, Pallas kernels for 30% -> 26%
where the time goes in v17:
time: 57.8 us; the launch traced here: 57.6 us
  starting transfers between devices  27.3 us (47%)
  Pallas kernels  22 us (38%)
  waiting for transfers between devices  7.2 us (12%)
  local copies, waits for them, and re-layouts  1.03 us (2%)
    ppermute x15, starting transfers between devices, on_device(): lax.ppermute(codes[n], 'depth', [(i, i ^ n) for i in range(count)])  26 us
    pallas_call x1, Pallas kernels, slab_codes(): pl.pallas_call(functools.partial(near_kernel, total, tile_cols, near), in...  8.34 us
    ppermute x15, waiting for transfers between devices, on_device(): lax.ppermute(codes[n], 'depth', [(i, i ^ n) for i in range(count)])  7.2 us
    pallas_call x1, Pallas kernels, slab_codes(): pl.pallas_call(functools.partial(open_kernel, total, tile_cols, near), in...  6.43 us
    pallas_call x1, Pallas kernels, slab_codes(): pl.pallas_call(functools.partial(close_kernel, total, tile_cols, near, op...  4.39 us
    pallas_call x1, Pallas kernels, composite(): pl.pallas_call(functools.partial(composite_kernel, total, slab_len), in_s...  2.87 us
    ppermute x1, starting transfers between devices, shifted(): lax.ppermute(value, axis, [(source, source + steps) for source in range(i...  1.29 us
  transfers between devices with their start and end apart: 16, of which 4 were waited for; matrix products, arithmetic and copies ran while one was open for 0% of the time, Pallas kernels for 26%

profile of v17, /device:TPU:0, one launch (start us, length us, event | category | flops | bytes accessed | tf_op | source)
XLA Modules:
  0.0 57.6 jit_solution(16571391500341254715)
XLA Ops:
  0.0 0.0 copy-start
  0.0 0.0 copy-start.2
  0.0 0.0 copy-start.1
  0.0 1.0 %slice_bitcast_fusion = bf16[16,8192]{1,0:T(8,128)(2,1)S(1)} fusion(bf16[32,16,8192]{2,1,0:T(8,128)(2,1)} %field_any.5), kind=kLoop, calls=%fused_computation | loop fusion | bytes 524288 | tf_op jit(solution)/shard_map/squeeze | solution.py:452
  1.0 1.3 %collective-permute-start = (bf16[16,8192]{1,0:T(8,128)(2,1)S(1)}, bf16[16,8192]{1,0:T(8,128)(2,1)S(1)}, u32[]{:S(2)}, u32[]{:S(2)}) collective-permute-start(bf16[16,8192]{1,0:T(8,128)(2,1)S(1)} %slice_bitcast_fusion), channel_id=1, source_target_pairs={{1,0},{2,1},{3,2},{4,3},{5,4},{6,5},{7,6},{8,7},{9,8},{10,9},{11,1... | collective-permute-start | bytes 786440 | tf_op jit(solution)/shard_map/ppermute | solution.py:35
  2.3 6.4 %open.1.state_any = f32[6,4,16,512]{3,2,1,0:T(8,128)} custom-call(f32[4]{0:T(128)} %transfer_any.7, s32[128]{0:T(128)} %start_any.5, s32[128]{0:T(128)} %end_any.5, bf16[32,16,8192]{2,1,0:T(8,128)(2,1)} %field_any.5, f32[16,8192]{1,0:T(8,128)} %jitter_any.5), custom_call_target="tpu_custom_call" | custom-call | flops 31457280 | bytes 3145728 | tf_op jit(solution)/shard_map/open/pallas_call | solution.py:325
  8.8 0.0 copy-start.3
  8.8 0.0 collective-permute-done.halo_any
  8.8 0.0 copy-done
  8.8 0.0 copy-done.2
  8.8 0.0 copy-done.1
  8.8 4.4 %close.1 = (s16[4,16,512]{2,1,0:T(8,128)(2,1)S(1)}, s16[4,16,512]{2,1,0:T(8,128)(2,1)S(1)}, s16[4,16,512]{2,1,0:T(8,128)(2,1)S(1)}, s16[4,16,512]{2,1,0:T(8,128)...) custom-call(f32[4]{0:T(128)S(1)} %copy-done, ...), custom_call_target="tpu_custom_call" | custom-call | flops 10485760 | bytes 1048576 | tf_op jit(solution)/shard_map/close/pallas_call | solution.py:340
  13.2 4.8 %collective-permute-start.9 = (s16[4,16,512]{2,1,0:T(8,128)(2,1)S(1)}, s16[4,16,512]{2,1,0:T(8,128)(2,1)S(1)}, u32[]{:S(2)}, u32[]{:S(2)}) collective-permute-start(s16[4,16,512]{2,1,0:T(8,128)(2,1)S(1)} %get-tuple-element.30), channel_id=1, source_target_pairs={{0,9},{1,8},{2,11},{3,10},{4,13},{5,12},{6,15},{7,14},{8,1},{9,0},... | collective-permute-start | bytes 196616 | tf_op jit(solution)/shard_map/ppermute | solution.py:456
  18.0 1.3 %collective-permute-start.10 = (s16[4,16,512]{2,1,0:T(8,128)(2,1)S(1)}, s16[4,16,512]{2,1,0:T(8,128)(2,1)S(1)}, u32[]{:S(2)}, u32[]{:S(2)}) collective-permute-start(s16[4,16,512]{2,1,0:T(8,128)(2,1)S(1)} %get-tuple-element.31), channel_id=1, source_target_pairs={{0,10},{1,11},{2,8},{3,9},{4,14},{5,15},{6,12},{7,13},{8,2},{9,3},... | collective-permute-start | bytes 196616 | tf_op jit(solution)/shard_map/ppermute | solution.py:456
  19.3 2.7 %collective-permute-start.11 = (s16[4,16,512]{2,1,0:T(8,128)(2,1)S(1)}, s16[4,16,512]{2,1,0:T(8,128)(2,1)S(1)}, u32[]{:S(2)}, u32[]{:S(2)}) collective-permute-start(s16[4,16,512]{2,1,0:T(8,128)(2,1)S(1)} %get-tuple-element.32), channel_id=1, source_target_pairs={{0,11},{1,10},{2,9},{3,8},{4,15},{5,14},{6,13},{7,12},{8,3},{9,2},... | collective-permute-start | bytes 196616 | tf_op jit(solution)/shard_map/ppermute | solution.py:456
  22.0 1.3 %collective-permute-start.12 = (s16[4,16,512]{2,1,0:T(8,128)(2,1)S(1)}, s16[4,16,512]{2,1,0:T(8,128)(2,1)S(1)}, u32[]{:S(2)}, u32[]{:S(2)}) collective-permute-start(s16[4,16,512]{2,1,0:T(8,128)(2,1)S(1)} %get-tuple-element.33), channel_id=1, source_target_pairs={{0,12},{1,13},{2,14},{3,15},{4,8},{5,9},{6,10},{7,11},{8,4},{9,5},... | collective-permute-start | bytes 196616 | tf_op jit(solution)/shard_map/ppermute | solution.py:456
  23.4 1.7 %collective-permute-start.13 = (s16[4,16,512]{2,1,0:T(8,128)(2,1)S(1)}, s16[4,16,512]{2,1,0:T(8,128)(2,1)S(1)}, u32[]{:S(2)}, u32[]{:S(2)}) collective-permute-start(s16[4,16,512]{2,1,0:T(8,128)(2,1)S(1)} %get-tuple-element.34), channel_id=1, source_target_pairs={{0,13},{1,12},{2,15},{3,14},{4,9},{5,8},{6,11},{7,10},{8,5},{9,4},... | collective-permute-start | bytes 196616 | tf_op jit(solution)/shard_map/ppermute | solution.py:456
  25.1 0.0 collective-permute-done.9.refs_9_
  25.1 5.5 %collective-permute-start.14 = (s16[4,16,512]{2,1,0:T(8,128)(2,1)S(1)}, s16[4,16,512]{2,1,0:T(8,128)(2,1)S(1)}, u32[]{:S(2)}, u32[]{:S(2)}) collective-permute-start(s16[4,16,512]{2,1,0:T(8,128)(2,1)S(1)} %get-tuple-element.35), channel_id=1, source_target_pairs={{0,14},{1,15},{2,12},{3,13},{4,10},{5,11},{6,8},{7,9},{8,6},{9,7},... | collective-permute-start | bytes 196616 | tf_op jit(solution)/shard_map/ppermute | solution.py:456
  30.6 0.0 collective-permute-done.10.refs_10_
  30.6 3.2 %collective-permute-start.15 = (s16[4,16,512]{2,1,0:T(8,128)(2,1)S(1)}, s16[4,16,512]{2,1,0:T(8,128)(2,1)S(1)}, u32[]{:S(2)}, u32[]{:S(2)}) collective-permute-start(s16[4,16,512]{2,1,0:T(8,128)(2,1)S(1)} %get-tuple-element.36), channel_id=1, source_target_pairs={{0,15},{1,14},{2,13},{3,12},{4,11},{5,10},{6,9},{7,8},{8,7},{9,6},... | collective-permute-start | bytes 196616 | tf_op jit(solution)/shard_map/ppermute | solution.py:456
  33.8 8.3 %near.1 = (s16[4,16,512]{2,1,0:T(8,128)(2,1)S(1)}, s16[4,16,512]{2,1,0:T(8,128)(2,1)S(1)}, s16[4,16,512]{2,1,0:T(8,128)(2,1)S(1)}, s16[4,16,512]{2,1,0:T(8,128)(...) custom-call(f32[4]{0:T(128)S(1)} %copy-done, ...), custom_call_target="tpu_custom_call" | custom-call | flops 41943040 | bytes 4194304 | tf_op jit(solution)/shard_map/near/pallas_call | solution.py:358
  42.2 0.0 collective-permute-done.11.refs_11_
  42.2 0.1 collective-permute-start.8
  42.3 0.0 collective-permute-done.12.refs_12_
  42.3 0.5 collective-permute-start.1
  42.7 0.0 collective-permute-done.13.refs_13_
  42.8 0.9 %collective-permute-start.2 = (s16[4,16,512]{2,1,0:T(8,128)(2,1)S(1)}, s16[4,16,512]{2,1,0:T(8,128)(2,1)S(1)}, u32[]{:S(2)}, u32[]{:S(2)}) collective-permute-start(s16[4,16,512]{2,1,0:T(8,128)(2,1)S(1)} %get-tuple-element.24), channel_id=1, source_target_pairs={{0,2},{1,3},{2,0},{3,1},{4,6},{5,7},{6,4},{7,5},{8,10},{9,11},{10,... | collective-permute-start | bytes 196616 | tf_op jit(solution)/shard_map/ppermute | solution.py:456
  43.7 0.0 collective-permute-done.14.refs_14_
  43.7 0.5 collective-permute-start.3
  44.2 0.0 collective-permute-done.15.refs_15_
  44.2 1.2 %collective-permute-start.4 = (s16[4,16,512]{2,1,0:T(8,128)(2,1)S(1)}, s16[4,16,512]{2,1,0:T(8,128)(2,1)S(1)}, u32[]{:S(2)}, u32[]{:S(2)}) collective-permute-start(s16[4,16,512]{2,1,0:T(8,128)(2,1)S(1)} %get-tuple-element.26), channel_id=1, source_target_pairs={{0,4},{1,5},{2,6},{3,7},{4,0},{5,1},{6,2},{7,3},{8,12},{9,13},{10,... | collective-permute-start | bytes 196616 | tf_op jit(solution)/shard_map/ppermute | solution.py:456
  45.4 2.1 %collective-permute-done.8.refs_8_ = s16[4,16,512]{2,1,0:T(8,128)(2,1)S(1)} collective-permute-done((s16[4,16,512]{2,1,0:T(8,128)(2,1)S(1)}, s16[4,16,512]{2,1,0:T(8,128)(2,1)S(1)}, u32[]{:S(2)}, u32[]{:S(2)}) %collective-permute-start.8) | collective-permute-done | bytes 65568 | tf_op jit(solution)/shard_map/ppermute | solution.py:456
  47.6 0.0 collective-permute-start.5
  47.6 0.0 collective-permute-done.1.refs_1_
  47.6 1.7 %collective-permute-start.6 = (s16[4,16,512]{2,1,0:T(8,128)(2,1)S(1)}, s16[4,16,512]{2,1,0:T(8,128)(2,1)S(1)}, u32[]{:S(2)}, u32[]{:S(2)}) collective-permute-start(s16[4,16,512]{2,1,0:T(8,128)(2,1)S(1)} %get-tuple-element.28), channel_id=1, source_target_pairs={{0,6},{1,7},{2,4},{3,5},{4,2},{5,3},{6,0},{7,1},{8,14},{9,15},{10,... | collective-permute-start | bytes 196616 | tf_op jit(solution)/shard_map/ppermute | solution.py:456
  49.3 0.0 collective-permute-done.2.refs_2_
  49.3 0.4 collective-permute-start.7
  49.7 0.0 collective-permute-done.3.refs_3_
  49.7 0.0 collective-permute-done.4.refs_4_
  49.7 2.2 %collective-permute-done.5.refs_5_ = s16[4,16,512]{2,1,0:T(8,128)(2,1)S(1)} collective-permute-done((s16[4,16,512]{2,1,0:T(8,128)(2,1)S(1)}, s16[4,16,512]{2,1,0:T(8,128)(2,1)S(1)}, u32[]{:S(2)}, u32[]{:S(2)}) %collective-permute-start.5) | collective-permute-done | bytes 65568 | tf_op jit(solution)/shard_map/ppermute | solution.py:456
  52.0 1.6 %collective-permute-done.6.refs_6_ = s16[4,16,512]{2,1,0:T(8,128)(2,1)S(1)} collective-permute-done((s16[4,16,512]{2,1,0:T(8,128)(2,1)S(1)}, s16[4,16,512]{2,1,0:T(8,128)(2,1)S(1)}, u32[]{:S(2)}, u32[]{:S(2)}) %collective-permute-start.6) | collective-permute-done | bytes 65568 | tf_op jit(solution)/shard_map/ppermute | solution.py:456
  53.6 1.2 %collective-permute-done.7.refs_7_ = s16[4,16,512]{2,1,0:T(8,128)(2,1)S(1)} collective-permute-done((s16[4,16,512]{2,1,0:T(8,128)(2,1)S(1)}, s16[4,16,512]{2,1,0:T(8,128)(2,1)S(1)}, u32[]{:S(2)}, u32[]{:S(2)}) %collective-permute-start.7) | collective-permute-done | bytes 65568 | tf_op jit(solution)/shard_map/ppermute | solution.py:456
  54.8 0.0 copy-done.3
  54.8 2.9 %composite.1 = f32[4,16,512]{2,1,0:T(8,128)} custom-call(s32[16]{0:T(128)S(1)} %copy-done.3, f32[4]{0:T(128)S(1)} %copy-done, s16[4,16,512]{2,1,0:T(8,128)(2,1)S(1)} %get-tuple-element.22.refs_0_, s16[4,16,512]{2,1,0:T(8,128)(2,1)S(1)} %collective-permute-done.1.refs_1_, s16[4,16,512]{2,1,0:T(8,128)(2,1)S(1)} %collective-permute-done.2.refs_2_, ...), custom_call_target="tpu_custom_call" | custom-call | tf_op jit(solution)/shard_map/composite/pallas_call | solution.py:428
Async XLA Ops:
  0.0 8.8 %copy-start = (f32[4]{0:T(128)S(1)}, f32[4]{0:T(128)}, u32[]{:S(2)}) copy-start(f32[4]{0:T(128)} %transfer_any.7) | copy-start | bytes 52
  0.0 8.8 %copy-start.2 = (s32[128]{0:T(128)S(1)}, s32[128]{0:T(128)}, u32[]{:S(2)}) copy-start(s32[128]{0:T(128)} %end_any.5) | copy-start | bytes 1540
  0.0 8.8 %copy-start.1 = (s32[128]{0:T(128)S(1)}, s32[128]{0:T(128)}, u32[]{:S(2)}) copy-start(s32[128]{0:T(128)} %start_any.5) | copy-start | bytes 1540
  1.0 7.8 %collective-permute-start = (bf16[16,8192]{1,0:T(8,128)(2,1)S(1)}, bf16[16,8192]{1,0:T(8,128)(2,1)S(1)}, u32[]{:S(2)}, u32[]{:S(2)}) collective-permute-start(bf16[16,8192]{1,0:T(8,128)(2,1)S(1)} %slice_bitcast_fusion), channel_id=1, source_target_pairs={{1,0},{2,1},{3,2},{4,3},{5,4},{6,5},{7,6},{8,7},{9,8},{10,9},{11,1... | collective-permute-start | bytes 786440 | tf_op jit(solution)/shard_map/ppermute | solution.py:35
  8.8 46.0 %copy-start.3 = (s32[16]{0:T(128)S(1)}, s32[16]{0:T(128)}, u32[]{:S(2)}) copy-start(s32[16]{0:T(128)} %order_any.1) | copy-start | bytes 196
  13.2 11.9 %collective-permute-start.9 = (s16[4,16,512]{2,1,0:T(8,128)(2,1)S(1)}, s16[4,16,512]{2,1,0:T(8,128)(2,1)S(1)}, u32[]{:S(2)}, u32[]{:S(2)}) collective-permute-start(s16[4,16,512]{2,1,0:T(8,128)(2,1)S(1)} %get-tuple-element.30), channel_id=1, source_target_pairs={{0,9},{1,8},{2,11},{3,10},{4,13},{5,12},{6,15},{7,14},{8,1},{9,0},... | collective-permute-start | bytes 196616 | tf_op jit(solution)/shard_map/ppermute | solution.py:456
  18.0 12.6 %collective-permute-start.10 = (s16[4,16,512]{2,1,0:T(8,128)(2,1)S(1)}, s16[4,16,512]{2,1,0:T(8,128)(2,1)S(1)}, u32[]{:S(2)}, u32[]{:S(2)}) collective-permute-start(s16[4,16,512]{2,1,0:T(8,128)(2,1)S(1)} %get-tuple-element.31), channel_id=1, source_target_pairs={{0,10},{1,11},{2,8},{3,9},{4,14},{5,15},{6,12},{7,13},{8,2},{9,3},... | collective-permute-start | bytes 196616 | tf_op jit(solution)/shard_map/ppermute | solution.py:456
  19.3 22.9 %collective-permute-start.11 = (s16[4,16,512]{2,1,0:T(8,128)(2,1)S(1)}, s16[4,16,512]{2,1,0:T(8,128)(2,1)S(1)}, u32[]{:S(2)}, u32[]{:S(2)}) collective-permute-start(s16[4,16,512]{2,1,0:T(8,128)(2,1)S(1)} %get-tuple-element.32), channel_id=1, source_target_pairs={{0,11},{1,10},{2,9},{3,8},{4,15},{5,14},{6,13},{7,12},{8,3},{9,2},... | collective-permute-start | bytes 196616 | tf_op jit(solution)/shard_map/ppermute | solution.py:456
  22.0 20.2 %collective-permute-start.12 = (s16[4,16,512]{2,1,0:T(8,128)(2,1)S(1)}, s16[4,16,512]{2,1,0:T(8,128)(2,1)S(1)}, u32[]{:S(2)}, u32[]{:S(2)}) collective-permute-start(s16[4,16,512]{2,1,0:T(8,128)(2,1)S(1)} %get-tuple-element.33), channel_id=1, source_target_pairs={{0,12},{1,13},{2,14},{3,15},{4,8},{5,9},{6,10},{7,11},{8,4},{9,5},... | collective-permute-start | bytes 196616 | tf_op jit(solution)/shard_map/ppermute | solution.py:456
  23.4 19.4 %collective-permute-start.13 = (s16[4,16,512]{2,1,0:T(8,128)(2,1)S(1)}, s16[4,16,512]{2,1,0:T(8,128)(2,1)S(1)}, u32[]{:S(2)}, u32[]{:S(2)}) collective-permute-start(s16[4,16,512]{2,1,0:T(8,128)(2,1)S(1)} %get-tuple-element.34), channel_id=1, source_target_pairs={{0,13},{1,12},{2,15},{3,14},{4,9},{5,8},{6,11},{7,10},{8,5},{9,4},... | collective-permute-start | bytes 196616 | tf_op jit(solution)/shard_map/ppermute | solution.py:456
  25.1 18.5 %collective-permute-start.14 = (s16[4,16,512]{2,1,0:T(8,128)(2,1)S(1)}, s16[4,16,512]{2,1,0:T(8,128)(2,1)S(1)}, u32[]{:S(2)}, u32[]{:S(2)}) collective-permute-start(s16[4,16,512]{2,1,0:T(8,128)(2,1)S(1)} %get-tuple-element.35), channel_id=1, source_target_pairs={{0,14},{1,15},{2,12},{3,13},{4,10},{5,11},{6,8},{7,9},{8,6},{9,7},... | collective-permute-start | bytes 196616 | tf_op jit(solution)/shard_map/ppermute | solution.py:456
  30.6 13.6 %collective-permute-start.15 = (s16[4,16,512]{2,1,0:T(8,128)(2,1)S(1)}, s16[4,16,512]{2,1,0:T(8,128)(2,1)S(1)}, u32[]{:S(2)}, u32[]{:S(2)}) collective-permute-start(s16[4,16,512]{2,1,0:T(8,128)(2,1)S(1)} %get-tuple-element.36), channel_id=1, source_target_pairs={{0,15},{1,14},{2,13},{3,12},{4,11},{5,10},{6,9},{7,8},{8,7},{9,6},... | collective-permute-start | bytes 196616 | tf_op jit(solution)/shard_map/ppermute | solution.py:456
  42.2 5.4 %collective-permute-start.8 = (s16[4,16,512]{2,1,0:T(8,128)(2,1)S(1)}, s16[4,16,512]{2,1,0:T(8,128)(2,1)S(1)}, u32[]{:S(2)}, u32[]{:S(2)}) collective-permute-start(s16[4,16,512]{2,1,0:T(8,128)(2,1)S(1)} %get-tuple-element.21.far_any), channel_id=1, source_target_pairs={{0,8},{1,9},{2,10},{3,11},{4,12},{5,13},{6,14},{7,15},{8,0},{9,1},... | collective-permute-start | bytes 196616 | tf_op jit(solution)/shard_map/ppermute | solution.py:456
  42.3 5.3 %collective-permute-start.1 = (s16[4,16,512]{2,1,0:T(8,128)(2,1)S(1)}, s16[4,16,512]{2,1,0:T(8,128)(2,1)S(1)}, u32[]{:S(2)}, u32[]{:S(2)}) collective-permute-start(s16[4,16,512]{2,1,0:T(8,128)(2,1)S(1)} %get-tuple-element.23), channel_id=1, source_target_pairs={{0,1},{1,0},{2,3},{3,2},{4,5},{5,4},{6,7},{7,6},{8,9},{9,8},{10,11... | collective-permute-start | bytes 196616 | tf_op jit(solution)/shard_map/ppermute | solution.py:456
  42.8 6.5 %collective-permute-start.2 = (s16[4,16,512]{2,1,0:T(8,128)(2,1)S(1)}, s16[4,16,512]{2,1,0:T(8,128)(2,1)S(1)}, u32[]{:S(2)}, u32[]{:S(2)}) collective-permute-start(s16[4,16,512]{2,1,0:T(8,128)(2,1)S(1)} %get-tuple-element.24), channel_id=1, source_target_pairs={{0,2},{1,3},{2,0},{3,1},{4,6},{5,7},{6,4},{7,5},{8,10},{9,11},{10,... | collective-permute-start | bytes 196616 | tf_op jit(solution)/shard_map/ppermute | solution.py:456
  43.7 6.1 %collective-permute-start.3 = (s16[4,16,512]{2,1,0:T(8,128)(2,1)S(1)}, s16[4,16,512]{2,1,0:T(8,128)(2,1)S(1)}, u32[]{:S(2)}, u32[]{:S(2)}) collective-permute-start(s16[4,16,512]{2,1,0:T(8,128)(2,1)S(1)} %get-tuple-element.25), channel_id=1, source_target_pairs={{0,3},{1,2},{2,1},{3,0},{4,7},{5,6},{6,5},{7,4},{8,11},{9,10},{10,... | collective-permute-start | bytes 196616 | tf_op jit(solution)/shard_map/ppermute | solution.py:456
  44.2 5.5 %collective-permute-start.4 = (s16[4,16,512]{2,1,0:T(8,128)(2,1)S(1)}, s16[4,16,512]{2,1,0:T(8,128)(2,1)S(1)}, u32[]{:S(2)}, u32[]{:S(2)}) collective-permute-start(s16[4,16,512]{2,1,0:T(8,128)(2,1)S(1)} %get-tuple-element.26), channel_id=1, source_target_pairs={{0,4},{1,5},{2,6},{3,7},{4,0},{5,1},{6,2},{7,3},{8,12},{9,13},{10,... | collective-permute-start | bytes 196616 | tf_op jit(solution)/shard_map/ppermute | solution.py:456
  47.6 4.4 %collective-permute-start.5 = (s16[4,16,512]{2,1,0:T(8,128)(2,1)S(1)}, s16[4,16,512]{2,1,0:T(8,128)(2,1)S(1)}, u32[]{:S(2)}, u32[]{:S(2)}) collective-permute-start(s16[4,16,512]{2,1,0:T(8,128)(2,1)S(1)} %get-tuple-element.27), channel_id=1, source_target_pairs={{0,5},{1,4},{2,7},{3,6},{4,1},{5,0},{6,3},{7,2},{8,13},{9,12},{10,... | collective-permute-start | bytes 196616 | tf_op jit(solution)/shard_map/ppermute | solution.py:456
  47.6 6.0 %collective-permute-start.6 = (s16[4,16,512]{2,1,0:T(8,128)(2,1)S(1)}, s16[4,16,512]{2,1,0:T(8,128)(2,1)S(1)}, u32[]{:S(2)}, u32[]{:S(2)}) collective-permute-start(s16[4,16,512]{2,1,0:T(8,128)(2,1)S(1)} %get-tuple-element.28), channel_id=1, source_target_pairs={{0,6},{1,7},{2,4},{3,5},{4,2},{5,3},{6,0},{7,1},{8,14},{9,15},{10,... | collective-permute-start | bytes 196616 | tf_op jit(solution)/shard_map/ppermute | solution.py:456
  49.3 5.5 %collective-permute-start.7 = (s16[4,16,512]{2,1,0:T(8,128)(2,1)S(1)}, s16[4,16,512]{2,1,0:T(8,128)(2,1)S(1)}, u32[]{:S(2)}, u32[]{:S(2)}) collective-permute-start(s16[4,16,512]{2,1,0:T(8,128)(2,1)S(1)} %get-tuple-element.29), channel_id=1, source_target_pairs={{0,7},{1,6},{2,5},{3,4},{4,3},{5,2},{6,1},{7,0},{8,15},{9,14},{10,... | collective-permute-start | bytes 196616 | tf_op jit(solution)/shard_map/ppermute | solution.py:456

commit v18 on v16

--- a/solution.py
+++ b/solution.py
@@ -378,7 +378,7 @@
     image_any, order_ref, transfer_ref, code_ref, out_ref, sems, out_sems = refs[near:]
     count, _, rows, width = code_ref.shape
     here = lax.axis_index("depth")
-    pairs = [(near_any, code_ref.at[here ^ n]) for n, near_any in enumerate(near_anys)]
+    pairs = [(near_any, code_ref.at[here ^ n]) for n, near_any in zip(reversed(range(near)), near_anys)]
     if near:
         for n in range(count // near - 1):
             group = n + jnp.where(n >= here // near, 1, 0)
@@ -458,8 +458,8 @@
     if width != UNIT:
         codes = codes.transpose(1, 2, 0, 3).reshape(4, rows, count, width).transpose(2, 0, 1, 3)
     received = lax.all_to_all(codes, "depth", split_axis=0, concat_axis=0, tiled=True)
-    swapped = [lax.ppermute(near_codes[n], "depth", [(i, i ^ n) for i in range(count)]) for n in range(1, near)]
-    return composite(received, [*near_codes[:1], *swapped], transfer, depth_order, total, slab_len)
+    swapped = [lax.ppermute(near_codes[n], "depth", [(i, i ^ n) for i in range(count)]) for n in reversed(range(1, near))]
+    return composite(received, [*swapped, *near_codes[:1]], transfer, depth_order, total, slab_len)
 
 
 def solution(mesh):

time: 49.6 us -> 49.2 us (level)
  transfers between devices with their start and end apart: 9 -> 9, of which waited for: 6 -> 4; matrix products, arithmetic and copies ran while one was open for 0% -> 0% of each run, Pallas kernels for 30% -> 30%
where the time goes in v18:
time: 49.2 us; the launch traced here: 48.9 us
  Pallas kernels  21 us (43%)
  starting transfers between devices  17 us (35%)
  waiting for transfers between devices  9.75 us (20%)
  local copies, waits for them, and re-layouts  1.05 us (2%)
    ppermute x7, waiting for transfers between devices, on_device(): lax.ppermute(near_codes[n], 'depth', [(i, i ^ n) for i in range(count)])  9.74 us
    pallas_call x1, Pallas kernels, slab_codes(): pl.pallas_call(functools.partial(near_kernel, total, tile_cols, near), in...  8.36 us
    all_to_all x1, starting transfers between devices, on_device(): lax.all_to_all(codes, 'depth', split_axis=0, concat_axis=0, tiled=True)  8.16 us
    ppermute x7, starting transfers between devices, on_device(): lax.ppermute(near_codes[n], 'depth', [(i, i ^ n) for i in range(count)])  7.53 us
    pallas_call x1, Pallas kernels, slab_codes(): pl.pallas_call(functools.partial(open_kernel, total, tile_cols, near), in...  6.46 us
    pallas_call x1, Pallas kernels, slab_codes(): pl.pallas_call(functools.partial(close_kernel, total, tile_cols, near, op...  4.1 us
    pallas_call x1, Pallas kernels, composite(): pl.pallas_call(functools.partial(composite_kernel, total, slab_len, near)...  2.08 us
    ppermute x1, starting transfers between devices, shifted(): lax.ppermute(value, axis, [(source, source + steps) for source in range(i...  1.29 us
  transfers between devices with their start and end apart: 9, of which 4 were waited for; matrix products, arithmetic and copies ran while one was open for 0% of the time, Pallas kernels for 30%

profile of v18, /device:TPU:0, one launch (start us, length us, event | category | flops | bytes accessed | tf_op | source)
XLA Modules:
  0.0 48.9 jit_solution(2086655577349918250)
XLA Ops:
  0.0 0.0 copy-start.2
  0.0 0.0 copy-start.3
  0.0 0.0 copy-start
  0.0 0.0 copy-start.1
  0.0 1.0 %slice_bitcast_fusion = bf16[16,8192]{1,0:T(8,128)(2,1)S(1)} fusion(bf16[32,16,8192]{2,1,0:T(8,128)(2,1)} %field_any.5), kind=kLoop, calls=%fused_computation | loop fusion | bytes 524288 | tf_op jit(solution)/shard_map/squeeze | solution.py:456
  1.0 1.3 %collective-permute-start = (bf16[16,8192]{1,0:T(8,128)(2,1)S(1)}, bf16[16,8192]{1,0:T(8,128)(2,1)S(1)}, u32[]{:S(2)}, u32[]{:S(2)}) collective-permute-start(bf16[16,8192]{1,0:T(8,128)(2,1)S(1)} %slice_bitcast_fusion), channel_id=1, source_target_pairs={{1,0},{2,1},{3,2},{4,3},{5,4},{6,5},{7,6},{8,7},{9,8},{10,9},{11,1... | collective-permute-start | bytes 786440 | tf_op jit(solution)/shard_map/ppermute | solution.py:35
  2.3 6.5 %open.1.state_any = f32[6,4,16,512]{3,2,1,0:T(8,128)} custom-call(f32[4]{0:T(128)} %transfer_any.7, s32[128]{0:T(128)} %start_any.5, s32[128]{0:T(128)} %end_any.5, bf16[32,16,8192]{2,1,0:T(8,128)(2,1)} %field_any.5, f32[16,8192]{1,0:T(8,128)} %jitter_any.5), custom_call_target="tpu_custom_call" | custom-call | flops 31457280 | bytes 3145728 | tf_op jit(solution)/shard_map/open/pallas_call | solution.py:326
  8.8 0.0 collective-permute-done.halo_any
  8.8 0.0 copy-done.2
  8.8 0.0 copy-done.3
  8.8 0.0 copy-done
  8.8 0.0 copy-done.1
  8.9 4.1 %close.1.far_any = s16[16,4,16,512]{3,2,1,0:T(8,128)(2,1)} custom-call(f32[4]{0:T(128)S(1)} %copy-done.1, s32[128]{0:T(128)S(1)} %copy-done.2, s32[128]{0:T(128)S(1)} %copy-done.3, bf16[32,16,8192]{2,1,0:T(8,128)(2,1)} %field_any.5, bf16[16,8192]{1,0:T(8,128)(2,1)S(1)} %collective-permute-done.halo_any, f32[16,8192]{1,0:T(8,128)S(1)} %copy-done, ...), custom_call_target="tpu_custom_call" | custom-call | flops 10485760 | bytes 1048576 | tf_op jit(solution)/shard_map/close/pallas_call | solution.py:341
  13.0 0.0 copy-start.4
  13.0 8.2 %all-to-all-start = ((s16[16,4,16,512]{3,2,1,0:T(8,128)(2,1)}), s16[16,4,16,512]{3,2,1,0:T(8,128)(2,1)S(1)}, u32[]{:S(2)}, u32[]{:S(2)}) async-start(s16[16,4,16,512]{3,2,1,0:T(8,128)(2,1)} %close.1.far_any), calls=%async_computation | async-start | bytes 2097152 | tf_op jit(solution)/shard_map/all_to_all | solution.py:460
  21.1 8.4 %near.1 = (s16[4,16,512]{2,1,0:T(8,128)(2,1)S(1)}, s16[4,16,512]{2,1,0:T(8,128)(2,1)S(1)}, s16[4,16,512]{2,1,0:T(8,128)(2,1)S(1)}, s16[4,16,512]{2,1,0:T(8,128)(...) custom-call(f32[4]{0:T(128)S(1)} %copy-done.1, ...), custom_call_target="tpu_custom_call" | custom-call | flops 41943040 | bytes 4194304 | tf_op jit(solution)/shard_map/near/pallas_call | solution.py:359
  29.5 2.6 %collective-permute-start.1 = (s16[4,16,512]{2,1,0:T(8,128)(2,1)S(1)}, s16[4,16,512]{2,1,0:T(8,128)(2,1)S(1)}, u32[]{:S(2)}, u32[]{:S(2)}) collective-permute-start(s16[4,16,512]{2,1,0:T(8,128)(2,1)S(1)} %get-tuple-element.13), channel_id=1, source_target_pairs={{0,7},{1,6},{2,5},{3,4},{4,3},{5,2},{6,1},{7,0},{8,15},{9,14},{10,... | collective-permute-start | bytes 196616 | tf_op jit(solution)/shard_map/ppermute | solution.py:461
  32.1 0.4 collective-permute-start.2
  32.5 1.3 %collective-permute-start.3 = (s16[4,16,512]{2,1,0:T(8,128)(2,1)S(1)}, s16[4,16,512]{2,1,0:T(8,128)(2,1)S(1)}, u32[]{:S(2)}, u32[]{:S(2)}) collective-permute-start(s16[4,16,512]{2,1,0:T(8,128)(2,1)S(1)} %get-tuple-element.15), channel_id=1, source_target_pairs={{0,5},{1,4},{2,7},{3,6},{4,1},{5,0},{6,3},{7,2},{8,13},{9,12},{10,... | collective-permute-start | bytes 196616 | tf_op jit(solution)/shard_map/ppermute | solution.py:461
  33.9 0.4 collective-permute-start.4
  34.2 1.4 %collective-permute-start.5 = (s16[4,16,512]{2,1,0:T(8,128)(2,1)S(1)}, s16[4,16,512]{2,1,0:T(8,128)(2,1)S(1)}, u32[]{:S(2)}, u32[]{:S(2)}) collective-permute-start(s16[4,16,512]{2,1,0:T(8,128)(2,1)S(1)} %get-tuple-element.17), channel_id=1, source_target_pairs={{0,3},{1,2},{2,1},{3,0},{4,7},{5,6},{6,5},{7,4},{8,11},{9,10},{10,... | collective-permute-start | bytes 196616 | tf_op jit(solution)/shard_map/ppermute | solution.py:461
  35.7 5.6 %collective-permute-done.1.refs_0_ = s16[4,16,512]{2,1,0:T(8,128)(2,1)S(1)} collective-permute-done((s16[4,16,512]{2,1,0:T(8,128)(2,1)S(1)}, s16[4,16,512]{2,1,0:T(8,128)(2,1)S(1)}, u32[]{:S(2)}, u32[]{:S(2)}) %collective-permute-start.1) | collective-permute-done | bytes 65568 | tf_op jit(solution)/shard_map/ppermute | solution.py:461
  41.2 1.4 %collective-permute-start.6 = (s16[4,16,512]{2,1,0:T(8,128)(2,1)S(1)}, s16[4,16,512]{2,1,0:T(8,128)(2,1)S(1)}, u32[]{:S(2)}, u32[]{:S(2)}) collective-permute-start(s16[4,16,512]{2,1,0:T(8,128)(2,1)S(1)} %get-tuple-element.18), channel_id=1, source_target_pairs={{0,2},{1,3},{2,0},{3,1},{4,6},{5,7},{6,4},{7,5},{8,10},{9,11},{10,... | collective-permute-start | bytes 196616 | tf_op jit(solution)/shard_map/ppermute | solution.py:461
  42.6 0.4 collective-permute-done.2.refs_1_
  43.0 0.0 collective-permute-start.7
  43.0 1.4 %collective-permute-done.3.refs_2_ = s16[4,16,512]{2,1,0:T(8,128)(2,1)S(1)} collective-permute-done((s16[4,16,512]{2,1,0:T(8,128)(2,1)S(1)}, s16[4,16,512]{2,1,0:T(8,128)(2,1)S(1)}, u32[]{:S(2)}, u32[]{:S(2)}) %collective-permute-start.3) | collective-permute-done | bytes 65568 | tf_op jit(solution)/shard_map/ppermute | solution.py:461
  44.4 2.4 %collective-permute-done.4.refs_3_ = s16[4,16,512]{2,1,0:T(8,128)(2,1)S(1)} collective-permute-done((s16[4,16,512]{2,1,0:T(8,128)(2,1)S(1)}, s16[4,16,512]{2,1,0:T(8,128)(2,1)S(1)}, u32[]{:S(2)}, u32[]{:S(2)}) %collective-permute-start.4) | collective-permute-done | bytes 65568 | tf_op jit(solution)/shard_map/ppermute | solution.py:461
  46.8 0.0 collective-permute-done.5.refs_4_
  46.8 0.0 collective-permute-done.6.refs_5_
  46.8 0.0 collective-permute-done.7.refs_6_
  46.8 0.0 all-to-all-done.code_any
  46.8 0.0 copy-done.4
  46.8 2.1 %composite.1 = f32[4,16,512]{2,1,0:T(8,128)} custom-call(s32[16]{0:T(128)S(1)} %copy-done.4, f32[4]{0:T(128)S(1)} %copy-done.1, s16[16,4,16,512]{3,2,1,0:T(8,128)(2,1)S(1)} %all-to-all-done.code_any, s16[4,16,512]{2,1,0:T(8,128)(2,1)S(1)} %collective-permute-done.1.refs_0_, s16[4,16,512]{2,1,0:T(8,128)(2,1)S(1)} %collective-permute-done.2.refs_1_, ...), custom_call_target="tpu_custom_call" | custom-call | tf_op jit(solution)/shard_map/composite/pallas_call | solution.py:432
Async XLA Ops:
  0.0 8.8 %copy-start.2 = (s32[128]{0:T(128)S(1)}, s32[128]{0:T(128)}, u32[]{:S(2)}) copy-start(s32[128]{0:T(128)} %start_any.5) | copy-start | bytes 1540
  0.0 8.8 %copy-start.3 = (s32[128]{0:T(128)S(1)}, s32[128]{0:T(128)}, u32[]{:S(2)}) copy-start(s32[128]{0:T(128)} %end_any.5) | copy-start | bytes 1540
  0.0 8.8 %copy-start = (f32[16,8192]{1,0:T(8,128)S(1)}, f32[16,8192]{1,0:T(8,128)}, u32[]{:S(2)}) copy-start(f32[16,8192]{1,0:T(8,128)} %jitter_any.5) | copy-start | bytes 1572868
  0.0 8.8 %copy-start.1 = (f32[4]{0:T(128)S(1)}, f32[4]{0:T(128)}, u32[]{:S(2)}) copy-start(f32[4]{0:T(128)} %transfer_any.7) | copy-start | bytes 52
  1.0 7.8 %collective-permute-start = (bf16[16,8192]{1,0:T(8,128)(2,1)S(1)}, bf16[16,8192]{1,0:T(8,128)(2,1)S(1)}, u32[]{:S(2)}, u32[]{:S(2)}) collective-permute-start(bf16[16,8192]{1,0:T(8,128)(2,1)S(1)} %slice_bitcast_fusion), channel_id=1, source_target_pairs={{1,0},{2,1},{3,2},{4,3},{5,4},{6,5},{7,6},{8,7},{9,8},{10,9},{11,1... | collective-permute-start | bytes 786440 | tf_op jit(solution)/shard_map/ppermute | solution.py:35
  13.0 33.9 %copy-start.4 = (s32[16]{0:T(128)S(1)}, s32[16]{0:T(128)}, u32[]{:S(2)}) copy-start(s32[16]{0:T(128)} %order_any.1) | copy-start | bytes 196
  13.0 33.8 %all-to-all-start = ((s16[16,4,16,512]{3,2,1,0:T(8,128)(2,1)}), s16[16,4,16,512]{3,2,1,0:T(8,128)(2,1)S(1)}, u32[]{:S(2)}, u32[]{:S(2)}) async-start(s16[16,4,16,512]{3,2,1,0:T(8,128)(2,1)} %close.1.far_any), calls=%async_computation | async-start | bytes 2097152 | tf_op jit(solution)/shard_map/all_to_all | solution.py:460
  29.5 11.7 %collective-permute-start.1 = (s16[4,16,512]{2,1,0:T(8,128)(2,1)S(1)}, s16[4,16,512]{2,1,0:T(8,128)(2,1)S(1)}, u32[]{:S(2)}, u32[]{:S(2)}) collective-permute-start(s16[4,16,512]{2,1,0:T(8,128)(2,1)S(1)} %get-tuple-element.13), channel_id=1, source_target_pairs={{0,7},{1,6},{2,5},{3,4},{4,3},{5,2},{6,1},{7,0},{8,15},{9,14},{10,... | collective-permute-start | bytes 196616 | tf_op jit(solution)/shard_map/ppermute | solution.py:461
  32.1 10.9 %collective-permute-start.2 = (s16[4,16,512]{2,1,0:T(8,128)(2,1)S(1)}, s16[4,16,512]{2,1,0:T(8,128)(2,1)S(1)}, u32[]{:S(2)}, u32[]{:S(2)}) collective-permute-start(s16[4,16,512]{2,1,0:T(8,128)(2,1)S(1)} %get-tuple-element.14), channel_id=1, source_target_pairs={{0,6},{1,7},{2,4},{3,5},{4,2},{5,3},{6,0},{7,1},{8,14},{9,15},{10,... | collective-permute-start | bytes 196616 | tf_op jit(solution)/shard_map/ppermute | solution.py:461
  32.5 11.9 %collective-permute-start.3 = (s16[4,16,512]{2,1,0:T(8,128)(2,1)S(1)}, s16[4,16,512]{2,1,0:T(8,128)(2,1)S(1)}, u32[]{:S(2)}, u32[]{:S(2)}) collective-permute-start(s16[4,16,512]{2,1,0:T(8,128)(2,1)S(1)} %get-tuple-element.15), channel_id=1, source_target_pairs={{0,5},{1,4},{2,7},{3,6},{4,1},{5,0},{6,3},{7,2},{8,13},{9,12},{10,... | collective-permute-start | bytes 196616 | tf_op jit(solution)/shard_map/ppermute | solution.py:461
  33.9 12.9 %collective-permute-start.4 = (s16[4,16,512]{2,1,0:T(8,128)(2,1)S(1)}, s16[4,16,512]{2,1,0:T(8,128)(2,1)S(1)}, u32[]{:S(2)}, u32[]{:S(2)}) collective-permute-start(s16[4,16,512]{2,1,0:T(8,128)(2,1)S(1)} %get-tuple-element.16), channel_id=1, source_target_pairs={{0,4},{1,5},{2,6},{3,7},{4,0},{5,1},{6,2},{7,3},{8,12},{9,13},{10,... | collective-permute-start | bytes 196616 | tf_op jit(solution)/shard_map/ppermute | solution.py:461
  34.2 12.6 %collective-permute-start.5 = (s16[4,16,512]{2,1,0:T(8,128)(2,1)S(1)}, s16[4,16,512]{2,1,0:T(8,128)(2,1)S(1)}, u32[]{:S(2)}, u32[]{:S(2)}) collective-permute-start(s16[4,16,512]{2,1,0:T(8,128)(2,1)S(1)} %get-tuple-element.17), channel_id=1, source_target_pairs={{0,3},{1,2},{2,1},{3,0},{4,7},{5,6},{6,5},{7,4},{8,11},{9,10},{10,... | collective-permute-start | bytes 196616 | tf_op jit(solution)/shard_map/ppermute | solution.py:461
  41.2 5.6 %collective-permute-start.6 = (s16[4,16,512]{2,1,0:T(8,128)(2,1)S(1)}, s16[4,16,512]{2,1,0:T(8,128)(2,1)S(1)}, u32[]{:S(2)}, u32[]{:S(2)}) collective-permute-start(s16[4,16,512]{2,1,0:T(8,128)(2,1)S(1)} %get-tuple-element.18), channel_id=1, source_target_pairs={{0,2},{1,3},{2,0},{3,1},{4,6},{5,7},{6,4},{7,5},{8,10},{9,11},{10,... | collective-permute-start | bytes 196616 | tf_op jit(solution)/shard_map/ppermute | solution.py:461
  43.0 3.8 %collective-permute-start.7 = (s16[4,16,512]{2,1,0:T(8,128)(2,1)S(1)}, s16[4,16,512]{2,1,0:T(8,128)(2,1)S(1)}, u32[]{:S(2)}, u32[]{:S(2)}) collective-permute-start(s16[4,16,512]{2,1,0:T(8,128)(2,1)S(1)} %get-tuple-element.19), channel_id=1, source_target_pairs={{0,1},{1,0},{2,3},{3,2},{4,5},{5,4},{6,7},{7,6},{8,9},{9,8},{10,11... | collective-permute-start | bytes 196616 | tf_op jit(solution)/shard_map/ppermute | solution.py:461

commit v19 on v18

--- a/solution.py
+++ b/solution.py
@@ -138,6 +138,9 @@
     def close(self, n):
         return self.here ^ n
 
+    def close_first(self):
+        return self.here // self.near * self.near
+
 
 def columns(piece, col=0, size=UNIT):
     return pl.ds(pl.multiple_of(piece * UNIT + col, LANES), size)
@@ -159,7 +162,8 @@
     arrival = functools.partial(field_copy, field_any, plane_ref, sems, piece_of)
     for unit in range(2):
         arrival(unit).start()
-    pairs = [(transfer_any, transfer_ref), (start_any, start_ref), (end_any, end_ref), (jitter_any, jitter_ref)]
+    pairs = [(transfer_any, transfer_ref), (start_any, start_ref), (end_any, end_ref)]
+    pairs.append((jitter_any.at[:, columns(piece_of(0), 0, units * UNIT)], jitter_ref))
     *early, jitter_copy = start_all(pairs, few_sems)
     base = lax.axis_index("depth") * slab_len
     for copy in early:
@@ -172,8 +176,7 @@
     jitter_copy.wait()
 
     def compute(unit, cols, place):
-        jitter = jitter_ref[:, columns(piece_of(unit), cols.start, LANES)]
-        return march(gain_ref, plane_ref, unit, cols, place, jitter, levels)
+        return march(gain_ref, plane_ref, unit, cols, place, jitter_ref[:, place], levels)
 
     def store(unit, cols, result):
         sums, before = result
@@ -212,8 +215,10 @@
     arrival = functools.partial(field_copy, field_any, plane_ref, sems, later)
     for unit in range(2):
         arrival(unit).start()
-    pairs = [(transfer_any, transfer_ref), (start_any, start_ref), (end_any, end_ref), (jitter_any, jitter_ref)]
-    pairs += [(halo_any, halo_ref), (state_any, state_ref), (field_any.at[slab_len - 1], last_ref)]
+    mine = columns(piece_of(0), 0, (opened + units) * UNIT)
+    pairs = [(transfer_any, transfer_ref), (start_any, start_ref), (end_any, end_ref)]
+    pairs += [(jitter_any.at[:, mine], jitter_ref), (halo_any.at[:, mine], halo_ref), (state_any, state_ref)]
+    pairs.append((field_any.at[slab_len - 1, :, columns(piece_of(0), 0, opened * UNIT)], last_ref))
     copies = start_all(pairs, few_sems)
     base = lax.axis_index("depth") * slab_len
     for copy in copies[:3]:
@@ -227,7 +232,7 @@
         copy.wait()
 
     def compute(unit, cols, place):
-        whole = columns(later(unit), cols.start, LANES)
+        whole = columns(opened + unit, cols.start, LANES)
         jitter = jitter_ref[:, whole]
         return coder.codes(*march(gain_ref, plane_ref, unit, cols, place, jitter, coder.levels, halo_ref[:, whole]))
 
@@ -248,10 +253,9 @@
         copy.wait()
 
     def finish(unit, cols, place):
-        whole = columns(piece_of(unit), cols.start, LANES)
-        jitter = jitter_ref[:, whole]
-        lower = last_ref[:, whole].astype(jnp.float32)
-        upper = halo_ref[:, whole].astype(jnp.float32)
+        jitter = jitter_ref[:, place]
+        lower = last_ref[:, place].astype(jnp.float32)
+        upper = halo_ref[:, place].astype(jnp.float32)
         value = (1.0 - jitter) * lower + jitter * upper
         before = state_ref[unit, 3, :, cols]
         beyond = before + last_gain_ref[0:1, place] * value
@@ -273,8 +277,10 @@
     arrival = functools.partial(field_copy, field_any, plane_ref, sems, piece_of)
     for unit in range(2):
         arrival(unit).start()
-    pairs = [(transfer_any, transfer_ref), (start_any, start_ref), (end_any, end_ref), (jitter_any, jitter_ref)]
-    copies = start_all(pairs + [(halo_any, halo_ref)], few_sems)
+    first = Pieces(near).close_first()
+    mine = columns(first, 0, near * UNIT)
+    pairs = [(transfer_any, transfer_ref), (start_any, start_ref), (end_any, end_ref)]
+    copies = start_all(pairs + [(jitter_any.at[:, mine], jitter_ref), (halo_any.at[:, mine], halo_ref)], few_sems)
     base = lax.axis_index("depth") * slab_len
     for copy in copies[:3]:
         copy.wait()
@@ -286,7 +292,7 @@
         copy.wait()
 
     def compute(unit, cols, place):
-        whole = columns(piece_of(unit), cols.start, LANES)
+        whole = columns(piece_of(unit) - first, cols.start, LANES)
         jitter = jitter_ref[:, whole]
         return coder.codes(*march(gain_ref, plane_ref, unit, cols, place, jitter, coder.levels, halo_ref[:, whole]))
 
@@ -309,8 +315,6 @@
     tile_cols = cols // ntiles
     own = pl.BlockSpec(memory_space=pl.ANY)
     scalars = [pltpu.SMEM(transfer.shape, transfer.dtype)] + [pltpu.SMEM((ntiles,), jnp.int32)] * 2
-    plane = pltpu.VMEM((rows, cols), field.dtype)
-    lean = pltpu.VMEM((rows, cols), jnp.float32)
 
     def cost(units):
         work = slab_len * rows * units * UNIT
@@ -318,6 +322,9 @@
 
     def planes(units):
         return pltpu.VMEM((units, slab_len, rows, UNIT), field.dtype)
+
+    def flat(units, dtype):
+        return pltpu.VMEM((rows, units * UNIT), dtype)
 
     def table(samples, units):
         return pltpu.VMEM((samples, units * UNIT), jnp.float32)
@@ -329,7 +336,7 @@
         out_specs=own,
         out_shape=jax.ShapeDtypeStruct(state_shape, jnp.float32),
         scratch_shapes=scalars + [
-            planes(opened), lean, pltpu.VMEM(state_shape, jnp.float32), table(slab_len, opened),
+            planes(opened), flat(opened, jnp.float32), pltpu.VMEM(state_shape, jnp.float32), table(slab_len, opened),
             pltpu.SemaphoreType.DMA((4,)),
             pltpu.SemaphoreType.DMA((opened,)),
             pltpu.SemaphoreType.DMA((opened // 2,)),
@@ -344,8 +351,9 @@
         out_specs=own,
         out_shape=jax.ShapeDtypeStruct((pieces, 4, rows, UNIT), jnp.int16),
         scratch_shapes=scalars + [
-            planes(closed), plane, lean, pltpu.VMEM((opened + closed, 4, rows, UNIT), jnp.int16), table(slab_len, closed),
-            pltpu.VMEM(state_shape, jnp.float32), plane, table(SUBLANES, opened),
+            planes(closed), flat(opened + closed, field.dtype), flat(opened + closed, jnp.float32),
+            pltpu.VMEM((opened + closed, 4, rows, UNIT), jnp.int16), table(slab_len, closed),
+            pltpu.VMEM(state_shape, jnp.float32), flat(opened, field.dtype), table(SUBLANES, opened),
             pltpu.SemaphoreType.DMA((7,)),
             pltpu.SemaphoreType.DMA((closed,)),
             pltpu.SemaphoreType.DMA((opened + closed,)),
@@ -362,7 +370,7 @@
         out_specs=[own] * near,
         out_shape=[jax.ShapeDtypeStruct((4, rows, UNIT), jnp.int16)] * near,
         scratch_shapes=scalars + [
-            planes(near), plane, lean, pltpu.VMEM((near, 4, rows, UNIT), jnp.int16), table(slab_len, near),
+            planes(near), flat(near, field.dtype), flat(near, jnp.float32), pltpu.VMEM((near, 4, rows, UNIT), jnp.int16), table(slab_len, near),
             pltpu.SemaphoreType.DMA((5,)),
             pltpu.SemaphoreType.DMA((near,)),
             pltpu.SemaphoreType.DMA((near,)),
@@ -452,7 +460,7 @@
     slab_len, rows, cols = field.shape
     total = slab_len * count
     width = cols // count
-    near = NEAR if width == UNIT and count % (2 * NEAR) == 0 else 0
+    near = NEAR if width == UNIT and count == 2 * NEAR else 0
     halo = shifted(field[0], "depth", -1)
     codes, near_codes = slab_codes(field, halo, jitter, transfer, ray_start, ray_end, total, near)
     if width != UNIT:

time: 49.2 us -> 49.1 us (level)
  no operation moved by 1% of the time
where the time goes in v19:
time: 49.1 us; the launch traced here: 48.8 us
  Pallas kernels  20.8 us (42%)
  starting transfers between devices  17 us (35%)
  waiting for transfers between devices  9.83 us (20%)
  local copies, waits for them, and re-layouts  1.05 us (2%)
    ppermute x7, waiting for transfers between devices, on_device(): lax.ppermute(near_codes[n], 'depth', [(i, i ^ n) for i in range(count)])  9.82 us
    pallas_call x1, Pallas kernels, slab_codes(): pl.pallas_call(functools.partial(near_kernel, total, tile_cols, near), in...  8.28 us
    all_to_all x1, starting transfers between devices, on_device(): lax.all_to_all(codes, 'depth', split_axis=0, concat_axis=0, tiled=True)  8.16 us
    ppermute x7, starting transfers between devices, on_device(): lax.ppermute(near_codes[n], 'depth', [(i, i ^ n) for i in range(count)])  7.53 us
    pallas_call x1, Pallas kernels, slab_codes(): pl.pallas_call(functools.partial(open_kernel, total, tile_cols, near), in...  6.34 us
    pallas_call x1, Pallas kernels, slab_codes(): pl.pallas_call(functools.partial(close_kernel, total, tile_cols, near, op...  4.09 us
    pallas_call x1, Pallas kernels, composite(): pl.pallas_call(functools.partial(composite_kernel, total, slab_len, near)...  2.08 us
    ppermute x1, starting transfers between devices, shifted(): lax.ppermute(value, axis, [(source, source + steps) for source in range(i...  1.29 us
  transfers between devices with their start and end apart: 9, of which 4 were waited for; matrix products, arithmetic and copies ran while one was open for 0% of the time, Pallas kernels for 30%

profile of v19, /device:TPU:0, one launch (start us, length us, event | category | flops | bytes accessed | tf_op | source)
XLA Modules:
  0.0 48.8 jit_solution(16336532854329449234)
XLA Ops:
  0.0 0.0 copy-start.2
  0.0 0.0 copy-start.3
  0.0 0.0 copy-start
  0.0 0.0 copy-start.1
  0.0 1.0 %slice_bitcast_fusion = bf16[16,8192]{1,0:T(8,128)(2,1)S(1)} fusion(bf16[32,16,8192]{2,1,0:T(8,128)(2,1)} %field_any.5), kind=kLoop, calls=%fused_computation | loop fusion | bytes 524288 | tf_op jit(solution)/shard_map/squeeze | solution.py:464
  1.0 1.3 %collective-permute-start = (bf16[16,8192]{1,0:T(8,128)(2,1)S(1)}, bf16[16,8192]{1,0:T(8,128)(2,1)S(1)}, u32[]{:S(2)}, u32[]{:S(2)}) collective-permute-start(bf16[16,8192]{1,0:T(8,128)(2,1)S(1)} %slice_bitcast_fusion), channel_id=1, source_target_pairs={{1,0},{2,1},{3,2},{4,3},{5,4},{6,5},{7,6},{8,7},{9,8},{10,9},{11,1... | collective-permute-start | bytes 786440 | tf_op jit(solution)/shard_map/ppermute | solution.py:35
  2.3 6.3 %open.1.state_any = f32[6,4,16,512]{3,2,1,0:T(8,128)} custom-call(f32[4]{0:T(128)} %transfer_any.7, s32[128]{0:T(128)} %start_any.5, s32[128]{0:T(128)} %end_any.5, bf16[32,16,8192]{2,1,0:T(8,128)(2,1)} %field_any.5, f32[16,8192]{1,0:T(8,128)} %jitter_any.5), custom_call_target="tpu_custom_call" | custom-call | flops 31457280 | bytes 3145728 | tf_op jit(solution)/shard_map/open/pallas_call | solution.py:333
  8.7 0.0 collective-permute-done.halo_any
  8.7 0.0 copy-done.2
  8.7 0.0 copy-done.3
  8.7 0.0 copy-done
  8.7 0.0 copy-done.1
  8.7 4.1 %close.1.far_any = s16[16,4,16,512]{3,2,1,0:T(8,128)(2,1)} custom-call(f32[4]{0:T(128)S(1)} %copy-done.1, s32[128]{0:T(128)S(1)} %copy-done.2, s32[128]{0:T(128)S(1)} %copy-done.3, bf16[32,16,8192]{2,1,0:T(8,128)(2,1)} %field_any.5, bf16[16,8192]{1,0:T(8,128)(2,1)S(1)} %collective-permute-done.halo_any, f32[16,8192]{1,0:T(8,128)S(1)} %copy-done, ...), custom_call_target="tpu_custom_call" | custom-call | flops 10485760 | bytes 1048576 | tf_op jit(solution)/shard_map/close/pallas_call | solution.py:348
  12.8 0.0 copy-start.4
  12.9 8.2 %all-to-all-start = ((s16[16,4,16,512]{3,2,1,0:T(8,128)(2,1)}), s16[16,4,16,512]{3,2,1,0:T(8,128)(2,1)S(1)}, u32[]{:S(2)}, u32[]{:S(2)}) async-start(s16[16,4,16,512]{3,2,1,0:T(8,128)(2,1)} %close.1.far_any), calls=%async_computation | async-start | bytes 2097152 | tf_op jit(solution)/shard_map/all_to_all | solution.py:468
  21.0 8.3 %near.1 = (s16[4,16,512]{2,1,0:T(8,128)(2,1)S(1)}, s16[4,16,512]{2,1,0:T(8,128)(2,1)S(1)}, s16[4,16,512]{2,1,0:T(8,128)(2,1)S(1)}, s16[4,16,512]{2,1,0:T(8,128)(...) custom-call(f32[4]{0:T(128)S(1)} %copy-done.1, ...), custom_call_target="tpu_custom_call" | custom-call | flops 41943040 | bytes 4194304 | tf_op jit(solution)/shard_map/near/pallas_call | solution.py:367
  29.3 2.6 %collective-permute-start.1 = (s16[4,16,512]{2,1,0:T(8,128)(2,1)S(1)}, s16[4,16,512]{2,1,0:T(8,128)(2,1)S(1)}, u32[]{:S(2)}, u32[]{:S(2)}) collective-permute-start(s16[4,16,512]{2,1,0:T(8,128)(2,1)S(1)} %get-tuple-element.13), channel_id=1, source_target_pairs={{0,7},{1,6},{2,5},{3,4},{4,3},{5,2},{6,1},{7,0},{8,15},{9,14},{10,... | collective-permute-start | bytes 196616 | tf_op jit(solution)/shard_map/ppermute | solution.py:469
  31.9 0.4 collective-permute-start.2
  32.3 1.3 %collective-permute-start.3 = (s16[4,16,512]{2,1,0:T(8,128)(2,1)S(1)}, s16[4,16,512]{2,1,0:T(8,128)(2,1)S(1)}, u32[]{:S(2)}, u32[]{:S(2)}) collective-permute-start(s16[4,16,512]{2,1,0:T(8,128)(2,1)S(1)} %get-tuple-element.15), channel_id=1, source_target_pairs={{0,5},{1,4},{2,7},{3,6},{4,1},{5,0},{6,3},{7,2},{8,13},{9,12},{10,... | collective-permute-start | bytes 196616 | tf_op jit(solution)/shard_map/ppermute | solution.py:469
  33.7 0.4 collective-permute-start.4
  34.0 1.4 %collective-permute-start.5 = (s16[4,16,512]{2,1,0:T(8,128)(2,1)S(1)}, s16[4,16,512]{2,1,0:T(8,128)(2,1)S(1)}, u32[]{:S(2)}, u32[]{:S(2)}) collective-permute-start(s16[4,16,512]{2,1,0:T(8,128)(2,1)S(1)} %get-tuple-element.17), channel_id=1, source_target_pairs={{0,3},{1,2},{2,1},{3,0},{4,7},{5,6},{6,5},{7,4},{8,11},{9,10},{10,... | collective-permute-start | bytes 196616 | tf_op jit(solution)/shard_map/ppermute | solution.py:469
  35.5 5.7 %collective-permute-done.1.refs_0_ = s16[4,16,512]{2,1,0:T(8,128)(2,1)S(1)} collective-permute-done((s16[4,16,512]{2,1,0:T(8,128)(2,1)S(1)}, s16[4,16,512]{2,1,0:T(8,128)(2,1)S(1)}, u32[]{:S(2)}, u32[]{:S(2)}) %collective-permute-start.1) | collective-permute-done | bytes 65568 | tf_op jit(solution)/shard_map/ppermute | solution.py:469
  41.1 1.4 %collective-permute-start.6 = (s16[4,16,512]{2,1,0:T(8,128)(2,1)S(1)}, s16[4,16,512]{2,1,0:T(8,128)(2,1)S(1)}, u32[]{:S(2)}, u32[]{:S(2)}) collective-permute-start(s16[4,16,512]{2,1,0:T(8,128)(2,1)S(1)} %get-tuple-element.18), channel_id=1, source_target_pairs={{0,2},{1,3},{2,0},{3,1},{4,6},{5,7},{6,4},{7,5},{8,10},{9,11},{10,... | collective-permute-start | bytes 196616 | tf_op jit(solution)/shard_map/ppermute | solution.py:469
  42.5 0.4 collective-permute-done.2.refs_1_
  42.9 0.0 collective-permute-start.7
  42.9 1.4 %collective-permute-done.3.refs_2_ = s16[4,16,512]{2,1,0:T(8,128)(2,1)S(1)} collective-permute-done((s16[4,16,512]{2,1,0:T(8,128)(2,1)S(1)}, s16[4,16,512]{2,1,0:T(8,128)(2,1)S(1)}, u32[]{:S(2)}, u32[]{:S(2)}) %collective-permute-start.3) | collective-permute-done | bytes 65568 | tf_op jit(solution)/shard_map/ppermute | solution.py:469
  44.3 2.4 %collective-permute-done.4.refs_3_ = s16[4,16,512]{2,1,0:T(8,128)(2,1)S(1)} collective-permute-done((s16[4,16,512]{2,1,0:T(8,128)(2,1)S(1)}, s16[4,16,512]{2,1,0:T(8,128)(2,1)S(1)}, u32[]{:S(2)}, u32[]{:S(2)}) %collective-permute-start.4) | collective-permute-done | bytes 65568 | tf_op jit(solution)/shard_map/ppermute | solution.py:469
  46.7 0.0 collective-permute-done.5.refs_4_
  46.7 0.0 collective-permute-done.6.refs_5_
  46.7 0.0 collective-permute-done.7.refs_6_
  46.7 0.0 all-to-all-done.code_any
  46.7 0.0 copy-done.4
  46.7 2.1 %composite.1 = f32[4,16,512]{2,1,0:T(8,128)} custom-call(s32[16]{0:T(128)S(1)} %copy-done.4, f32[4]{0:T(128)S(1)} %copy-done.1, s16[16,4,16,512]{3,2,1,0:T(8,128)(2,1)S(1)} %all-to-all-done.code_any, s16[4,16,512]{2,1,0:T(8,128)(2,1)S(1)} %collective-permute-done.1.refs_0_, s16[4,16,512]{2,1,0:T(8,128)(2,1)S(1)} %collective-permute-done.2.refs_1_, ...), custom_call_target="tpu_custom_call" | custom-call | tf_op jit(solution)/shard_map/composite/pallas_call | solution.py:440
Async XLA Ops:
  0.0 8.7 %copy-start.2 = (s32[128]{0:T(128)S(1)}, s32[128]{0:T(128)}, u32[]{:S(2)}) copy-start(s32[128]{0:T(128)} %start_any.5) | copy-start | bytes 1540
  0.0 8.7 %copy-start.3 = (s32[128]{0:T(128)S(1)}, s32[128]{0:T(128)}, u32[]{:S(2)}) copy-start(s32[128]{0:T(128)} %end_any.5) | copy-start | bytes 1540
  0.0 8.7 %copy-start = (f32[16,8192]{1,0:T(8,128)S(1)}, f32[16,8192]{1,0:T(8,128)}, u32[]{:S(2)}) copy-start(f32[16,8192]{1,0:T(8,128)} %jitter_any.5) | copy-start | bytes 1572868
  0.0 8.7 %copy-start.1 = (f32[4]{0:T(128)S(1)}, f32[4]{0:T(128)}, u32[]{:S(2)}) copy-start(f32[4]{0:T(128)} %transfer_any.7) | copy-start | bytes 52
  1.0 7.7 %collective-permute-start = (bf16[16,8192]{1,0:T(8,128)(2,1)S(1)}, bf16[16,8192]{1,0:T(8,128)(2,1)S(1)}, u32[]{:S(2)}, u32[]{:S(2)}) collective-permute-start(bf16[16,8192]{1,0:T(8,128)(2,1)S(1)} %slice_bitcast_fusion), channel_id=1, source_target_pairs={{1,0},{2,1},{3,2},{4,3},{5,4},{6,5},{7,6},{8,7},{9,8},{10,9},{11,1... | collective-permute-start | bytes 786440 | tf_op jit(solution)/shard_map/ppermute | solution.py:35
  12.8 33.9 %copy-start.4 = (s32[16]{0:T(128)S(1)}, s32[16]{0:T(128)}, u32[]{:S(2)}) copy-start(s32[16]{0:T(128)} %order_any.1) | copy-start | bytes 196
  12.9 33.8 %all-to-all-start = ((s16[16,4,16,512]{3,2,1,0:T(8,128)(2,1)}), s16[16,4,16,512]{3,2,1,0:T(8,128)(2,1)S(1)}, u32[]{:S(2)}, u32[]{:S(2)}) async-start(s16[16,4,16,512]{3,2,1,0:T(8,128)(2,1)} %close.1.far_any), calls=%async_computation | async-start | bytes 2097152 | tf_op jit(solution)/shard_map/all_to_all | solution.py:468
  29.3 11.8 %collective-permute-start.1 = (s16[4,16,512]{2,1,0:T(8,128)(2,1)S(1)}, s16[4,16,512]{2,1,0:T(8,128)(2,1)S(1)}, u32[]{:S(2)}, u32[]{:S(2)}) collective-permute-start(s16[4,16,512]{2,1,0:T(8,128)(2,1)S(1)} %get-tuple-element.13), channel_id=1, source_target_pairs={{0,7},{1,6},{2,5},{3,4},{4,3},{5,2},{6,1},{7,0},{8,15},{9,14},{10,... | collective-permute-start | bytes 196616 | tf_op jit(solution)/shard_map/ppermute | solution.py:469
  31.9 11.0 %collective-permute-start.2 = (s16[4,16,512]{2,1,0:T(8,128)(2,1)S(1)}, s16[4,16,512]{2,1,0:T(8,128)(2,1)S(1)}, u32[]{:S(2)}, u32[]{:S(2)}) collective-permute-start(s16[4,16,512]{2,1,0:T(8,128)(2,1)S(1)} %get-tuple-element.14), channel_id=1, source_target_pairs={{0,6},{1,7},{2,4},{3,5},{4,2},{5,3},{6,0},{7,1},{8,14},{9,15},{10,... | collective-permute-start | bytes 196616 | tf_op jit(solution)/shard_map/ppermute | solution.py:469
  32.3 12.0 %collective-permute-start.3 = (s16[4,16,512]{2,1,0:T(8,128)(2,1)S(1)}, s16[4,16,512]{2,1,0:T(8,128)(2,1)S(1)}, u32[]{:S(2)}, u32[]{:S(2)}) collective-permute-start(s16[4,16,512]{2,1,0:T(8,128)(2,1)S(1)} %get-tuple-element.15), channel_id=1, source_target_pairs={{0,5},{1,4},{2,7},{3,6},{4,1},{5,0},{6,3},{7,2},{8,13},{9,12},{10,... | collective-permute-start | bytes 196616 | tf_op jit(solution)/shard_map/ppermute | solution.py:469
  33.7 13.0 %collective-permute-start.4 = (s16[4,16,512]{2,1,0:T(8,128)(2,1)S(1)}, s16[4,16,512]{2,1,0:T(8,128)(2,1)S(1)}, u32[]{:S(2)}, u32[]{:S(2)}) collective-permute-start(s16[4,16,512]{2,1,0:T(8,128)(2,1)S(1)} %get-tuple-element.16), channel_id=1, source_target_pairs={{0,4},{1,5},{2,6},{3,7},{4,0},{5,1},{6,2},{7,3},{8,12},{9,13},{10,... | collective-permute-start | bytes 196616 | tf_op jit(solution)/shard_map/ppermute | solution.py:469
  34.0 12.6 %collective-permute-start.5 = (s16[4,16,512]{2,1,0:T(8,128)(2,1)S(1)}, s16[4,16,512]{2,1,0:T(8,128)(2,1)S(1)}, u32[]{:S(2)}, u32[]{:S(2)}) collective-permute-start(s16[4,16,512]{2,1,0:T(8,128)(2,1)S(1)} %get-tuple-element.17), channel_id=1, source_target_pairs={{0,3},{1,2},{2,1},{3,0},{4,7},{5,6},{6,5},{7,4},{8,11},{9,10},{10,... | collective-permute-start | bytes 196616 | tf_op jit(solution)/shard_map/ppermute | solution.py:469
  41.1 5.6 %collective-permute-start.6 = (s16[4,16,512]{2,1,0:T(8,128)(2,1)S(1)}, s16[4,16,512]{2,1,0:T(8,128)(2,1)S(1)}, u32[]{:S(2)}, u32[]{:S(2)}) collective-permute-start(s16[4,16,512]{2,1,0:T(8,128)(2,1)S(1)} %get-tuple-element.18), channel_id=1, source_target_pairs={{0,2},{1,3},{2,0},{3,1},{4,6},{5,7},{6,4},{7,5},{8,10},{9,11},{10,... | collective-permute-start | bytes 196616 | tf_op jit(solution)/shard_map/ppermute | solution.py:469
  42.9 3.8 %collective-permute-start.7 = (s16[4,16,512]{2,1,0:T(8,128)(2,1)S(1)}, s16[4,16,512]{2,1,0:T(8,128)(2,1)S(1)}, u32[]{:S(2)}, u32[]{:S(2)}) collective-permute-start(s16[4,16,512]{2,1,0:T(8,128)(2,1)S(1)} %get-tuple-element.19), channel_id=1, source_target_pairs={{0,1},{1,0},{2,3},{3,2},{4,5},{5,4},{6,7},{7,6},{8,9},{9,8},{10,11... | collective-permute-start | bytes 196616 | tf_op jit(solution)/shard_map/ppermute | solution.py:469

commit v20 on v19

--- a/solution.py
+++ b/solution.py
@@ -106,16 +106,16 @@
     lax.fori_loop(0, count, step, 0)
 
 
-def each_pair(units, arrive, compute, store, leave):
+def each_group(units, group, arrive, compute, store, leave):
     def step(n):
-        places = [(2 * n + u, c) for u in range(2) for c in range(0, UNIT, LANES)]
+        places = [(group * n + u, c) for u in range(group) for c in range(0, UNIT, LANES)]
         arrive(n)
         results = [compute(unit, pl.ds(c, LANES), pl.ds(pl.multiple_of(unit * UNIT + c, LANES), LANES)) for unit, c in places]
         for (unit, c), result in zip(places, results):
             store(unit, pl.ds(c, LANES), result)
         leave(n)
 
-    loop(units // 2, step)
+    loop(units // group, step)
 
 
 def start_all(pairs, sems):
@@ -187,7 +187,7 @@
         place = pl.ds(2 * n, 2)
         return pltpu.make_async_copy(state_ref.at[place], state_any.at[place], out_sems.at[n])
 
-    each_pair(units, functools.partial(arrive_pair, arrival), compute, store, lambda n: leave(n).start())
+    each_group(units, 2, functools.partial(arrive_pair, arrival), compute, store, lambda n: leave(n).start())
     loop(units // 2, lambda n: leave(n).wait())
 
 
@@ -247,7 +247,7 @@
         for u in range(2):
             leave(first + 2 * n + u).start()
 
-    each_pair(units, functools.partial(arrive_pair, arrival), compute, functools.partial(store, opened),
+    each_group(units, 2, functools.partial(arrive_pair, arrival), compute, functools.partial(store, opened),
               functools.partial(leave_pair, opened))
     for copy in copies[5:]:
         copy.wait()
@@ -264,7 +264,13 @@
         moment(sums, weight, value, coder.levels)
         return coder.codes(sums, beyond)
 
-    each_pair(opened, lambda n: None, finish, functools.partial(store, 0), functools.partial(leave_pair, 0))
+    group = math.gcd(opened, 3)
+
+    def leave_finished(n):
+        for u in range(group):
+            leave(group * n + u).start()
+
+    each_group(opened, group, lambda n: None, finish, functools.partial(store, 0), leave_finished)
     loop(out_ref.shape[0], lambda unit: leave(unit).wait())
 
 
@@ -300,7 +306,7 @@
         for i, code in enumerate(codes):
             out_ref[unit, i, :, cols] = code
 
-    each_pair(units, functools.partial(arrive_pair, arrival), compute, store, lambda n: None)
+    each_group(units, 2, functools.partial(arrive_pair, arrival), compute, store, lambda n: None)
     pairs = [(out_ref.at[unit], out_anys[unit]) for unit in range(units)]
     for copy in start_all(pairs, out_sems):
         copy.wait()
@@ -422,7 +428,7 @@
 
         zero = jnp.zeros(shape, jnp.float32)
         first = jnp.full(shape, -lift(color_span))
-        shift, *colors = lax.fori_loop(0, count, step, (first, zero, zero, zero), unroll=math.gcd(count, 4))
+        shift, *colors = lax.fori_loop(0, count, step, (first, zero, zero, zero), unroll=math.gcd(count, 16))
         for i in range(3):
             out_ref[i, :, cols] = colors[i] * (unit * (TOP / (transfer_ref[i] + jnp.full(shape, TOP))))
         out_ref[3, :, cols] = 1.0 - jnp.exp2(first - shift)

time: 49.1 us -> 49.1 us (level)
  no operation moved by 1% of the time
where the time goes in v20:
time: 49.1 us; the launch traced here: 48.7 us
  Pallas kernels  20.7 us (42%)
  starting transfers between devices  17 us (35%)
  waiting for transfers between devices  9.83 us (20%)
  local copies, waits for them, and re-layouts  1.05 us (2%)
    ppermute x7, waiting for transfers between devices, on_device(): lax.ppermute(near_codes[n], 'depth', [(i, i ^ n) for i in range(count)])  9.82 us
    pallas_call x1, Pallas kernels, slab_codes(): pl.pallas_call(functools.partial(near_kernel, total, tile_cols, near), in...  8.28 us
    all_to_all x1, starting transfers between devices, on_device(): lax.all_to_all(codes, 'depth', split_axis=0, concat_axis=0, tiled=True)  8.16 us
    ppermute x7, starting transfers between devices, on_device(): lax.ppermute(near_codes[n], 'depth', [(i, i ^ n) for i in range(count)])  7.53 us
    pallas_call x1, Pallas kernels, slab_codes(): pl.pallas_call(functools.partial(open_kernel, total, tile_cols, near), in...  6.34 us
    pallas_call x1, Pallas kernels, slab_codes(): pl.pallas_call(functools.partial(close_kernel, total, tile_cols, near, op...  4.1 us
    pallas_call x1, Pallas kernels, composite(): pl.pallas_call(functools.partial(composite_kernel, total, slab_len, near)...  2.01 us
    ppermute x1, starting transfers between devices, shifted(): lax.ppermute(value, axis, [(source, source + steps) for source in range(i...  1.29 us
  transfers between devices with their start and end apart: 9, of which 4 were waited for; matrix products, arithmetic and copies ran while one was open for 0% of the time, Pallas kernels for 30%

profile of v20, /device:TPU:0, one launch (start us, length us, event | category | flops | bytes accessed | tf_op | source)
XLA Modules:
  0.0 48.7 jit_solution(10635721917778930118)
XLA Ops:
  0.0 0.0 copy-start.2
  0.0 0.0 copy-start.3
  0.0 0.0 copy-start
  0.0 0.0 copy-start.1
  0.0 1.0 %slice_bitcast_fusion = bf16[16,8192]{1,0:T(8,128)(2,1)S(1)} fusion(bf16[32,16,8192]{2,1,0:T(8,128)(2,1)} %field_any.5), kind=kLoop, calls=%fused_computation | loop fusion | bytes 524288 | tf_op jit(solution)/shard_map/squeeze | solution.py:470
  1.0 1.3 %collective-permute-start = (bf16[16,8192]{1,0:T(8,128)(2,1)S(1)}, bf16[16,8192]{1,0:T(8,128)(2,1)S(1)}, u32[]{:S(2)}, u32[]{:S(2)}) collective-permute-start(bf16[16,8192]{1,0:T(8,128)(2,1)S(1)} %slice_bitcast_fusion), channel_id=1, source_target_pairs={{1,0},{2,1},{3,2},{4,3},{5,4},{6,5},{7,6},{8,7},{9,8},{10,9},{11,1... | collective-permute-start | bytes 786440 | tf_op jit(solution)/shard_map/ppermute | solution.py:35
  2.3 6.3 %open.1.state_any = f32[6,4,16,512]{3,2,1,0:T(8,128)} custom-call(f32[4]{0:T(128)} %transfer_any.7, s32[128]{0:T(128)} %start_any.5, s32[128]{0:T(128)} %end_any.5, bf16[32,16,8192]{2,1,0:T(8,128)(2,1)} %field_any.5, f32[16,8192]{1,0:T(8,128)} %jitter_any.5), custom_call_target="tpu_custom_call" | custom-call | flops 31457280 | bytes 3145728 | tf_op jit(solution)/shard_map/open/pallas_call | solution.py:339
  8.7 0.0 collective-permute-done.halo_any
  8.7 0.0 copy-done.2
  8.7 0.0 copy-done.3
  8.7 0.0 copy-done
  8.7 0.0 copy-done.1
  8.7 4.1 %close.1.far_any = s16[16,4,16,512]{3,2,1,0:T(8,128)(2,1)} custom-call(f32[4]{0:T(128)S(1)} %copy-done.1, s32[128]{0:T(128)S(1)} %copy-done.2, s32[128]{0:T(128)S(1)} %copy-done.3, bf16[32,16,8192]{2,1,0:T(8,128)(2,1)} %field_any.5, bf16[16,8192]{1,0:T(8,128)(2,1)S(1)} %collective-permute-done.halo_any, f32[16,8192]{1,0:T(8,128)S(1)} %copy-done, ...), custom_call_target="tpu_custom_call" | custom-call | flops 10485760 | bytes 1048576 | tf_op jit(solution)/shard_map/close/pallas_call | solution.py:354
  12.8 0.0 copy-start.4
  12.9 8.2 %all-to-all-start = ((s16[16,4,16,512]{3,2,1,0:T(8,128)(2,1)}), s16[16,4,16,512]{3,2,1,0:T(8,128)(2,1)S(1)}, u32[]{:S(2)}, u32[]{:S(2)}) async-start(s16[16,4,16,512]{3,2,1,0:T(8,128)(2,1)} %close.1.far_any), calls=%async_computation | async-start | bytes 2097152 | tf_op jit(solution)/shard_map/all_to_all | solution.py:474
  21.0 8.3 %near.1 = (s16[4,16,512]{2,1,0:T(8,128)(2,1)S(1)}, s16[4,16,512]{2,1,0:T(8,128)(2,1)S(1)}, s16[4,16,512]{2,1,0:T(8,128)(2,1)S(1)}, s16[4,16,512]{2,1,0:T(8,128)(...) custom-call(f32[4]{0:T(128)S(1)} %copy-done.1, ...), custom_call_target="tpu_custom_call" | custom-call | flops 41943040 | bytes 4194304 | tf_op jit(solution)/shard_map/near/pallas_call | solution.py:373
  29.3 2.6 %collective-permute-start.1 = (s16[4,16,512]{2,1,0:T(8,128)(2,1)S(1)}, s16[4,16,512]{2,1,0:T(8,128)(2,1)S(1)}, u32[]{:S(2)}, u32[]{:S(2)}) collective-permute-start(s16[4,16,512]{2,1,0:T(8,128)(2,1)S(1)} %get-tuple-element.13), channel_id=1, source_target_pairs={{0,7},{1,6},{2,5},{3,4},{4,3},{5,2},{6,1},{7,0},{8,15},{9,14},{10,... | collective-permute-start | bytes 196616 | tf_op jit(solution)/shard_map/ppermute | solution.py:475
  31.9 0.4 collective-permute-start.2
  32.3 1.3 %collective-permute-start.3 = (s16[4,16,512]{2,1,0:T(8,128)(2,1)S(1)}, s16[4,16,512]{2,1,0:T(8,128)(2,1)S(1)}, u32[]{:S(2)}, u32[]{:S(2)}) collective-permute-start(s16[4,16,512]{2,1,0:T(8,128)(2,1)S(1)} %get-tuple-element.15), channel_id=1, source_target_pairs={{0,5},{1,4},{2,7},{3,6},{4,1},{5,0},{6,3},{7,2},{8,13},{9,12},{10,... | collective-permute-start | bytes 196616 | tf_op jit(solution)/shard_map/ppermute | solution.py:475
  33.7 0.4 collective-permute-start.4
  34.0 1.4 %collective-permute-start.5 = (s16[4,16,512]{2,1,0:T(8,128)(2,1)S(1)}, s16[4,16,512]{2,1,0:T(8,128)(2,1)S(1)}, u32[]{:S(2)}, u32[]{:S(2)}) collective-permute-start(s16[4,16,512]{2,1,0:T(8,128)(2,1)S(1)} %get-tuple-element.17), channel_id=1, source_target_pairs={{0,3},{1,2},{2,1},{3,0},{4,7},{5,6},{6,5},{7,4},{8,11},{9,10},{10,... | collective-permute-start | bytes 196616 | tf_op jit(solution)/shard_map/ppermute | solution.py:475
  35.5 5.7 %collective-permute-done.1.refs_0_ = s16[4,16,512]{2,1,0:T(8,128)(2,1)S(1)} collective-permute-done((s16[4,16,512]{2,1,0:T(8,128)(2,1)S(1)}, s16[4,16,512]{2,1,0:T(8,128)(2,1)S(1)}, u32[]{:S(2)}, u32[]{:S(2)}) %collective-permute-start.1) | collective-permute-done | bytes 65568 | tf_op jit(solution)/shard_map/ppermute | solution.py:475
  41.1 1.4 %collective-permute-start.6 = (s16[4,16,512]{2,1,0:T(8,128)(2,1)S(1)}, s16[4,16,512]{2,1,0:T(8,128)(2,1)S(1)}, u32[]{:S(2)}, u32[]{:S(2)}) collective-permute-start(s16[4,16,512]{2,1,0:T(8,128)(2,1)S(1)} %get-tuple-element.18), channel_id=1, source_target_pairs={{0,2},{1,3},{2,0},{3,1},{4,6},{5,7},{6,4},{7,5},{8,10},{9,11},{10,... | collective-permute-start | bytes 196616 | tf_op jit(solution)/shard_map/ppermute | solution.py:475
  42.5 0.4 collective-permute-done.2.refs_1_
  42.9 0.0 collective-permute-start.7
  42.9 1.4 %collective-permute-done.3.refs_2_ = s16[4,16,512]{2,1,0:T(8,128)(2,1)S(1)} collective-permute-done((s16[4,16,512]{2,1,0:T(8,128)(2,1)S(1)}, s16[4,16,512]{2,1,0:T(8,128)(2,1)S(1)}, u32[]{:S(2)}, u32[]{:S(2)}) %collective-permute-start.3) | collective-permute-done | bytes 65568 | tf_op jit(solution)/shard_map/ppermute | solution.py:475
  44.3 2.4 %collective-permute-done.4.refs_3_ = s16[4,16,512]{2,1,0:T(8,128)(2,1)S(1)} collective-permute-done((s16[4,16,512]{2,1,0:T(8,128)(2,1)S(1)}, s16[4,16,512]{2,1,0:T(8,128)(2,1)S(1)}, u32[]{:S(2)}, u32[]{:S(2)}) %collective-permute-start.4) | collective-permute-done | bytes 65568 | tf_op jit(solution)/shard_map/ppermute | solution.py:475
  46.7 0.0 collective-permute-done.5.refs_4_
  46.7 0.0 collective-permute-done.6.refs_5_
  46.7 0.0 collective-permute-done.7.refs_6_
  46.7 0.0 all-to-all-done.code_any
  46.7 0.0 copy-done.4
  46.7 2.0 %composite.1 = f32[4,16,512]{2,1,0:T(8,128)} custom-call(s32[16]{0:T(128)S(1)} %copy-done.4, f32[4]{0:T(128)S(1)} %copy-done.1, s16[16,4,16,512]{3,2,1,0:T(8,128)(2,1)S(1)} %all-to-all-done.code_any, s16[4,16,512]{2,1,0:T(8,128)(2,1)S(1)} %collective-permute-done.1.refs_0_, s16[4,16,512]{2,1,0:T(8,128)(2,1)S(1)} %collective-permute-done.2.refs_1_, ...), custom_call_target="tpu_custom_call" | custom-call | tf_op jit(solution)/shard_map/composite/pallas_call | solution.py:446
Async XLA Ops:
  0.0 8.7 %copy-start.2 = (s32[128]{0:T(128)S(1)}, s32[128]{0:T(128)}, u32[]{:S(2)}) copy-start(s32[128]{0:T(128)} %start_any.5) | copy-start | bytes 1540
  0.0 8.7 %copy-start.3 = (s32[128]{0:T(128)S(1)}, s32[128]{0:T(128)}, u32[]{:S(2)}) copy-start(s32[128]{0:T(128)} %end_any.5) | copy-start | bytes 1540
  0.0 8.7 %copy-start = (f32[16,8192]{1,0:T(8,128)S(1)}, f32[16,8192]{1,0:T(8,128)}, u32[]{:S(2)}) copy-start(f32[16,8192]{1,0:T(8,128)} %jitter_any.5) | copy-start | bytes 1572868
  0.0 8.7 %copy-start.1 = (f32[4]{0:T(128)S(1)}, f32[4]{0:T(128)}, u32[]{:S(2)}) copy-start(f32[4]{0:T(128)} %transfer_any.7) | copy-start | bytes 52
  1.0 7.7 %collective-permute-start = (bf16[16,8192]{1,0:T(8,128)(2,1)S(1)}, bf16[16,8192]{1,0:T(8,128)(2,1)S(1)}, u32[]{:S(2)}, u32[]{:S(2)}) collective-permute-start(bf16[16,8192]{1,0:T(8,128)(2,1)S(1)} %slice_bitcast_fusion), channel_id=1, source_target_pairs={{1,0},{2,1},{3,2},{4,3},{5,4},{6,5},{7,6},{8,7},{9,8},{10,9},{11,1... | collective-permute-start | bytes 786440 | tf_op jit(solution)/shard_map/ppermute | solution.py:35
  12.8 33.8 %copy-start.4 = (s32[16]{0:T(128)S(1)}, s32[16]{0:T(128)}, u32[]{:S(2)}) copy-start(s32[16]{0:T(128)} %order_any.1) | copy-start | bytes 196
  12.9 33.8 %all-to-all-start = ((s16[16,4,16,512]{3,2,1,0:T(8,128)(2,1)}), s16[16,4,16,512]{3,2,1,0:T(8,128)(2,1)S(1)}, u32[]{:S(2)}, u32[]{:S(2)}) async-start(s16[16,4,16,512]{3,2,1,0:T(8,128)(2,1)} %close.1.far_any), calls=%async_computation | async-start | bytes 2097152 | tf_op jit(solution)/shard_map/all_to_all | solution.py:474
  29.3 11.8 %collective-permute-start.1 = (s16[4,16,512]{2,1,0:T(8,128)(2,1)S(1)}, s16[4,16,512]{2,1,0:T(8,128)(2,1)S(1)}, u32[]{:S(2)}, u32[]{:S(2)}) collective-permute-start(s16[4,16,512]{2,1,0:T(8,128)(2,1)S(1)} %get-tuple-element.13), channel_id=1, source_target_pairs={{0,7},{1,6},{2,5},{3,4},{4,3},{5,2},{6,1},{7,0},{8,15},{9,14},{10,... | collective-permute-start | bytes 196616 | tf_op jit(solution)/shard_map/ppermute | solution.py:475
  31.9 11.0 %collective-permute-start.2 = (s16[4,16,512]{2,1,0:T(8,128)(2,1)S(1)}, s16[4,16,512]{2,1,0:T(8,128)(2,1)S(1)}, u32[]{:S(2)}, u32[]{:S(2)}) collective-permute-start(s16[4,16,512]{2,1,0:T(8,128)(2,1)S(1)} %get-tuple-element.14), channel_id=1, source_target_pairs={{0,6},{1,7},{2,4},{3,5},{4,2},{5,3},{6,0},{7,1},{8,14},{9,15},{10,... | collective-permute-start | bytes 196616 | tf_op jit(solution)/shard_map/ppermute | solution.py:475
  32.3 12.0 %collective-permute-start.3 = (s16[4,16,512]{2,1,0:T(8,128)(2,1)S(1)}, s16[4,16,512]{2,1,0:T(8,128)(2,1)S(1)}, u32[]{:S(2)}, u32[]{:S(2)}) collective-permute-start(s16[4,16,512]{2,1,0:T(8,128)(2,1)S(1)} %get-tuple-element.15), channel_id=1, source_target_pairs={{0,5},{1,4},{2,7},{3,6},{4,1},{5,0},{6,3},{7,2},{8,13},{9,12},{10,... | collective-permute-start | bytes 196616 | tf_op jit(solution)/shard_map/ppermute | solution.py:475
  33.7 13.0 %collective-permute-start.4 = (s16[4,16,512]{2,1,0:T(8,128)(2,1)S(1)}, s16[4,16,512]{2,1,0:T(8,128)(2,1)S(1)}, u32[]{:S(2)}, u32[]{:S(2)}) collective-permute-start(s16[4,16,512]{2,1,0:T(8,128)(2,1)S(1)} %get-tuple-element.16), channel_id=1, source_target_pairs={{0,4},{1,5},{2,6},{3,7},{4,0},{5,1},{6,2},{7,3},{8,12},{9,13},{10,... | collective-permute-start | bytes 196616 | tf_op jit(solution)/shard_map/ppermute | solution.py:475
  34.0 12.6 %collective-permute-start.5 = (s16[4,16,512]{2,1,0:T(8,128)(2,1)S(1)}, s16[4,16,512]{2,1,0:T(8,128)(2,1)S(1)}, u32[]{:S(2)}, u32[]{:S(2)}) collective-permute-start(s16[4,16,512]{2,1,0:T(8,128)(2,1)S(1)} %get-tuple-element.17), channel_id=1, source_target_pairs={{0,3},{1,2},{2,1},{3,0},{4,7},{5,6},{6,5},{7,4},{8,11},{9,10},{10,... | collective-permute-start | bytes 196616 | tf_op jit(solution)/shard_map/ppermute | solution.py:475
  41.1 5.6 %collective-permute-start.6 = (s16[4,16,512]{2,1,0:T(8,128)(2,1)S(1)}, s16[4,16,512]{2,1,0:T(8,128)(2,1)S(1)}, u32[]{:S(2)}, u32[]{:S(2)}) collective-permute-start(s16[4,16,512]{2,1,0:T(8,128)(2,1)S(1)} %get-tuple-element.18), channel_id=1, source_target_pairs={{0,2},{1,3},{2,0},{3,1},{4,6},{5,7},{6,4},{7,5},{8,10},{9,11},{10,... | collective-permute-start | bytes 196616 | tf_op jit(solution)/shard_map/ppermute | solution.py:475
  42.9 3.8 %collective-permute-start.7 = (s16[4,16,512]{2,1,0:T(8,128)(2,1)S(1)}, s16[4,16,512]{2,1,0:T(8,128)(2,1)S(1)}, u32[]{:S(2)}, u32[]{:S(2)}) collective-permute-start(s16[4,16,512]{2,1,0:T(8,128)(2,1)S(1)} %get-tuple-element.19), channel_id=1, source_target_pairs={{0,1},{1,0},{2,3},{3,2},{4,5},{5,4},{6,7},{7,6},{8,9},{9,8},{10,11... | collective-permute-start | bytes 196616 | tf_op jit(solution)/shard_map/ppermute | solution.py:475

commit v21 on v20

--- a/solution.py
+++ b/solution.py
@@ -160,11 +160,11 @@
     units, slab_len, rows, _ = plane_ref.shape
     piece_of = Pieces(near).far
     arrival = functools.partial(field_copy, field_any, plane_ref, sems, piece_of)
+    early = start_all([(transfer_any, transfer_ref), (start_any, start_ref), (end_any, end_ref)], few_sems)
     for unit in range(2):
         arrival(unit).start()
-    pairs = [(transfer_any, transfer_ref), (start_any, start_ref), (end_any, end_ref)]
-    pairs.append((jitter_any.at[:, columns(piece_of(0), 0, units * UNIT)], jitter_ref))
-    *early, jitter_copy = start_all(pairs, few_sems)
+    jitter_copy = pltpu.make_async_copy(jitter_any.at[:, columns(piece_of(0), 0, units * UNIT)], jitter_ref, few_sems.at[3])
+    jitter_copy.start()
     base = lax.axis_index("depth") * slab_len
     for copy in early:
         copy.wait()
@@ -213,13 +213,13 @@
     piece_of = Pieces(near).far
     later = lambda unit: piece_of(opened + unit)
     arrival = functools.partial(field_copy, field_any, plane_ref, sems, later)
+    copies = start_all([(transfer_any, transfer_ref), (start_any, start_ref), (end_any, end_ref)], few_sems)
     for unit in range(2):
         arrival(unit).start()
     mine = columns(piece_of(0), 0, (opened + units) * UNIT)
-    pairs = [(transfer_any, transfer_ref), (start_any, start_ref), (end_any, end_ref)]
-    pairs += [(jitter_any.at[:, mine], jitter_ref), (halo_any.at[:, mine], halo_ref), (state_any, state_ref)]
+    pairs = [(jitter_any.at[:, mine], jitter_ref), (halo_any.at[:, mine], halo_ref), (state_any, state_ref)]
     pairs.append((field_any.at[slab_len - 1, :, columns(piece_of(0), 0, opened * UNIT)], last_ref))
-    copies = start_all(pairs, few_sems)
+    copies += start_all(pairs, few_sems.at[pl.ds(3, len(pairs))])
     base = lax.axis_index("depth") * slab_len
     for copy in copies[:3]:
         copy.wait()
@@ -281,12 +281,12 @@
     units, slab_len, rows, _ = plane_ref.shape
     piece_of = Pieces(near).close
     arrival = functools.partial(field_copy, field_any, plane_ref, sems, piece_of)
+    copies = start_all([(transfer_any, transfer_ref), (start_any, start_ref), (end_any, end_ref)], few_sems)
     for unit in range(2):
         arrival(unit).start()
     first = Pieces(near).close_first()
     mine = columns(first, 0, near * UNIT)
-    pairs = [(transfer_any, transfer_ref), (start_any, start_ref), (end_any, end_ref)]
-    copies = start_all(pairs + [(jitter_any.at[:, mine], jitter_ref), (halo_any.at[:, mine], halo_ref)], few_sems)
+    copies += start_all([(jitter_any.at[:, mine], jitter_ref), (halo_any.at[:, mine], halo_ref)], few_sems.at[pl.ds(3, 2)])
     base = lax.axis_index("depth") * slab_len
     for copy in copies[:3]:
         copy.wait()

time: 49.1 us -> 49.1 us (level)
  no operation moved by 1% of the time
where the time goes in v21:
time: 49.1 us; the launch traced here: 48.7 us
  Pallas kernels  20.7 us (42%)
  starting transfers between devices  17 us (35%)
  waiting for transfers between devices  9.83 us (20%)
  local copies, waits for them, and re-layouts  1.05 us (2%)
    ppermute x7, waiting for transfers between devices, on_device(): lax.ppermute(near_codes[n], 'depth', [(i, i ^ n) for i in range(count)])  9.82 us
    pallas_call x1, Pallas kernels, slab_codes(): pl.pallas_call(functools.partial(near_kernel, total, tile_cols, near), in...  8.28 us
    all_to_all x1, starting transfers between devices, on_device(): lax.all_to_all(codes, 'depth', split_axis=0, concat_axis=0, tiled=True)  8.16 us
    ppermute x7, starting transfers between devices, on_device(): lax.ppermute(near_codes[n], 'depth', [(i, i ^ n) for i in range(count)])  7.53 us
    pallas_call x1, Pallas kernels, slab_codes(): pl.pallas_call(functools.partial(open_kernel, total, tile_cols, near), in...  6.35 us
    pallas_call x1, Pallas kernels, slab_codes(): pl.pallas_call(functools.partial(close_kernel, total, tile_cols, near, op...  4.1 us
    pallas_call x1, Pallas kernels, composite(): pl.pallas_call(functools.partial(composite_kernel, total, slab_len, near)...  2.01 us
    ppermute x1, starting transfers between devices, shifted(): lax.ppermute(value, axis, [(source, source + steps) for source in range(i...  1.29 us
  transfers between devices with their start and end apart: 9, of which 4 were waited for; matrix products, arithmetic and copies ran while one was open for 0% of the time, Pallas kernels for 30%

profile of v21, /device:TPU:0, one launch (start us, length us, event | category | flops | bytes accessed | tf_op | source)
XLA Modules:
  0.0 48.7 jit_solution(11258655698950938665)
XLA Ops:
  0.0 0.0 copy-start.2
  0.0 0.0 copy-start.3
  0.0 0.0 copy-start
  0.0 0.0 copy-start.1
  0.0 1.0 %slice_bitcast_fusion = bf16[16,8192]{1,0:T(8,128)(2,1)S(1)} fusion(bf16[32,16,8192]{2,1,0:T(8,128)(2,1)} %field_any.5), kind=kLoop, calls=%fused_computation | loop fusion | bytes 524288 | tf_op jit(solution)/shard_map/squeeze | solution.py:470
  1.0 1.3 %collective-permute-start = (bf16[16,8192]{1,0:T(8,128)(2,1)S(1)}, bf16[16,8192]{1,0:T(8,128)(2,1)S(1)}, u32[]{:S(2)}, u32[]{:S(2)}) collective-permute-start(bf16[16,8192]{1,0:T(8,128)(2,1)S(1)} %slice_bitcast_fusion), channel_id=1, source_target_pairs={{1,0},{2,1},{3,2},{4,3},{5,4},{6,5},{7,6},{8,7},{9,8},{10,9},{11,1... | collective-permute-start | bytes 786440 | tf_op jit(solution)/shard_map/ppermute | solution.py:35
  2.3 6.3 %open.1.state_any = f32[6,4,16,512]{3,2,1,0:T(8,128)} custom-call(f32[4]{0:T(128)} %transfer_any.7, s32[128]{0:T(128)} %start_any.5, s32[128]{0:T(128)} %end_any.5, bf16[32,16,8192]{2,1,0:T(8,128)(2,1)} %field_any.5, f32[16,8192]{1,0:T(8,128)} %jitter_any.5), custom_call_target="tpu_custom_call" | custom-call | flops 31457280 | bytes 3145728 | tf_op jit(solution)/shard_map/open/pallas_call | solution.py:339
  8.7 0.0 collective-permute-done.halo_any
  8.7 0.0 copy-done.2
  8.7 0.0 copy-done.3
  8.7 0.0 copy-done
  8.7 0.0 copy-done.1
  8.7 4.1 %close.1.far_any = s16[16,4,16,512]{3,2,1,0:T(8,128)(2,1)} custom-call(f32[4]{0:T(128)S(1)} %copy-done.1, s32[128]{0:T(128)S(1)} %copy-done.2, s32[128]{0:T(128)S(1)} %copy-done.3, bf16[32,16,8192]{2,1,0:T(8,128)(2,1)} %field_any.5, bf16[16,8192]{1,0:T(8,128)(2,1)S(1)} %collective-permute-done.halo_any, f32[16,8192]{1,0:T(8,128)S(1)} %copy-done, ...), custom_call_target="tpu_custom_call" | custom-call | flops 10485760 | bytes 1048576 | tf_op jit(solution)/shard_map/close/pallas_call | solution.py:354
  12.8 0.0 copy-start.4
  12.9 8.2 %all-to-all-start = ((s16[16,4,16,512]{3,2,1,0:T(8,128)(2,1)}), s16[16,4,16,512]{3,2,1,0:T(8,128)(2,1)S(1)}, u32[]{:S(2)}, u32[]{:S(2)}) async-start(s16[16,4,16,512]{3,2,1,0:T(8,128)(2,1)} %close.1.far_any), calls=%async_computation | async-start | bytes 2097152 | tf_op jit(solution)/shard_map/all_to_all | solution.py:474
  21.0 8.3 %near.1 = (s16[4,16,512]{2,1,0:T(8,128)(2,1)S(1)}, s16[4,16,512]{2,1,0:T(8,128)(2,1)S(1)}, s16[4,16,512]{2,1,0:T(8,128)(2,1)S(1)}, s16[4,16,512]{2,1,0:T(8,128)(...) custom-call(f32[4]{0:T(128)S(1)} %copy-done.1, ...), custom_call_target="tpu_custom_call" | custom-call | flops 41943040 | bytes 4194304 | tf_op jit(solution)/shard_map/near/pallas_call | solution.py:373
  29.3 2.6 %collective-permute-start.1 = (s16[4,16,512]{2,1,0:T(8,128)(2,1)S(1)}, s16[4,16,512]{2,1,0:T(8,128)(2,1)S(1)}, u32[]{:S(2)}, u32[]{:S(2)}) collective-permute-start(s16[4,16,512]{2,1,0:T(8,128)(2,1)S(1)} %get-tuple-element.13), channel_id=1, source_target_pairs={{0,7},{1,6},{2,5},{3,4},{4,3},{5,2},{6,1},{7,0},{8,15},{9,14},{10,... | collective-permute-start | bytes 196616 | tf_op jit(solution)/shard_map/ppermute | solution.py:475
  32.0 0.4 collective-permute-start.2
  32.3 1.3 %collective-permute-start.3 = (s16[4,16,512]{2,1,0:T(8,128)(2,1)S(1)}, s16[4,16,512]{2,1,0:T(8,128)(2,1)S(1)}, u32[]{:S(2)}, u32[]{:S(2)}) collective-permute-start(s16[4,16,512]{2,1,0:T(8,128)(2,1)S(1)} %get-tuple-element.15), channel_id=1, source_target_pairs={{0,5},{1,4},{2,7},{3,6},{4,1},{5,0},{6,3},{7,2},{8,13},{9,12},{10,... | collective-permute-start | bytes 196616 | tf_op jit(solution)/shard_map/ppermute | solution.py:475
  33.7 0.4 collective-permute-start.4
  34.0 1.4 %collective-permute-start.5 = (s16[4,16,512]{2,1,0:T(8,128)(2,1)S(1)}, s16[4,16,512]{2,1,0:T(8,128)(2,1)S(1)}, u32[]{:S(2)}, u32[]{:S(2)}) collective-permute-start(s16[4,16,512]{2,1,0:T(8,128)(2,1)S(1)} %get-tuple-element.17), channel_id=1, source_target_pairs={{0,3},{1,2},{2,1},{3,0},{4,7},{5,6},{6,5},{7,4},{8,11},{9,10},{10,... | collective-permute-start | bytes 196616 | tf_op jit(solution)/shard_map/ppermute | solution.py:475
  35.5 5.7 %collective-permute-done.1.refs_0_ = s16[4,16,512]{2,1,0:T(8,128)(2,1)S(1)} collective-permute-done((s16[4,16,512]{2,1,0:T(8,128)(2,1)S(1)}, s16[4,16,512]{2,1,0:T(8,128)(2,1)S(1)}, u32[]{:S(2)}, u32[]{:S(2)}) %collective-permute-start.1) | collective-permute-done | bytes 65568 | tf_op jit(solution)/shard_map/ppermute | solution.py:475
  41.1 1.4 %collective-permute-start.6 = (s16[4,16,512]{2,1,0:T(8,128)(2,1)S(1)}, s16[4,16,512]{2,1,0:T(8,128)(2,1)S(1)}, u32[]{:S(2)}, u32[]{:S(2)}) collective-permute-start(s16[4,16,512]{2,1,0:T(8,128)(2,1)S(1)} %get-tuple-element.18), channel_id=1, source_target_pairs={{0,2},{1,3},{2,0},{3,1},{4,6},{5,7},{6,4},{7,5},{8,10},{9,11},{10,... | collective-permute-start | bytes 196616 | tf_op jit(solution)/shard_map/ppermute | solution.py:475
  42.5 0.4 collective-permute-done.2.refs_1_
  42.9 0.0 collective-permute-start.7
  42.9 1.4 %collective-permute-done.3.refs_2_ = s16[4,16,512]{2,1,0:T(8,128)(2,1)S(1)} collective-permute-done((s16[4,16,512]{2,1,0:T(8,128)(2,1)S(1)}, s16[4,16,512]{2,1,0:T(8,128)(2,1)S(1)}, u32[]{:S(2)}, u32[]{:S(2)}) %collective-permute-start.3) | collective-permute-done | bytes 65568 | tf_op jit(solution)/shard_map/ppermute | solution.py:475
  44.3 2.4 %collective-permute-done.4.refs_3_ = s16[4,16,512]{2,1,0:T(8,128)(2,1)S(1)} collective-permute-done((s16[4,16,512]{2,1,0:T(8,128)(2,1)S(1)}, s16[4,16,512]{2,1,0:T(8,128)(2,1)S(1)}, u32[]{:S(2)}, u32[]{:S(2)}) %collective-permute-start.4) | collective-permute-done | bytes 65568 | tf_op jit(solution)/shard_map/ppermute | solution.py:475
  46.7 0.0 collective-permute-done.5.refs_4_
  46.7 0.0 collective-permute-done.6.refs_5_
  46.7 0.0 collective-permute-done.7.refs_6_
  46.7 0.0 all-to-all-done.code_any
  46.7 0.0 copy-done.4
  46.7 2.0 %composite.1 = f32[4,16,512]{2,1,0:T(8,128)} custom-call(s32[16]{0:T(128)S(1)} %copy-done.4, f32[4]{0:T(128)S(1)} %copy-done.1, s16[16,4,16,512]{3,2,1,0:T(8,128)(2,1)S(1)} %all-to-all-done.code_any, s16[4,16,512]{2,1,0:T(8,128)(2,1)S(1)} %collective-permute-done.1.refs_0_, s16[4,16,512]{2,1,0:T(8,128)(2,1)S(1)} %collective-permute-done.2.refs_1_, ...), custom_call_target="tpu_custom_call" | custom-call | tf_op jit(solution)/shard_map/composite/pallas_call | solution.py:446
Async XLA Ops:
  0.0 8.7 %copy-start.2 = (s32[128]{0:T(128)S(1)}, s32[128]{0:T(128)}, u32[]{:S(2)}) copy-start(s32[128]{0:T(128)} %start_any.5) | copy-start | bytes 1540
  0.0 8.7 %copy-start.3 = (s32[128]{0:T(128)S(1)}, s32[128]{0:T(128)}, u32[]{:S(2)}) copy-start(s32[128]{0:T(128)} %end_any.5) | copy-start | bytes 1540
  0.0 8.7 %copy-start = (f32[16,8192]{1,0:T(8,128)S(1)}, f32[16,8192]{1,0:T(8,128)}, u32[]{:S(2)}) copy-start(f32[16,8192]{1,0:T(8,128)} %jitter_any.5) | copy-start | bytes 1572868
  0.0 8.7 %copy-start.1 = (f32[4]{0:T(128)S(1)}, f32[4]{0:T(128)}, u32[]{:S(2)}) copy-start(f32[4]{0:T(128)} %transfer_any.7) | copy-start | bytes 52
  1.0 7.7 %collective-permute-start = (bf16[16,8192]{1,0:T(8,128)(2,1)S(1)}, bf16[16,8192]{1,0:T(8,128)(2,1)S(1)}, u32[]{:S(2)}, u32[]{:S(2)}) collective-permute-start(bf16[16,8192]{1,0:T(8,128)(2,1)S(1)} %slice_bitcast_fusion), channel_id=1, source_target_pairs={{1,0},{2,1},{3,2},{4,3},{5,4},{6,5},{7,6},{8,7},{9,8},{10,9},{11,1... | collective-permute-start | bytes 786440 | tf_op jit(solution)/shard_map/ppermute | solution.py:35
  12.8 33.8 %copy-start.4 = (s32[16]{0:T(128)S(1)}, s32[16]{0:T(128)}, u32[]{:S(2)}) copy-start(s32[16]{0:T(128)} %order_any.1) | copy-start | bytes 196
  12.9 33.8 %all-to-all-start = ((s16[16,4,16,512]{3,2,1,0:T(8,128)(2,1)}), s16[16,4,16,512]{3,2,1,0:T(8,128)(2,1)S(1)}, u32[]{:S(2)}, u32[]{:S(2)}) async-start(s16[16,4,16,512]{3,2,1,0:T(8,128)(2,1)} %close.1.far_any), calls=%async_computation | async-start | bytes 2097152 | tf_op jit(solution)/shard_map/all_to_all | solution.py:474
  29.3 11.8 %collective-permute-start.1 = (s16[4,16,512]{2,1,0:T(8,128)(2,1)S(1)}, s16[4,16,512]{2,1,0:T(8,128)(2,1)S(1)}, u32[]{:S(2)}, u32[]{:S(2)}) collective-permute-start(s16[4,16,512]{2,1,0:T(8,128)(2,1)S(1)} %get-tuple-element.13), channel_id=1, source_target_pairs={{0,7},{1,6},{2,5},{3,4},{4,3},{5,2},{6,1},{7,0},{8,15},{9,14},{10,... | collective-permute-start | bytes 196616 | tf_op jit(solution)/shard_map/ppermute | solution.py:475
  32.0 11.0 %collective-permute-start.2 = (s16[4,16,512]{2,1,0:T(8,128)(2,1)S(1)}, s16[4,16,512]{2,1,0:T(8,128)(2,1)S(1)}, u32[]{:S(2)}, u32[]{:S(2)}) collective-permute-start(s16[4,16,512]{2,1,0:T(8,128)(2,1)S(1)} %get-tuple-element.14), channel_id=1, source_target_pairs={{0,6},{1,7},{2,4},{3,5},{4,2},{5,3},{6,0},{7,1},{8,14},{9,15},{10,... | collective-permute-start | bytes 196616 | tf_op jit(solution)/shard_map/ppermute | solution.py:475
  32.3 12.0 %collective-permute-start.3 = (s16[4,16,512]{2,1,0:T(8,128)(2,1)S(1)}, s16[4,16,512]{2,1,0:T(8,128)(2,1)S(1)}, u32[]{:S(2)}, u32[]{:S(2)}) collective-permute-start(s16[4,16,512]{2,1,0:T(8,128)(2,1)S(1)} %get-tuple-element.15), channel_id=1, source_target_pairs={{0,5},{1,4},{2,7},{3,6},{4,1},{5,0},{6,3},{7,2},{8,13},{9,12},{10,... | collective-permute-start | bytes 196616 | tf_op jit(solution)/shard_map/ppermute | solution.py:475
  33.7 13.0 %collective-permute-start.4 = (s16[4,16,512]{2,1,0:T(8,128)(2,1)S(1)}, s16[4,16,512]{2,1,0:T(8,128)(2,1)S(1)}, u32[]{:S(2)}, u32[]{:S(2)}) collective-permute-start(s16[4,16,512]{2,1,0:T(8,128)(2,1)S(1)} %get-tuple-element.16), channel_id=1, source_target_pairs={{0,4},{1,5},{2,6},{3,7},{4,0},{5,1},{6,2},{7,3},{8,12},{9,13},{10,... | collective-permute-start | bytes 196616 | tf_op jit(solution)/shard_map/ppermute | solution.py:475
  34.0 12.6 %collective-permute-start.5 = (s16[4,16,512]{2,1,0:T(8,128)(2,1)S(1)}, s16[4,16,512]{2,1,0:T(8,128)(2,1)S(1)}, u32[]{:S(2)}, u32[]{:S(2)}) collective-permute-start(s16[4,16,512]{2,1,0:T(8,128)(2,1)S(1)} %get-tuple-element.17), channel_id=1, source_target_pairs={{0,3},{1,2},{2,1},{3,0},{4,7},{5,6},{6,5},{7,4},{8,11},{9,10},{10,... | collective-permute-start | bytes 196616 | tf_op jit(solution)/shard_map/ppermute | solution.py:475
  41.1 5.6 %collective-permute-start.6 = (s16[4,16,512]{2,1,0:T(8,128)(2,1)S(1)}, s16[4,16,512]{2,1,0:T(8,128)(2,1)S(1)}, u32[]{:S(2)}, u32[]{:S(2)}) collective-permute-start(s16[4,16,512]{2,1,0:T(8,128)(2,1)S(1)} %get-tuple-element.18), channel_id=1, source_target_pairs={{0,2},{1,3},{2,0},{3,1},{4,6},{5,7},{6,4},{7,5},{8,10},{9,11},{10,... | collective-permute-start | bytes 196616 | tf_op jit(solution)/shard_map/ppermute | solution.py:475
  42.9 3.8 %collective-permute-start.7 = (s16[4,16,512]{2,1,0:T(8,128)(2,1)S(1)}, s16[4,16,512]{2,1,0:T(8,128)(2,1)S(1)}, u32[]{:S(2)}, u32[]{:S(2)}) collective-permute-start(s16[4,16,512]{2,1,0:T(8,128)(2,1)S(1)} %get-tuple-element.19), channel_id=1, source_target_pairs={{0,1},{1,0},{2,3},{3,2},{4,5},{5,4},{6,7},{7,6},{8,9},{9,8},{10,11... | collective-permute-start | bytes 196616 | tf_op jit(solution)/shard_map/ppermute | solution.py:475

commit v22 on v20

--- a/solution.py
+++ b/solution.py
@@ -135,8 +135,8 @@
             return n
         return n + jnp.where(n >= self.here // self.near * self.near, self.near, 0)
 
-    def close(self, n):
-        return self.here ^ n
+    def close(self, top, jump, unit):
+        return self.here ^ (top - unit - jnp.where(unit >= jump, 2, 0))
 
     def close_first(self):
         return self.here // self.near * self.near
@@ -274,12 +274,13 @@
     loop(out_ref.shape[0], lambda unit: leave(unit).wait())
 
 
-def near_kernel(total, tile_cols, near, transfer_any, start_any, end_any, field_any, halo_any, jitter_any, far_any, *refs):
-    del far_any
-    out_anys = refs[:near]
-    transfer_ref, start_ref, end_ref, plane_ref, halo_ref, jitter_ref, out_ref, gain_ref, few_sems, sems, out_sems = refs[near:]
+def near_kernel(total, tile_cols, near, top, jump, transfer_any, start_any, end_any, field_any, halo_any, jitter_any, prior_any,
+                *refs):
+    del prior_any
+    out_anys, refs = refs[:-11], refs[-11:]
+    transfer_ref, start_ref, end_ref, plane_ref, halo_ref, jitter_ref, out_ref, gain_ref, few_sems, sems, out_sems = refs
     units, slab_len, rows, _ = plane_ref.shape
-    piece_of = Pieces(near).close
+    piece_of = functools.partial(Pieces(near).close, top, jump)
     arrival = functools.partial(field_copy, field_any, plane_ref, sems, piece_of)
     for unit in range(2):
         arrival(unit).start()
@@ -368,31 +369,35 @@
         cost_estimate=cost(closed),
         name="close",
     )(transfer, ray_start, ray_end, field, halo, jitter, state)
-    if not near:
-        return far, []
-    return far, pl.pallas_call(
-        functools.partial(near_kernel, total, tile_cols, near),
-        in_specs=[own] * 7,
-        out_specs=[own] * near,
-        out_shape=[jax.ShapeDtypeStruct((4, rows, UNIT), jnp.int16)] * near,
-        scratch_shapes=scalars + [
-            planes(near), flat(near, field.dtype), flat(near, jnp.float32), pltpu.VMEM((near, 4, rows, UNIT), jnp.int16), table(slab_len, near),
-            pltpu.SemaphoreType.DMA((5,)),
-            pltpu.SemaphoreType.DMA((near,)),
-            pltpu.SemaphoreType.DMA((near,)),
-        ],
-        compiler_params=pltpu.CompilerParams(vmem_limit_bytes=CLOSE_BYTES),
-        cost_estimate=cost(near),
-        name="near",
-    )(transfer, ray_start, ray_end, field, halo, jitter, far)
-
-
-def composite_kernel(total, slab_len, near, order_any, transfer_any, code_any, *refs):
+
+    def near_codes(top, jump, units, prior):
+        return pl.pallas_call(
+            functools.partial(near_kernel, total, tile_cols, near, top, jump),
+            in_specs=[own] * 7,
+            out_specs=[own] * units,
+            out_shape=[jax.ShapeDtypeStruct((4, rows, UNIT), jnp.int16)] * units,
+            scratch_shapes=scalars + [
+                planes(units), flat(near, field.dtype), flat(near, jnp.float32),
+                pltpu.VMEM((units, 4, rows, UNIT), jnp.int16), table(slab_len, units),
+                pltpu.SemaphoreType.DMA((5,)),
+                pltpu.SemaphoreType.DMA((units,)),
+                pltpu.SemaphoreType.DMA((units,)),
+            ],
+            compiler_params=pltpu.CompilerParams(vmem_limit_bytes=CLOSE_BYTES),
+            cost_estimate=cost(units),
+            name="near",
+        )(transfer, ray_start, ray_end, field, halo, jitter, prior)
+
+    return far, near_codes
+
+
+def composite_kernel(total, slab_len, nears, order_any, transfer_any, code_any, *refs):
+    near = len(nears)
     near_anys = refs[:near]
     image_any, order_ref, transfer_ref, code_ref, out_ref, sems, out_sems = refs[near:]
     count, _, rows, width = code_ref.shape
     here = lax.axis_index("depth")
-    pairs = [(near_any, code_ref.at[here ^ n]) for n, near_any in zip(reversed(range(near)), near_anys)]
+    pairs = [(near_any, code_ref.at[here ^ n]) for n, near_any in zip(nears, near_anys)]
     if near:
         for n in range(count // near - 1):
             group = n + jnp.where(n >= here // near, 1, 0)
@@ -444,7 +449,7 @@
     blocks = width // math.gcd(width, 2 * LANES)
     own = pl.BlockSpec(memory_space=pl.ANY)
     return pl.pallas_call(
-        functools.partial(composite_kernel, total, slab_len, near),
+        functools.partial(composite_kernel, total, slab_len, tuple(near_codes)),
         in_specs=[own] * (3 + near),
         out_specs=own,
         out_shape=jax.ShapeDtypeStruct((4, rows, width), jnp.float32),
@@ -458,7 +463,7 @@
         ],
         compiler_params=pltpu.CompilerParams(vmem_limit_bytes=SMALL_BYTES),
         name="composite",
-    )(depth_order, transfer, codes, *near_codes)
+    )(depth_order, transfer, codes, *near_codes.values())
 
 
 def on_device(field, jitter, transfer, depth_order, ray_start, ray_end):
@@ -468,12 +473,23 @@
     width = cols // count
     near = NEAR if width == UNIT and count == 2 * NEAR else 0
     halo = shifted(field[0], "depth", -1)
-    codes, near_codes = slab_codes(field, halo, jitter, transfer, ray_start, ray_end, total, near)
+    codes, codes_near = slab_codes(field, halo, jitter, transfer, ray_start, ray_end, total, near)
     if width != UNIT:
         codes = codes.transpose(1, 2, 0, 3).reshape(4, rows, count, width).transpose(2, 0, 1, 3)
     received = lax.all_to_all(codes, "depth", split_axis=0, concat_axis=0, tiled=True)
-    swapped = [lax.ppermute(near_codes[n], "depth", [(i, i ^ n) for i in range(count)]) for n in reversed(range(1, near))]
-    return composite(received, [*swapped, *near_codes[:1]], transfer, depth_order, total, slab_len)
+    if not near:
+        return composite(received, {}, transfer, depth_order, total, slab_len)
+
+    def swapped(codes, n):
+        return lax.ppermute(codes, "depth", [(i, i ^ n) for i in range(count)])
+
+    top = near - 1
+    first = codes_near(top, near - 4, near - 2, codes)
+    near_codes = {top - n: swapped(first[n], top - n) for n in range(near - 4)}
+    near_codes[1] = swapped(first[near - 4], 1)
+    second = codes_near(3, 2, 2, near_codes[1])
+    near_codes.update({3: swapped(second[0], 3), 2: swapped(second[1], 2), 0: first[near - 3]})
+    return composite(received, near_codes, transfer, depth_order, total, slab_len)
 
 
 def solution(mesh):

time: 49.1 us -> 49 us (level)
  waiting for transfers between devices: 9.83 us -> 8.11 us
  Pallas kernels: 20.7 us -> 22 us
    ppermute x7, waiting for transfers between devices: 9.82 us -> 8.1 us  [swapped(): return lax.ppermute(codes, 'depth', [(i, i ^ n) for i in range(count)])]
    pallas_call x2 -> x3, Pallas kernels: 10.3 us -> 11.5 us  [the longest x2 9.55 us: near_codes(): pl.pallas_call(functools.partial(near_kernel, total, tile_cols, near, top...]
  transfers between devices with their start and end apart: 9 -> 9, of which waited for: 4 -> 4; matrix products, arithmetic and copies ran while one was open for 0% -> 0% of each run, Pallas kernels for 30% -> 33%
where the time goes in v22:
time: 49 us; the launch traced here: 48.7 us
  Pallas kernels  22 us (45%)
  starting transfers between devices  17.4 us (36%)
  waiting for transfers between devices  8.11 us (17%)
  local copies, waits for them, and re-layouts  1.05 us (2%)
    pallas_call x2, Pallas kernels, near_codes(): pl.pallas_call(functools.partial(near_kernel, total, tile_cols, near, top...  9.55 us
    all_to_all x1, starting transfers between devices, on_device(): lax.all_to_all(codes, 'depth', split_axis=0, concat_axis=0, tiled=True)  8.17 us
    ppermute x7, waiting for transfers between devices, swapped(): return lax.ppermute(codes, 'depth', [(i, i ^ n) for i in range(count)])  8.1 us
    ppermute x7, starting transfers between devices, swapped(): return lax.ppermute(codes, 'depth', [(i, i ^ n) for i in range(count)])  7.95 us
    pallas_call x1, Pallas kernels, slab_codes(): pl.pallas_call(functools.partial(open_kernel, total, tile_cols, near), in...  6.31 us
    pallas_call x1, Pallas kernels, slab_codes(): pl.pallas_call(functools.partial(close_kernel, total, tile_cols, near, op...  4.1 us
    pallas_call x1, Pallas kernels, composite(): pl.pallas_call(functools.partial(composite_kernel, total, slab_len, tuple...  2 us
    ppermute x1, starting transfers between devices, shifted(): lax.ppermute(value, axis, [(source, source + steps) for source in range(i...  1.29 us
  transfers between devices with their start and end apart: 9, of which 4 were waited for; matrix products, arithmetic and copies ran while one was open for 0% of the time, Pallas kernels for 33%

profile of v22, /device:TPU:0, one launch (start us, length us, event | category | flops | bytes accessed | tf_op | source)
XLA Modules:
  0.0 48.7 jit_solution(7428137349484033341)
XLA Ops:
  0.0 0.0 copy-start.2
  0.0 0.0 copy-start.3
  0.0 0.0 copy-start
  0.0 0.0 copy-start.1
  0.0 1.0 %slice_bitcast_fusion = bf16[16,8192]{1,0:T(8,128)(2,1)S(1)} fusion(bf16[32,16,8192]{2,1,0:T(8,128)(2,1)} %field_any.7), kind=kLoop, calls=%fused_computation | loop fusion | bytes 524288 | tf_op jit(solution)/shard_map/squeeze | solution.py:475
  1.0 1.3 %collective-permute-start = (bf16[16,8192]{1,0:T(8,128)(2,1)S(1)}, bf16[16,8192]{1,0:T(8,128)(2,1)S(1)}, u32[]{:S(2)}, u32[]{:S(2)}) collective-permute-start(bf16[16,8192]{1,0:T(8,128)(2,1)S(1)} %slice_bitcast_fusion), channel_id=1, source_target_pairs={{1,0},{2,1},{3,2},{4,3},{5,4},{6,5},{7,6},{8,7},{9,8},{10,9},{11,1... | collective-permute-start | bytes 786440 | tf_op jit(solution)/shard_map/ppermute | solution.py:35
  2.3 6.3 %open.1.state_any = f32[6,4,16,512]{3,2,1,0:T(8,128)} custom-call(f32[4]{0:T(128)} %transfer_any.9, s32[128]{0:T(128)} %start_any.7, s32[128]{0:T(128)} %end_any.7, bf16[32,16,8192]{2,1,0:T(8,128)(2,1)} %field_any.7, f32[16,8192]{1,0:T(8,128)} %jitter_any.7), custom_call_target="tpu_custom_call" | custom-call | flops 31457280 | bytes 3145728 | tf_op jit(solution)/shard_map/open/pallas_call | solution.py:340
  8.7 0.0 collective-permute-done.halo_any
  8.7 0.0 copy-done.2
  8.7 0.0 copy-done.3
  8.7 0.0 copy-done
  8.7 0.0 copy-done.1
  8.7 4.1 %close.1.prior_any = s16[16,4,16,512]{3,2,1,0:T(8,128)(2,1)} custom-call(f32[4]{0:T(128)S(1)} %copy-done.1, s32[128]{0:T(128)S(1)} %copy-done.2, s32[128]{0:T(128)S(1)} %copy-done.3, bf16[32,16,8192]{2,1,0:T(8,128)(2,1)} %field_any.7, bf16[16,8192]{1,0:T(8,128)(2,1)S(1)} %collective-permute-done.halo_any, f32[16,8192]{1,0:T(8,128)S(1)} %copy-done, ...), custom_call_target="tpu_custom_call" | custom-call | flops 10485760 | bytes 1048576 | tf_op jit(solution)/shard_map/close/pallas_call | solution.py:355
  12.8 8.2 %all-to-all-start = ((s16[16,4,16,512]{3,2,1,0:T(8,128)(2,1)}), s16[16,4,16,512]{3,2,1,0:T(8,128)(2,1)S(1)}, u32[]{:S(2)}, u32[]{:S(2)}) async-start(s16[16,4,16,512]{3,2,1,0:T(8,128)(2,1)} %close.1.prior_any), calls=%async_computation | async-start | bytes 2097152 | tf_op jit(solution)/shard_map/all_to_all | solution.py:479
  21.0 0.0 copy-start.4
  21.0 6.5 %near.2 = (s16[4,16,512]{2,1,0:T(8,128)(2,1)S(1)}, s16[4,16,512]{2,1,0:T(8,128)(2,1)S(1)}, s16[4,16,512]{2,1,0:T(8,128)(2,1)S(1)}, s16[4,16,512]{2,1,0:T(8,128)(...) custom-call(f32[4]{0:T(128)S(1)} %copy-done.1, s32[128]{0:T(128)S(1)} %copy-done.2, ...), custom_call_target="tpu_custom_call" | custom-call | flops 31457280 | bytes 3145728 | tf_op jit(solution)/shard_map/near/pallas_call | solution.py:374
  27.6 0.5 collective-permute-start.5
  28.0 2.5 %collective-permute-start.1 = (s16[4,16,512]{2,1,0:T(8,128)(2,1)S(1)}, s16[4,16,512]{2,1,0:T(8,128)(2,1)S(1)}, u32[]{:S(2)}, u32[]{:S(2)}) collective-permute-start(s16[4,16,512]{2,1,0:T(8,128)(2,1)S(1)} %get-tuple-element.13), channel_id=1, source_target_pairs={{0,7},{1,6},{2,5},{3,4},{4,3},{5,2},{6,1},{7,0},{8,15},{9,14},{10,... | collective-permute-start | bytes 196616 | tf_op jit(solution)/shard_map/ppermute | solution.py:484
  30.6 0.1 collective-permute-start.2
  30.7 1.4 %collective-permute-start.3 = (s16[4,16,512]{2,1,0:T(8,128)(2,1)S(1)}, s16[4,16,512]{2,1,0:T(8,128)(2,1)S(1)}, u32[]{:S(2)}, u32[]{:S(2)}) collective-permute-start(s16[4,16,512]{2,1,0:T(8,128)(2,1)S(1)} %get-tuple-element.15), channel_id=1, source_target_pairs={{0,5},{1,4},{2,7},{3,6},{4,1},{5,0},{6,3},{7,2},{8,13},{9,12},{10,... | collective-permute-start | bytes 196616 | tf_op jit(solution)/shard_map/ppermute | solution.py:484
  32.1 0.5 %collective-permute-start.4 = (s16[4,16,512]{2,1,0:T(8,128)(2,1)S(1)}, s16[4,16,512]{2,1,0:T(8,128)(2,1)S(1)}, u32[]{:S(2)}, u32[]{:S(2)}) collective-permute-start(s16[4,16,512]{2,1,0:T(8,128)(2,1)S(1)} %get-tuple-element.16), channel_id=1, source_target_pairs={{0,4},{1,5},{2,6},{3,7},{4,0},{5,1},{6,2},{7,3},{8,12},{9,13},{10,... | collective-permute-start | bytes 196616 | tf_op jit(solution)/shard_map/ppermute | solution.py:484
  32.6 0.0 collective-permute-done.5.prior_any.refs_4_
  32.6 3.0 %near.3 = (s16[4,16,512]{2,1,0:T(8,128)(2,1)S(1)}, s16[4,16,512]{2,1,0:T(8,128)(2,1)S(1)}) custom-call(f32[4]{0:T(128)S(1)} %copy-done.1, s32[128]{0:T(128)S(1)} %copy-done.2, s32[128]{0:T(128)S(1)} %copy-done.3, bf16[32,16,8192]{2,1,0:T(8,128)(2,1)} %field_any.7, bf16[16,8192]{1,0:T(8,128)(2,1)S(1)} %collective-permute-done.halo_any, ...), custom_call_target="tpu_custom_call" | custom-call | flops 10485760 | bytes 1048576 | tf_op jit(solution)/shard_map/near/pallas_call | solution.py:374
  35.6 1.5 %collective-permute-start.6 = (s16[4,16,512]{2,1,0:T(8,128)(2,1)S(1)}, s16[4,16,512]{2,1,0:T(8,128)(2,1)S(1)}, u32[]{:S(2)}, u32[]{:S(2)}) collective-permute-start(s16[4,16,512]{2,1,0:T(8,128)(2,1)S(1)} %get-tuple-element.18), channel_id=1, source_target_pairs={{0,3},{1,2},{2,1},{3,0},{4,7},{5,6},{6,5},{7,4},{8,11},{9,10},{10,... | collective-permute-start | bytes 196616 | tf_op jit(solution)/shard_map/ppermute | solution.py:484
  37.1 4.0 %collective-permute-done.1.refs_0_ = s16[4,16,512]{2,1,0:T(8,128)(2,1)S(1)} collective-permute-done((s16[4,16,512]{2,1,0:T(8,128)(2,1)S(1)}, s16[4,16,512]{2,1,0:T(8,128)(2,1)S(1)}, u32[]{:S(2)}, u32[]{:S(2)}) %collective-permute-start.1) | collective-permute-done | bytes 65568 | tf_op jit(solution)/shard_map/ppermute | solution.py:484
  41.1 1.4 %collective-permute-start.7 = (s16[4,16,512]{2,1,0:T(8,128)(2,1)S(1)}, s16[4,16,512]{2,1,0:T(8,128)(2,1)S(1)}, u32[]{:S(2)}, u32[]{:S(2)}) collective-permute-start(s16[4,16,512]{2,1,0:T(8,128)(2,1)S(1)} %get-tuple-element.19), channel_id=1, source_target_pairs={{0,2},{1,3},{2,0},{3,1},{4,6},{5,7},{6,4},{7,5},{8,10},{9,11},{10,... | collective-permute-start | bytes 196616 | tf_op jit(solution)/shard_map/ppermute | solution.py:484
  42.5 0.4 collective-permute-done.2.refs_1_
  42.9 1.4 %collective-permute-done.3.refs_2_ = s16[4,16,512]{2,1,0:T(8,128)(2,1)S(1)} collective-permute-done((s16[4,16,512]{2,1,0:T(8,128)(2,1)S(1)}, s16[4,16,512]{2,1,0:T(8,128)(2,1)S(1)}, u32[]{:S(2)}, u32[]{:S(2)}) %collective-permute-start.3) | collective-permute-done | bytes 65568 | tf_op jit(solution)/shard_map/ppermute | solution.py:484
  44.3 2.3 %collective-permute-done.4.refs_3_ = s16[4,16,512]{2,1,0:T(8,128)(2,1)S(1)} collective-permute-done((s16[4,16,512]{2,1,0:T(8,128)(2,1)S(1)}, s16[4,16,512]{2,1,0:T(8,128)(2,1)S(1)}, u32[]{:S(2)}, u32[]{:S(2)}) %collective-permute-start.4) | collective-permute-done | bytes 65568 | tf_op jit(solution)/shard_map/ppermute | solution.py:484
  46.6 0.0 collective-permute-done.6.refs_5_
  46.6 0.0 collective-permute-done.7.refs_6_
  46.6 0.0 all-to-all-done.code_any
  46.6 0.0 copy-done.4
  46.7 2.0 %composite.1 = f32[4,16,512]{2,1,0:T(8,128)} custom-call(s32[16]{0:T(128)S(1)} %copy-done.4, f32[4]{0:T(128)S(1)} %copy-done.1, s16[16,4,16,512]{3,2,1,0:T(8,128)(2,1)S(1)} %all-to-all-done.code_any, s16[4,16,512]{2,1,0:T(8,128)(2,1)S(1)} %collective-permute-done.1.refs_0_, s16[4,16,512]{2,1,0:T(8,128)(2,1)S(1)} %collective-permute-done.2.refs_1_, ...), custom_call_target="tpu_custom_call" | custom-call | tf_op jit(solution)/shard_map/composite/pallas_call | solution.py:451
Async XLA Ops:
  0.0 8.7 %copy-start.2 = (s32[128]{0:T(128)S(1)}, s32[128]{0:T(128)}, u32[]{:S(2)}) copy-start(s32[128]{0:T(128)} %start_any.7) | copy-start | bytes 1540
  0.0 8.7 %copy-start.3 = (s32[128]{0:T(128)S(1)}, s32[128]{0:T(128)}, u32[]{:S(2)}) copy-start(s32[128]{0:T(128)} %end_any.7) | copy-start | bytes 1540
  0.0 8.7 %copy-start = (f32[16,8192]{1,0:T(8,128)S(1)}, f32[16,8192]{1,0:T(8,128)}, u32[]{:S(2)}) copy-start(f32[16,8192]{1,0:T(8,128)} %jitter_any.7) | copy-start | bytes 1572868
  0.0 8.7 %copy-start.1 = (f32[4]{0:T(128)S(1)}, f32[4]{0:T(128)}, u32[]{:S(2)}) copy-start(f32[4]{0:T(128)} %transfer_any.9) | copy-start | bytes 52
  1.0 7.6 %collective-permute-start = (bf16[16,8192]{1,0:T(8,128)(2,1)S(1)}, bf16[16,8192]{1,0:T(8,128)(2,1)S(1)}, u32[]{:S(2)}, u32[]{:S(2)}) collective-permute-start(bf16[16,8192]{1,0:T(8,128)(2,1)S(1)} %slice_bitcast_fusion), channel_id=1, source_target_pairs={{1,0},{2,1},{3,2},{4,3},{5,4},{6,5},{7,6},{8,7},{9,8},{10,9},{11,1... | collective-permute-start | bytes 786440 | tf_op jit(solution)/shard_map/ppermute | solution.py:35
  12.8 33.8 %all-to-all-start = ((s16[16,4,16,512]{3,2,1,0:T(8,128)(2,1)}), s16[16,4,16,512]{3,2,1,0:T(8,128)(2,1)S(1)}, u32[]{:S(2)}, u32[]{:S(2)}) async-start(s16[16,4,16,512]{3,2,1,0:T(8,128)(2,1)} %close.1.prior_any), calls=%async_computation | async-start | bytes 2097152 | tf_op jit(solution)/shard_map/all_to_all | solution.py:479
  21.0 25.6 %copy-start.4 = (s32[16]{0:T(128)S(1)}, s32[16]{0:T(128)}, u32[]{:S(2)}) copy-start(s32[16]{0:T(128)} %order_any.1) | copy-start | bytes 196
  27.6 5.1 %collective-permute-start.5 = (s16[4,16,512]{2,1,0:T(8,128)(2,1)S(1)}, s16[4,16,512]{2,1,0:T(8,128)(2,1)S(1)}, u32[]{:S(2)}, u32[]{:S(2)}) collective-permute-start(s16[4,16,512]{2,1,0:T(8,128)(2,1)S(1)} %get-tuple-element.17), channel_id=1, source_target_pairs={{0,1},{1,0},{2,3},{3,2},{4,5},{5,4},{6,7},{7,6},{8,9},{9,8},{10,11... | collective-permute-start | bytes 196616 | tf_op jit(solution)/shard_map/ppermute | solution.py:484
  28.0 13.1 %collective-permute-start.1 = (s16[4,16,512]{2,1,0:T(8,128)(2,1)S(1)}, s16[4,16,512]{2,1,0:T(8,128)(2,1)S(1)}, u32[]{:S(2)}, u32[]{:S(2)}) collective-permute-start(s16[4,16,512]{2,1,0:T(8,128)(2,1)S(1)} %get-tuple-element.13), channel_id=1, source_target_pairs={{0,7},{1,6},{2,5},{3,4},{4,3},{5,2},{6,1},{7,0},{8,15},{9,14},{10,... | collective-permute-start | bytes 196616 | tf_op jit(solution)/shard_map/ppermute | solution.py:484
  30.6 12.3 %collective-permute-start.2 = (s16[4,16,512]{2,1,0:T(8,128)(2,1)S(1)}, s16[4,16,512]{2,1,0:T(8,128)(2,1)S(1)}, u32[]{:S(2)}, u32[]{:S(2)}) collective-permute-start(s16[4,16,512]{2,1,0:T(8,128)(2,1)S(1)} %get-tuple-element.14), channel_id=1, source_target_pairs={{0,6},{1,7},{2,4},{3,5},{4,2},{5,3},{6,0},{7,1},{8,14},{9,15},{10,... | collective-permute-start | bytes 196616 | tf_op jit(solution)/shard_map/ppermute | solution.py:484
  30.7 13.6 %collective-permute-start.3 = (s16[4,16,512]{2,1,0:T(8,128)(2,1)S(1)}, s16[4,16,512]{2,1,0:T(8,128)(2,1)S(1)}, u32[]{:S(2)}, u32[]{:S(2)}) collective-permute-start(s16[4,16,512]{2,1,0:T(8,128)(2,1)S(1)} %get-tuple-element.15), channel_id=1, source_target_pairs={{0,5},{1,4},{2,7},{3,6},{4,1},{5,0},{6,3},{7,2},{8,13},{9,12},{10,... | collective-permute-start | bytes 196616 | tf_op jit(solution)/shard_map/ppermute | solution.py:484
  32.1 14.6 %collective-permute-start.4 = (s16[4,16,512]{2,1,0:T(8,128)(2,1)S(1)}, s16[4,16,512]{2,1,0:T(8,128)(2,1)S(1)}, u32[]{:S(2)}, u32[]{:S(2)}) collective-permute-start(s16[4,16,512]{2,1,0:T(8,128)(2,1)S(1)} %get-tuple-element.16), channel_id=1, source_target_pairs={{0,4},{1,5},{2,6},{3,7},{4,0},{5,1},{6,2},{7,3},{8,12},{9,13},{10,... | collective-permute-start | bytes 196616 | tf_op jit(solution)/shard_map/ppermute | solution.py:484
  35.6 11.0 %collective-permute-start.6 = (s16[4,16,512]{2,1,0:T(8,128)(2,1)S(1)}, s16[4,16,512]{2,1,0:T(8,128)(2,1)S(1)}, u32[]{:S(2)}, u32[]{:S(2)}) collective-permute-start(s16[4,16,512]{2,1,0:T(8,128)(2,1)S(1)} %get-tuple-element.18), channel_id=1, source_target_pairs={{0,3},{1,2},{2,1},{3,0},{4,7},{5,6},{6,5},{7,4},{8,11},{9,10},{10,... | collective-permute-start | bytes 196616 | tf_op jit(solution)/shard_map/ppermute | solution.py:484
  41.1 5.5 %collective-permute-start.7 = (s16[4,16,512]{2,1,0:T(8,128)(2,1)S(1)}, s16[4,16,512]{2,1,0:T(8,128)(2,1)S(1)}, u32[]{:S(2)}, u32[]{:S(2)}) collective-permute-start(s16[4,16,512]{2,1,0:T(8,128)(2,1)S(1)} %get-tuple-element.19), channel_id=1, source_target_pairs={{0,2},{1,3},{2,0},{3,1},{4,6},{5,7},{6,4},{7,5},{8,10},{9,11},{10,... | collective-permute-start | bytes 196616 | tf_op jit(solution)/shard_map/ppermute | solution.py:484

commit v23 on v20

--- a/solution.py
+++ b/solution.py
@@ -461,13 +461,32 @@
     )(depth_order, transfer, codes, *near_codes)
 
 
+def first_plane(field):
+    own = pl.BlockSpec(memory_space=pl.ANY)
+
+    def kernel(field_any, plane_any, sem):
+        copy = pltpu.make_async_copy(field_any.at[0], plane_any, sem)
+        copy.start()
+        copy.wait()
+
+    return pl.pallas_call(
+        kernel,
+        in_specs=[own],
+        out_specs=own,
+        out_shape=jax.ShapeDtypeStruct(field.shape[1:], field.dtype),
+        scratch_shapes=[pltpu.SemaphoreType.DMA],
+        compiler_params=pltpu.CompilerParams(vmem_limit_bytes=OPEN_BYTES),
+        name="first_plane",
+    )(field)
+
+
 def on_device(field, jitter, transfer, depth_order, ray_start, ray_end):
     count = lax.axis_size("depth")
     slab_len, rows, cols = field.shape
     total = slab_len * count
     width = cols // count
     near = NEAR if width == UNIT and count == 2 * NEAR else 0
-    halo = shifted(field[0], "depth", -1)
+    halo = shifted(first_plane(field), "depth", -1)
     codes, near_codes = slab_codes(field, halo, jitter, transfer, ray_start, ray_end, total, near)
     if width != UNIT:
         codes = codes.transpose(1, 2, 0, 3).reshape(4, rows, count, width).transpose(2, 0, 1, 3)

time: 49.1 us -> 57.1 us (1.16)
  Pallas kernels: 20.7 us -> 29.8 us
  local copies, waits for them, and re-layouts: 1.05 us -> 0.02 us
    pallas_call x0 -> x1, Pallas kernels: none -> 9.05 us  [first_plane(): pl.pallas_call(kernel, in_specs=[own], out_specs=own, out_shape=jax.Shape...]
    squeeze x1 -> x0, local copies, waits for them, and re-layouts: 1.03 us -> none  [on_device(): halo = shifted(field[0], 'depth', -1)]
  transfers between devices with their start and end apart: 9 -> 9, of which waited for: 4 -> 4; matrix products, arithmetic and copies ran while one was open for 0% -> 0% of each run, Pallas kernels for 30% -> 26%
where the time goes in v23:
time: 57.1 us; the launch traced here: 56.7 us
  Pallas kernels  29.8 us (52%)
  starting transfers between devices  17 us (30%)
  waiting for transfers between devices  9.83 us (17%)
    ppermute x7, waiting for transfers between devices, on_device(): lax.ppermute(near_codes[n], 'depth', [(i, i ^ n) for i in range(count)])  9.82 us
    pallas_call x1, Pallas kernels, first_plane(): pl.pallas_call(kernel, in_specs=[own], out_specs=own, out_shape=jax.Shape...  9.05 us
    pallas_call x1, Pallas kernels, slab_codes(): pl.pallas_call(functools.partial(near_kernel, total, tile_cols, near), in...  8.28 us
    all_to_all x1, starting transfers between devices, on_device(): lax.all_to_all(codes, 'depth', split_axis=0, concat_axis=0, tiled=True)  8.16 us
    ppermute x7, starting transfers between devices, on_device(): lax.ppermute(near_codes[n], 'depth', [(i, i ^ n) for i in range(count)])  7.53 us
    pallas_call x1, Pallas kernels, slab_codes(): pl.pallas_call(functools.partial(open_kernel, total, tile_cols, near), in...  6.34 us
    pallas_call x1, Pallas kernels, slab_codes(): pl.pallas_call(functools.partial(close_kernel, total, tile_cols, near, op...  4.1 us
    pallas_call x1, Pallas kernels, composite(): pl.pallas_call(functools.partial(composite_kernel, total, slab_len, near)...  2.01 us
  transfers between devices with their start and end apart: 9, of which 4 were waited for; matrix products, arithmetic and copies ran while one was open for 0% of the time, Pallas kernels for 26%

profile of v23, /device:TPU:0, one launch (start us, length us, event | category | flops | bytes accessed | tf_op | source)
XLA Modules:
  0.0 56.7 jit_solution(5854911559521627815)
XLA Ops:
  0.0 0.0 copy-start.2
  0.0 0.0 copy-start.3
  0.0 0.0 copy-start
  0.0 0.0 copy-start.1
  0.0 9.0 %first_plane.1 = bf16[16,8192]{1,0:T(8,128)(2,1)} custom-call(bf16[32,16,8192]{2,1,0:T(8,128)(2,1)} %field_any.7), custom_call_target="tpu_custom_call" | custom-call | tf_op jit(solution)/shard_map/first_plane/pallas_call | solution.py:472
  9.1 1.3 %collective-permute-start = (bf16[16,8192]{1,0:T(8,128)(2,1)}, bf16[16,8192]{1,0:T(8,128)(2,1)S(1)}, u32[]{:S(2)}, u32[]{:S(2)}) collective-permute-start(bf16[16,8192]{1,0:T(8,128)(2,1)} %first_plane.1), channel_id=1, source_target_pairs={{1,0},{2,1},{3,2},{4,3},{5,4},{6,5},{7,6},{8,7},{9,8},{10,9},{11,1... | collective-permute-start | bytes 786440 | tf_op jit(solution)/shard_map/ppermute | solution.py:35
  10.4 6.3 %open.1.state_any = f32[6,4,16,512]{3,2,1,0:T(8,128)} custom-call(f32[4]{0:T(128)} %transfer_any.7, s32[128]{0:T(128)} %start_any.5, s32[128]{0:T(128)} %end_any.5, bf16[32,16,8192]{2,1,0:T(8,128)(2,1)} %field_any.7, f32[16,8192]{1,0:T(8,128)} %jitter_any.5), custom_call_target="tpu_custom_call" | custom-call | flops 31457280 | bytes 3145728 | tf_op jit(solution)/shard_map/open/pallas_call | solution.py:339
  16.7 0.0 collective-permute-done.halo_any
  16.7 0.0 copy-done.2
  16.7 0.0 copy-done.3
  16.7 0.0 copy-done
  16.8 0.0 copy-done.1
  16.8 4.1 %close.1.far_any = s16[16,4,16,512]{3,2,1,0:T(8,128)(2,1)} custom-call(f32[4]{0:T(128)S(1)} %copy-done.1, s32[128]{0:T(128)S(1)} %copy-done.2, s32[128]{0:T(128)S(1)} %copy-done.3, bf16[32,16,8192]{2,1,0:T(8,128)(2,1)} %field_any.7, bf16[16,8192]{1,0:T(8,128)(2,1)S(1)} %collective-permute-done.halo_any, f32[16,8192]{1,0:T(8,128)S(1)} %copy-done, ...), custom_call_target="tpu_custom_call" | custom-call | flops 10485760 | bytes 1048576 | tf_op jit(solution)/shard_map/close/pallas_call | solution.py:354
  20.9 0.0 copy-start.4
  20.9 8.2 %all-to-all-start = ((s16[16,4,16,512]{3,2,1,0:T(8,128)(2,1)}), s16[16,4,16,512]{3,2,1,0:T(8,128)(2,1)S(1)}, u32[]{:S(2)}, u32[]{:S(2)}) async-start(s16[16,4,16,512]{3,2,1,0:T(8,128)(2,1)} %close.1.far_any), calls=%async_computation | async-start | bytes 2097152 | tf_op jit(solution)/shard_map/all_to_all | solution.py:493
  29.1 8.3 %near.1 = (s16[4,16,512]{2,1,0:T(8,128)(2,1)S(1)}, s16[4,16,512]{2,1,0:T(8,128)(2,1)S(1)}, s16[4,16,512]{2,1,0:T(8,128)(2,1)S(1)}, s16[4,16,512]{2,1,0:T(8,128)(...) custom-call(f32[4]{0:T(128)S(1)} %copy-done.1, ...), custom_call_target="tpu_custom_call" | custom-call | flops 41943040 | bytes 4194304 | tf_op jit(solution)/shard_map/near/pallas_call | solution.py:373
  37.3 2.6 %collective-permute-start.1 = (s16[4,16,512]{2,1,0:T(8,128)(2,1)S(1)}, s16[4,16,512]{2,1,0:T(8,128)(2,1)S(1)}, u32[]{:S(2)}, u32[]{:S(2)}) collective-permute-start(s16[4,16,512]{2,1,0:T(8,128)(2,1)S(1)} %get-tuple-element.13), channel_id=1, source_target_pairs={{0,7},{1,6},{2,5},{3,4},{4,3},{5,2},{6,1},{7,0},{8,15},{9,14},{10,... | collective-permute-start | bytes 196616 | tf_op jit(solution)/shard_map/ppermute | solution.py:494
  40.0 0.4 collective-permute-start.2
  40.4 1.3 %collective-permute-start.3 = (s16[4,16,512]{2,1,0:T(8,128)(2,1)S(1)}, s16[4,16,512]{2,1,0:T(8,128)(2,1)S(1)}, u32[]{:S(2)}, u32[]{:S(2)}) collective-permute-start(s16[4,16,512]{2,1,0:T(8,128)(2,1)S(1)} %get-tuple-element.15), channel_id=1, source_target_pairs={{0,5},{1,4},{2,7},{3,6},{4,1},{5,0},{6,3},{7,2},{8,13},{9,12},{10,... | collective-permute-start | bytes 196616 | tf_op jit(solution)/shard_map/ppermute | solution.py:494
  41.7 0.4 collective-permute-start.4
  42.0 1.4 %collective-permute-start.5 = (s16[4,16,512]{2,1,0:T(8,128)(2,1)S(1)}, s16[4,16,512]{2,1,0:T(8,128)(2,1)S(1)}, u32[]{:S(2)}, u32[]{:S(2)}) collective-permute-start(s16[4,16,512]{2,1,0:T(8,128)(2,1)S(1)} %get-tuple-element.17), channel_id=1, source_target_pairs={{0,3},{1,2},{2,1},{3,0},{4,7},{5,6},{6,5},{7,4},{8,11},{9,10},{10,... | collective-permute-start | bytes 196616 | tf_op jit(solution)/shard_map/ppermute | solution.py:494
  43.5 5.7 %collective-permute-done.1.refs_0_ = s16[4,16,512]{2,1,0:T(8,128)(2,1)S(1)} collective-permute-done((s16[4,16,512]{2,1,0:T(8,128)(2,1)S(1)}, s16[4,16,512]{2,1,0:T(8,128)(2,1)S(1)}, u32[]{:S(2)}, u32[]{:S(2)}) %collective-permute-start.1) | collective-permute-done | bytes 65568 | tf_op jit(solution)/shard_map/ppermute | solution.py:494
  49.1 1.4 %collective-permute-start.6 = (s16[4,16,512]{2,1,0:T(8,128)(2,1)S(1)}, s16[4,16,512]{2,1,0:T(8,128)(2,1)S(1)}, u32[]{:S(2)}, u32[]{:S(2)}) collective-permute-start(s16[4,16,512]{2,1,0:T(8,128)(2,1)S(1)} %get-tuple-element.18), channel_id=1, source_target_pairs={{0,2},{1,3},{2,0},{3,1},{4,6},{5,7},{6,4},{7,5},{8,10},{9,11},{10,... | collective-permute-start | bytes 196616 | tf_op jit(solution)/shard_map/ppermute | solution.py:494
  50.5 0.4 collective-permute-done.2.refs_1_
  50.9 0.0 collective-permute-start.7
  50.9 1.4 %collective-permute-done.3.refs_2_ = s16[4,16,512]{2,1,0:T(8,128)(2,1)S(1)} collective-permute-done((s16[4,16,512]{2,1,0:T(8,128)(2,1)S(1)}, s16[4,16,512]{2,1,0:T(8,128)(2,1)S(1)}, u32[]{:S(2)}, u32[]{:S(2)}) %collective-permute-start.3) | collective-permute-done | bytes 65568 | tf_op jit(solution)/shard_map/ppermute | solution.py:494
  52.3 2.4 %collective-permute-done.4.refs_3_ = s16[4,16,512]{2,1,0:T(8,128)(2,1)S(1)} collective-permute-done((s16[4,16,512]{2,1,0:T(8,128)(2,1)S(1)}, s16[4,16,512]{2,1,0:T(8,128)(2,1)S(1)}, u32[]{:S(2)}, u32[]{:S(2)}) %collective-permute-start.4) | collective-permute-done | bytes 65568 | tf_op jit(solution)/shard_map/ppermute | solution.py:494
  54.7 0.0 collective-permute-done.5.refs_4_
  54.7 0.0 collective-permute-done.6.refs_5_
  54.7 0.0 collective-permute-done.7.refs_6_
  54.7 0.0 all-to-all-done.code_any
  54.7 0.0 copy-done.4
  54.7 2.0 %composite.1 = f32[4,16,512]{2,1,0:T(8,128)} custom-call(s32[16]{0:T(128)S(1)} %copy-done.4, f32[4]{0:T(128)S(1)} %copy-done.1, s16[16,4,16,512]{3,2,1,0:T(8,128)(2,1)S(1)} %all-to-all-done.code_any, s16[4,16,512]{2,1,0:T(8,128)(2,1)S(1)} %collective-permute-done.1.refs_0_, s16[4,16,512]{2,1,0:T(8,128)(2,1)S(1)} %collective-permute-done.2.refs_1_, ...), custom_call_target="tpu_custom_call" | custom-call | tf_op jit(solution)/shard_map/composite/pallas_call | solution.py:446
Async XLA Ops:
  0.0 16.7 %copy-start.2 = (s32[128]{0:T(128)S(1)}, s32[128]{0:T(128)}, u32[]{:S(2)}) copy-start(s32[128]{0:T(128)} %start_any.5) | copy-start | bytes 1540
  0.0 16.7 %copy-start.3 = (s32[128]{0:T(128)S(1)}, s32[128]{0:T(128)}, u32[]{:S(2)}) copy-start(s32[128]{0:T(128)} %end_any.5) | copy-start | bytes 1540
  0.0 16.7 %copy-start = (f32[16,8192]{1,0:T(8,128)S(1)}, f32[16,8192]{1,0:T(8,128)}, u32[]{:S(2)}) copy-start(f32[16,8192]{1,0:T(8,128)} %jitter_any.5) | copy-start | bytes 1572868
  0.0 16.8 %copy-start.1 = (f32[4]{0:T(128)S(1)}, f32[4]{0:T(128)}, u32[]{:S(2)}) copy-start(f32[4]{0:T(128)} %transfer_any.7) | copy-start | bytes 52
  9.1 7.7 %collective-permute-start = (bf16[16,8192]{1,0:T(8,128)(2,1)}, bf16[16,8192]{1,0:T(8,128)(2,1)S(1)}, u32[]{:S(2)}, u32[]{:S(2)}) collective-permute-start(bf16[16,8192]{1,0:T(8,128)(2,1)} %first_plane.1), channel_id=1, source_target_pairs={{1,0},{2,1},{3,2},{4,3},{5,4},{6,5},{7,6},{8,7},{9,8},{10,9},{11,1... | collective-permute-start | bytes 786440 | tf_op jit(solution)/shard_map/ppermute | solution.py:35
  20.9 33.8 %copy-start.4 = (s32[16]{0:T(128)S(1)}, s32[16]{0:T(128)}, u32[]{:S(2)}) copy-start(s32[16]{0:T(128)} %order_any.1) | copy-start | bytes 196
  20.9 33.8 %all-to-all-start = ((s16[16,4,16,512]{3,2,1,0:T(8,128)(2,1)}), s16[16,4,16,512]{3,2,1,0:T(8,128)(2,1)S(1)}, u32[]{:S(2)}, u32[]{:S(2)}) async-start(s16[16,4,16,512]{3,2,1,0:T(8,128)(2,1)} %close.1.far_any), calls=%async_computation | async-start | bytes 2097152 | tf_op jit(solution)/shard_map/all_to_all | solution.py:493
  37.3 11.8 %collective-permute-start.1 = (s16[4,16,512]{2,1,0:T(8,128)(2,1)S(1)}, s16[4,16,512]{2,1,0:T(8,128)(2,1)S(1)}, u32[]{:S(2)}, u32[]{:S(2)}) collective-permute-start(s16[4,16,512]{2,1,0:T(8,128)(2,1)S(1)} %get-tuple-element.13), channel_id=1, source_target_pairs={{0,7},{1,6},{2,5},{3,4},{4,3},{5,2},{6,1},{7,0},{8,15},{9,14},{10,... | collective-permute-start | bytes 196616 | tf_op jit(solution)/shard_map/ppermute | solution.py:494
  40.0 11.0 %collective-permute-start.2 = (s16[4,16,512]{2,1,0:T(8,128)(2,1)S(1)}, s16[4,16,512]{2,1,0:T(8,128)(2,1)S(1)}, u32[]{:S(2)}, u32[]{:S(2)}) collective-permute-start(s16[4,16,512]{2,1,0:T(8,128)(2,1)S(1)} %get-tuple-element.14), channel_id=1, source_target_pairs={{0,6},{1,7},{2,4},{3,5},{4,2},{5,3},{6,0},{7,1},{8,14},{9,15},{10,... | collective-permute-start | bytes 196616 | tf_op jit(solution)/shard_map/ppermute | solution.py:494
  40.4 12.0 %collective-permute-start.3 = (s16[4,16,512]{2,1,0:T(8,128)(2,1)S(1)}, s16[4,16,512]{2,1,0:T(8,128)(2,1)S(1)}, u32[]{:S(2)}, u32[]{:S(2)}) collective-permute-start(s16[4,16,512]{2,1,0:T(8,128)(2,1)S(1)} %get-tuple-element.15), channel_id=1, source_target_pairs={{0,5},{1,4},{2,7},{3,6},{4,1},{5,0},{6,3},{7,2},{8,13},{9,12},{10,... | collective-permute-start | bytes 196616 | tf_op jit(solution)/shard_map/ppermute | solution.py:494
  41.7 13.0 %collective-permute-start.4 = (s16[4,16,512]{2,1,0:T(8,128)(2,1)S(1)}, s16[4,16,512]{2,1,0:T(8,128)(2,1)S(1)}, u32[]{:S(2)}, u32[]{:S(2)}) collective-permute-start(s16[4,16,512]{2,1,0:T(8,128)(2,1)S(1)} %get-tuple-element.16), channel_id=1, source_target_pairs={{0,4},{1,5},{2,6},{3,7},{4,0},{5,1},{6,2},{7,3},{8,12},{9,13},{10,... | collective-permute-start | bytes 196616 | tf_op jit(solution)/shard_map/ppermute | solution.py:494
  42.0 12.6 %collective-permute-start.5 = (s16[4,16,512]{2,1,0:T(8,128)(2,1)S(1)}, s16[4,16,512]{2,1,0:T(8,128)(2,1)S(1)}, u32[]{:S(2)}, u32[]{:S(2)}) collective-permute-start(s16[4,16,512]{2,1,0:T(8,128)(2,1)S(1)} %get-tuple-element.17), channel_id=1, source_target_pairs={{0,3},{1,2},{2,1},{3,0},{4,7},{5,6},{6,5},{7,4},{8,11},{9,10},{10,... | collective-permute-start | bytes 196616 | tf_op jit(solution)/shard_map/ppermute | solution.py:494
  49.1 5.6 %collective-permute-start.6 = (s16[4,16,512]{2,1,0:T(8,128)(2,1)S(1)}, s16[4,16,512]{2,1,0:T(8,128)(2,1)S(1)}, u32[]{:S(2)}, u32[]{:S(2)}) collective-permute-start(s16[4,16,512]{2,1,0:T(8,128)(2,1)S(1)} %get-tuple-element.18), channel_id=1, source_target_pairs={{0,2},{1,3},{2,0},{3,1},{4,6},{5,7},{6,4},{7,5},{8,10},{9,11},{10,... | collective-permute-start | bytes 196616 | tf_op jit(solution)/shard_map/ppermute | solution.py:494
  50.9 3.8 %collective-permute-start.7 = (s16[4,16,512]{2,1,0:T(8,128)(2,1)S(1)}, s16[4,16,512]{2,1,0:T(8,128)(2,1)S(1)}, u32[]{:S(2)}, u32[]{:S(2)}) collective-permute-start(s16[4,16,512]{2,1,0:T(8,128)(2,1)S(1)} %get-tuple-element.19), channel_id=1, source_target_pairs={{0,1},{1,0},{2,3},{3,2},{4,5},{5,4},{6,7},{7,6},{8,9},{9,8},{10,11... | collective-permute-start | bytes 196616 | tf_op jit(solution)/shard_map/ppermute | solution.py:494

commit v24 on v20

--- a/solution.py
+++ b/solution.py
@@ -184,11 +184,10 @@
             state_ref[unit, i, :, cols] = value
 
     def leave(n):
-        place = pl.ds(2 * n, 2)
-        return pltpu.make_async_copy(state_ref.at[place], state_any.at[place], out_sems.at[n])
-
-    each_group(units, 2, functools.partial(arrive_pair, arrival), compute, store, lambda n: leave(n).start())
-    loop(units // 2, lambda n: leave(n).wait())
+        return pltpu.make_async_copy(state_ref.at[n], state_any.at[n], out_sems.at[n])
+
+    each_group(units, 1, lambda n: arrival(n).wait(), compute, store, lambda n: leave(n).start())
+    loop(units, lambda n: leave(n).wait())
 
 
 class Coder:
@@ -345,7 +344,7 @@
             planes(opened), flat(opened, jnp.float32), pltpu.VMEM(state_shape, jnp.float32), table(slab_len, opened),
             pltpu.SemaphoreType.DMA((4,)),
             pltpu.SemaphoreType.DMA((opened,)),
-            pltpu.SemaphoreType.DMA((opened // 2,)),
+            pltpu.SemaphoreType.DMA((opened,)),
         ],
         compiler_params=pltpu.CompilerParams(vmem_limit_bytes=OPEN_BYTES),
         cost_estimate=cost(opened),

time: 49.1 us -> 49 us (level)
  no operation moved by 1% of the time
where the time goes in v24:
time: 49 us; the launch traced here: 48.7 us
  Pallas kernels  20.7 us (42%)
  starting transfers between devices  17 us (35%)
  waiting for transfers between devices  9.83 us (20%)
  local copies, waits for them, and re-layouts  1.05 us (2%)
    ppermute x7, waiting for transfers between devices, on_device(): lax.ppermute(near_codes[n], 'depth', [(i, i ^ n) for i in range(count)])  9.82 us
    pallas_call x1, Pallas kernels, slab_codes(): pl.pallas_call(functools.partial(near_kernel, total, tile_cols, near), in...  8.28 us
    all_to_all x1, starting transfers between devices, on_device(): lax.all_to_all(codes, 'depth', split_axis=0, concat_axis=0, tiled=True)  8.16 us
    ppermute x7, starting transfers between devices, on_device(): lax.ppermute(near_codes[n], 'depth', [(i, i ^ n) for i in range(count)])  7.53 us
    pallas_call x1, Pallas kernels, slab_codes(): pl.pallas_call(functools.partial(open_kernel, total, tile_cols, near), in...  6.34 us
    pallas_call x1, Pallas kernels, slab_codes(): pl.pallas_call(functools.partial(close_kernel, total, tile_cols, near, op...  4.1 us
    pallas_call x1, Pallas kernels, composite(): pl.pallas_call(functools.partial(composite_kernel, total, slab_len, near)...  2.01 us
    ppermute x1, starting transfers between devices, shifted(): lax.ppermute(value, axis, [(source, source + steps) for source in range(i...  1.29 us
  transfers between devices with their start and end apart: 9, of which 4 were waited for; matrix products, arithmetic and copies ran while one was open for 0% of the time, Pallas kernels for 30%

profile of v24, /device:TPU:0, one launch (start us, length us, event | category | flops | bytes accessed | tf_op | source)
XLA Modules:
  0.0 48.7 jit_solution(10002705494621090791)
XLA Ops:
  0.0 0.0 copy-start.2
  0.0 0.0 copy-start.3
  0.0 0.0 copy-start
  0.0 0.0 copy-start.1
  0.0 1.0 %slice_bitcast_fusion = bf16[16,8192]{1,0:T(8,128)(2,1)S(1)} fusion(bf16[32,16,8192]{2,1,0:T(8,128)(2,1)} %field_any.5), kind=kLoop, calls=%fused_computation | loop fusion | bytes 524288 | tf_op jit(solution)/shard_map/squeeze | solution.py:469
  1.0 1.3 %collective-permute-start = (bf16[16,8192]{1,0:T(8,128)(2,1)S(1)}, bf16[16,8192]{1,0:T(8,128)(2,1)S(1)}, u32[]{:S(2)}, u32[]{:S(2)}) collective-permute-start(bf16[16,8192]{1,0:T(8,128)(2,1)S(1)} %slice_bitcast_fusion), channel_id=1, source_target_pairs={{1,0},{2,1},{3,2},{4,3},{5,4},{6,5},{7,6},{8,7},{9,8},{10,9},{11,1... | collective-permute-start | bytes 786440 | tf_op jit(solution)/shard_map/ppermute | solution.py:35
  2.3 6.3 %open.1.state_any = f32[6,4,16,512]{3,2,1,0:T(8,128)} custom-call(f32[4]{0:T(128)} %transfer_any.7, s32[128]{0:T(128)} %start_any.5, s32[128]{0:T(128)} %end_any.5, bf16[32,16,8192]{2,1,0:T(8,128)(2,1)} %field_any.5, f32[16,8192]{1,0:T(8,128)} %jitter_any.5), custom_call_target="tpu_custom_call" | custom-call | flops 31457280 | bytes 3145728 | tf_op jit(solution)/shard_map/open/pallas_call | solution.py:338
  8.7 0.0 collective-permute-done.halo_any
  8.7 0.0 copy-done.2
  8.7 0.0 copy-done.3
  8.7 0.0 copy-done
  8.7 0.0 copy-done.1
  8.7 4.1 %close.1.far_any = s16[16,4,16,512]{3,2,1,0:T(8,128)(2,1)} custom-call(f32[4]{0:T(128)S(1)} %copy-done.1, s32[128]{0:T(128)S(1)} %copy-done.2, s32[128]{0:T(128)S(1)} %copy-done.3, bf16[32,16,8192]{2,1,0:T(8,128)(2,1)} %field_any.5, bf16[16,8192]{1,0:T(8,128)(2,1)S(1)} %collective-permute-done.halo_any, f32[16,8192]{1,0:T(8,128)S(1)} %copy-done, ...), custom_call_target="tpu_custom_call" | custom-call | flops 10485760 | bytes 1048576 | tf_op jit(solution)/shard_map/close/pallas_call | solution.py:353
  12.8 0.0 copy-start.4
  12.8 8.2 %all-to-all-start = ((s16[16,4,16,512]{3,2,1,0:T(8,128)(2,1)}), s16[16,4,16,512]{3,2,1,0:T(8,128)(2,1)S(1)}, u32[]{:S(2)}, u32[]{:S(2)}) async-start(s16[16,4,16,512]{3,2,1,0:T(8,128)(2,1)} %close.1.far_any), calls=%async_computation | async-start | bytes 2097152 | tf_op jit(solution)/shard_map/all_to_all | solution.py:473
  21.0 8.3 %near.1 = (s16[4,16,512]{2,1,0:T(8,128)(2,1)S(1)}, s16[4,16,512]{2,1,0:T(8,128)(2,1)S(1)}, s16[4,16,512]{2,1,0:T(8,128)(2,1)S(1)}, s16[4,16,512]{2,1,0:T(8,128)(...) custom-call(f32[4]{0:T(128)S(1)} %copy-done.1, ...), custom_call_target="tpu_custom_call" | custom-call | flops 41943040 | bytes 4194304 | tf_op jit(solution)/shard_map/near/pallas_call | solution.py:372
  29.3 2.6 %collective-permute-start.1 = (s16[4,16,512]{2,1,0:T(8,128)(2,1)S(1)}, s16[4,16,512]{2,1,0:T(8,128)(2,1)S(1)}, u32[]{:S(2)}, u32[]{:S(2)}) collective-permute-start(s16[4,16,512]{2,1,0:T(8,128)(2,1)S(1)} %get-tuple-element.13), channel_id=1, source_target_pairs={{0,7},{1,6},{2,5},{3,4},{4,3},{5,2},{6,1},{7,0},{8,15},{9,14},{10,... | collective-permute-start | bytes 196616 | tf_op jit(solution)/shard_map/ppermute | solution.py:474
  31.9 0.4 collective-permute-start.2
  32.3 1.3 %collective-permute-start.3 = (s16[4,16,512]{2,1,0:T(8,128)(2,1)S(1)}, s16[4,16,512]{2,1,0:T(8,128)(2,1)S(1)}, u32[]{:S(2)}, u32[]{:S(2)}) collective-permute-start(s16[4,16,512]{2,1,0:T(8,128)(2,1)S(1)} %get-tuple-element.15), channel_id=1, source_target_pairs={{0,5},{1,4},{2,7},{3,6},{4,1},{5,0},{6,3},{7,2},{8,13},{9,12},{10,... | collective-permute-start | bytes 196616 | tf_op jit(solution)/shard_map/ppermute | solution.py:474
  33.7 0.4 collective-permute-start.4
  34.0 1.4 %collective-permute-start.5 = (s16[4,16,512]{2,1,0:T(8,128)(2,1)S(1)}, s16[4,16,512]{2,1,0:T(8,128)(2,1)S(1)}, u32[]{:S(2)}, u32[]{:S(2)}) collective-permute-start(s16[4,16,512]{2,1,0:T(8,128)(2,1)S(1)} %get-tuple-element.17), channel_id=1, source_target_pairs={{0,3},{1,2},{2,1},{3,0},{4,7},{5,6},{6,5},{7,4},{8,11},{9,10},{10,... | collective-permute-start | bytes 196616 | tf_op jit(solution)/shard_map/ppermute | solution.py:474
  35.4 5.7 %collective-permute-done.1.refs_0_ = s16[4,16,512]{2,1,0:T(8,128)(2,1)S(1)} collective-permute-done((s16[4,16,512]{2,1,0:T(8,128)(2,1)S(1)}, s16[4,16,512]{2,1,0:T(8,128)(2,1)S(1)}, u32[]{:S(2)}, u32[]{:S(2)}) %collective-permute-start.1) | collective-permute-done | bytes 65568 | tf_op jit(solution)/shard_map/ppermute | solution.py:474
  41.1 1.4 %collective-permute-start.6 = (s16[4,16,512]{2,1,0:T(8,128)(2,1)S(1)}, s16[4,16,512]{2,1,0:T(8,128)(2,1)S(1)}, u32[]{:S(2)}, u32[]{:S(2)}) collective-permute-start(s16[4,16,512]{2,1,0:T(8,128)(2,1)S(1)} %get-tuple-element.18), channel_id=1, source_target_pairs={{0,2},{1,3},{2,0},{3,1},{4,6},{5,7},{6,4},{7,5},{8,10},{9,11},{10,... | collective-permute-start | bytes 196616 | tf_op jit(solution)/shard_map/ppermute | solution.py:474
  42.5 0.4 collective-permute-done.2.refs_1_
  42.9 0.0 collective-permute-start.7
  42.9 1.4 %collective-permute-done.3.refs_2_ = s16[4,16,512]{2,1,0:T(8,128)(2,1)S(1)} collective-permute-done((s16[4,16,512]{2,1,0:T(8,128)(2,1)S(1)}, s16[4,16,512]{2,1,0:T(8,128)(2,1)S(1)}, u32[]{:S(2)}, u32[]{:S(2)}) %collective-permute-start.3) | collective-permute-done | bytes 65568 | tf_op jit(solution)/shard_map/ppermute | solution.py:474
  44.3 2.4 %collective-permute-done.4.refs_3_ = s16[4,16,512]{2,1,0:T(8,128)(2,1)S(1)} collective-permute-done((s16[4,16,512]{2,1,0:T(8,128)(2,1)S(1)}, s16[4,16,512]{2,1,0:T(8,128)(2,1)S(1)}, u32[]{:S(2)}, u32[]{:S(2)}) %collective-permute-start.4) | collective-permute-done | bytes 65568 | tf_op jit(solution)/shard_map/ppermute | solution.py:474
  46.7 0.0 collective-permute-done.5.refs_4_
  46.7 0.0 collective-permute-done.6.refs_5_
  46.7 0.0 collective-permute-done.7.refs_6_
  46.7 0.0 all-to-all-done.code_any
  46.7 0.0 copy-done.4
  46.7 2.0 %composite.1 = f32[4,16,512]{2,1,0:T(8,128)} custom-call(s32[16]{0:T(128)S(1)} %copy-done.4, f32[4]{0:T(128)S(1)} %copy-done.1, s16[16,4,16,512]{3,2,1,0:T(8,128)(2,1)S(1)} %all-to-all-done.code_any, s16[4,16,512]{2,1,0:T(8,128)(2,1)S(1)} %collective-permute-done.1.refs_0_, s16[4,16,512]{2,1,0:T(8,128)(2,1)S(1)} %collective-permute-done.2.refs_1_, ...), custom_call_target="tpu_custom_call" | custom-call | tf_op jit(solution)/shard_map/composite/pallas_call | solution.py:445
Async XLA Ops:
  0.0 8.7 %copy-start.2 = (s32[128]{0:T(128)S(1)}, s32[128]{0:T(128)}, u32[]{:S(2)}) copy-start(s32[128]{0:T(128)} %start_any.5) | copy-start | bytes 1540
  0.0 8.7 %copy-start.3 = (s32[128]{0:T(128)S(1)}, s32[128]{0:T(128)}, u32[]{:S(2)}) copy-start(s32[128]{0:T(128)} %end_any.5) | copy-start | bytes 1540
  0.0 8.7 %copy-start = (f32[16,8192]{1,0:T(8,128)S(1)}, f32[16,8192]{1,0:T(8,128)}, u32[]{:S(2)}) copy-start(f32[16,8192]{1,0:T(8,128)} %jitter_any.5) | copy-start | bytes 1572868
  0.0 8.7 %copy-start.1 = (f32[4]{0:T(128)S(1)}, f32[4]{0:T(128)}, u32[]{:S(2)}) copy-start(f32[4]{0:T(128)} %transfer_any.7) | copy-start | bytes 52
  1.0 7.6 %collective-permute-start = (bf16[16,8192]{1,0:T(8,128)(2,1)S(1)}, bf16[16,8192]{1,0:T(8,128)(2,1)S(1)}, u32[]{:S(2)}, u32[]{:S(2)}) collective-permute-start(bf16[16,8192]{1,0:T(8,128)(2,1)S(1)} %slice_bitcast_fusion), channel_id=1, source_target_pairs={{1,0},{2,1},{3,2},{4,3},{5,4},{6,5},{7,6},{8,7},{9,8},{10,9},{11,1... | collective-permute-start | bytes 786440 | tf_op jit(solution)/shard_map/ppermute | solution.py:35
  12.8 33.8 %copy-start.4 = (s32[16]{0:T(128)S(1)}, s32[16]{0:T(128)}, u32[]{:S(2)}) copy-start(s32[16]{0:T(128)} %order_any.1) | copy-start | bytes 196
  12.8 33.8 %all-to-all-start = ((s16[16,4,16,512]{3,2,1,0:T(8,128)(2,1)}), s16[16,4,16,512]{3,2,1,0:T(8,128)(2,1)S(1)}, u32[]{:S(2)}, u32[]{:S(2)}) async-start(s16[16,4,16,512]{3,2,1,0:T(8,128)(2,1)} %close.1.far_any), calls=%async_computation | async-start | bytes 2097152 | tf_op jit(solution)/shard_map/all_to_all | solution.py:473
  29.3 11.8 %collective-permute-start.1 = (s16[4,16,512]{2,1,0:T(8,128)(2,1)S(1)}, s16[4,16,512]{2,1,0:T(8,128)(2,1)S(1)}, u32[]{:S(2)}, u32[]{:S(2)}) collective-permute-start(s16[4,16,512]{2,1,0:T(8,128)(2,1)S(1)} %get-tuple-element.13), channel_id=1, source_target_pairs={{0,7},{1,6},{2,5},{3,4},{4,3},{5,2},{6,1},{7,0},{8,15},{9,14},{10,... | collective-permute-start | bytes 196616 | tf_op jit(solution)/shard_map/ppermute | solution.py:474
  31.9 11.0 %collective-permute-start.2 = (s16[4,16,512]{2,1,0:T(8,128)(2,1)S(1)}, s16[4,16,512]{2,1,0:T(8,128)(2,1)S(1)}, u32[]{:S(2)}, u32[]{:S(2)}) collective-permute-start(s16[4,16,512]{2,1,0:T(8,128)(2,1)S(1)} %get-tuple-element.14), channel_id=1, source_target_pairs={{0,6},{1,7},{2,4},{3,5},{4,2},{5,3},{6,0},{7,1},{8,14},{9,15},{10,... | collective-permute-start | bytes 196616 | tf_op jit(solution)/shard_map/ppermute | solution.py:474
  32.3 12.0 %collective-permute-start.3 = (s16[4,16,512]{2,1,0:T(8,128)(2,1)S(1)}, s16[4,16,512]{2,1,0:T(8,128)(2,1)S(1)}, u32[]{:S(2)}, u32[]{:S(2)}) collective-permute-start(s16[4,16,512]{2,1,0:T(8,128)(2,1)S(1)} %get-tuple-element.15), channel_id=1, source_target_pairs={{0,5},{1,4},{2,7},{3,6},{4,1},{5,0},{6,3},{7,2},{8,13},{9,12},{10,... | collective-permute-start | bytes 196616 | tf_op jit(solution)/shard_map/ppermute | solution.py:474
  33.7 13.0 %collective-permute-start.4 = (s16[4,16,512]{2,1,0:T(8,128)(2,1)S(1)}, s16[4,16,512]{2,1,0:T(8,128)(2,1)S(1)}, u32[]{:S(2)}, u32[]{:S(2)}) collective-permute-start(s16[4,16,512]{2,1,0:T(8,128)(2,1)S(1)} %get-tuple-element.16), channel_id=1, source_target_pairs={{0,4},{1,5},{2,6},{3,7},{4,0},{5,1},{6,2},{7,3},{8,12},{9,13},{10,... | collective-permute-start | bytes 196616 | tf_op jit(solution)/shard_map/ppermute | solution.py:474
  34.0 12.6 %collective-permute-start.5 = (s16[4,16,512]{2,1,0:T(8,128)(2,1)S(1)}, s16[4,16,512]{2,1,0:T(8,128)(2,1)S(1)}, u32[]{:S(2)}, u32[]{:S(2)}) collective-permute-start(s16[4,16,512]{2,1,0:T(8,128)(2,1)S(1)} %get-tuple-element.17), channel_id=1, source_target_pairs={{0,3},{1,2},{2,1},{3,0},{4,7},{5,6},{6,5},{7,4},{8,11},{9,10},{10,... | collective-permute-start | bytes 196616 | tf_op jit(solution)/shard_map/ppermute | solution.py:474
  41.1 5.6 %collective-permute-start.6 = (s16[4,16,512]{2,1,0:T(8,128)(2,1)S(1)}, s16[4,16,512]{2,1,0:T(8,128)(2,1)S(1)}, u32[]{:S(2)}, u32[]{:S(2)}) collective-permute-start(s16[4,16,512]{2,1,0:T(8,128)(2,1)S(1)} %get-tuple-element.18), channel_id=1, source_target_pairs={{0,2},{1,3},{2,0},{3,1},{4,6},{5,7},{6,4},{7,5},{8,10},{9,11},{10,... | collective-permute-start | bytes 196616 | tf_op jit(solution)/shard_map/ppermute | solution.py:474
  42.9 3.8 %collective-permute-start.7 = (s16[4,16,512]{2,1,0:T(8,128)(2,1)S(1)}, s16[4,16,512]{2,1,0:T(8,128)(2,1)S(1)}, u32[]{:S(2)}, u32[]{:S(2)}) collective-permute-start(s16[4,16,512]{2,1,0:T(8,128)(2,1)S(1)} %get-tuple-element.19), channel_id=1, source_target_pairs={{0,1},{1,0},{2,3},{3,2},{4,5},{5,4},{6,7},{7,6},{8,9},{9,8},{10,11... | collective-permute-start | bytes 196616 | tf_op jit(solution)/shard_map/ppermute | solution.py:474
